TPU v7x, 512 devices: a whole 4x4x16 slice. The times are simulated.
512 devices in a mesh: shot: 4 (over x), gx: 4 (over y_lo, core), gy: 32 (over y_hi, z).
Axes of the slice: x: 4, y: 4 (y_hi: 2, y_lo: 2; y = y_hi * 2 + y_lo), z: 16, core: 2. Of those that a mesh axis runs over, the one named last changes fastest.
Arguments:
- model_vel2: float32 [128, 512, 512], P('gx', 'gy', 'shot'), may hold values from 0.04 to 0.18
- offsets: int32 [4], P('shot'), may hold values from 0 to 256
- wave_prev: float32 [4, 128, 512, 256], P('shot', 'gx', 'gy'), may hold values from -6 to 6
- wave_cur: float32 [4, 128, 512, 256], P('shot', 'gx', 'gy'), may hold values from -1.5 to 1.5
- adj_cur: float32 [4, 128, 512, 256], P('shot', 'gx', 'gy'), may hold values from -1.5 to 1.5
- adj_next: float32 [4, 128, 512, 256], P('shot', 'gx', 'gy'), may hold values from -0.6 to 0.6
- src_cell: int32 [4, 3], P('shot'), may hold values from 0 to 511, as said below
- src_amp: float32 [4, 2], P('shot'), may hold values from -32 to 32
- rec_cell: int32 [4, 256, 3], P('shot'), may hold values from 0 to 511, as said below
- rec_res: float32 [4, 256, 2], P('shot'), may hold values from -4 to 4
Outputs:
- model_grad: float32 [128, 512, 512], P('gx', 'gy', 'shot')
- adj_out: float32 [4, 128, 512, 256], P('shot', 'gx', 'gy')
Inputs may be any that keep to these rules, and one draw needn't show every extreme that they name: Each shot group's aperture lies inside the model's depth: offsets[s] + 256 <= 512. `src_cell`: each row is a cell (x, y, z) of the aperture: 0 <= x < 128, 0 <= y < 512, 0 <= z < 256. `rec_cell`: each row is a cell (x, y, z) of the aperture: 0 <= x < 128, 0 <= y < 512, 0 <= z < 256; receivers may coincide.
All inputs are finite; a program needn't handle non-finite values.
Results may differ from a plain program's by a relative error of at most 0.0065.
Values sent between devices are 32-bit elements; how exact they have to be, the bound alone decides.
No kernel may reach another device: no remote copies, remote signals or barrier semaphores. Data moves between devices by JAX's collectives and lax.ppermute only.
A program may use at most 64 MiB of HBM per device.

v0:
```python
import jax
import jax.numpy as jnp
from jax import lax
from jax.sharding import PartitionSpec as P

COEF = (-205.0 / 72.0, 8.0 / 5.0, -1.0 / 5.0, 8.0 / 315.0, -1.0 / 560.0)


def extended(value, sides, width):
    for axis, dim in sides:
        size, length = (lax.axis_size(axis), value.shape[dim])
        up = [(i, (i + 1) % size) for i in range(size - 1)]
        down = [(j, i) for i, j in up]
        last = lax.slice_in_dim(value, length - width, length, axis=dim)
        leading = lax.slice_in_dim(value, 0, width, axis=dim)
        before = lax.ppermute(last, axis, up)
        after = lax.ppermute(leading, axis, down)
        value = jnp.concatenate([before, value, after], axis=dim)
    return value


def stencil(ext):
    size_x = ext.shape[0] - 8
    size_y = ext.shape[1] - 8
    depth = ext.shape[2]
    full = jnp.pad(ext, ((0, 0), (0, 0), (4, 4)))
    centre = full[4 : 4 + size_x, 4 : 4 + size_y, 4 : 4 + depth]
    total = 3.0 * COEF[0] * centre
    for k in range(1, 5):
        near = (
            full[4 + k : 4 + k + size_x, 4 : 4 + size_y, 4 : 4 + depth]
            + full[4 - k : 4 - k + size_x, 4 : 4 + size_y, 4 : 4 + depth]
        )
        near = (
            near
            + full[4 : 4 + size_x, 4 + k : 4 + k + size_y, 4 : 4 + depth]
            + full[4 : 4 + size_x, 4 - k : 4 - k + size_y, 4 : 4 + depth]
        )
        near = (
            near
            + full[4 : 4 + size_x, 4 : 4 + size_y, 4 + k : 4 + k + depth]
            + full[4 : 4 + size_x, 4 : 4 + size_y, 4 - k : 4 - k + depth]
        )
        total = total + COEF[k] * near
    return total


def inject(field, cells, amounts, base_x, base_y, margin):
    local_x = cells[:, 0] - base_x + margin
    local_y = cells[:, 1] - base_y + margin
    inside = (
        (local_x >= 0) & (local_x < field.shape[0]) & (local_y >= 0) & (local_y < field.shape[1])
    )
    local_x = jnp.where(inside, local_x, field.shape[0])
    return field.at[local_x, local_y, cells[:, 2]].add(amounts, mode="drop")


def forward_edges(field):
    return stencil(extended(field, (("gx", 0), ("gy", 1)), 4))


def closing_edges(field):
    return stencil(extended(field, (("gx", 0), ("gy", 1)), 4))


def adjoint_edges(field):
    return stencil(extended(field, (("gx", 0), ("gy", 1)), 4))


def local(
    model_vel2,
    offsets,
    wave_prev,
    wave_cur,
    adj_cur,
    adj_next,
    src_cell,
    src_amp,
    rec_cell,
    rec_res,
):
    cells_x = wave_cur.shape[1]
    cells_y = wave_cur.shape[2]
    depth = wave_cur.shape[3]
    base_x = lax.axis_index("gx") * cells_x
    base_y = lax.axis_index("gy") * cells_y
    start = offsets[0]
    column = lax.all_gather(model_vel2, "shot", axis=2, tiled=True)
    vel = lax.dynamic_slice_in_dim(column, start, depth, 2)
    wave0 = wave_prev[0]
    wave1 = wave_cur[0]
    adj4 = adj_cur[0]
    adj5 = adj_next[0]
    cells = rec_cell[0]
    lap1 = forward_edges(wave1)
    image4 = adjoint_edges(vel * adj4)
    wave2 = 2.0 * wave1 - wave0 + vel * lap1
    wave2 = inject(wave2, src_cell, src_amp[0, 0:1], base_x, base_y, 0)
    adj3 = 2.0 * adj4 - adj5 + image4
    adj3 = inject(adj3, cells, rec_res[0, :, 0], base_x, base_y, 0)
    lap2 = forward_edges(wave2)
    image3 = adjoint_edges(vel * adj3)
    wave3 = 2.0 * wave2 - wave1 + vel * lap2
    wave3 = inject(wave3, src_cell, src_amp[0, 1:2], base_x, base_y, 0)
    lap3 = closing_edges(wave3)
    adj2 = 2.0 * adj3 - adj4 + image3
    adj2 = inject(adj2, cells, rec_res[0, :, 1], base_x, base_y, 0)
    grad = adj4 * lap3 + adj3 * lap2 + adj2 * lap1
    placed = lax.dynamic_update_slice(
        jnp.zeros((cells_x, cells_y, column.shape[2]), jnp.float32),
        grad,
        (jnp.int32(0), jnp.int32(0), start),
    )
    owned = lax.psum_scatter(placed, "shot", scatter_dimension=2, tiled=True)
    return (owned, adj2[None])


def solution(mesh):
    return jax.shard_map(
        local,
        mesh=mesh,
        in_specs=(
            P("gx", "gy", "shot"),
            P("shot"),
            P("shot", "gx", "gy", None),
            P("shot", "gx", "gy", None),
            P("shot", "gx", "gy", None),
            P("shot", "gx", "gy", None),
            P("shot", None),
            P("shot", None),
            P("shot", None, None),
            P("shot", None, None),
        ),
        out_specs=(P("gx", "gy", "shot"), P("shot", "gx", "gy", None)),
        check_vma=False,
    )
```

profile of v0, /device:TPU:24, one launch (start us, length us, event | category | flops | bytes accessed | tf_op | source)
XLA Modules:
  0.0 222.7 jit_solution(3145218879666455632)
XLA Ops:
  8.9 2.1 collective-permute-start
  11.0 2.2 %collective-permute-start.1 = (f32[4,16,256]{2,1,0:T(8,128)S(1)}, f32[4,16,256]{2,1,0:T(8,128)S(1)}, u32[]{:S(2)}, u32[]{:S(2)}) collective-permute-start(f32[4,16,256]{2,1,0:T(8,128)S(1)} %get-tuple-element.58), channel_id=1, source_target_pairs={{0,32},{32,64},{64,96},{1,33},{33,65},{65,97},{2,34},{34,66},{66,9... | collective-permute-start | bytes 196616 | tf_op jit(solution)/shard_map/ppermute | solution.py:16
  17.6 11.9 %collective-permute-start.2 = (f32[40,4,256]{2,1,0:T(4,128)S(1)}, f32[40,4,256]{2,1,0:T(4,128)S(1)}, u32[]{:S(2)}, u32[]{:S(2)}) collective-permute-start(f32[40,4,256]{2,1,0:T(4,128)S(1)} %get-tuple-element.49), channel_id=1, source_target_pairs={{1,0},{2,1},{3,2},{4,3},{5,4},{6,5},{7,6},{8,7},{9,8},{10,9},{11,1... | collective-permute-start | bytes 491528 | tf_op jit(solution)/shard_map/ppermute | solution.py:17
  29.6 1.9 collective-permute-start.3
  36.7 3.7 %collective-permute-done.3 = f32[40,4,256]{2,1,0:T(4,128)S(1)} collective-permute-done((f32[40,4,256]{2,1,0:T(4,128)S(1)}, f32[40,4,256]{2,1,0:T(4,128)S(1)}, u32[]{:S(2)}, u32[]{:S(2)}) %collective-permute-start.3) | collective-permute-done | bytes 163872 | tf_op jit(solution)/shard_map/ppermute | solution.py:16
  42.6 5.3 %all-gather.2.cloned.1.call-done = f32[32,16,512]{2,1,0:T(8,128)} async-done(((f32[32,16,128]{2,1,0:T(8,128)}), f32[32,16,512]{2,1,0:T(8,128)}) %all-gather.2.cloned.1.call-update) | async-done | bytes 1048592 | tf_op jit(solution)/shard_map/all_gather | solution.py:88
  47.9 1.5 bitcast_multiply_fusion
  49.4 1.9 collective-permute-start.12
  51.3 2.4 %collective-permute-start.13 = (f32[4,16,256]{2,1,0:T(8,128)S(1)}, f32[4,16,256]{2,1,0:T(8,128)S(1)}, u32[]{:S(2)}, u32[]{:S(2)}) collective-permute-start(f32[4,16,256]{2,1,0:T(8,128)S(1)} %get-tuple-element.53), channel_id=1, source_target_pairs={{0,32},{32,64},{64,96},{1,33},{33,65},{65,97},{2,34},{34,66},{66,9... | collective-permute-start | bytes 196616 | tf_op jit(solution)/shard_map/ppermute | solution.py:16
  53.7 4.7 %fusion.156 = (f32[32,16,256]{2,1,0:T(8,128)S(1)}, f32[32,16,256]{2,1,0:T(8,128)}) fusion(f32[1,32,16,256]{3,2,1,0:T(8,128)S(1)} %copy-done.11, f32[32,16,512]{2,1,0:T(8,128)} %all-gather.2.cloned.1.call-done, s32[]{:T(128)S(6)} %select_n.42, f32[1,32,16,256]{3,2,1,0:T(8,128)S(1)} %copy-done, f32[40,24,264]{2,1,0:T(8,128)S(1)} %select_maximum_fusion.16, ...), kind=kLoop, calls=%fused_computation.282 | loop fusion | flops 5373952 | bytes 11665412 | tf_op jit(solution)/shard_map/add | solution.py:97
  61.8 3.2 %collective-permute-start.4 = (f32[4,16,256]{2,1,0:T(8,128)S(1)}, f32[4,16,256]{2,1,0:T(8,128)S(1)}, u32[]{:S(2)}, u32[]{:S(2)}) collective-permute-start(f32[4,16,256]{2,1,0:T(8,128)S(1)} %get-tuple-element.57), channel_id=1, source_target_pairs={{32,0},{64,32},{96,64},{33,1},{65,33},{97,65},{34,2},{66,34},{98,6... | collective-permute-start | bytes 196616 | tf_op jit(solution)/shard_map/ppermute | solution.py:17
  64.9 1.9 collective-permute-start.5
  66.9 6.8 %collective-permute-start.14 = (f32[40,4,256]{2,1,0:T(4,128)S(1)}, f32[40,4,256]{2,1,0:T(4,128)S(1)}, u32[]{:S(2)}, u32[]{:S(2)}) collective-permute-start(f32[40,4,256]{2,1,0:T(4,128)S(1)} %get-tuple-element.37), channel_id=1, source_target_pairs={{1,0},{2,1},{3,2},{4,3},{5,4},{6,5},{7,6},{8,7},{9,8},{10,9},{11,1... | collective-permute-start | bytes 491528 | tf_op jit(solution)/shard_map/ppermute | solution.py:17
  73.8 1.9 collective-permute-start.15
  76.5 7.5 %collective-permute-start.6 = (f32[40,4,256]{2,1,0:T(4,128)}, f32[40,4,256]{2,1,0:T(4,128)S(1)}, u32[]{:S(2)}, u32[]{:S(2)}) collective-permute-start(f32[40,4,256]{2,1,0:T(4,128)} %get-tuple-element.45), channel_id=1, source_target_pairs={{1,0},{2,1},{3,2},{4,3},{5,4},{6,5},{7,6},{8,7},{9,8},{10,9},{11,1... | collective-permute-start | bytes 491528 | tf_op jit(solution)/shard_map/ppermute | solution.py:17
  84.0 1.9 collective-permute-start.7
  87.3 1.9 fusion.39
  89.2 16.3 %scatter_fusion = f32[32,16,256]{2,1,0:T(8,128)S(1)} fusion(f32[32,16,256]{2,1,0:T(8,128)S(1)} %fusion.39, s32[256]{0:T(256)S(1)} %bitcast.46, f32[256]{0:T(256)S(1)} %bitcast.55), kind=kCustom, calls=%fused_computation | custom fusion | flops 256 | bytes 6144 | tf_op jit(solution)/shard_map/scatter-add | solution.py:55
  106.9 2.2 collective-permute-start.16
  109.1 2.1 collective-permute-start.17
  112.6 2.6 %multiply_add_fusion = (f32[32,16,256]{2,1,0:T(8,128)S(1)}, f32[32,16,256]{2,1,0:T(8,128)}) fusion(f32[32,16,256]{2,1,0:T(8,128)S(1)} %scatter-add.24, f32[32,16,512]{2,1,0:T(8,128)S(1)} %copy-done.7, s32[]{:T(128)S(6)} %select_n.42, f32[1,32,16,256]{3,2,1,0:T(8,128)S(1)} %copy-done, f32[40,24,264]{2,1,0:T(8,128)S(1)} %select_maximum_fusion.12, ...), kind=kLoop, calls=%fused_computation.286 | loop fusion | flops 5373952 | bytes 11141124 | tf_op jit(solution)/shard_map/add | solution.py:103
  118.5 3.4 %collective-permute-start.8 = (f32[4,16,256]{2,1,0:T(8,128)S(1)}, f32[4,16,256]{2,1,0:T(8,128)S(1)}, u32[]{:S(2)}, u32[]{:S(2)}) collective-permute-start(f32[4,16,256]{2,1,0:T(8,128)S(1)} %get-tuple-element.54), channel_id=1, source_target_pairs={{32,0},{64,32},{96,64},{33,1},{65,33},{97,65},{34,2},{66,34},{98,6... | collective-permute-start | bytes 196616 | tf_op jit(solution)/shard_map/ppermute | solution.py:17
  121.9 1.9 collective-permute-start.9
  123.9 7.9 %collective-permute-start.18 = (f32[40,4,256]{2,1,0:T(4,128)S(1)}, f32[40,4,256]{2,1,0:T(4,128)S(1)}, u32[]{:S(2)}, u32[]{:S(2)}) collective-permute-start(f32[40,4,256]{2,1,0:T(4,128)S(1)} %get-tuple-element.33), channel_id=1, source_target_pairs={{1,0},{2,1},{3,2},{4,3},{5,4},{6,5},{7,6},{8,7},{9,8},{10,9},{11,1... | collective-permute-start | bytes 491528 | tf_op jit(solution)/shard_map/ppermute | solution.py:17
  131.8 1.9 collective-permute-start.19
  134.5 7.5 %collective-permute-start.10 = (f32[40,4,256]{2,1,0:T(4,128)}, f32[40,4,256]{2,1,0:T(4,128)S(1)}, u32[]{:S(2)}, u32[]{:S(2)}) collective-permute-start(f32[40,4,256]{2,1,0:T(4,128)} %get-tuple-element.41), channel_id=1, source_target_pairs={{1,0},{2,1},{3,2},{4,3},{5,4},{6,5},{7,6},{8,7},{9,8},{10,9},{11,1... | collective-permute-start | bytes 491528 | tf_op jit(solution)/shard_map/ppermute | solution.py:17
  142.0 2.1 collective-permute-start.11
  145.3 2.5 %fusion.10 = f32[32,16,256]{2,1,0:T(8,128)} fusion(f32[32,16,256]{2,1,0:T(8,128)S(1)} %dynamic-slice_multiply_fusion, f32[4,16,256]{2,1,0:T(8,128)S(1)} %collective-permute-done.17, f32[4,16,256]{2,1,0:T(8,128)S(1)} %collective-permute-done.16, f32[40,24,264]{2,1,0:T(8,128)S(1)} %select_maximum_fusion, f32[40,20,256]{2,1,0:T(8,128)S(1)} %get-tuple-element.31, ...), kind=kLoop, calls=%fused_computation.104 | loop fusion | flops 5242880 | bytes 10616832 | tf_op jit(solution)/shard_map/add | solution.py:106
  147.9 34.0 %scatter_fusion.1 = f32[32,16,256]{2,1,0:T(8,128)} fusion(f32[32,16,256]{2,1,0:T(8,128)} %fusion.10, s32[256]{0:T(256)S(1)} %bitcast.47, f32[256]{0:T(256)S(1)} %bitcast.54), kind=kCustom, calls=%fused_computation.1 | custom fusion | flops 256 | bytes 6144 | tf_op jit(solution)/shard_map/scatter-add | solution.py:55
  183.5 2.0 fusion.70
  185.6 6.0 %dynamic_update_slice.3 = f32[32,16,512]{2,1,0:T(8,128)S(1)} dynamic-update-slice(f32[32,16,512]{2,1,0:T(8,128)S(1)} %broadcast_in_dim.10, f32[32,16,256]{2,1,0:T(8,128)S(1)} %fusion.70, s32[]{:T(128)} %constant.65.clone.1, s32[]{:T(128)} %constant.65.clone.1, s32[]{:T(128)S(6)} %select_n.42) | dynamic-update-slice | bytes 1048580 | tf_op jit(solution)/shard_map/dynamic_update_slice | solution.py:109
  192.7 23.2 %reduce-scatter.2.cloned.1.call-done = f32[32,16,128]{2,1,0:T(8,128)} async-done(((f32[32,16,512]{2,1,0:T(8,128)}), f32[32,16,128]{2,1,0:T(8,128)}) %reduce-scatter.2.cloned.1.call-update) | async-done | bytes 262160 | tf_op jit(solution)/shard_map/reduce_scatter | solution.py:114
  (87 shorter events, 20.7 us)
Async XLA Ops:
  7.2 28.8 %copy-start.15 = (s32[3]{0:T(128)S(1)}, s32[3]{0:T(128)}, u32[]{:S(2)}) copy-start(s32[3]{0:T(128)} %constant.81.clone.1) | copy-start | bytes 40
  7.2 33.2 %copy-start = (f32[1,32,16,256]{3,2,1,0:T(8,128)S(1)}, f32[1,32,16,256]{3,2,1,0:T(8,128)}, u32[]{:S(2)}) copy-start(f32[1,32,16,256]{3,2,1,0:T(8,128)} %param.17) | copy-start | bytes 1572868
  7.2 24.3 %copy-start.14 = (f32[1,2]{1,0:T(1,128)S(1)}, f32[1,2]{1,0:T(1,128)}, u32[]{:S(2)}) copy-start(f32[1,2]{1,0:T(1,128)} %param.21) | copy-start | bytes 28
  7.2 40.7 %all-gather.2.cloned.1.call-start = ((), (), s32[]{:S(2)}) async-start(), calls=%async_computation.1 | async-start | bytes 1310720 | tf_op jit(solution)/shard_map/all_gather | solution.py:88
  7.9 208.0 %reduce-scatter.2.cloned.1.call-start = ((), (), s32[]{:S(2)}) async-start(), calls=%async_computation.2 | async-start | bytes 1310720 | tf_op jit(solution)/shard_map/reduce_scatter | solution.py:114
  8.9 6.4 %collective-permute-start = (f32[4,16,256]{2,1,0:T(8,128)S(1)}, f32[4,16,256]{2,1,0:T(8,128)S(1)}, u32[]{:S(2)}, u32[]{:S(2)}) collective-permute-start(f32[4,16,256]{2,1,0:T(8,128)S(1)} %get-tuple-element.59), channel_id=1, source_target_pairs={{32,0},{64,32},{96,64},{33,1},{65,33},{97,65},{34,2},{66,34},{98,6... | collective-permute-start | bytes 196616 | tf_op jit(solution)/shard_map/ppermute | solution.py:17
  11.0 5.6 %collective-permute-start.1 = (f32[4,16,256]{2,1,0:T(8,128)S(1)}, f32[4,16,256]{2,1,0:T(8,128)S(1)}, u32[]{:S(2)}, u32[]{:S(2)}) collective-permute-start(f32[4,16,256]{2,1,0:T(8,128)S(1)} %get-tuple-element.58), channel_id=1, source_target_pairs={{0,32},{32,64},{64,96},{1,33},{33,65},{65,97},{2,34},{34,66},{66,9... | collective-permute-start | bytes 196616 | tf_op jit(solution)/shard_map/ppermute | solution.py:16
  17.6 19.1 %collective-permute-start.2 = (f32[40,4,256]{2,1,0:T(4,128)S(1)}, f32[40,4,256]{2,1,0:T(4,128)S(1)}, u32[]{:S(2)}, u32[]{:S(2)}) collective-permute-start(f32[40,4,256]{2,1,0:T(4,128)S(1)} %get-tuple-element.49), channel_id=1, source_target_pairs={{1,0},{2,1},{3,2},{4,3},{5,4},{6,5},{7,6},{8,7},{9,8},{10,9},{11,1... | collective-permute-start | bytes 491528 | tf_op jit(solution)/shard_map/ppermute | solution.py:17
  29.6 10.8 %collective-permute-start.3 = (f32[40,4,256]{2,1,0:T(4,128)S(1)}, f32[40,4,256]{2,1,0:T(4,128)S(1)}, u32[]{:S(2)}, u32[]{:S(2)}) collective-permute-start(f32[40,4,256]{2,1,0:T(4,128)S(1)} %get-tuple-element.48), channel_id=1, source_target_pairs={{0,1},{1,2},{2,3},{3,4},{4,5},{5,6},{6,7},{7,8},{8,9},{9,10},{10,1... | collective-permute-start | bytes 491528 | tf_op jit(solution)/shard_map/ppermute | solution.py:16
  41.8 6.1 %copy-start.3 = (f32[1,32,16,256]{3,2,1,0:T(8,128)S(1)}, f32[1,32,16,256]{3,2,1,0:T(8,128)}, u32[]{:S(2)}) copy-start(f32[1,32,16,256]{3,2,1,0:T(8,128)} %param.18) | copy-start | bytes 1572868
  47.9 5.8 %copy-start.1 = (f32[40,20,256]{2,1,0:T(8,128)S(1)}, f32[40,20,256]{2,1,0:T(8,128)}, u32[]{:S(2)}) copy-start(f32[40,20,256]{2,1,0:T(8,128)} %get-tuple-element.46) | copy-start | bytes 2457604
  47.9 5.8 %copy-start.11 = (f32[1,32,16,256]{3,2,1,0:T(8,128)S(1)}, f32[1,32,16,256]{3,2,1,0:T(8,128)}, u32[]{:S(2)}) copy-start(f32[1,32,16,256]{3,2,1,0:T(8,128)} %param.16) | copy-start | bytes 1572868
  49.4 17.5 %collective-permute-start.12 = (f32[4,16,256]{2,1,0:T(8,128)S(1)}, f32[4,16,256]{2,1,0:T(8,128)S(1)}, u32[]{:S(2)}, u32[]{:S(2)}) collective-permute-start(f32[4,16,256]{2,1,0:T(8,128)S(1)} %get-tuple-element.52), channel_id=1, source_target_pairs={{32,0},{64,32},{96,64},{33,1},{65,33},{97,65},{34,2},{66,34},{98,6... | collective-permute-start | bytes 196616 | tf_op jit(solution)/shard_map/ppermute | solution.py:17
  51.3 15.6 %collective-permute-start.13 = (f32[4,16,256]{2,1,0:T(8,128)S(1)}, f32[4,16,256]{2,1,0:T(8,128)S(1)}, u32[]{:S(2)}, u32[]{:S(2)}) collective-permute-start(f32[4,16,256]{2,1,0:T(8,128)S(1)} %get-tuple-element.53), channel_id=1, source_target_pairs={{0,32},{32,64},{64,96},{1,33},{33,65},{65,97},{2,34},{34,66},{66,9... | collective-permute-start | bytes 196616 | tf_op jit(solution)/shard_map/ppermute | solution.py:16
  53.7 21.9 %copy-start.13 = (f32[1,256,2]{1,2,0:T(2,128)S(1)}, f32[1,256,2]{1,2,0:T(2,128)}, u32[]{:S(2)}) copy-start(f32[1,256,2]{1,2,0:T(2,128)} %param.23) | copy-start | bytes 6148
  61.8 13.9 %collective-permute-start.4 = (f32[4,16,256]{2,1,0:T(8,128)S(1)}, f32[4,16,256]{2,1,0:T(8,128)S(1)}, u32[]{:S(2)}, u32[]{:S(2)}) collective-permute-start(f32[4,16,256]{2,1,0:T(8,128)S(1)} %get-tuple-element.57), channel_id=1, source_target_pairs={{32,0},{64,32},{96,64},{33,1},{65,33},{97,65},{34,2},{66,34},{98,6... | collective-permute-start | bytes 196616 | tf_op jit(solution)/shard_map/ppermute | solution.py:17
  64.9 10.8 %collective-permute-start.5 = (f32[4,16,256]{2,1,0:T(8,128)S(1)}, f32[4,16,256]{2,1,0:T(8,128)S(1)}, u32[]{:S(2)}, u32[]{:S(2)}) collective-permute-start(f32[4,16,256]{2,1,0:T(8,128)S(1)} %get-tuple-element.56), channel_id=1, source_target_pairs={{0,32},{32,64},{64,96},{1,33},{33,65},{65,97},{2,34},{34,66},{66,9... | collective-permute-start | bytes 196616 | tf_op jit(solution)/shard_map/ppermute | solution.py:16
  66.9 19.0 %collective-permute-start.14 = (f32[40,4,256]{2,1,0:T(4,128)S(1)}, f32[40,4,256]{2,1,0:T(4,128)S(1)}, u32[]{:S(2)}, u32[]{:S(2)}) collective-permute-start(f32[40,4,256]{2,1,0:T(4,128)S(1)} %get-tuple-element.37), channel_id=1, source_target_pairs={{1,0},{2,1},{3,2},{4,3},{5,4},{6,5},{7,6},{8,7},{9,8},{10,9},{11,1... | collective-permute-start | bytes 491528 | tf_op jit(solution)/shard_map/ppermute | solution.py:17
  73.8 12.2 %collective-permute-start.15 = (f32[40,4,256]{2,1,0:T(4,128)S(1)}, f32[40,4,256]{2,1,0:T(4,128)S(1)}, u32[]{:S(2)}, u32[]{:S(2)}) collective-permute-start(f32[40,4,256]{2,1,0:T(4,128)S(1)} %get-tuple-element.36), channel_id=1, source_target_pairs={{0,1},{1,2},{2,3},{3,4},{4,5},{5,6},{6,7},{7,8},{8,9},{9,10},{10,1... | collective-permute-start | bytes 491528 | tf_op jit(solution)/shard_map/ppermute | solution.py:16
  76.5 34.7 %collective-permute-start.6 = (f32[40,4,256]{2,1,0:T(4,128)}, f32[40,4,256]{2,1,0:T(4,128)S(1)}, u32[]{:S(2)}, u32[]{:S(2)}) collective-permute-start(f32[40,4,256]{2,1,0:T(4,128)} %get-tuple-element.45), channel_id=1, source_target_pairs={{1,0},{2,1},{3,2},{4,3},{5,4},{6,5},{7,6},{8,7},{9,8},{10,9},{11,1... | collective-permute-start | bytes 491528 | tf_op jit(solution)/shard_map/ppermute | solution.py:17
  84.0 27.2 %collective-permute-start.7 = (f32[40,4,256]{2,1,0:T(4,128)}, f32[40,4,256]{2,1,0:T(4,128)S(1)}, u32[]{:S(2)}, u32[]{:S(2)}) collective-permute-start(f32[40,4,256]{2,1,0:T(4,128)} %get-tuple-element.44), channel_id=1, source_target_pairs={{0,1},{1,2},{2,3},{3,4},{4,5},{5,6},{6,7},{7,8},{8,9},{9,10},{10,1... | collective-permute-start | bytes 491528 | tf_op jit(solution)/shard_map/ppermute | solution.py:16
  106.9 17.0 %collective-permute-start.16 = (f32[4,16,256]{2,1,0:T(8,128)S(1)}, f32[4,16,256]{2,1,0:T(8,128)S(1)}, u32[]{:S(2)}, u32[]{:S(2)}) collective-permute-start(f32[4,16,256]{2,1,0:T(8,128)S(1)} %get-tuple-element.50), channel_id=1, source_target_pairs={{32,0},{64,32},{96,64},{33,1},{65,33},{97,65},{34,2},{66,34},{98,6... | collective-permute-start | bytes 196616 | tf_op jit(solution)/shard_map/ppermute | solution.py:17
  109.1 14.8 %collective-permute-start.17 = (f32[4,16,256]{2,1,0:T(8,128)S(1)}, f32[4,16,256]{2,1,0:T(8,128)S(1)}, u32[]{:S(2)}, u32[]{:S(2)}) collective-permute-start(f32[4,16,256]{2,1,0:T(8,128)S(1)} %get-tuple-element.51), channel_id=1, source_target_pairs={{0,32},{32,64},{64,96},{1,33},{33,65},{65,97},{2,34},{34,66},{66,9... | collective-permute-start | bytes 196616 | tf_op jit(solution)/shard_map/ppermute | solution.py:16
  111.4 1.2 copy-start.7
  118.5 15.3 %collective-permute-start.8 = (f32[4,16,256]{2,1,0:T(8,128)S(1)}, f32[4,16,256]{2,1,0:T(8,128)S(1)}, u32[]{:S(2)}, u32[]{:S(2)}) collective-permute-start(f32[4,16,256]{2,1,0:T(8,128)S(1)} %get-tuple-element.54), channel_id=1, source_target_pairs={{32,0},{64,32},{96,64},{33,1},{65,33},{97,65},{34,2},{66,34},{98,6... | collective-permute-start | bytes 196616 | tf_op jit(solution)/shard_map/ppermute | solution.py:17
  121.9 11.8 %collective-permute-start.9 = (f32[4,16,256]{2,1,0:T(8,128)S(1)}, f32[4,16,256]{2,1,0:T(8,128)S(1)}, u32[]{:S(2)}, u32[]{:S(2)}) collective-permute-start(f32[4,16,256]{2,1,0:T(8,128)S(1)} %get-tuple-element.55), channel_id=1, source_target_pairs={{0,32},{32,64},{64,96},{1,33},{33,65},{65,97},{2,34},{34,66},{66,9... | collective-permute-start | bytes 196616 | tf_op jit(solution)/shard_map/ppermute | solution.py:16
  123.9 20.2 %collective-permute-start.18 = (f32[40,4,256]{2,1,0:T(4,128)S(1)}, f32[40,4,256]{2,1,0:T(4,128)S(1)}, u32[]{:S(2)}, u32[]{:S(2)}) collective-permute-start(f32[40,4,256]{2,1,0:T(4,128)S(1)} %get-tuple-element.33), channel_id=1, source_target_pairs={{1,0},{2,1},{3,2},{4,3},{5,4},{6,5},{7,6},{8,7},{9,8},{10,9},{11,1... | collective-permute-start | bytes 491528 | tf_op jit(solution)/shard_map/ppermute | solution.py:17
  131.8 12.3 %collective-permute-start.19 = (f32[40,4,256]{2,1,0:T(4,128)S(1)}, f32[40,4,256]{2,1,0:T(4,128)S(1)}, u32[]{:S(2)}, u32[]{:S(2)}) collective-permute-start(f32[40,4,256]{2,1,0:T(4,128)S(1)} %get-tuple-element.32), channel_id=1, source_target_pairs={{0,1},{1,2},{2,3},{3,4},{4,5},{5,6},{6,7},{7,8},{8,9},{9,10},{10,1... | collective-permute-start | bytes 491528 | tf_op jit(solution)/shard_map/ppermute | solution.py:16
  134.5 47.4 %collective-permute-start.10 = (f32[40,4,256]{2,1,0:T(4,128)}, f32[40,4,256]{2,1,0:T(4,128)S(1)}, u32[]{:S(2)}, u32[]{:S(2)}) collective-permute-start(f32[40,4,256]{2,1,0:T(4,128)} %get-tuple-element.41), channel_id=1, source_target_pairs={{1,0},{2,1},{3,2},{4,3},{5,4},{6,5},{7,6},{8,7},{9,8},{10,9},{11,1... | collective-permute-start | bytes 491528 | tf_op jit(solution)/shard_map/ppermute | solution.py:17
  142.0 39.9 %collective-permute-start.11 = (f32[40,4,256]{2,1,0:T(4,128)S(1)}, f32[40,4,256]{2,1,0:T(4,128)S(1)}, u32[]{:S(2)}, u32[]{:S(2)}) collective-permute-start(f32[40,4,256]{2,1,0:T(4,128)S(1)} %get-tuple-element.40), channel_id=1, source_target_pairs={{0,1},{1,2},{2,3},{3,4},{4,5},{5,6},{6,7},{7,8},{8,9},{9,10},{10,1... | collective-permute-start | bytes 491528 | tf_op jit(solution)/shard_map/ppermute | solution.py:16
  182.0 1.3 copy-start.9
  182.0 1.5 copy-start.10
  (6 other events, 6.5 us)
Sparse Core Ops, SparseCore 0:
  10.1 37.7 all-gather.1
  192.8 23.0 reduce-scatter.1
where the time goes:
time: 225 us; the launch traced here: 223 us
  other arithmetic  76 us (34%)
  starting transfers between devices  74.9 us (33%)
  waiting for transfers between devices  34.1 us (15%)
  between operations  23.7 us (11%)
  local copies, waits for them, and re-layouts  14.1 us (6%)
    ppermute x10, starting transfers between devices, extended(): after = lax.ppermute(leading, axis, down)  54.4 us
    scatter-add x2, other arithmetic, inject(): return field.at[local_x, local_y, cells[:, 2]].add(amounts, mode='drop')  50.2 us
    reduce_scatter x1, waiting for transfers between devices, local(): owned = lax.psum_scatter(placed, 'shot', scatter_dimension=2, tiled=True)  23.2 us
    ppermute x10, starting transfers between devices, extended(): before = lax.ppermute(last, axis, up)  20.4 us
    concatenate x15, other arithmetic, extended(): value = jnp.concatenate([before, value, after], axis=dim)  8.55 us
    dynamic_update_slice x1, local copies, waits for them, and re-layouts, local(): lax.dynamic_update_slice(jnp.zeros((cells_x, cells_y, column.shape[2]), j...  6.03 us
    all_gather x1, waiting for transfers between devices, local(): column = lax.all_gather(model_vel2, 'shot', axis=2, tiled=True)  5.32 us
    ppermute x10, waiting for transfers between devices, extended(): before = lax.ppermute(last, axis, up)  4.92 us
  transfers between devices with their start and end apart: 22, of which 4 were waited for; matrix products, arithmetic and copies ran while one was open for 34% of the time, Pallas kernels for 0%

commit v1 on v0

v1 whole, which is shorter than its diff:
```python
import functools

import jax
import jax.numpy as jnp
from jax import lax
from jax.experimental import pallas as pl
from jax.experimental.pallas import tpu as pltpu
from jax.sharding import PartitionSpec as P

COEF = (-205.0 / 72.0, 8.0 / 5.0, -1.0 / 5.0, 8.0 / 315.0, -1.0 / 560.0)
F32 = jnp.float32
HALF = 128


def swap(value, axis, odd):
    pairs = []
    for i in range(odd, lax.axis_size(axis) - 1, 2):
        pairs += [(i, i + 1), (i + 1, i)]
    return lax.ppermute(value, axis, pairs)


def shift(value, axis, distance):
    size = lax.axis_size(axis)
    return lax.ppermute(value, axis, [(i, (i + distance) % size) for i in range(size)])


def exchange(payload):
    ya, yb, xa, xb = payload
    return swap(ya, "gy", 0), swap(yb, "gy", 1), swap(xa, "gx", 0), swap(xb, "gx", 1)


def call(body, out_shape, scratch=(), smem=0, n_in=0, flops=0):
    vmem = pl.BlockSpec(memory_space=pltpu.VMEM)
    scal = pl.BlockSpec(memory_space=pltpu.SMEM)
    return pl.pallas_call(
        body,
        out_shape=out_shape,
        in_specs=[scal] * smem + [vmem] * n_in,
        out_specs=jax.tree.map(lambda _: vmem, out_shape),
        scratch_shapes=list(scratch),
        compiler_params=pltpu.CompilerParams(vmem_limit_bytes=24 * 1024 * 1024),
        cost_estimate=pl.CostEstimate(flops=flops, bytes_accessed=1 << 20, transcendentals=0),
    )


def shaped(*dims):
    return jax.ShapeDtypeStruct(dims, F32)


def even(axis):
    return lax.rem(lax.axis_index(axis), 2) == 0


def put_edges(field, row, ya, yb, xa, xb, plane):
    even_y, even_x = even("gy"), even("gx")
    size_x, size_y = field.shape[0], field.shape[1]
    first, last = field[:, 0:4, :], field[:, size_y - 4 : size_y, :]
    ya[:, row : row + 4, :] = jnp.where(even_y, last, first)
    yb[:, row : row + 4, :] = jnp.where(even_y, first, last)
    top = size_x - 4
    xa[plane : plane + 4] = field[pl.ds(jnp.where(even_x, top, 0), 4)]
    xb[plane : plane + 4] = field[pl.ds(jnp.where(even_x, 0, top), 4)]


def fill(space, field, halos, row, plane):
    ya, yb, xa, xb = halos
    even_y, even_x = even("gy"), even("gx")
    size_x, size_y = field.shape[0], field.shape[1]
    place_a = jnp.where(even_x, size_x + 4, 0)
    place_b = jnp.where(even_x, 0, size_x + 4)
    for h in range(2):
        z = slice(h * HALF, (h + 1) * HALF)
        space[h, 4 : size_x + 4, 8 : size_y + 8, :] = field[:, :, z]
        space[h, pl.ds(place_a, 4), 8 : size_y + 8, :] = xa[plane : plane + 4, :, z]
        space[h, pl.ds(place_b, 4), 8 : size_y + 8, :] = xb[plane : plane + 4, :, z]
        a, b = ya[:, row : row + 4, z], yb[:, row : row + 4, z]
        space[h, 4 : size_x + 4, 4:8, :] = jnp.where(even_y, b, a)
        space[h, 4 : size_x + 4, size_y + 8 : size_y + 12, :] = jnp.where(even_y, a, b)


def depth_part(field, band, out):
    size_x, size_y, depth = field.shape

    def body(i, _):
        part = field[pl.ds(i * 8, 8)].reshape(8 * size_y, depth)
        done = jnp.dot(part, band[...], precision=lax.Precision.HIGHEST, preferred_element_type=F32)
        out[pl.ds(i * 8, 8)] = done.reshape(8, size_y, depth)
        return 0

    lax.fori_loop(0, size_x // 8, body, 0)


def laplacian(space, depthwise, x, h, size_y):
    centre = space[h, x + 4, 8 : size_y + 8, :]
    total = (3.0 * COEF[0]) * centre + depthwise[x, :, h * HALF : (h + 1) * HALF]
    for k in range(1, 5):
        near = space[h, x + 4 + k, 8 : size_y + 8, :] + space[h, x + 4 - k, 8 : size_y + 8, :]
        near = near + space[h, x + 4, 8 + k : size_y + 8 + k, :] + space[h, x + 4, 8 - k : size_y + 8 - k, :]
        total = total + COEF[k] * near
    return total


def add_source(cell, amount, field):
    size_x, size_y, depth = field.shape
    x = cell[0, 0] - lax.axis_index("gx") * size_x
    y = cell[0, 1] - lax.axis_index("gy") * size_y

    @pl.when((x >= 0) & (x < size_x) & (y >= 0) & (y < size_y))
    def _():
        at = (lax.broadcasted_iota(jnp.int32, (size_y, depth), 0) == y) & (
            lax.broadcasted_iota(jnp.int32, (size_y, depth), 1) == cell[0, 2]
        )
        field[x] = field[x] + jnp.where(at, amount, 0.0)


def edges_kernel(field, ya, yb, xa, xb):
    even_y, even_x = even("gy"), even("gx")
    size_x, size_y = field.shape[0], field.shape[1]
    half = size_x // 2
    for row in range(2):
        x = slice(row * half, (row + 1) * half)
        first, last = field[x, 0:4, :], field[x, size_y - 4 : size_y, :]
        ya[:, row * 4 : row * 4 + 4, :] = jnp.where(even_y, last, first)
        yb[:, row * 4 : row * 4 + 4, :] = jnp.where(even_y, first, last)
    top = size_x - 4
    xa[...] = field[pl.ds(jnp.where(even_x, top, 0), 4)]
    xb[...] = field[pl.ds(jnp.where(even_x, 0, top), 4)]


def tables_kernel(size_x, size_y, cells, res, band, inject0, inject1):
    depth = band.shape[0]
    i = lax.broadcasted_iota(jnp.int32, (depth, depth), 0)
    j = lax.broadcasted_iota(jnp.int32, (depth, depth), 1)
    away = jnp.abs(i - j)
    total = jnp.zeros((depth, depth), F32)
    for k in range(1, 5):
        total = jnp.where(away == k, COEF[k], total)
    band[...] = total
    count = cells.shape[1]
    lanes = 128
    pad = jnp.zeros((count, lanes - 3), jnp.int32)
    where = jnp.concatenate([cells[0], pad], axis=1).astype(F32)
    rows = jnp.transpose(where)[0:8].astype(jnp.int32)
    amounts = jnp.transpose(jnp.concatenate([res[0], jnp.zeros((count, lanes - 2), F32)], axis=1))
    x = rows[0:1, :] - lax.axis_index("gx") * size_x
    y = rows[1:2, :] - lax.axis_index("gy") * size_y
    inside = (x >= 0) & (x < size_x) & (y >= 0) & (y < size_y)
    place = jnp.where(inside, x * size_y + y, -1)
    deep = jnp.where(
        lax.broadcasted_iota(jnp.int32, (count, depth), 1) == cells[0, :, 2:3], 1.0, 0.0
    ).astype(F32)
    for n, out in enumerate((inject0, inject1)):
        for part in range(4):
            size = size_x * size_y // 4
            at = lax.broadcasted_iota(jnp.int32, (size, count), 0) + part * size
            flat = jnp.where(at == place, amounts[n : n + 1, :], 0.0)
            done = jnp.dot(flat, deep, precision=lax.Precision.HIGHEST, preferred_element_type=F32)
            out[part * size_x // 4 : (part + 1) * size_x // 4] = done.reshape(size_x // 4, size_y, depth)


def first_kernel(wave1, band, ya, yb, xa, xb, lap1, space, depthwise):
    size_x, size_y = wave1.shape[0], wave1.shape[1]
    even_y, even_x = even("gy"), even("gx")
    half = size_x // 2
    place_a = jnp.where(even_x, size_x + 4, 0)
    place_b = jnp.where(even_x, 0, size_x + 4)
    for h in range(2):
        z = slice(h * HALF, (h + 1) * HALF)
        space[h, 4 : size_x + 4, 8 : size_y + 8, :] = wave1[:, :, z]
        space[h, pl.ds(place_a, 4), 8 : size_y + 8, :] = xa[:, :, z]
        space[h, pl.ds(place_b, 4), 8 : size_y + 8, :] = xb[:, :, z]
        for row in range(2):
            a, b = ya[:, row * 4 : row * 4 + 4, z], yb[:, row * 4 : row * 4 + 4, z]
            x = slice(4 + row * half, 4 + (row + 1) * half)
            space[h, x, 4:8, :] = jnp.where(even_y, b, a)
            space[h, x, size_y + 8 : size_y + 12, :] = jnp.where(even_y, a, b)
    depth_part(wave1, band, depthwise)

    def body(x, _):
        for h in range(2):
            lap1[x, :, h * HALF : (h + 1) * HALF] = laplacian(space, depthwise, x, h, size_y)
        return 0

    lax.fori_loop(0, size_x, body, 0, unroll=2)


def second_kernel(
    offsets, cell, amp, tile0, tile1, tile2, tile3, lap1, wave0, wave1, adj4,
    vel, wave2, image, ya, yb, xa, xb, column,
):
    size_x, size_y = wave1.shape[0], wave1.shape[1]
    me = lax.axis_index("shot")
    for d, tile in enumerate((tile0, tile1, tile2, tile3)):
        column[lax.rem(me - d + 4, 4)] = tile[...]
    start = offsets[0]
    low = start // HALF
    shift_by = lax.rem(start, HALF)
    back = lax.rem(HALF - shift_by, HALF)
    third = jnp.minimum(low + 2, 3)

    def body(x, _):
        lane = lax.broadcasted_iota(jnp.int32, (size_y, HALF), 1)
        rolled = [pltpu.roll(column[i, x], back, 1) for i in (low, low + 1, third)]
        for h in range(2):
            z = slice(h * HALF, (h + 1) * HALF)
            v = jnp.where(lane < HALF - shift_by, rolled[h], rolled[h + 1])
            vel[x, :, z] = v
            image[x, :, z] = v * adj4[x, :, z]
            wave2[x, :, z] = 2.0 * wave1[x, :, z] - wave0[x, :, z] + v * lap1[x, :, z]
        return 0

    lax.fori_loop(0, size_x, body, 0, unroll=2)
    add_source(cell, amp[0, 0], wave2)
    put_edges(wave2, 0, ya, yb, xa, xb, 0)
    put_edges(image, 4, ya, yb, xa, xb, 4)


def third_kernel(
    cell, amp, ya, yb, xa, xb, wave1, wave2, adj4, adj5, vel, image, band, inject,
    lap2, wave3, adj3, image3, pya, pyb, pxa, pxb, space, depthwise, space2, depthwise2,
):
    size_x, size_y = wave1.shape[0], wave1.shape[1]
    halos = (ya, yb, xa, xb)
    fill(space, wave2, halos, 0, 0)
    fill(space2, image, halos, 4, 4)
    depth_part(wave2, band, depthwise)
    depth_part(image, band, depthwise2)

    def body(x, _):
        for h in range(2):
            z = slice(h * HALF, (h + 1) * HALF)
            v = vel[x, :, z]
            lap = laplacian(space, depthwise, x, h, size_y)
            lap2[x, :, z] = lap
            wave3[x, :, z] = 2.0 * wave2[x, :, z] - wave1[x, :, z] + v * lap
            adj = 2.0 * adj4[x, :, z] - adj5[x, :, z] + laplacian(space2, depthwise2, x, h, size_y)
            adj = adj + inject[x, :, z]
            adj3[x, :, z] = adj
            image3[x, :, z] = v * adj
        return 0

    lax.fori_loop(0, size_x, body, 0, unroll=2)
    add_source(cell, amp[0, 1], wave3)
    put_edges(wave3, 0, pya, pyb, pxa, pxb, 0)
    put_edges(image3, 4, pya, pyb, pxa, pxb, 4)


def fourth_kernel(
    offsets, ya, yb, xa, xb, wave3, image3, adj3, adj4, lap1, lap2, band, inject,
    adj2, placed, space, depthwise, space2, depthwise2, column,
):
    size_x, size_y = wave3.shape[0], wave3.shape[1]
    halos = (ya, yb, xa, xb)
    fill(space, wave3, halos, 0, 0)
    fill(space2, image3, halos, 4, 4)
    depth_part(wave3, band, depthwise)
    depth_part(image3, band, depthwise2)
    start = offsets[0]
    low = start // HALF
    shift_by = lax.rem(start, HALF)
    column[...] = jnp.zeros_like(column)

    def body(x, _):
        lane = lax.broadcasted_iota(jnp.int32, (size_y, HALF), 1)
        rolled = []
        for h in range(2):
            z = slice(h * HALF, (h + 1) * HALF)
            lap3 = laplacian(space, depthwise, x, h, size_y)
            old, mid = adj4[x, :, z], adj3[x, :, z]
            adj = 2.0 * mid - old + laplacian(space2, depthwise2, x, h, size_y)
            adj = adj + inject[x, :, z]
            adj2[x, :, z] = adj
            grad = old * lap3 + mid * lap2[x, :, z] + adj * lap1[x, :, z]
            rolled.append(pltpu.roll(grad, shift_by, 1))
        high = lane >= shift_by
        column[low, x] = jnp.where(high, rolled[0], 0.0)
        column[low + 1, x] = jnp.where(high, rolled[1], rolled[0])
        column[low + 2, x] = jnp.where(high, 0.0, rolled[1])
        return 0

    lax.fori_loop(0, size_x, body, 0, unroll=2)
    placed[...] = column[0:4]


def sum_kernel(parts, out):
    out[...] = (parts[0] + parts[1]) + (parts[2] + parts[3])


def local(model_vel2, offsets, wave_prev, wave_cur, adj_cur, adj_next, src_cell, src_amp, rec_cell, rec_res):
    size_x, size_y, depth = wave_cur.shape[1:]
    wave0, wave1, adj4, adj5 = wave_prev[0], wave_cur[0], adj_cur[0], adj_next[0]
    block = shaped(size_x, size_y, depth)
    edge_y, edge_x = shaped(size_x, 8, depth), shaped(8, size_y, depth)
    space = pltpu.VMEM((2, size_x + 8, size_y + 16, HALF), F32)
    whole = pltpu.VMEM((size_x, size_y, depth), F32)
    five = pltpu.VMEM((5, size_x, size_y, HALF), F32)

    tiles = [model_vel2] + [shift(model_vel2, "shot", d) for d in (1, 2, 3)]
    edges = call(
        edges_kernel,
        (shaped(size_x // 2, 8, depth),) * 2 + (shaped(4, size_y, depth),) * 2,
        n_in=1,
    )(wave1)
    halos = exchange(edges)
    band, inject0, inject1 = call(
        functools.partial(tables_kernel, size_x, size_y), (shaped(depth, depth), block, block), n_in=2
    )(rec_cell, rec_res)
    lap1 = call(first_kernel, block, (space, whole), n_in=6)(wave1, band, *halos)
    vel, wave2, image, *edges = call(
        second_kernel, (block,) * 3 + (edge_y,) * 2 + (edge_x,) * 2,
        (pltpu.VMEM((4, size_x, size_y, HALF), F32),), smem=3, n_in=8,
    )(offsets, src_cell, src_amp, *tiles, lap1, wave0, wave1, adj4)
    halos = exchange(edges)
    lap2, wave3, adj3, image3, *edges = call(
        third_kernel, (block,) * 4 + (edge_y,) * 2 + (edge_x,) * 2, (space, whole) * 2, smem=2, n_in=12
    )(src_cell, src_amp, *halos, wave1, wave2, adj4, adj5, vel, image, band, inject0)
    halos = exchange(edges)
    adj2, placed = call(
        fourth_kernel, (block, shaped(4, size_x, size_y, HALF)), (space, whole) * 2 + (five,), smem=1, n_in=12
    )(offsets, *halos, wave3, image3, adj3, adj4, lap1, lap2, band, inject1)
    parts = lax.all_to_all(placed, "shot", 0, 0)
    owned = call(sum_kernel, shaped(size_x, size_y, HALF), n_in=1)(parts)
    return owned, adj2[None]


def solution(mesh):
    return jax.shard_map(
        local,
        mesh=mesh,
        in_specs=(
            P("gx", "gy", "shot"),
            P("shot"),
            P("shot", "gx", "gy", None),
            P("shot", "gx", "gy", None),
            P("shot", "gx", "gy", None),
            P("shot", "gx", "gy", None),
            P("shot", None),
            P("shot", None),
            P("shot", None, None),
            P("shot", None, None),
        ),
        out_specs=(P("gx", "gy", "shot"), P("shot", "gx", "gy", None)),
        check_vma=False,
    )
```

time: 225 us -> 102 us (0.45)
  the two profiles are of different devices: /device:TPU:24 before, /device:TPU:17 now
where the time goes in v1:
time: 102 us; the launch traced here: 101 us
  starting transfers between devices  58.1 us (57%)
  Pallas kernels  16.7 us (16%)
  blocking collectives  15.8 us (15%)
  waiting for transfers between devices  6.56 us (6%)
  local copies, waits for them, and re-layouts  2.5 us (2%)
  between operations  1.63 us (2%)
    ppermute x12, starting transfers between devices, swap(): return lax.ppermute(value, axis, pairs)  46.9 us
    all_to_all x1, blocking collectives, local(): parts = lax.all_to_all(placed, 'shot', 0, 0)  15.8 us
    ppermute x3, starting transfers between devices, shift(): lax.ppermute(value, axis, [(i, (i + distance) % size) for i in range(size)])  11.2 us
    ppermute x12, waiting for transfers between devices, swap(): return lax.ppermute(value, axis, pairs)  6.55 us
    pallas_call x1, Pallas kernels, local(): call(fourth_kernel, (block, shaped(4, size_x, size_y, HALF)), (space, who...  6.11 us
    pallas_call x1, Pallas kernels, local(): call(third_kernel, (block,) * 4 + (edge_y,) * 2 + (edge_x,) * 2, (space,...  4.56 us
    unnamed x22, local copies, waits for them, and re-layouts  2.5 us
    pallas_call x1, Pallas kernels, local(): call(second_kernel, (block,) * 3 + (edge_y,) * 2 + (edge_x,) * 2, (pltpu....  2.17 us
  transfers between devices with their start and end apart: 15, of which 2 were waited for; matrix products, arithmetic and copies ran while one was open for 0% of the time, Pallas kernels for 3%

profile of v1, /device:TPU:17, one launch (start us, length us, event | category | flops | bytes accessed | tf_op | source)
XLA Modules:
  0.0 101.3 jit_solution(11633522844191454143)
XLA Ops:
  0.6 4.7 %collective-permute-start.1 = (f32[32,16,128]{2,1,0:T(8,128)}, f32[32,16,128]{2,1,0:T(8,128)S(1)}, u32[]{:S(2)}, u32[]{:S(2)}) collective-permute-start(f32[32,16,128]{2,1,0:T(8,128)} %tile0.1), channel_id=1, source_target_pairs={{0,256},{128,384},{256,0},{384,128},{1,257},{129,385},{257,1},{385... | collective-permute-start | bytes 786440 | tf_op jit(solution)/shard_map/ppermute | solution.py:24
  5.3 2.2 %collective-permute-start = (f32[32,16,128]{2,1,0:T(8,128)}, f32[32,16,128]{2,1,0:T(8,128)S(1)}, u32[]{:S(2)}, u32[]{:S(2)}) collective-permute-start(f32[32,16,128]{2,1,0:T(8,128)} %tile0.1), channel_id=1, source_target_pairs={{0,128},{128,256},{256,384},{384,0},{1,129},{129,257},{257,385},{3... | collective-permute-start | bytes 786440 | tf_op jit(solution)/shard_map/ppermute | solution.py:24
  7.5 4.3 %collective-permute-start.2 = (f32[32,16,128]{2,1,0:T(8,128)}, f32[32,16,128]{2,1,0:T(8,128)S(1)}, u32[]{:S(2)}, u32[]{:S(2)}) collective-permute-start(f32[32,16,128]{2,1,0:T(8,128)} %tile0.1), channel_id=1, source_target_pairs={{0,384},{128,0},{256,128},{384,256},{1,385},{129,1},{257,129},{385... | collective-permute-start | bytes 786440 | tf_op jit(solution)/shard_map/ppermute | solution.py:24
  11.8 1.0 %copy-done = f32[1,32,16,256]{3,2,1,0:T(8,128)S(1)} copy-done((f32[1,32,16,256]{3,2,1,0:T(8,128)S(1)}, f32[1,32,16,256]{3,2,1,0:T(8,128)}, u32[]{:S(2)}) %copy-start) | copy-done | bytes 524312
  12.8 0.1 shard_map.114
  12.9 3.6 %collective-permute-start.5 = (f32[4,16,256]{2,1,0:T(8,128)S(1)}, f32[4,16,256]{2,1,0:T(8,128)S(1)}, u32[]{:S(2)}, u32[]{:S(2)}) collective-permute-start(f32[4,16,256]{2,1,0:T(8,128)S(1)} %get-tuple-element.29), channel_id=1, source_target_pairs={{0,32},{32,0},{64,96},{96,64},{1,33},{33,1},{65,97},{97,65},{2,34}... | collective-permute-start | bytes 196616 | tf_op jit(solution)/shard_map/ppermute | solution.py:19
  16.5 0.0 copy-start.8
  16.5 2.8 %collective-permute-start.6 = (f32[4,16,256]{2,1,0:T(8,128)S(1)}, f32[4,16,256]{2,1,0:T(8,128)S(1)}, u32[]{:S(2)}, u32[]{:S(2)}) collective-permute-start(f32[4,16,256]{2,1,0:T(8,128)S(1)} %get-tuple-element.30), channel_id=1, source_target_pairs={{32,64},{64,32},{33,65},{65,33},{34,66},{66,34},{35,67},{67,35},{3... | collective-permute-start | bytes 196616 | tf_op jit(solution)/shard_map/ppermute | solution.py:19
  19.3 3.5 %collective-permute-start.3 = (f32[16,8,256]{2,1,0:T(8,128)S(1)}, f32[16,8,256]{2,1,0:T(8,128)S(1)}, u32[]{:S(2)}, u32[]{:S(2)}) collective-permute-start(f32[16,8,256]{2,1,0:T(8,128)S(1)} %get-tuple-element.27), channel_id=1, source_target_pairs={{0,1},{1,0},{2,3},{3,2},{4,5},{5,4},{6,7},{7,6},{8,9},{9,8},{10,11... | collective-permute-start | bytes 393224 | tf_op jit(solution)/shard_map/ppermute | solution.py:19
  22.9 10.3 %collective-permute-start.4 = (f32[16,8,256]{2,1,0:T(8,128)S(1)}, f32[16,8,256]{2,1,0:T(8,128)S(1)}, u32[]{:S(2)}, u32[]{:S(2)}) collective-permute-start(f32[16,8,256]{2,1,0:T(8,128)S(1)} %get-tuple-element.28), channel_id=1, source_target_pairs={{1,2},{2,1},{3,4},{4,3},{5,6},{6,5},{7,8},{8,7},{9,10},{10,9},{11,... | collective-permute-start | bytes 393224 | tf_op jit(solution)/shard_map/ppermute | solution.py:19
  33.9 0.1 copy.12.cells
  34.0 0.5 copy-done.9
  34.5 0.1 copy.13.res
  34.7 1.2 %shard_map.113 = (f32[256,256]{1,0:T(8,128)S(1)}, f32[32,16,256]{2,1,0:T(8,128)S(1)}, f32[32,16,256]{2,1,0:T(8,128)S(1)}) custom-call(s32[1,256,3]{2,1,0:T(8,128)S(1)} %copy.12.cells, f32[1,256,2]{2,1,0:T(8,128)S(1)} %copy.13.res), custom_call_target="tpu_custom_call" | custom-call | bytes 1048576 | tf_op jit(solution)/shard_map/pallas_call | solution.py:305
  36.0 1.8 %shard_map.115.lap1 = f32[32,16,256]{2,1,0:T(8,128)S(1)} custom-call(f32[32,16,256]{2,1,0:T(8,128)S(1)} %bitcast.6, f32[256,256]{1,0:T(8,128)S(1)} %get-tuple-element.26.band, f32[16,8,256]{2,1,0:T(8,128)S(1)} %collective-permute-done.3.ya, f32[16,8,256]{2,1,0:T(8,128)S(1)} %collective-permute-done.4.yb, f32[4,16,256]{2,1,0:T(8,128)S(1)} %collective-permute-done.5.xa, ...), custom_call_target="tpu_custom_call" | custom-call | bytes 1048576 | tf_op jit(solution)/shard_map/pallas_call | solution.py:308
  37.8 0.6 copy-done.6
  38.4 0.0 copy-done.7
  38.4 2.2 %shard_map.116 = (f32[32,16,256]{2,1,0:T(8,128)S(1)}, f32[32,16,256]{2,1,0:T(8,128)S(1)}, f32[32,16,256]{2,1,0:T(8,128)S(1)}, f32[32,8,256]{2,1,0:T(8,128)S(1)},...) custom-call(s32[1]{0:T(128)S(6)} %copy.14.offsets, s32[1,3]{1,0:T(1,128)S(1)} %copy-done.6, ...), custom_call_target="tpu_custom_call" | custom-call | bytes 1048576 | tf_op jit(solution)/shard_map/pallas_call | solution.py:309
  40.6 1.9 %collective-permute-start.7 = (f32[32,8,256]{2,1,0:T(8,128)S(1)}, f32[32,8,256]{2,1,0:T(8,128)S(1)}, u32[]{:S(2)}, u32[]{:S(2)}) collective-permute-start(f32[32,8,256]{2,1,0:T(8,128)S(1)} %get-tuple-element.31), channel_id=1, source_target_pairs={{0,1},{1,0},{2,3},{3,2},{4,5},{5,4},{6,7},{7,6},{8,9},{9,8},{10,11... | collective-permute-start | bytes 786440 | tf_op jit(solution)/shard_map/ppermute | solution.py:19
  42.6 6.8 %collective-permute-start.8 = (f32[32,8,256]{2,1,0:T(8,128)S(1)}, f32[32,8,256]{2,1,0:T(8,128)S(1)}, u32[]{:S(2)}, u32[]{:S(2)}) collective-permute-start(f32[32,8,256]{2,1,0:T(8,128)S(1)} %get-tuple-element.32), channel_id=1, source_target_pairs={{1,2},{2,1},{3,4},{4,3},{5,6},{6,5},{7,8},{8,7},{9,10},{10,9},{11,... | collective-permute-start | bytes 786440 | tf_op jit(solution)/shard_map/ppermute | solution.py:19
  49.4 1.9 %collective-permute-start.9 = (f32[8,16,256]{2,1,0:T(8,128)S(1)}, f32[8,16,256]{2,1,0:T(8,128)S(1)}, u32[]{:S(2)}, u32[]{:S(2)}) collective-permute-start(f32[8,16,256]{2,1,0:T(8,128)S(1)} %get-tuple-element.33), channel_id=1, source_target_pairs={{0,32},{32,0},{64,96},{96,64},{1,33},{33,1},{65,97},{97,65},{2,34}... | collective-permute-start | bytes 393224 | tf_op jit(solution)/shard_map/ppermute | solution.py:19
  51.3 4.7 %collective-permute-start.10 = (f32[8,16,256]{2,1,0:T(8,128)S(1)}, f32[8,16,256]{2,1,0:T(8,128)S(1)}, u32[]{:S(2)}, u32[]{:S(2)}) collective-permute-start(f32[8,16,256]{2,1,0:T(8,128)S(1)} %get-tuple-element.34), channel_id=1, source_target_pairs={{32,64},{64,32},{33,65},{65,33},{34,66},{66,34},{35,67},{67,35},{3... | collective-permute-start | bytes 393224 | tf_op jit(solution)/shard_map/ppermute | solution.py:19
  56.0 2.6 %collective-permute-done.10.xb = f32[8,16,256]{2,1,0:T(8,128)S(1)} collective-permute-done((f32[8,16,256]{2,1,0:T(8,128)S(1)}, f32[8,16,256]{2,1,0:T(8,128)S(1)}, u32[]{:S(2)}, u32[]{:S(2)}) %collective-permute-start.10) | collective-permute-done | bytes 131104 | tf_op jit(solution)/shard_map/ppermute | solution.py:19
  58.6 4.6 %shard_map.117 = (f32[32,16,256]{2,1,0:T(8,128)S(1)}, f32[32,16,256]{2,1,0:T(8,128)S(1)}, f32[32,16,256]{2,1,0:T(8,128)S(1)}, f32[32,16,256]{2,1,0:T(8,128)S(1)}...) custom-call(s32[1,3]{1,0:T(1,128)S(1)} %copy-done.6, ...), custom_call_target="tpu_custom_call" | custom-call | bytes 1048576 | tf_op jit(solution)/shard_map/pallas_call | solution.py:314
  63.2 1.9 %collective-permute-start.11 = (f32[32,8,256]{2,1,0:T(8,128)S(1)}, f32[32,8,256]{2,1,0:T(8,128)S(1)}, u32[]{:S(2)}, u32[]{:S(2)}) collective-permute-start(f32[32,8,256]{2,1,0:T(8,128)S(1)} %get-tuple-element.39), channel_id=1, source_target_pairs={{0,1},{1,0},{2,3},{3,2},{4,5},{5,4},{6,7},{7,6},{8,9},{9,8},{10,11... | collective-permute-start | bytes 786440 | tf_op jit(solution)/shard_map/ppermute | solution.py:19
  65.1 4.5 %collective-permute-start.12 = (f32[32,8,256]{2,1,0:T(8,128)S(1)}, f32[32,8,256]{2,1,0:T(8,128)S(1)}, u32[]{:S(2)}, u32[]{:S(2)}) collective-permute-start(f32[32,8,256]{2,1,0:T(8,128)S(1)} %get-tuple-element.40), channel_id=1, source_target_pairs={{1,2},{2,1},{3,4},{4,3},{5,6},{6,5},{7,8},{8,7},{9,10},{10,9},{11,... | collective-permute-start | bytes 786440 | tf_op jit(solution)/shard_map/ppermute | solution.py:19
  69.6 2.6 %collective-permute-start.13 = (f32[8,16,256]{2,1,0:T(8,128)S(1)}, f32[8,16,256]{2,1,0:T(8,128)S(1)}, u32[]{:S(2)}, u32[]{:S(2)}) collective-permute-start(f32[8,16,256]{2,1,0:T(8,128)S(1)} %get-tuple-element.41), channel_id=1, source_target_pairs={{0,32},{32,0},{64,96},{96,64},{1,33},{33,1},{65,97},{97,65},{2,34}... | collective-permute-start | bytes 393224 | tf_op jit(solution)/shard_map/ppermute | solution.py:19
  72.3 2.4 %collective-permute-start.14 = (f32[8,16,256]{2,1,0:T(8,128)S(1)}, f32[8,16,256]{2,1,0:T(8,128)S(1)}, u32[]{:S(2)}, u32[]{:S(2)}) collective-permute-start(f32[8,16,256]{2,1,0:T(8,128)S(1)} %get-tuple-element.42), channel_id=1, source_target_pairs={{32,64},{64,32},{33,65},{65,33},{34,66},{66,34},{35,67},{67,35},{3... | collective-permute-start | bytes 393224 | tf_op jit(solution)/shard_map/ppermute | solution.py:19
  74.7 3.9 %collective-permute-done.14.xb = f32[8,16,256]{2,1,0:T(8,128)S(1)} collective-permute-done((f32[8,16,256]{2,1,0:T(8,128)S(1)}, f32[8,16,256]{2,1,0:T(8,128)S(1)}, u32[]{:S(2)}, u32[]{:S(2)}) %collective-permute-start.14) | collective-permute-done | bytes 131104 | tf_op jit(solution)/shard_map/ppermute | solution.py:19
  78.6 6.1 %shard_map.118 = (f32[32,16,256]{2,1,0:T(8,128)}, f32[4,32,16,128]{3,2,1,0:T(8,128)S(1)}) custom-call(s32[1]{0:T(128)S(6)} %copy.14.offsets, f32[32,8,256]{2,1,0:T(8,128)S(1)} %collective-permute-done.11.ya, f32[32,8,256]{2,1,0:T(8,128)S(1)} %collective-permute-done.12.yb, f32[8,16,256]{2,1,0:T(8,128)S(1)} %collective-permute-done.13.xa, ...), custom_call_target="tpu_custom_call" | custom-call | bytes 1048576 | tf_op jit(solution)/shard_map/pallas_call | solution.py:318
  84.7 15.8 %all_to_all.5.parts = f32[4,32,16,128]{3,2,1,0:T(8,128)S(1)} all-to-all(f32[4,32,16,128]{3,2,1,0:T(8,128)S(1)} %get-tuple-element.48), channel_id=1, replica_groups=mesh['shot'=4,'gx'=4,'gy'=32] {'shot'}, dimensions={0} | all-to-all | bytes 2097152 | tf_op jit(solution)/shard_map/all_to_all | solution.py:321
  100.5 0.8 shard_map.119
  (28 shorter events, 0.1 us)
Async XLA Ops:
  0.6 37.1 %collective-permute-start.1 = (f32[32,16,128]{2,1,0:T(8,128)}, f32[32,16,128]{2,1,0:T(8,128)S(1)}, u32[]{:S(2)}, u32[]{:S(2)}) collective-permute-start(f32[32,16,128]{2,1,0:T(8,128)} %tile0.1), channel_id=1, source_target_pairs={{0,256},{128,384},{256,0},{384,128},{1,257},{129,385},{257,1},{385... | collective-permute-start | bytes 786440 | tf_op jit(solution)/shard_map/ppermute | solution.py:24
  5.3 32.5 %collective-permute-start = (f32[32,16,128]{2,1,0:T(8,128)}, f32[32,16,128]{2,1,0:T(8,128)S(1)}, u32[]{:S(2)}, u32[]{:S(2)}) collective-permute-start(f32[32,16,128]{2,1,0:T(8,128)} %tile0.1), channel_id=1, source_target_pairs={{0,128},{128,256},{256,384},{384,0},{1,129},{129,257},{257,385},{3... | collective-permute-start | bytes 786440 | tf_op jit(solution)/shard_map/ppermute | solution.py:24
  7.5 30.2 %collective-permute-start.2 = (f32[32,16,128]{2,1,0:T(8,128)}, f32[32,16,128]{2,1,0:T(8,128)S(1)}, u32[]{:S(2)}, u32[]{:S(2)}) collective-permute-start(f32[32,16,128]{2,1,0:T(8,128)} %tile0.1), channel_id=1, source_target_pairs={{0,384},{128,0},{256,128},{384,256},{1,385},{129,1},{257,129},{385... | collective-permute-start | bytes 786440 | tf_op jit(solution)/shard_map/ppermute | solution.py:24
  11.8 1.0 %copy-start = (f32[1,32,16,256]{3,2,1,0:T(8,128)S(1)}, f32[1,32,16,256]{3,2,1,0:T(8,128)}, u32[]{:S(2)}) copy-start(f32[1,32,16,256]{3,2,1,0:T(8,128)} %param.13) | copy-start | bytes 1572868
  12.8 23.1 %copy-start.1 = (f32[1,32,16,256]{3,2,1,0:T(8,128)S(1)}, f32[1,32,16,256]{3,2,1,0:T(8,128)}, u32[]{:S(2)}) copy-start(f32[1,32,16,256]{3,2,1,0:T(8,128)} %param.13) | copy-start | bytes 1572868
  12.9 6.4 %collective-permute-start.5 = (f32[4,16,256]{2,1,0:T(8,128)S(1)}, f32[4,16,256]{2,1,0:T(8,128)S(1)}, u32[]{:S(2)}, u32[]{:S(2)}) collective-permute-start(f32[4,16,256]{2,1,0:T(8,128)S(1)} %get-tuple-element.29), channel_id=1, source_target_pairs={{0,32},{32,0},{64,96},{96,64},{1,33},{33,1},{65,97},{97,65},{2,34}... | collective-permute-start | bytes 196616 | tf_op jit(solution)/shard_map/ppermute | solution.py:19
  16.5 17.3 %copy-start.8 = (s32[1,256,3]{1,0,2:T(1,128)S(1)}, s32[1,256,3]{1,0,2:T(1,128)}, u32[]{:S(2)}) copy-start(s32[1,256,3]{1,0,2:T(1,128)} %param.18) | copy-start | bytes 9220
  16.5 6.4 %collective-permute-start.6 = (f32[4,16,256]{2,1,0:T(8,128)S(1)}, f32[4,16,256]{2,1,0:T(8,128)S(1)}, u32[]{:S(2)}, u32[]{:S(2)}) collective-permute-start(f32[4,16,256]{2,1,0:T(8,128)S(1)} %get-tuple-element.30), channel_id=1, source_target_pairs={{32,64},{64,32},{33,65},{65,33},{34,66},{66,34},{35,67},{67,35},{3... | collective-permute-start | bytes 196616 | tf_op jit(solution)/shard_map/ppermute | solution.py:19
  19.3 16.6 %collective-permute-start.3 = (f32[16,8,256]{2,1,0:T(8,128)S(1)}, f32[16,8,256]{2,1,0:T(8,128)S(1)}, u32[]{:S(2)}, u32[]{:S(2)}) collective-permute-start(f32[16,8,256]{2,1,0:T(8,128)S(1)} %get-tuple-element.27), channel_id=1, source_target_pairs={{0,1},{1,0},{2,3},{3,2},{4,5},{5,4},{6,7},{7,6},{8,9},{9,8},{10,11... | collective-permute-start | bytes 393224 | tf_op jit(solution)/shard_map/ppermute | solution.py:19
  22.9 13.0 %collective-permute-start.4 = (f32[16,8,256]{2,1,0:T(8,128)S(1)}, f32[16,8,256]{2,1,0:T(8,128)S(1)}, u32[]{:S(2)}, u32[]{:S(2)}) collective-permute-start(f32[16,8,256]{2,1,0:T(8,128)S(1)} %get-tuple-element.28), channel_id=1, source_target_pairs={{1,2},{2,1},{3,4},{4,3},{5,6},{6,5},{7,8},{8,7},{9,10},{10,9},{11,... | collective-permute-start | bytes 393224 | tf_op jit(solution)/shard_map/ppermute | solution.py:19
  33.8 0.7 copy-start.9
  35.9 1.9 %copy-start.2 = (f32[1,32,16,256]{3,2,1,0:T(8,128)S(1)}, f32[1,32,16,256]{3,2,1,0:T(8,128)}, u32[]{:S(2)}) copy-start(f32[1,32,16,256]{3,2,1,0:T(8,128)} %param.14) | copy-start | bytes 1572868
  35.9 1.9 %copy-start.3 = (f32[1,32,16,256]{3,2,1,0:T(8,128)S(1)}, f32[1,32,16,256]{3,2,1,0:T(8,128)}, u32[]{:S(2)}) copy-start(f32[1,32,16,256]{3,2,1,0:T(8,128)} %param.12) | copy-start | bytes 1572868
  36.0 1.9 %copy-start.5 = (f32[32,16,128]{2,1,0:T(8,128)S(1)}, f32[32,16,128]{2,1,0:T(8,128)}, u32[]{:S(2)}) copy-start(f32[32,16,128]{2,1,0:T(8,128)} %tile0.1) | copy-start | bytes 786436
  37.8 0.7 copy-start.6
  37.8 0.7 copy-start.7
  38.4 20.2 %copy-start.4 = (f32[1,32,16,256]{3,2,1,0:T(8,128)S(1)}, f32[1,32,16,256]{3,2,1,0:T(8,128)}, u32[]{:S(2)}) copy-start(f32[1,32,16,256]{3,2,1,0:T(8,128)} %param.15) | copy-start | bytes 1572868
  40.6 18.0 %collective-permute-start.7 = (f32[32,8,256]{2,1,0:T(8,128)S(1)}, f32[32,8,256]{2,1,0:T(8,128)S(1)}, u32[]{:S(2)}, u32[]{:S(2)}) collective-permute-start(f32[32,8,256]{2,1,0:T(8,128)S(1)} %get-tuple-element.31), channel_id=1, source_target_pairs={{0,1},{1,0},{2,3},{3,2},{4,5},{5,4},{6,7},{7,6},{8,9},{9,8},{10,11... | collective-permute-start | bytes 786440 | tf_op jit(solution)/shard_map/ppermute | solution.py:19
  42.6 16.1 %collective-permute-start.8 = (f32[32,8,256]{2,1,0:T(8,128)S(1)}, f32[32,8,256]{2,1,0:T(8,128)S(1)}, u32[]{:S(2)}, u32[]{:S(2)}) collective-permute-start(f32[32,8,256]{2,1,0:T(8,128)S(1)} %get-tuple-element.32), channel_id=1, source_target_pairs={{1,2},{2,1},{3,4},{4,3},{5,6},{6,5},{7,8},{8,7},{9,10},{10,9},{11,... | collective-permute-start | bytes 786440 | tf_op jit(solution)/shard_map/ppermute | solution.py:19
  49.4 6.6 %collective-permute-start.9 = (f32[8,16,256]{2,1,0:T(8,128)S(1)}, f32[8,16,256]{2,1,0:T(8,128)S(1)}, u32[]{:S(2)}, u32[]{:S(2)}) collective-permute-start(f32[8,16,256]{2,1,0:T(8,128)S(1)} %get-tuple-element.33), channel_id=1, source_target_pairs={{0,32},{32,0},{64,96},{96,64},{1,33},{33,1},{65,97},{97,65},{2,34}... | collective-permute-start | bytes 393224 | tf_op jit(solution)/shard_map/ppermute | solution.py:19
  51.3 7.3 %collective-permute-start.10 = (f32[8,16,256]{2,1,0:T(8,128)S(1)}, f32[8,16,256]{2,1,0:T(8,128)S(1)}, u32[]{:S(2)}, u32[]{:S(2)}) collective-permute-start(f32[8,16,256]{2,1,0:T(8,128)S(1)} %get-tuple-element.34), channel_id=1, source_target_pairs={{32,64},{64,32},{33,65},{65,33},{34,66},{66,34},{35,67},{67,35},{3... | collective-permute-start | bytes 393224 | tf_op jit(solution)/shard_map/ppermute | solution.py:19
  63.2 15.3 %collective-permute-start.11 = (f32[32,8,256]{2,1,0:T(8,128)S(1)}, f32[32,8,256]{2,1,0:T(8,128)S(1)}, u32[]{:S(2)}, u32[]{:S(2)}) collective-permute-start(f32[32,8,256]{2,1,0:T(8,128)S(1)} %get-tuple-element.39), channel_id=1, source_target_pairs={{0,1},{1,0},{2,3},{3,2},{4,5},{5,4},{6,7},{7,6},{8,9},{9,8},{10,11... | collective-permute-start | bytes 786440 | tf_op jit(solution)/shard_map/ppermute | solution.py:19
  65.1 13.4 %collective-permute-start.12 = (f32[32,8,256]{2,1,0:T(8,128)S(1)}, f32[32,8,256]{2,1,0:T(8,128)S(1)}, u32[]{:S(2)}, u32[]{:S(2)}) collective-permute-start(f32[32,8,256]{2,1,0:T(8,128)S(1)} %get-tuple-element.40), channel_id=1, source_target_pairs={{1,2},{2,1},{3,4},{4,3},{5,6},{6,5},{7,8},{8,7},{9,10},{10,9},{11,... | collective-permute-start | bytes 786440 | tf_op jit(solution)/shard_map/ppermute | solution.py:19
  69.6 5.0 %collective-permute-start.13 = (f32[8,16,256]{2,1,0:T(8,128)S(1)}, f32[8,16,256]{2,1,0:T(8,128)S(1)}, u32[]{:S(2)}, u32[]{:S(2)}) collective-permute-start(f32[8,16,256]{2,1,0:T(8,128)S(1)} %get-tuple-element.41), channel_id=1, source_target_pairs={{0,32},{32,0},{64,96},{96,64},{1,33},{33,1},{65,97},{97,65},{2,34}... | collective-permute-start | bytes 393224 | tf_op jit(solution)/shard_map/ppermute | solution.py:19
  72.3 6.3 %collective-permute-start.14 = (f32[8,16,256]{2,1,0:T(8,128)S(1)}, f32[8,16,256]{2,1,0:T(8,128)S(1)}, u32[]{:S(2)}, u32[]{:S(2)}) collective-permute-start(f32[8,16,256]{2,1,0:T(8,128)S(1)} %get-tuple-element.42), channel_id=1, source_target_pairs={{32,64},{64,32},{33,65},{65,33},{34,66},{66,34},{35,67},{67,35},{3... | collective-permute-start | bytes 393224 | tf_op jit(solution)/shard_map/ppermute | solution.py:19

commit v2 on v1

v2 whole, which is shorter than its diff:
```python
import functools

import jax
import jax.numpy as jnp
import numpy as np
from jax import lax
from jax.experimental import pallas as pl
from jax.experimental.pallas import tpu as pltpu
from jax.sharding import PartitionSpec as P

COEF = (-205.0 / 72.0, 8.0 / 5.0, -1.0 / 5.0, 8.0 / 315.0, -1.0 / 560.0)
SCALE = 5040.0
WEIGHT = (0.0, 8064.0, -1008.0, 128.0, -9.0)
F32 = jnp.float32
HALF = 128


def swap(value, axis, odd):
    pairs = []
    for i in range(odd, lax.axis_size(axis) - 1, 2):
        pairs += [(i, i + 1), (i + 1, i)]
    return lax.ppermute(value, axis, pairs)


def swap_shot(value, odd):
    size = lax.axis_size("shot")
    pairs = []
    for i in range(odd, size, 2):
        pairs += [(i, (i + 1) % size), ((i + 1) % size, i)]
    return lax.ppermute(value, "shot", pairs)


def swap_across(value):
    size = lax.axis_size("shot")
    return lax.ppermute(value, "shot", [(i, (i + size // 2) % size) for i in range(size)])


def exchange(payload):
    ya, yb, xa, xb = payload
    return swap(yb, "gy", 1), swap(ya, "gy", 0), swap(xb, "gx", 1), swap(xa, "gx", 0)


def call(body, out_shape, scratch=(), smem=0, n_in=0, room=4, aliases=None):
    vmem = pl.BlockSpec(memory_space=pltpu.VMEM)
    scal = pl.BlockSpec(memory_space=pltpu.SMEM)
    return pl.pallas_call(
        body,
        out_shape=out_shape,
        in_specs=[scal] * smem + [vmem] * n_in,
        out_specs=jax.tree.map(lambda _: vmem, out_shape),
        scratch_shapes=list(scratch),
        input_output_aliases=aliases or {},
        compiler_params=pltpu.CompilerParams(vmem_limit_bytes=room << 20),
    )


def shaped(*dims):
    return jax.ShapeDtypeStruct(dims, F32)


def even(axis):
    return lax.rem(lax.axis_index(axis), 2) == 0


def weight(distance):
    distance = np.abs(distance)
    return np.where(distance <= 4, np.take(np.asarray(WEIGHT), np.minimum(distance, 4)), 0.0)


def difference_tables(size_y, depth, chunk):
    z = np.arange(depth)
    along_z = weight(z[:, None] - z[None, :])
    row = np.arange(chunk * size_y)
    x, y = row // size_y, row % size_y
    along_y = np.where(x[:, None] == x[None, :], weight(y[:, None] - y[None, :]), 0.0)
    edge = np.arange(chunk * 8)
    edge_x, edge_field, edge_row = edge // 8, edge % 8 // 4, edge % 4
    outer = np.zeros((2, 2, chunk * size_y, 2, chunk * 8))
    for parity in range(2):
        for field in range(2):
            for message in range(2):
                place = edge_row + size_y if parity == message else edge_row - 4
                use = (x[:, None] == edge_x[None, :]) & (edge_field[None, :] == field)
                outer[parity, field, :, message] = np.where(use, weight(y[:, None] - place[None, :]), 0.0)
    outer = outer.reshape(2, 2, chunk * size_y, 2 * chunk * 8)
    return (
        jnp.asarray(np.concatenate([along_z] * 3, axis=0), jnp.bfloat16),
        jnp.asarray(np.concatenate([along_y] * 3, axis=1), jnp.bfloat16),
        jnp.asarray(np.concatenate([outer] * 3, axis=3), jnp.bfloat16),
    )


def three(value):
    first = value.astype(jnp.bfloat16)
    rest = value - first.astype(F32)
    second = rest.astype(jnp.bfloat16)
    return first, second, (rest - second.astype(F32)).astype(jnp.bfloat16)


def product(a, b):
    return jnp.dot(a, b, preferred_element_type=F32)


def flat_part(field, along_y, along_z, out):
    size_x, size_y, depth = field.shape
    chunk = along_y.shape[0] // size_y
    for at in range(0, size_x, chunk):
        parts = three(field[at : at + chunk].reshape(chunk * size_y, depth))
        total = product(jnp.concatenate(parts, axis=1), along_z[...])
        total = total + product(along_y[...], jnp.concatenate(parts, axis=0))
        out[at : at + chunk] = total.reshape(chunk, size_y, depth)


def outer_part(ya, yb, at, outer, field, size_y):
    depth = ya.shape[2]
    chunk = outer.shape[2] // size_y
    a, b = (three(m[at : at + chunk].reshape(chunk * 8, depth)) for m in (ya, yb))
    stacked = jnp.concatenate([a[0], b[0], a[1], b[1], a[2], b[2]], axis=0)
    parity = jnp.where(even("gy"), 0, 1)
    return product(outer[parity, field], stacked).reshape(chunk, size_y, depth)


def outside_x(xa, xb, plane, out):
    even_x = even("gx")
    low = [jnp.where(even_x, xb[plane + i], xa[plane + i]) for i in range(4)]
    high = [jnp.where(even_x, xa[plane + i], xb[plane + i]) for i in range(4)]
    for i in range(4):
        first, last = 0.0, 0.0
        for k in range(i + 1, 5):
            first = first + COEF[k] * low[4 + i - k]
            last = last + COEF[k] * high[k - i - 1]
        out[i] = first
        out[7 - i] = last


def outer_parts(ya, yb, xa, xb, outer, size_x, size_y, sides, extras):
    chunk = outer.shape[2] // size_y
    for field, (side, extra) in enumerate(zip(sides, extras)):
        outside_x(xa, xb, 4 * field, side)
        for at in range(0, size_x, chunk):
            extra[at : at + chunk] = outer_part(ya, yb, at, outer, field, size_y) * (1.0 / SCALE)
        extra[0:4] = extra[0:4] + side[0:4]
        extra[size_x - 4 : size_x] = extra[size_x - 4 : size_x] + side[4:8]


def across(plane, x, z):
    total = (3.0 * COEF[0]) * plane(x, z)
    for k in range(1, 5):
        near = [p for p in (plane(x - k, z), plane(x + k, z)) if p is not None]
        if near:
            total = total + COEF[k] * sum(near[1:], near[0])
    return total


def within(field):
    size_x = field.shape[0]
    return lambda x, z: field[x, :, z] if 0 <= x < size_x else None


def halves():
    return [slice(h * HALF, (h + 1) * HALF) for h in range(2)]


def put_edges(field, row, ya, yb, xa, xb, plane):
    even_y, even_x = even("gy"), even("gx")
    size_x, size_y = field.shape[0], field.shape[1]
    first, last = field[:, 0:4, :], field[:, size_y - 4 : size_y, :]
    ya[:, row : row + 4, :] = jnp.where(even_y, last, first)
    yb[:, row : row + 4, :] = jnp.where(even_y, first, last)
    top = size_x - 4
    xa[plane : plane + 4] = field[pl.ds(jnp.where(even_x, top, 0), 4)]
    xb[plane : plane + 4] = field[pl.ds(jnp.where(even_x, 0, top), 4)]


def add_source(cell, amount, field):
    size_x, size_y, depth = field.shape
    x = cell[0, 0] - lax.axis_index("gx") * size_x
    y = cell[0, 1] - lax.axis_index("gy") * size_y

    @pl.when((x >= 0) & (x < size_x) & (y >= 0) & (y < size_y))
    def _():
        at = (lax.broadcasted_iota(jnp.int32, (size_y, depth), 0) == y) & (
            lax.broadcasted_iota(jnp.int32, (size_y, depth), 1) == cell[0, 2]
        )
        field[x] = field[x] + jnp.where(at, amount, 0.0)


def edges_kernel(field, ya, yb, xa, xb):
    even_y, even_x = even("gy"), even("gx")
    size_x, size_y = field.shape[0], field.shape[1]
    half = size_x // 2
    for part in range(2):
        x = slice(part * half, (part + 1) * half)
        first, last = field[x, 0:4, :], field[x, size_y - 4 : size_y, :]
        ya[:, part * 4 : part * 4 + 4, :] = jnp.where(even_y, last, first)
        yb[:, part * 4 : part * 4 + 4, :] = jnp.where(even_y, first, last)
    top = size_x - 4
    xa[...] = field[pl.ds(jnp.where(even_x, top, 0), 4)]
    xb[...] = field[pl.ds(jnp.where(even_x, 0, top), 4)]


def tables_kernel(size_x, size_y, cells, res, inject0, inject1):
    depth = inject0.shape[2]
    count = cells.shape[1]
    pad = jnp.zeros((count, HALF - 3), jnp.int32)
    rows = jnp.transpose(jnp.concatenate([cells[0], pad], axis=1).astype(F32))[0:8].astype(jnp.int32)
    x = rows[0:1, :] - lax.axis_index("gx") * size_x
    y = rows[1:2, :] - lax.axis_index("gy") * size_y
    inside = (x >= 0) & (x < size_x) & (y >= 0) & (y < size_y)
    place = jnp.where(inside, x * size_y + y, -1)
    deep = lax.broadcasted_iota(jnp.int32, (count, depth), 1) == cells[0, :, 2:3]
    parts = [three(jnp.where(deep, res[0, :, n : n + 1], 0.0)) for n in range(2)]
    spread = jnp.concatenate([jnp.concatenate([parts[0][i], parts[1][i]], axis=1) for i in range(3)], axis=0)
    half = size_x // 2
    for part in range(2):
        at = lax.broadcasted_iota(jnp.int32, (half * size_y, count), 0) + part * half * size_y
        flat = jnp.where(at == place, 1.0, 0.0).astype(jnp.bfloat16)
        done = product(jnp.concatenate([flat] * 3, axis=1), spread)
        for n, out in enumerate((inject0, inject1)):
            block = done[:, n * depth : (n + 1) * depth]
            out[part * half : (part + 1) * half] = block.reshape(half, size_y, depth)


def first_kernel(wave1, yb, ya, xb, xa, along_y, along_z, outer, lap1, flat, space):
    size_x, size_y = wave1.shape[0], wave1.shape[1]
    even_x = even("gx")
    flat_part(wave1, along_y, along_z, flat)
    half = size_x // 2
    for part in range(2):
        x = slice(part * half, (part + 1) * half)
        flat[x] = flat[x] + outer_part(ya, yb, 0, outer, part, size_y)
    space[4 : size_x + 4] = wave1[...]
    space[pl.ds(jnp.where(even_x, size_x + 4, 0), 4)] = xa[...]
    space[pl.ds(jnp.where(even_x, 0, size_x + 4), 4)] = xb[...]
    for x in range(size_x):
        for z in halves():
            lap = across(lambda i, z: space[i + 4, :, z], x, z)
            lap1[x, :, z] = lap + flat[x, :, z] * (1.0 / SCALE)


def second_kernel(
    offsets, cell, amp, tile, tile_a, tile_b, tile_ab, lap1, wave0, wave1, adj4,
    vel, wave2, image, ya, yb, xa, xb, column,
):
    size_x, size_y = wave1.shape[0], wave1.shape[1]
    me = lax.axis_index("shot")
    turn = jnp.where(even("shot"), 1, 3)
    for part, away in ((tile, 0), (tile_a, turn), (tile_ab, 2), (tile_b, 4 - turn)):
        column[lax.rem(me + away, 4)] = part[...]
    start = offsets[0]
    low = start // HALF
    shift_by = lax.rem(start, HALF)
    back = lax.rem(HALF - shift_by, HALF)
    third = jnp.minimum(low + 2, 3)

    def body(x, _):
        lane = lax.broadcasted_iota(jnp.int32, (size_y, HALF), 1)
        rolled = [pltpu.roll(column[i, x], back, 1) for i in (low, low + 1, third)]
        for h, z in enumerate(halves()):
            v = jnp.where(lane < HALF - shift_by, rolled[h], rolled[h + 1])
            vel[x, :, z] = v
            image[x, :, z] = v * adj4[x, :, z]
            wave2[x, :, z] = 2.0 * wave1[x, :, z] - wave0[x, :, z] + v * lap1[x, :, z]
        return 0

    lax.fori_loop(0, size_x, body, 0, unroll=4)
    add_source(cell, amp[0, 0], wave2)
    put_edges(wave2, 0, ya, yb, xa, xb, 0)
    put_edges(image, 4, ya, yb, xa, xb, 4)


def third_inner_kernel(
    wave1, wave2, adj4, adj5, vel, image, inject, along_y, along_z,
    lap2, wave3, adj3, flat, flat2,
):
    flat_part(wave2, along_y, along_z, flat)
    flat_part(image, along_y, along_z, flat2)
    for x in range(wave1.shape[0]):
        for z in halves():
            lap = across(within(wave2), x, z) + flat[x, :, z] * (1.0 / SCALE)
            lap2[x, :, z] = lap
            wave3[x, :, z] = 2.0 * wave2[x, :, z] - wave1[x, :, z] + vel[x, :, z] * lap
            adj = across(within(image), x, z) + flat2[x, :, z] * (1.0 / SCALE)
            adj3[x, :, z] = 2.0 * adj4[x, :, z] - adj5[x, :, z] + adj + inject[x, :, z]


def third_kernel(
    cell, amp, yb, ya, xb, xa, lap2_in, wave3_in, adj3_in, vel, outer,
    lap2, wave3, adj3, image3, pya, pyb, pxa, pxb, side, side2, extra, extra2,
):
    size_x, size_y = vel.shape[0], vel.shape[1]
    outer_parts(ya, yb, xa, xb, outer, size_x, size_y, (side, side2), (extra, extra2))

    def body(x, _):
        v = vel[x]
        lap2[x] = lap2_in[x] + extra[x]
        wave3[x] = wave3_in[x] + v * extra[x]
        adj = adj3_in[x] + extra2[x]
        adj3[x] = adj
        image3[x] = v * adj
        return 0

    lax.fori_loop(0, size_x, body, 0, unroll=4)
    add_source(cell, amp[0, 1], wave3)
    put_edges(wave3, 0, pya, pyb, pxa, pxb, 0)
    put_edges(image3, 4, pya, pyb, pxa, pxb, 4)


def fourth_inner_kernel(
    wave3, image3, adj3, adj4, lap1, lap2, inject, along_y, along_z,
    adj2, grad, flat, flat2,
):
    flat_part(wave3, along_y, along_z, flat)
    flat_part(image3, along_y, along_z, flat2)
    for x in range(wave3.shape[0]):
        for z in halves():
            lap3 = across(within(wave3), x, z) + flat[x, :, z] * (1.0 / SCALE)
            adj = across(within(image3), x, z) + flat2[x, :, z] * (1.0 / SCALE)
            old, mid = adj4[x, :, z], adj3[x, :, z]
            adj = 2.0 * mid - old + adj + inject[x, :, z]
            adj2[x, :, z] = adj
            grad[x, :, z] = old * lap3 + mid * lap2[x, :, z] + adj * lap1[x, :, z]


def fourth_kernel(
    offsets, yb, ya, xb, xa, grad_in, adj4, lap1, outer,
    far0, far1, near_a, near_b, own, extra2, side, side2, extra,
):
    size_x, size_y = adj4.shape[0], adj4.shape[1]
    outer_parts(ya, yb, xa, xb, outer, size_x, size_y, (side, side2), (extra, extra2))
    start = offsets[0]
    low = start // HALF
    shift_by = lax.rem(start, HALF)
    me = lax.axis_index("shot")
    turn = jnp.where(even("shot"), 1, 3)
    which = [lax.rem(me + away, 4) - low for away in (2, turn, 4 - turn, 0)]
    half = size_x // 2

    def body(x, far, at):
        lane = lax.broadcasted_iota(jnp.int32, (size_y, HALF), 1)
        rolled = []
        for z in halves():
            grad = grad_in[x, :, z] + adj4[x, :, z] * extra[x, :, z] + lap1[x, :, z] * extra2[x, :, z]
            rolled.append(pltpu.roll(grad, shift_by, 1))
        high = lane >= shift_by
        first = jnp.where(high, rolled[0], 0.0)
        second = jnp.where(high, rolled[1], rolled[0])
        third = jnp.where(high, 0.0, rolled[1])
        for n, (out, place) in zip(which, ((far, at), (near_a, x), (near_b, x), (own, x))):
            value = jnp.where(n == 0, first, jnp.where(n == 1, second, third))
            out[place] = jnp.where((n >= 0) & (n <= 2), value, 0.0)
        return 0

    lax.fori_loop(0, half, lambda x, _: body(x, far0, x), 0, unroll=4)
    lax.fori_loop(half, size_x, lambda x, _: body(x, far1, x - half), 0, unroll=4)


def adjoint_kernel(adj2_in, extra, adj2):
    adj2[...] = adj2_in[...] + extra[...]


def pass_kernel(first, near_in, far, near):
    planes = pl.ds(first, far.shape[0])
    near[planes] = near_in[planes] + far[...]


def sum_kernel(own, a, b, out):
    out[...] = own[...] + (a[...] + b[...])


def local(model_vel2, offsets, wave_prev, wave_cur, adj_cur, adj_next, src_cell, src_amp, rec_cell, rec_res):
    size_x, size_y, depth = wave_cur.shape[1:]
    wave0, wave1, adj4, adj5 = wave_prev[0], wave_cur[0], adj_cur[0], adj_next[0]
    block = shaped(size_x, size_y, depth)
    edge_y, edge_x = shaped(size_x, 8, depth), shaped(8, size_y, depth)
    tile, half = shaped(size_x, size_y, HALF), shaped(size_x // 2, size_y, HALF)
    whole = pltpu.VMEM((size_x, size_y, depth), F32)
    side = pltpu.VMEM((8, size_y, depth), F32)
    along_z, along_y, outer = difference_tables(size_y, depth, size_x // 2)

    tile_a, tile_b = swap_shot(model_vel2, 0), swap_shot(model_vel2, 1)
    tile_ab = swap_across(model_vel2)
    edges = call(
        edges_kernel, (shaped(size_x // 2, 8, depth),) * 2 + (shaped(4, size_y, depth),) * 2, n_in=1
    )(wave1)
    halos = exchange(edges)
    inject0, inject1 = call(functools.partial(tables_kernel, size_x, size_y), (block, block), n_in=2, room=8)(
        rec_cell, rec_res
    )
    lap1 = call(
        first_kernel, block, (whole, pltpu.VMEM((size_x + 8, size_y, depth), F32)), n_in=8, room=8
    )(wave1, *halos, along_y, along_z, outer)
    vel, wave2, image, *edges = call(
        second_kernel, (block,) * 3 + (edge_y,) * 2 + (edge_x,) * 2,
        (pltpu.VMEM((4, size_x, size_y, HALF), F32),), smem=3, n_in=8, room=8,
    )(offsets, src_cell, src_amp, model_vel2, tile_a, tile_b, tile_ab, lap1, wave0, wave1, adj4)
    halos = exchange(edges)
    inner = call(third_inner_kernel, (block,) * 3, (whole,) * 2, n_in=9, room=10)(
        wave1, wave2, adj4, adj5, vel, image, inject0, along_y, along_z
    )
    lap2, wave3, adj3, image3, *edges = call(
        third_kernel, (block,) * 4 + (edge_y,) * 2 + (edge_x,) * 2, (side, side, whole, whole), smem=2, n_in=9,
        room=10, aliases={6: 0, 7: 1, 8: 2},
    )(src_cell, src_amp, *halos, *inner, vel, outer)
    halos = exchange(edges)
    inner_adj2, inner_grad = call(fourth_inner_kernel, (block,) * 2, (whole,) * 2, n_in=9, room=10)(
        wave3, image3, adj3, adj4, lap1, lap2, inject1, along_y, along_z
    )
    far0, far1, near_a, near_b, own, extra = call(
        fourth_kernel, (half, half, tile, tile, tile, block), (side, side, whole), smem=1, n_in=8, room=10
    )(offsets, *halos, inner_grad, adj4, lap1, outer)
    from_a, from_b = swap_shot(far0, 0), swap_shot(far1, 1)
    near_b = call(functools.partial(pass_kernel, 0), tile, n_in=2, aliases={0: 0})(near_b, from_a)
    near_a = call(functools.partial(pass_kernel, size_x // 2), tile, n_in=2, aliases={0: 0})(near_a, from_b)
    got_b, got_a = swap_shot(near_b, 1), swap_shot(near_a, 0)
    adj2 = call(adjoint_kernel, block, n_in=2)(inner_adj2, extra)
    owned = call(sum_kernel, tile, n_in=3)(own, got_a, got_b)
    return owned, adj2[None]


def solution(mesh):
    return jax.shard_map(
        local,
        mesh=mesh,
        in_specs=(
            P("gx", "gy", "shot"),
            P("shot"),
            P("shot", "gx", "gy", None),
            P("shot", "gx", "gy", None),
            P("shot", "gx", "gy", None),
            P("shot", "gx", "gy", None),
            P("shot", None),
            P("shot", None),
            P("shot", None, None),
            P("shot", None, None),
        ),
        out_specs=(P("gx", "gy", "shot"), P("shot", "gx", "gy", None)),
        check_vma=False,
    )
```

time: 102 us -> 104 us (1.020)
  the two profiles are of different devices: /device:TPU:17 before, /device:TPU:24 now
where the time goes in v2:
time: 104 us; the launch traced here: 103 us
  starting transfers between devices  63.2 us (61%)
  waiting for transfers between devices  14 us (13%)
  Pallas kernels  12.5 us (12%)
  local copies, waits for them, and re-layouts  11.3 us (11%)
  between operations  1.72 us (2%)
    ppermute x12, starting transfers between devices, swap(): return lax.ppermute(value, axis, pairs)  39.6 us
    ppermute x6, starting transfers between devices, swap_shot(): return lax.ppermute(value, 'shot', pairs)  20 us
    unnamed x46, local copies, waits for them, and re-layouts  11.3 us
    ppermute x12, waiting for transfers between devices, swap(): return lax.ppermute(value, axis, pairs)  8.24 us
    ppermute x6, waiting for transfers between devices, swap_shot(): return lax.ppermute(value, 'shot', pairs)  5.77 us
    ppermute x1, starting transfers between devices, swap_across(): lax.ppermute(value, 'shot', [(i, (i + size // 2) % size) for i in range(s...  3.63 us
    pallas_call x1, Pallas kernels, local(): call(second_kernel, (block,) * 3 + (edge_y,) * 2 + (edge_x,) * 2, (pltpu....  2.45 us
    pallas_call x1, Pallas kernels, local(): call(third_kernel, (block,) * 4 + (edge_y,) * 2 + (edge_x,) * 2, (side, s...  2.11 us
  transfers between devices with their start and end apart: 19, of which 9 were waited for; matrix products, arithmetic and copies ran while one was open for 1% of the time, Pallas kernels for 6%

profile of v2, /device:TPU:24, one launch (start us, length us, event | category | flops | bytes accessed | tf_op | source)
XLA Modules:
  0.0 102.7 jit_solution(15345575000119066711)
XLA Ops:
  0.6 4.7 %collective-permute-start.1 = (f32[32,16,128]{2,1,0:T(8,128)}, f32[32,16,128]{2,1,0:T(8,128)S(1)}, u32[]{:S(2)}, u32[]{:S(2)}) collective-permute-start(f32[32,16,128]{2,1,0:T(8,128)} %tile.1), channel_id=1, source_target_pairs={{128,256},{256,128},{384,0},{0,384},{129,257},{257,129},{385,1},{1... | collective-permute-start | bytes 786440 | tf_op jit(solution)/shard_map/ppermute | solution.py:30
  5.3 2.1 %collective-permute-start = (f32[32,16,128]{2,1,0:T(8,128)}, f32[32,16,128]{2,1,0:T(8,128)S(1)}, u32[]{:S(2)}, u32[]{:S(2)}) collective-permute-start(f32[32,16,128]{2,1,0:T(8,128)} %tile.1), channel_id=1, source_target_pairs={{0,128},{128,0},{256,384},{384,256},{1,129},{129,1},{257,385},{385... | collective-permute-start | bytes 786440 | tf_op jit(solution)/shard_map/ppermute | solution.py:30
  7.4 3.6 %collective-permute-start.2 = (f32[32,16,128]{2,1,0:T(8,128)}, f32[32,16,128]{2,1,0:T(8,128)S(1)}, u32[]{:S(2)}, u32[]{:S(2)}) collective-permute-start(f32[32,16,128]{2,1,0:T(8,128)} %tile.1), channel_id=1, source_target_pairs={{0,256},{128,384},{256,0},{384,128},{1,257},{129,385},{257,1},{385... | collective-permute-start | bytes 786440 | tf_op jit(solution)/shard_map/ppermute | solution.py:35
  12.2 1.9 %collective-permute-start.5 = (f32[4,16,256]{2,1,0:T(8,128)S(1)}, f32[4,16,256]{2,1,0:T(8,128)S(1)}, u32[]{:S(2)}, u32[]{:S(2)}) collective-permute-start(f32[4,16,256]{2,1,0:T(8,128)S(1)} %get-tuple-element.36), channel_id=1, source_target_pairs={{32,64},{64,32},{33,65},{65,33},{34,66},{66,34},{35,67},{67,35},{3... | collective-permute-start | bytes 196616 | tf_op jit(solution)/shard_map/ppermute | solution.py:22
  14.1 1.9 %collective-permute-start.6 = (f32[4,16,256]{2,1,0:T(8,128)S(1)}, f32[4,16,256]{2,1,0:T(8,128)S(1)}, u32[]{:S(2)}, u32[]{:S(2)}) collective-permute-start(f32[4,16,256]{2,1,0:T(8,128)S(1)} %get-tuple-element.37), channel_id=1, source_target_pairs={{0,32},{32,0},{64,96},{96,64},{1,33},{33,1},{65,97},{97,65},{2,34}... | collective-permute-start | bytes 196616 | tf_op jit(solution)/shard_map/ppermute | solution.py:22
  16.1 1.7 %collective-permute-done.5.xb = f32[4,16,256]{2,1,0:T(8,128)S(1)} collective-permute-done((f32[4,16,256]{2,1,0:T(8,128)S(1)}, f32[4,16,256]{2,1,0:T(8,128)S(1)}, u32[]{:S(2)}, u32[]{:S(2)}) %collective-permute-start.5) | collective-permute-done | bytes 65568 | tf_op jit(solution)/shard_map/ppermute | solution.py:22
  17.8 12.1 %collective-permute-start.3 = (f32[16,8,256]{2,1,0:T(8,128)S(1)}, f32[16,8,256]{2,1,0:T(8,128)S(1)}, u32[]{:S(2)}, u32[]{:S(2)}) collective-permute-start(f32[16,8,256]{2,1,0:T(8,128)S(1)} %get-tuple-element.34), channel_id=1, source_target_pairs={{1,2},{2,1},{3,4},{4,3},{5,6},{6,5},{7,8},{8,7},{9,10},{10,9},{11,... | collective-permute-start | bytes 393224 | tf_op jit(solution)/shard_map/ppermute | solution.py:22
  29.9 1.9 %collective-permute-start.4 = (f32[16,8,256]{2,1,0:T(8,128)S(1)}, f32[16,8,256]{2,1,0:T(8,128)S(1)}, u32[]{:S(2)}, u32[]{:S(2)}) collective-permute-start(f32[16,8,256]{2,1,0:T(8,128)S(1)} %get-tuple-element.35), channel_id=1, source_target_pairs={{0,1},{1,0},{2,3},{3,2},{4,5},{5,4},{6,7},{7,6},{8,9},{9,8},{10,11... | collective-permute-start | bytes 393224 | tf_op jit(solution)/shard_map/ppermute | solution.py:22
  32.8 3.9 %collective-permute-done.4.ya = f32[16,8,256]{2,1,0:T(8,128)S(1)} collective-permute-done((f32[16,8,256]{2,1,0:T(8,128)S(1)}, f32[16,8,256]{2,1,0:T(8,128)S(1)}, u32[]{:S(2)}, u32[]{:S(2)}) %collective-permute-start.4) | collective-permute-done | bytes 131104 | tf_op jit(solution)/shard_map/ppermute | solution.py:22
  36.7 1.4 %copy-done = bf16[2,2,256,768]{3,2,1,0:T(8,128)(2,1)S(1)} copy-done((bf16[2,2,256,768]{3,2,1,0:T(8,128)(2,1)S(1)}, bf16[2,2,256,768]{3,2,1,0:T(8,128)(2,1)}, u32[]{:S(2)}) %copy-start) | copy-done | bytes 1572888
  38.1 1.0 %copy-done.4 = f32[1,32,16,256]{3,2,1,0:T(8,128)S(1)} copy-done((f32[1,32,16,256]{3,2,1,0:T(8,128)S(1)}, f32[1,32,16,256]{3,2,1,0:T(8,128)}, u32[]{:S(2)}) %copy-start.4) | copy-done | bytes 524312
  42.5 2.4 %shard_map.142 = (f32[32,16,256]{2,1,0:T(8,128)S(1)}, f32[32,16,256]{2,1,0:T(8,128)S(1)}, f32[32,16,256]{2,1,0:T(8,128)S(1)}, f32[32,8,256]{2,1,0:T(8,128)}, f32...) custom-call(s32[1]{0:T(128)S(6)} %copy.27.offsets, s32[1,3]{1,0:T(1,128)S(1)} %copy-done.18, ...), custom_call_target="tpu_custom_call" | custom-call | tf_op jit(solution)/shard_map/pallas_call | solution.py:393
  46.5 3.6 %collective-permute-start.7 = (f32[32,8,256]{2,1,0:T(8,128)}, f32[32,8,256]{2,1,0:T(8,128)}, u32[]{:S(2)}, u32[]{:S(2)}) collective-permute-start(f32[32,8,256]{2,1,0:T(8,128)} %get-tuple-element.38), channel_id=1, source_target_pairs={{1,2},{2,1},{3,4},{4,3},{5,6},{6,5},{7,8},{8,7},{9,10},{10,9},{11,... | collective-permute-start | bytes 786440 | tf_op jit(solution)/shard_map/ppermute | solution.py:22
  50.1 1.9 %collective-permute-start.8 = (f32[32,8,256]{2,1,0:T(8,128)}, f32[32,8,256]{2,1,0:T(8,128)}, u32[]{:S(2)}, u32[]{:S(2)}) collective-permute-start(f32[32,8,256]{2,1,0:T(8,128)} %get-tuple-element.39), channel_id=1, source_target_pairs={{0,1},{1,0},{2,3},{3,2},{4,5},{5,4},{6,7},{7,6},{8,9},{9,8},{10,11... | collective-permute-start | bytes 786440 | tf_op jit(solution)/shard_map/ppermute | solution.py:22
  52.1 1.9 %collective-permute-start.9 = (f32[8,16,256]{2,1,0:T(8,128)}, f32[8,16,256]{2,1,0:T(8,128)}, u32[]{:S(2)}, u32[]{:S(2)}) collective-permute-start(f32[8,16,256]{2,1,0:T(8,128)} %get-tuple-element.40), channel_id=1, source_target_pairs={{32,64},{64,32},{33,65},{65,33},{34,66},{66,34},{35,67},{67,35},{3... | collective-permute-start | bytes 393224 | tf_op jit(solution)/shard_map/ppermute | solution.py:22
  54.0 1.9 %collective-permute-start.10 = (f32[8,16,256]{2,1,0:T(8,128)}, f32[8,16,256]{2,1,0:T(8,128)}, u32[]{:S(2)}, u32[]{:S(2)}) collective-permute-start(f32[8,16,256]{2,1,0:T(8,128)} %get-tuple-element.41), channel_id=1, source_target_pairs={{0,32},{32,0},{64,96},{96,64},{1,33},{33,1},{65,97},{97,65},{2,34}... | collective-permute-start | bytes 393224 | tf_op jit(solution)/shard_map/ppermute | solution.py:22
  59.7 1.0 %copy-done.15 = f32[32,16,256]{2,1,0:T(8,128)S(1)} copy-done((f32[32,16,256]{2,1,0:T(8,128)S(1)}, f32[32,16,256]{2,1,0:T(8,128)}, u32[]{:S(2)}) %copy-start.15) | copy-done | bytes 524312
  60.7 1.6 %shard_map.144 = (f32[32,16,256]{2,1,0:T(8,128)S(1)}, f32[32,16,256]{2,1,0:T(8,128)S(1)}, f32[32,16,256]{2,1,0:T(8,128)S(1)}) custom-call(f32[32,16,256]{2,1,0:T(8,128)S(1)} %bitcast.12, f32[32,16,256]{2,1,0:T(8,128)S(1)} %copy-done.13, f32[32,16,256]{2,1,0:T(8,128)S(1)} %bitcast.6, f32[32,16,256]{2,1,0:T(8,128)S(1)} %bitcast.14, ...), custom_call_target="tpu_custom_call" | custom-call | tf_op jit(solution)/shard_map/pallas_call | solution.py:398
  62.4 2.1 %shard_map.145 = (f32[32,16,256]{2,1,0:T(8,128)S(1)}, f32[32,16,256]{2,1,0:T(8,128)S(1)}, f32[32,16,256]{2,1,0:T(8,128)S(1)}, f32[32,16,256]{2,1,0:T(8,128)S(1)}...) custom-call(s32[1,3]{1,0:T(1,128)S(1)} %copy-done.18, ...), custom_call_target="tpu_custom_call", output_to_operand_aliasing={{0}: (6, {}), {1}: (7, {}), {2}: (8, {})} | custom-call | tf_op jit(solution)/shard_map/pallas_call | solution.py:401
  64.5 5.9 %collective-permute-start.11 = (f32[32,8,256]{2,1,0:T(8,128)S(1)}, f32[32,8,256]{2,1,0:T(8,128)S(1)}, u32[]{:S(2)}, u32[]{:S(2)}) collective-permute-start(f32[32,8,256]{2,1,0:T(8,128)S(1)} %get-tuple-element.49), channel_id=1, source_target_pairs={{1,2},{2,1},{3,4},{4,3},{5,6},{6,5},{7,8},{8,7},{9,10},{10,9},{11,... | collective-permute-start | bytes 786440 | tf_op jit(solution)/shard_map/ppermute | solution.py:22
  70.4 1.9 %collective-permute-start.12 = (f32[32,8,256]{2,1,0:T(8,128)S(1)}, f32[32,8,256]{2,1,0:T(8,128)S(1)}, u32[]{:S(2)}, u32[]{:S(2)}) collective-permute-start(f32[32,8,256]{2,1,0:T(8,128)S(1)} %get-tuple-element.50), channel_id=1, source_target_pairs={{0,1},{1,0},{2,3},{3,2},{4,5},{5,4},{6,7},{7,6},{8,9},{9,8},{10,11... | collective-permute-start | bytes 786440 | tf_op jit(solution)/shard_map/ppermute | solution.py:22
  72.3 2.8 %collective-permute-start.13 = (f32[8,16,256]{2,1,0:T(8,128)S(1)}, f32[8,16,256]{2,1,0:T(8,128)S(1)}, u32[]{:S(2)}, u32[]{:S(2)}) collective-permute-start(f32[8,16,256]{2,1,0:T(8,128)S(1)} %get-tuple-element.51), channel_id=1, source_target_pairs={{32,64},{64,32},{33,65},{65,33},{34,66},{66,34},{35,67},{67,35},{3... | collective-permute-start | bytes 393224 | tf_op jit(solution)/shard_map/ppermute | solution.py:22
  75.0 1.9 %collective-permute-start.14 = (f32[8,16,256]{2,1,0:T(8,128)S(1)}, f32[8,16,256]{2,1,0:T(8,128)S(1)}, u32[]{:S(2)}, u32[]{:S(2)}) collective-permute-start(f32[8,16,256]{2,1,0:T(8,128)S(1)} %get-tuple-element.52), channel_id=1, source_target_pairs={{0,32},{32,0},{64,96},{96,64},{1,33},{33,1},{65,97},{97,65},{2,34}... | collective-permute-start | bytes 393224 | tf_op jit(solution)/shard_map/ppermute | solution.py:22
  77.0 1.4 %shard_map.146 = (f32[32,16,256]{2,1,0:T(8,128)S(1)}, f32[32,16,256]{2,1,0:T(8,128)S(1)}) custom-call(f32[32,16,256]{2,1,0:T(8,128)S(1)} %get-tuple-element.53.wave3, f32[32,16,256]{2,1,0:T(8,128)S(1)} %get-tuple-element.54.image3, f32[32,16,256]{2,1,0:T(8,128)S(1)} %get-tuple-element.55.adj3, f32[32,16,256]{2,1,0:T(8,128)S(1)} %bitcast.7, ...), custom_call_target="tpu_custom_call" | custom-call | tf_op jit(solution)/shard_map/pallas_call | solution.py:406
  78.8 1.9 %collective-permute-done.12.ya = f32[32,8,256]{2,1,0:T(8,128)S(1)} collective-permute-done((f32[32,8,256]{2,1,0:T(8,128)S(1)}, f32[32,8,256]{2,1,0:T(8,128)S(1)}, u32[]{:S(2)}, u32[]{:S(2)}) %collective-permute-start.12) | collective-permute-done | bytes 262176 | tf_op jit(solution)/shard_map/ppermute | solution.py:22
  80.7 1.4 %shard_map.147 = (f32[16,16,128]{2,1,0:T(8,128)S(1)}, f32[16,16,128]{2,1,0:T(8,128)S(1)}, f32[32,16,128]{2,1,0:T(8,128)S(1)}, f32[32,16,128]{2,1,0:T(8,128)S(1)}...) custom-call(s32[1]{0:T(128)S(6)} %copy.27.offsets, f32[32,8,256]{2,1,0:T(8,128)S(1)} %collective-permute-done.11.yb, ...), custom_call_target="tpu_custom_call" | custom-call | tf_op jit(solution)/shard_map/pallas_call | solution.py:409
  82.1 2.2 %collective-permute-start.17 = (f32[16,16,128]{2,1,0:T(8,128)S(1)}, f32[16,16,128]{2,1,0:T(8,128)S(1)}, u32[]{:S(2)}, u32[]{:S(2)}) collective-permute-start(f32[16,16,128]{2,1,0:T(8,128)S(1)} %get-tuple-element.63), channel_id=1, source_target_pairs={{0,128},{128,0},{256,384},{384,256},{1,129},{129,1},{257,385},{385... | collective-permute-start | bytes 393224 | tf_op jit(solution)/shard_map/ppermute | solution.py:30
  84.3 4.4 %collective-permute-start.15 = (f32[16,16,128]{2,1,0:T(8,128)S(1)}, f32[16,16,128]{2,1,0:T(8,128)S(1)}, u32[]{:S(2)}, u32[]{:S(2)}) collective-permute-start(f32[16,16,128]{2,1,0:T(8,128)S(1)} %get-tuple-element.61), channel_id=1, source_target_pairs={{128,256},{256,128},{384,0},{0,384},{129,257},{257,129},{385,1},{1... | collective-permute-start | bytes 393224 | tf_op jit(solution)/shard_map/ppermute | solution.py:30
  89.0 4.7 %collective-permute-start.18 = (f32[32,16,128]{2,1,0:T(8,128)S(1)}, f32[32,16,128]{2,1,0:T(8,128)S(1)}, u32[]{:S(2)}, u32[]{:S(2)}) collective-permute-start(f32[32,16,128]{2,1,0:T(8,128)S(1)} %shard_map.149), channel_id=1, source_target_pairs={{128,256},{256,128},{384,0},{0,384},{129,257},{257,129},{385,1},{1... | collective-permute-start | bytes 786440 | tf_op jit(solution)/shard_map/ppermute | solution.py:30
  93.7 1.9 %collective-permute-start.16 = (f32[32,16,128]{2,1,0:T(8,128)S(1)}, f32[32,16,128]{2,1,0:T(8,128)S(1)}, u32[]{:S(2)}, u32[]{:S(2)}) collective-permute-start(f32[32,16,128]{2,1,0:T(8,128)S(1)} %shard_map.148), channel_id=1, source_target_pairs={{0,128},{128,0},{256,384},{384,256},{1,129},{129,1},{257,385},{385... | collective-permute-start | bytes 786440 | tf_op jit(solution)/shard_map/ppermute | solution.py:30
  96.5 2.7 %collective-permute-done.18.b = f32[32,16,128]{2,1,0:T(8,128)S(1)} collective-permute-done((f32[32,16,128]{2,1,0:T(8,128)S(1)}, f32[32,16,128]{2,1,0:T(8,128)S(1)}, u32[]{:S(2)}, u32[]{:S(2)}) %collective-permute-start.18) | collective-permute-done | bytes 262176 | tf_op jit(solution)/shard_map/ppermute | solution.py:30
  99.2 2.8 %collective-permute-done.16.a = f32[32,16,128]{2,1,0:T(8,128)S(1)} collective-permute-done((f32[32,16,128]{2,1,0:T(8,128)S(1)}, f32[32,16,128]{2,1,0:T(8,128)S(1)}, u32[]{:S(2)}, u32[]{:S(2)}) %collective-permute-start.16) | collective-permute-done | bytes 262176 | tf_op jit(solution)/shard_map/ppermute | solution.py:30
  (64 shorter events, 12.2 us)
Async XLA Ops:
  0.6 41.5 %collective-permute-start.1 = (f32[32,16,128]{2,1,0:T(8,128)}, f32[32,16,128]{2,1,0:T(8,128)S(1)}, u32[]{:S(2)}, u32[]{:S(2)}) collective-permute-start(f32[32,16,128]{2,1,0:T(8,128)} %tile.1), channel_id=1, source_target_pairs={{128,256},{256,128},{384,0},{0,384},{129,257},{257,129},{385,1},{1... | collective-permute-start | bytes 786440 | tf_op jit(solution)/shard_map/ppermute | solution.py:30
  5.3 36.9 %collective-permute-start = (f32[32,16,128]{2,1,0:T(8,128)}, f32[32,16,128]{2,1,0:T(8,128)S(1)}, u32[]{:S(2)}, u32[]{:S(2)}) collective-permute-start(f32[32,16,128]{2,1,0:T(8,128)} %tile.1), channel_id=1, source_target_pairs={{0,128},{128,0},{256,384},{384,256},{1,129},{129,1},{257,385},{385... | collective-permute-start | bytes 786440 | tf_op jit(solution)/shard_map/ppermute | solution.py:30
  7.4 34.7 %collective-permute-start.2 = (f32[32,16,128]{2,1,0:T(8,128)}, f32[32,16,128]{2,1,0:T(8,128)S(1)}, u32[]{:S(2)}, u32[]{:S(2)}) collective-permute-start(f32[32,16,128]{2,1,0:T(8,128)} %tile.1), channel_id=1, source_target_pairs={{0,256},{128,384},{256,0},{384,128},{1,257},{129,385},{257,1},{385... | collective-permute-start | bytes 786440 | tf_op jit(solution)/shard_map/ppermute | solution.py:35
  11.1 1.0 %copy-start.3 = (f32[1,32,16,256]{3,2,1,0:T(8,128)S(1)}, f32[1,32,16,256]{3,2,1,0:T(8,128)}, u32[]{:S(2)}) copy-start(f32[1,32,16,256]{3,2,1,0:T(8,128)} %param.16) | copy-start | bytes 1572868
  12.2 5.6 %collective-permute-start.5 = (f32[4,16,256]{2,1,0:T(8,128)S(1)}, f32[4,16,256]{2,1,0:T(8,128)S(1)}, u32[]{:S(2)}, u32[]{:S(2)}) collective-permute-start(f32[4,16,256]{2,1,0:T(8,128)S(1)} %get-tuple-element.36), channel_id=1, source_target_pairs={{32,64},{64,32},{33,65},{65,33},{34,66},{66,34},{35,67},{67,35},{3... | collective-permute-start | bytes 196616 | tf_op jit(solution)/shard_map/ppermute | solution.py:22
  14.1 15.7 %collective-permute-start.6 = (f32[4,16,256]{2,1,0:T(8,128)S(1)}, f32[4,16,256]{2,1,0:T(8,128)S(1)}, u32[]{:S(2)}, u32[]{:S(2)}) collective-permute-start(f32[4,16,256]{2,1,0:T(8,128)S(1)} %get-tuple-element.37), channel_id=1, source_target_pairs={{0,32},{32,0},{64,96},{96,64},{1,33},{33,1},{65,97},{97,65},{2,34}... | collective-permute-start | bytes 196616 | tf_op jit(solution)/shard_map/ppermute | solution.py:22
  17.8 15.0 %collective-permute-start.3 = (f32[16,8,256]{2,1,0:T(8,128)S(1)}, f32[16,8,256]{2,1,0:T(8,128)S(1)}, u32[]{:S(2)}, u32[]{:S(2)}) collective-permute-start(f32[16,8,256]{2,1,0:T(8,128)S(1)} %get-tuple-element.34), channel_id=1, source_target_pairs={{1,2},{2,1},{3,4},{4,3},{5,6},{6,5},{7,8},{8,7},{9,10},{10,9},{11,... | collective-permute-start | bytes 393224 | tf_op jit(solution)/shard_map/ppermute | solution.py:22
  29.9 6.9 %collective-permute-start.4 = (f32[16,8,256]{2,1,0:T(8,128)S(1)}, f32[16,8,256]{2,1,0:T(8,128)S(1)}, u32[]{:S(2)}, u32[]{:S(2)}) collective-permute-start(f32[16,8,256]{2,1,0:T(8,128)S(1)} %get-tuple-element.35), channel_id=1, source_target_pairs={{0,1},{1,0},{2,3},{3,2},{4,5},{5,4},{6,7},{7,6},{8,9},{9,8},{10,11... | collective-permute-start | bytes 393224 | tf_op jit(solution)/shard_map/ppermute | solution.py:22
  31.8 10.4 %copy-start.18 = (s32[1,3]{1,0:T(1,128)S(1)}, s32[1,3]{1,0:T(1,128)}, u32[]{:S(2)}) copy-start(s32[1,3]{1,0:T(1,128)} %cell.3) | copy-start | bytes 40
  31.8 10.4 %copy-start.19 = (f32[1,2]{1,0:T(1,128)S(1)}, f32[1,2]{1,0:T(1,128)}, u32[]{:S(2)}) copy-start(f32[1,2]{1,0:T(1,128)} %amp.3) | copy-start | bytes 28
  36.7 1.4 %copy-start = (bf16[2,2,256,768]{3,2,1,0:T(8,128)(2,1)S(1)}, bf16[2,2,256,768]{3,2,1,0:T(8,128)(2,1)}, u32[]{:S(2)}) copy-start(bf16[2,2,256,768]{3,2,1,0:T(8,128)(2,1)} %constant.8.clone.outer) | copy-start | bytes 4718596
  41.2 1.2 %copy-start.10 = (f32[1,32,16,256]{3,2,1,0:T(8,128)S(1)}, f32[1,32,16,256]{3,2,1,0:T(8,128)}, u32[]{:S(2)}) copy-start(f32[1,32,16,256]{3,2,1,0:T(8,128)} %param.15) | copy-start | bytes 1572868
  41.2 1.3 %copy-start.17 = (f32[32,16,128]{2,1,0:T(8,128)S(1)}, f32[32,16,128]{2,1,0:T(8,128)}, u32[]{:S(2)}) copy-start(f32[32,16,128]{2,1,0:T(8,128)} %tile.1) | copy-start | bytes 786436
  42.4 13.5 %copy-start.20 = (s32[1,256,3]{1,0,2:T(1,128)S(1)}, s32[1,256,3]{1,0,2:T(1,128)}, u32[]{:S(2)}) copy-start(s32[1,256,3]{1,0,2:T(1,128)} %param.21) | copy-start | bytes 9220
  42.5 13.6 %copy-start.21 = (f32[1,256,2]{1,2,0:T(2,128)S(1)}, f32[1,256,2]{1,2,0:T(2,128)}, u32[]{:S(2)}) copy-start(f32[1,256,2]{1,2,0:T(2,128)} %param.22) | copy-start | bytes 6148
  42.5 16.1 %copy-start.5 = (f32[1,32,16,256]{3,2,1,0:T(8,128)S(1)}, f32[1,32,16,256]{3,2,1,0:T(8,128)}, u32[]{:S(2)}) copy-start(f32[1,32,16,256]{3,2,1,0:T(8,128)} %param.16) | copy-start | bytes 1572868
  42.5 16.1 %copy-start.7 = (bf16[256,768]{1,0:T(8,128)(2,1)S(1)}, bf16[256,768]{1,0:T(8,128)(2,1)}, u32[]{:S(2)}) copy-start(bf16[256,768]{1,0:T(8,128)(2,1)} %constant.7.clone.along_y) | copy-start | bytes 1179652
  42.5 16.1 %copy-start.9 = (bf16[768,256]{1,0:T(8,128)(2,1)S(1)}, bf16[768,256]{1,0:T(8,128)(2,1)}, u32[]{:S(2)}) copy-start(bf16[768,256]{1,0:T(8,128)(2,1)} %constant.6.clone.along_z) | copy-start | bytes 1179652
  42.5 16.1 %copy-start.11 = (f32[1,32,16,256]{3,2,1,0:T(8,128)S(1)}, f32[1,32,16,256]{3,2,1,0:T(8,128)}, u32[]{:S(2)}) copy-start(f32[1,32,16,256]{3,2,1,0:T(8,128)} %param.18) | copy-start | bytes 1572868
  46.5 15.8 %collective-permute-start.7 = (f32[32,8,256]{2,1,0:T(8,128)}, f32[32,8,256]{2,1,0:T(8,128)}, u32[]{:S(2)}, u32[]{:S(2)}) collective-permute-start(f32[32,8,256]{2,1,0:T(8,128)} %get-tuple-element.38), channel_id=1, source_target_pairs={{1,2},{2,1},{3,4},{4,3},{5,6},{6,5},{7,8},{8,7},{9,10},{10,9},{11,... | collective-permute-start | bytes 786440 | tf_op jit(solution)/shard_map/ppermute | solution.py:22
  50.1 12.2 %collective-permute-start.8 = (f32[32,8,256]{2,1,0:T(8,128)}, f32[32,8,256]{2,1,0:T(8,128)}, u32[]{:S(2)}, u32[]{:S(2)}) collective-permute-start(f32[32,8,256]{2,1,0:T(8,128)} %get-tuple-element.39), channel_id=1, source_target_pairs={{0,1},{1,0},{2,3},{3,2},{4,5},{5,4},{6,7},{7,6},{8,9},{9,8},{10,11... | collective-permute-start | bytes 786440 | tf_op jit(solution)/shard_map/ppermute | solution.py:22
  52.1 10.3 %collective-permute-start.9 = (f32[8,16,256]{2,1,0:T(8,128)}, f32[8,16,256]{2,1,0:T(8,128)}, u32[]{:S(2)}, u32[]{:S(2)}) collective-permute-start(f32[8,16,256]{2,1,0:T(8,128)} %get-tuple-element.40), channel_id=1, source_target_pairs={{32,64},{64,32},{33,65},{65,33},{34,66},{66,34},{35,67},{67,35},{3... | collective-permute-start | bytes 393224 | tf_op jit(solution)/shard_map/ppermute | solution.py:22
  54.0 8.4 %collective-permute-start.10 = (f32[8,16,256]{2,1,0:T(8,128)}, f32[8,16,256]{2,1,0:T(8,128)}, u32[]{:S(2)}, u32[]{:S(2)}) collective-permute-start(f32[8,16,256]{2,1,0:T(8,128)} %get-tuple-element.41), channel_id=1, source_target_pairs={{0,32},{32,0},{64,96},{96,64},{1,33},{33,1},{65,97},{97,65},{2,34}... | collective-permute-start | bytes 393224 | tf_op jit(solution)/shard_map/ppermute | solution.py:22
  60.7 1.7 %copy-start.1 = (bf16[2,2,256,768]{3,2,1,0:T(8,128)(2,1)S(1)}, bf16[2,2,256,768]{3,2,1,0:T(8,128)(2,1)}, u32[]{:S(2)}) copy-start(bf16[2,2,256,768]{3,2,1,0:T(8,128)(2,1)} %constant.8.clone.outer) | copy-start | bytes 4718596
  64.5 14.3 %collective-permute-start.11 = (f32[32,8,256]{2,1,0:T(8,128)S(1)}, f32[32,8,256]{2,1,0:T(8,128)S(1)}, u32[]{:S(2)}, u32[]{:S(2)}) collective-permute-start(f32[32,8,256]{2,1,0:T(8,128)S(1)} %get-tuple-element.49), channel_id=1, source_target_pairs={{1,2},{2,1},{3,4},{4,3},{5,6},{6,5},{7,8},{8,7},{9,10},{10,9},{11,... | collective-permute-start | bytes 786440 | tf_op jit(solution)/shard_map/ppermute | solution.py:22
  70.4 10.3 %collective-permute-start.12 = (f32[32,8,256]{2,1,0:T(8,128)S(1)}, f32[32,8,256]{2,1,0:T(8,128)S(1)}, u32[]{:S(2)}, u32[]{:S(2)}) collective-permute-start(f32[32,8,256]{2,1,0:T(8,128)S(1)} %get-tuple-element.50), channel_id=1, source_target_pairs={{0,1},{1,0},{2,3},{3,2},{4,5},{5,4},{6,7},{7,6},{8,9},{9,8},{10,11... | collective-permute-start | bytes 786440 | tf_op jit(solution)/shard_map/ppermute | solution.py:22
  72.3 6.3 %collective-permute-start.13 = (f32[8,16,256]{2,1,0:T(8,128)S(1)}, f32[8,16,256]{2,1,0:T(8,128)S(1)}, u32[]{:S(2)}, u32[]{:S(2)}) collective-permute-start(f32[8,16,256]{2,1,0:T(8,128)S(1)} %get-tuple-element.51), channel_id=1, source_target_pairs={{32,64},{64,32},{33,65},{65,33},{34,66},{66,34},{35,67},{67,35},{3... | collective-permute-start | bytes 393224 | tf_op jit(solution)/shard_map/ppermute | solution.py:22
  75.0 3.5 %collective-permute-start.14 = (f32[8,16,256]{2,1,0:T(8,128)S(1)}, f32[8,16,256]{2,1,0:T(8,128)S(1)}, u32[]{:S(2)}, u32[]{:S(2)}) collective-permute-start(f32[8,16,256]{2,1,0:T(8,128)S(1)} %get-tuple-element.52), channel_id=1, source_target_pairs={{0,32},{32,0},{64,96},{96,64},{1,33},{33,1},{65,97},{97,65},{2,34}... | collective-permute-start | bytes 393224 | tf_op jit(solution)/shard_map/ppermute | solution.py:22
  82.1 6.9 %collective-permute-start.17 = (f32[16,16,128]{2,1,0:T(8,128)S(1)}, f32[16,16,128]{2,1,0:T(8,128)S(1)}, u32[]{:S(2)}, u32[]{:S(2)}) collective-permute-start(f32[16,16,128]{2,1,0:T(8,128)S(1)} %get-tuple-element.63), channel_id=1, source_target_pairs={{0,128},{128,0},{256,384},{384,256},{1,129},{129,1},{257,385},{385... | collective-permute-start | bytes 393224 | tf_op jit(solution)/shard_map/ppermute | solution.py:30
  84.3 9.4 %collective-permute-start.15 = (f32[16,16,128]{2,1,0:T(8,128)S(1)}, f32[16,16,128]{2,1,0:T(8,128)S(1)}, u32[]{:S(2)}, u32[]{:S(2)}) collective-permute-start(f32[16,16,128]{2,1,0:T(8,128)S(1)} %get-tuple-element.61), channel_id=1, source_target_pairs={{128,256},{256,128},{384,0},{0,384},{129,257},{257,129},{385,1},{1... | collective-permute-start | bytes 393224 | tf_op jit(solution)/shard_map/ppermute | solution.py:30
  89.0 10.2 %collective-permute-start.18 = (f32[32,16,128]{2,1,0:T(8,128)S(1)}, f32[32,16,128]{2,1,0:T(8,128)S(1)}, u32[]{:S(2)}, u32[]{:S(2)}) collective-permute-start(f32[32,16,128]{2,1,0:T(8,128)S(1)} %shard_map.149), channel_id=1, source_target_pairs={{128,256},{256,128},{384,0},{0,384},{129,257},{257,129},{385,1},{1... | collective-permute-start | bytes 786440 | tf_op jit(solution)/shard_map/ppermute | solution.py:30
  93.7 8.3 %collective-permute-start.16 = (f32[32,16,128]{2,1,0:T(8,128)S(1)}, f32[32,16,128]{2,1,0:T(8,128)S(1)}, u32[]{:S(2)}, u32[]{:S(2)}) collective-permute-start(f32[32,16,128]{2,1,0:T(8,128)S(1)} %shard_map.148), channel_id=1, source_target_pairs={{0,128},{128,0},{256,384},{384,256},{1,129},{129,1},{257,385},{385... | collective-permute-start | bytes 786440 | tf_op jit(solution)/shard_map/ppermute | solution.py:30
  (9 other events, 8.7 us)

commit v3 on v2

--- a/solution.py
+++ b/solution.py
@@ -2,7 +2,6 @@
 
 import jax
 import jax.numpy as jnp
-import numpy as np
 from jax import lax
 from jax.experimental import pallas as pl
 from jax.experimental.pallas import tpu as pltpu
@@ -40,7 +39,7 @@
     return swap(yb, "gy", 1), swap(ya, "gy", 0), swap(xb, "gx", 1), swap(xa, "gx", 0)
 
 
-def call(body, out_shape, scratch=(), smem=0, n_in=0, room=4, aliases=None):
+def call(body, out_shape, scratch=(), smem=0, n_in=0, room=4, aliases=None, flops=0):
     vmem = pl.BlockSpec(memory_space=pltpu.VMEM)
     scal = pl.BlockSpec(memory_space=pltpu.SMEM)
     return pl.pallas_call(
@@ -50,6 +49,7 @@
         out_specs=jax.tree.map(lambda _: vmem, out_shape),
         scratch_shapes=list(scratch),
         input_output_aliases=aliases or {},
+        cost_estimate=pl.CostEstimate(flops=flops, bytes_accessed=0, transcendentals=0),
         compiler_params=pltpu.CompilerParams(vmem_limit_bytes=room << 20),
     )
 
@@ -63,31 +63,11 @@
 
 
 def weight(distance):
-    distance = np.abs(distance)
-    return np.where(distance <= 4, np.take(np.asarray(WEIGHT), np.minimum(distance, 4)), 0.0)
-
-
-def difference_tables(size_y, depth, chunk):
-    z = np.arange(depth)
-    along_z = weight(z[:, None] - z[None, :])
-    row = np.arange(chunk * size_y)
-    x, y = row // size_y, row % size_y
-    along_y = np.where(x[:, None] == x[None, :], weight(y[:, None] - y[None, :]), 0.0)
-    edge = np.arange(chunk * 8)
-    edge_x, edge_field, edge_row = edge // 8, edge % 8 // 4, edge % 4
-    outer = np.zeros((2, 2, chunk * size_y, 2, chunk * 8))
-    for parity in range(2):
-        for field in range(2):
-            for message in range(2):
-                place = edge_row + size_y if parity == message else edge_row - 4
-                use = (x[:, None] == edge_x[None, :]) & (edge_field[None, :] == field)
-                outer[parity, field, :, message] = np.where(use, weight(y[:, None] - place[None, :]), 0.0)
-    outer = outer.reshape(2, 2, chunk * size_y, 2 * chunk * 8)
-    return (
-        jnp.asarray(np.concatenate([along_z] * 3, axis=0), jnp.bfloat16),
-        jnp.asarray(np.concatenate([along_y] * 3, axis=1), jnp.bfloat16),
-        jnp.asarray(np.concatenate([outer] * 3, axis=3), jnp.bfloat16),
-    )
+    distance = jnp.abs(distance)
+    total = jnp.zeros(distance.shape, F32)
+    for k in range(1, 5):
+        total = jnp.where(distance == k, WEIGHT[k], total)
+    return total
 
 
 def three(value):
@@ -106,18 +86,18 @@
     chunk = along_y.shape[0] // size_y
     for at in range(0, size_x, chunk):
         parts = three(field[at : at + chunk].reshape(chunk * size_y, depth))
-        total = product(jnp.concatenate(parts, axis=1), along_z[...])
-        total = total + product(along_y[...], jnp.concatenate(parts, axis=0))
+        total = sum(product(part, along_z[...]) + product(along_y[...], part) for part in parts)
         out[at : at + chunk] = total.reshape(chunk, size_y, depth)
 
 
 def outer_part(ya, yb, at, outer, field, size_y):
     depth = ya.shape[2]
-    chunk = outer.shape[2] // size_y
-    a, b = (three(m[at : at + chunk].reshape(chunk * 8, depth)) for m in (ya, yb))
-    stacked = jnp.concatenate([a[0], b[0], a[1], b[1], a[2], b[2]], axis=0)
-    parity = jnp.where(even("gy"), 0, 1)
-    return product(outer[parity, field], stacked).reshape(chunk, size_y, depth)
+    chunk = outer.shape[1] // size_y
+    a, b = (m[at : at + chunk].reshape(chunk * 8, depth) for m in (ya, yb))
+    even_y = even("gy")
+    below, above = three(jnp.where(even_y, b, a)), three(jnp.where(even_y, a, b))
+    total = sum(product(outer[field], jnp.concatenate(pair, axis=0)) for pair in zip(below, above))
+    return total.reshape(chunk, size_y, depth)
 
 
 def outside_x(xa, xb, plane, out):
@@ -134,7 +114,7 @@
 
 
 def outer_parts(ya, yb, xa, xb, outer, size_x, size_y, sides, extras):
-    chunk = outer.shape[2] // size_y
+    chunk = outer.shape[1] // size_y
     for field, (side, extra) in enumerate(zip(sides, extras)):
         outside_x(xa, xb, 4 * field, side)
         for at in range(0, size_x, chunk):
@@ -170,19 +150,6 @@
     top = size_x - 4
     xa[plane : plane + 4] = field[pl.ds(jnp.where(even_x, top, 0), 4)]
     xb[plane : plane + 4] = field[pl.ds(jnp.where(even_x, 0, top), 4)]
-
-
-def add_source(cell, amount, field):
-    size_x, size_y, depth = field.shape
-    x = cell[0, 0] - lax.axis_index("gx") * size_x
-    y = cell[0, 1] - lax.axis_index("gy") * size_y
-
-    @pl.when((x >= 0) & (x < size_x) & (y >= 0) & (y < size_y))
-    def _():
-        at = (lax.broadcasted_iota(jnp.int32, (size_y, depth), 0) == y) & (
-            lax.broadcasted_iota(jnp.int32, (size_y, depth), 1) == cell[0, 2]
-        )
-        field[x] = field[x] + jnp.where(at, amount, 0.0)
 
 
 def edges_kernel(field, ya, yb, xa, xb):
@@ -199,47 +166,76 @@
     xb[...] = field[pl.ds(jnp.where(even_x, 0, top), 4)]
 
 
-def tables_kernel(size_x, size_y, cells, res, inject0, inject1):
+def tables_kernel(
+    size_x, size_y, cell, amp, cells, res, along_y, along_z, outer, source0, source1, inject0, inject1
+):
     depth = inject0.shape[2]
+    half = size_x // 2
+    rows = half * size_y
+
+    def index(shape, dim):
+        return lax.broadcasted_iota(jnp.int32, shape, dim)
+
+    along_z[...] = weight(index((depth, depth), 0) - index((depth, depth), 1)).astype(jnp.bfloat16)
+    here, there = index((rows, rows), 0), index((rows, rows), 1)
+    near = jnp.where(here // size_y == there // size_y, weight(here - there), 0.0)
+    along_y[...] = near.astype(jnp.bfloat16)
+    here, there = index((rows, half * 8), 0), index((rows, half * 8), 1)
+    y, row = lax.rem(here, size_y), lax.rem(there, 4)
+    below, above = weight(y - row + 4), weight(row + size_y - y)
+    for field in range(2):
+        use = (here // size_y == there // 8) & (lax.rem(there, 8) // 4 == field)
+        both = jnp.concatenate([jnp.where(use, below, 0.0), jnp.where(use, above, 0.0)], axis=1)
+        outer[field] = both.astype(jnp.bfloat16)
+
+    base_x, base_y = lax.axis_index("gx") * size_x, lax.axis_index("gy") * size_y
+    x, y = cell[0, 0] - base_x, cell[0, 1] - base_y
+    source0[...] = jnp.zeros_like(source0)
+    source1[...] = jnp.zeros_like(source1)
+
+    @pl.when((x >= 0) & (x < size_x) & (y >= 0) & (y < size_y))
+    def _():
+        at = (index((size_y, depth), 0) == y) & (index((size_y, depth), 1) == cell[0, 2])
+        source0[x] = jnp.where(at, amp[0, 0], 0.0)
+        source1[x] = jnp.where(at, amp[0, 1], 0.0)
+
     count = cells.shape[1]
-    pad = jnp.zeros((count, HALF - 3), jnp.int32)
-    rows = jnp.transpose(jnp.concatenate([cells[0], pad], axis=1).astype(F32))[0:8].astype(jnp.int32)
-    x = rows[0:1, :] - lax.axis_index("gx") * size_x
-    y = rows[1:2, :] - lax.axis_index("gy") * size_y
+    x, y = cells[0:1, :] - base_x, cells[1:2, :] - base_y
     inside = (x >= 0) & (x < size_x) & (y >= 0) & (y < size_y)
     place = jnp.where(inside, x * size_y + y, -1)
-    deep = lax.broadcasted_iota(jnp.int32, (count, depth), 1) == cells[0, :, 2:3]
-    parts = [three(jnp.where(deep, res[0, :, n : n + 1], 0.0)) for n in range(2)]
-    spread = jnp.concatenate([jnp.concatenate([parts[0][i], parts[1][i]], axis=1) for i in range(3)], axis=0)
-    half = size_x // 2
+    deep = index((depth, count), 0) == cells[2:3, :]
+    parts = [three(jnp.where(deep, res[n : n + 1, :], 0.0)) for n in range(2)]
     for part in range(2):
-        at = lax.broadcasted_iota(jnp.int32, (half * size_y, count), 0) + part * half * size_y
+        at = index((rows, count), 0) + part * rows
         flat = jnp.where(at == place, 1.0, 0.0).astype(jnp.bfloat16)
-        done = product(jnp.concatenate([flat] * 3, axis=1), spread)
         for n, out in enumerate((inject0, inject1)):
-            block = done[:, n * depth : (n + 1) * depth]
-            out[part * half : (part + 1) * half] = block.reshape(half, size_y, depth)
-
-
-def first_kernel(wave1, yb, ya, xb, xa, along_y, along_z, outer, lap1, flat, space):
+            done = sum(
+                lax.dot_general(flat, p, (((1,), (1,)), ((), ())), preferred_element_type=F32) for p in parts[n]
+            )
+            out[part * half : (part + 1) * half] = done.reshape(half, size_y, depth)
+
+
+def first_inner_kernel(wave1, yb, ya, along_y, along_z, outer, lap1, flat):
     size_x, size_y = wave1.shape[0], wave1.shape[1]
-    even_x = even("gx")
     flat_part(wave1, along_y, along_z, flat)
     half = size_x // 2
     for part in range(2):
         x = slice(part * half, (part + 1) * half)
         flat[x] = flat[x] + outer_part(ya, yb, 0, outer, part, size_y)
-    space[4 : size_x + 4] = wave1[...]
-    space[pl.ds(jnp.where(even_x, size_x + 4, 0), 4)] = xa[...]
-    space[pl.ds(jnp.where(even_x, 0, size_x + 4), 4)] = xb[...]
     for x in range(size_x):
         for z in halves():
-            lap = across(lambda i, z: space[i + 4, :, z], x, z)
-            lap1[x, :, z] = lap + flat[x, :, z] * (1.0 / SCALE)
+            lap1[x, :, z] = across(within(wave1), x, z) + flat[x, :, z] * (1.0 / SCALE)
+
+
+def first_kernel(inner, xb, xa, lap1, side):
+    size_x = lap1.shape[0]
+    outside_x(xa, xb, 0, side)
+    lap1[0:4] = inner[0:4] + side[0:4]
+    lap1[size_x - 4 : size_x] = inner[size_x - 4 : size_x] + side[4:8]
 
 
 def second_kernel(
-    offsets, cell, amp, tile, tile_a, tile_b, tile_ab, lap1, wave0, wave1, adj4,
+    offsets, tile, tile_a, tile_b, tile_ab, lap1, wave0, wave1, adj4, source,
     vel, wave2, image, ya, yb, xa, xb, column,
 ):
     size_x, size_y = wave1.shape[0], wave1.shape[1]
@@ -260,17 +256,16 @@
             v = jnp.where(lane < HALF - shift_by, rolled[h], rolled[h + 1])
             vel[x, :, z] = v
             image[x, :, z] = v * adj4[x, :, z]
-            wave2[x, :, z] = 2.0 * wave1[x, :, z] - wave0[x, :, z] + v * lap1[x, :, z]
+            wave2[x, :, z] = 2.0 * wave1[x, :, z] - wave0[x, :, z] + v * lap1[x, :, z] + source[x, :, z]
         return 0
 
     lax.fori_loop(0, size_x, body, 0, unroll=4)
-    add_source(cell, amp[0, 0], wave2)
     put_edges(wave2, 0, ya, yb, xa, xb, 0)
     put_edges(image, 4, ya, yb, xa, xb, 4)
 
 
 def third_inner_kernel(
-    wave1, wave2, adj4, adj5, vel, image, inject, along_y, along_z,
+    wave1, wave2, adj4, adj5, vel, image, source, inject, along_y, along_z,
     lap2, wave3, adj3, flat, flat2,
 ):
     flat_part(wave2, along_y, along_z, flat)
@@ -279,13 +274,13 @@
         for z in halves():
             lap = across(within(wave2), x, z) + flat[x, :, z] * (1.0 / SCALE)
             lap2[x, :, z] = lap
-            wave3[x, :, z] = 2.0 * wave2[x, :, z] - wave1[x, :, z] + vel[x, :, z] * lap
+            wave3[x, :, z] = 2.0 * wave2[x, :, z] - wave1[x, :, z] + vel[x, :, z] * lap + source[x, :, z]
             adj = across(within(image), x, z) + flat2[x, :, z] * (1.0 / SCALE)
             adj3[x, :, z] = 2.0 * adj4[x, :, z] - adj5[x, :, z] + adj + inject[x, :, z]
 
 
 def third_kernel(
-    cell, amp, yb, ya, xb, xa, lap2_in, wave3_in, adj3_in, vel, outer,
+    yb, ya, xb, xa, lap2_in, wave3_in, adj3_in, vel, outer,
     lap2, wave3, adj3, image3, pya, pyb, pxa, pxb, side, side2, extra, extra2,
 ):
     size_x, size_y = vel.shape[0], vel.shape[1]
@@ -301,7 +296,6 @@
         return 0
 
     lax.fori_loop(0, size_x, body, 0, unroll=4)
-    add_source(cell, amp[0, 1], wave3)
     put_edges(wave3, 0, pya, pyb, pxa, pxb, 0)
     put_edges(image3, 4, pya, pyb, pxa, pxb, 4)
 
@@ -376,7 +370,11 @@
     tile, half = shaped(size_x, size_y, HALF), shaped(size_x // 2, size_y, HALF)
     whole = pltpu.VMEM((size_x, size_y, depth), F32)
     side = pltpu.VMEM((8, size_y, depth), F32)
-    along_z, along_y, outer = difference_tables(size_y, depth, size_x // 2)
+    rows, bf16 = size_x // 2 * size_y, jnp.bfloat16
+    matrices = [
+        jax.ShapeDtypeStruct(dims, bf16)
+        for dims in ((rows, rows), (depth, depth), (2, rows, size_x // 2 * 16))
+    ]
 
     tile_a, tile_b = swap_shot(model_vel2, 0), swap_shot(model_vel2, 1)
     tile_ab = swap_across(model_vel2)
@@ -384,24 +382,25 @@
         edges_kernel, (shaped(size_x // 2, 8, depth),) * 2 + (shaped(4, size_y, depth),) * 2, n_in=1
     )(wave1)
     halos = exchange(edges)
-    inject0, inject1 = call(functools.partial(tables_kernel, size_x, size_y), (block, block), n_in=2, room=8)(
-        rec_cell, rec_res
-    )
-    lap1 = call(
-        first_kernel, block, (whole, pltpu.VMEM((size_x + 8, size_y, depth), F32)), n_in=8, room=8
-    )(wave1, *halos, along_y, along_z, outer)
+    along_y, along_z, outer, source0, source1, inject0, inject1 = call(
+        functools.partial(tables_kernel, size_x, size_y), (*matrices, block, block, block, block),
+        smem=2, n_in=2, room=8,
+    )(src_cell, src_amp, jnp.transpose(rec_cell[0]), jnp.transpose(rec_res[0]))
+    yb, ya, xb, xa = halos
+    lap1 = call(first_inner_kernel, block, (whole,), n_in=6, room=6)(wave1, yb, ya, along_y, along_z, outer)
+    lap1 = call(first_kernel, block, (side,), n_in=3, aliases={0: 0})(lap1, xb, xa)
     vel, wave2, image, *edges = call(
         second_kernel, (block,) * 3 + (edge_y,) * 2 + (edge_x,) * 2,
-        (pltpu.VMEM((4, size_x, size_y, HALF), F32),), smem=3, n_in=8, room=8,
-    )(offsets, src_cell, src_amp, model_vel2, tile_a, tile_b, tile_ab, lap1, wave0, wave1, adj4)
+        (pltpu.VMEM((4, size_x, size_y, HALF), F32),), smem=1, n_in=9, room=8,
+    )(offsets, model_vel2, tile_a, tile_b, tile_ab, lap1, wave0, wave1, adj4, source0)
     halos = exchange(edges)
-    inner = call(third_inner_kernel, (block,) * 3, (whole,) * 2, n_in=9, room=10)(
-        wave1, wave2, adj4, adj5, vel, image, inject0, along_y, along_z
+    inner = call(third_inner_kernel, (block,) * 3, (whole,) * 2, n_in=10, room=10)(
+        wave1, wave2, adj4, adj5, vel, image, source1, inject0, along_y, along_z
     )
     lap2, wave3, adj3, image3, *edges = call(
-        third_kernel, (block,) * 4 + (edge_y,) * 2 + (edge_x,) * 2, (side, side, whole, whole), smem=2, n_in=9,
-        room=10, aliases={6: 0, 7: 1, 8: 2},
-    )(src_cell, src_amp, *halos, *inner, vel, outer)
+        third_kernel, (block,) * 4 + (edge_y,) * 2 + (edge_x,) * 2, (side, side, whole, whole), n_in=9,
+        room=10, aliases={4: 0, 5: 1, 6: 2},
+    )(*halos, *inner, vel, outer)
     halos = exchange(edges)
     inner_adj2, inner_grad = call(fourth_inner_kernel, (block,) * 2, (whole,) * 2, n_in=9, room=10)(
         wave3, image3, adj3, adj4, lap1, lap2, inject1, along_y, along_z

time: 104 us -> 92.9 us (0.89)
  local copies, waits for them, and re-layouts: 11.3 us -> 2.78 us
  Pallas kernels: 12.5 us -> 10.6 us
    unnamed x46 -> x21, local copies, waits for them, and re-layouts: 11.3 us -> 2.78 us
    pallas_call x1, Pallas kernels: 2.45 us -> 1.02 us  [local(): call(second_kernel, (block,) * 3 + (edge_y,) * 2 + (edge_x,) * 2, (pltpu....]
    pallas_call x3 -> x4, Pallas kernels: 3.38 us -> 3.89 us  [the longest x1 1.48 us: local(): call(third_inner_kernel, (block,) * 3, (whole,) * 2, n_in=10, room=10)]
  transfers between devices with their start and end apart: 19 -> 19, of which waited for: 9 -> 11; matrix products, arithmetic and copies ran while one was open for 1% -> 0% of each run, Pallas kernels for 6% -> 7%
where the time goes in v3:
time: 92.9 us; the launch traced here: 91.7 us
  starting transfers between devices  63.7 us (69%)
  waiting for transfers between devices  13 us (14%)
  Pallas kernels  10.6 us (11%)
  local copies, waits for them, and re-layouts  2.78 us (3%)
  between operations  1.66 us (2%)
    ppermute x12, starting transfers between devices, swap(): return lax.ppermute(value, axis, pairs)  39.8 us
    ppermute x6, starting transfers between devices, swap_shot(): return lax.ppermute(value, 'shot', pairs)  20.2 us
    ppermute x12, waiting for transfers between devices, swap(): return lax.ppermute(value, axis, pairs)  7.43 us
    ppermute x6, waiting for transfers between devices, swap_shot(): return lax.ppermute(value, 'shot', pairs)  5.53 us
    ppermute x1, starting transfers between devices, swap_across(): lax.ppermute(value, 'shot', [(i, (i + size // 2) % size) for i in range(s...  3.63 us
    unnamed x21, local copies, waits for them, and re-layouts  2.78 us
  transfers between devices with their start and end apart: 19, of which 11 were waited for; matrix products, arithmetic and copies ran while one was open for 0% of the time, Pallas kernels for 7%

profile of v3, /device:TPU:24, one launch (start us, length us, event | category | flops | bytes accessed | tf_op | source)
XLA Modules:
  0.0 91.7 jit_solution(854086514352917135)
XLA Ops:
  0.6 4.7 %collective-permute-start.1 = (f32[32,16,128]{2,1,0:T(8,128)}, f32[32,16,128]{2,1,0:T(8,128)S(1)}, u32[]{:S(2)}, u32[]{:S(2)}) collective-permute-start(f32[32,16,128]{2,1,0:T(8,128)} %tile.1), channel_id=1, source_target_pairs={{128,256},{256,128},{384,0},{0,384},{129,257},{257,129},{385,1},{1... | collective-permute-start | bytes 786440 | tf_op jit(solution)/shard_map/ppermute | solution.py:29
  5.3 2.1 %collective-permute-start = (f32[32,16,128]{2,1,0:T(8,128)}, f32[32,16,128]{2,1,0:T(8,128)S(1)}, u32[]{:S(2)}, u32[]{:S(2)}) collective-permute-start(f32[32,16,128]{2,1,0:T(8,128)} %tile.1), channel_id=1, source_target_pairs={{0,128},{128,0},{256,384},{384,256},{1,129},{129,1},{257,385},{385... | collective-permute-start | bytes 786440 | tf_op jit(solution)/shard_map/ppermute | solution.py:29
  7.4 3.6 %collective-permute-start.2 = (f32[32,16,128]{2,1,0:T(8,128)}, f32[32,16,128]{2,1,0:T(8,128)S(1)}, u32[]{:S(2)}, u32[]{:S(2)}) collective-permute-start(f32[32,16,128]{2,1,0:T(8,128)} %tile.1), channel_id=1, source_target_pairs={{0,256},{128,384},{256,0},{384,128},{1,257},{129,385},{257,1},{385... | collective-permute-start | bytes 786440 | tf_op jit(solution)/shard_map/ppermute | solution.py:34
  11.1 1.0 %copy-done = f32[1,32,16,256]{3,2,1,0:T(8,128)S(1)} copy-done((f32[1,32,16,256]{3,2,1,0:T(8,128)S(1)}, f32[1,32,16,256]{3,2,1,0:T(8,128)}, u32[]{:S(2)}) %copy-start) | copy-done | bytes 524312
  12.2 12.2 %collective-permute-start.3 = (f32[16,8,256]{2,1,0:T(8,128)S(1)}, f32[16,8,256]{2,1,0:T(8,128)S(1)}, u32[]{:S(2)}, u32[]{:S(2)}) collective-permute-start(f32[16,8,256]{2,1,0:T(8,128)S(1)} %get-tuple-element.39), channel_id=1, source_target_pairs={{1,2},{2,1},{3,4},{4,3},{5,6},{6,5},{7,8},{8,7},{9,10},{10,9},{11,... | collective-permute-start | bytes 393224 | tf_op jit(solution)/shard_map/ppermute | solution.py:21
  24.4 1.9 %collective-permute-start.4 = (f32[16,8,256]{2,1,0:T(8,128)S(1)}, f32[16,8,256]{2,1,0:T(8,128)S(1)}, u32[]{:S(2)}, u32[]{:S(2)}) collective-permute-start(f32[16,8,256]{2,1,0:T(8,128)S(1)} %get-tuple-element.40), channel_id=1, source_target_pairs={{0,1},{1,0},{2,3},{3,2},{4,5},{5,4},{6,7},{7,6},{8,9},{9,8},{10,11... | collective-permute-start | bytes 393224 | tf_op jit(solution)/shard_map/ppermute | solution.py:21
  26.4 1.1 %collective-permute-done.3.yb = f32[16,8,256]{2,1,0:T(8,128)S(1)} collective-permute-done((f32[16,8,256]{2,1,0:T(8,128)S(1)}, f32[16,8,256]{2,1,0:T(8,128)S(1)}, u32[]{:S(2)}, u32[]{:S(2)}) %collective-permute-start.3) | collective-permute-done | bytes 131104 | tf_op jit(solution)/shard_map/ppermute | solution.py:21
  27.4 1.9 %collective-permute-start.5 = (f32[4,16,256]{2,1,0:T(8,128)S(1)}, f32[4,16,256]{2,1,0:T(8,128)S(1)}, u32[]{:S(2)}, u32[]{:S(2)}) collective-permute-start(f32[4,16,256]{2,1,0:T(8,128)S(1)} %get-tuple-element.44), channel_id=1, source_target_pairs={{32,64},{64,32},{33,65},{65,33},{34,66},{66,34},{35,67},{67,35},{3... | collective-permute-start | bytes 196616 | tf_op jit(solution)/shard_map/ppermute | solution.py:21
  29.3 2.0 %collective-permute-done.4.ya = f32[16,8,256]{2,1,0:T(8,128)S(1)} collective-permute-done((f32[16,8,256]{2,1,0:T(8,128)S(1)}, f32[16,8,256]{2,1,0:T(8,128)S(1)}, u32[]{:S(2)}, u32[]{:S(2)}) %collective-permute-start.4) | collective-permute-done | bytes 131104 | tf_op jit(solution)/shard_map/ppermute | solution.py:21
  31.3 1.9 %collective-permute-start.6 = (f32[4,16,256]{2,1,0:T(8,128)S(1)}, f32[4,16,256]{2,1,0:T(8,128)S(1)}, u32[]{:S(2)}, u32[]{:S(2)}) collective-permute-start(f32[4,16,256]{2,1,0:T(8,128)S(1)} %get-tuple-element.45), channel_id=1, source_target_pairs={{0,32},{32,0},{64,96},{96,64},{1,33},{33,1},{65,97},{97,65},{2,34}... | collective-permute-start | bytes 196616 | tf_op jit(solution)/shard_map/ppermute | solution.py:21
  34.6 1.4 %shard_map.114 = (bf16[256,256]{1,0:T(8,128)(2,1)S(1)}, bf16[256,256]{1,0:T(8,128)(2,1)S(1)}, bf16[2,256,256]{2,1,0:T(8,128)(2,1)S(1)}, f32[32,16,256]{2,1,0:T(8...) custom-call(s32[1,3]{1,0:T(1,128)S(1)} %copy-done.7, ...), custom_call_target="tpu_custom_call" | custom-call | tf_op jit(solution)/shard_map/pallas_call | solution.py:385
  38.2 1.0 %shard_map.117 = (f32[32,16,256]{2,1,0:T(8,128)S(1)}, f32[32,16,256]{2,1,0:T(8,128)S(1)}, f32[32,16,256]{2,1,0:T(8,128)S(1)}, f32[32,8,256]{2,1,0:T(8,128)S(1)},...) custom-call(s32[1]{0:T(128)S(6)} %copy.27.offsets, f32[32,16,128]{2,1,0:T(8,128)S(1)} %copy-done.5, ...), custom_call_target="tpu_custom_call" | custom-call | tf_op jit(solution)/shard_map/pallas_call | solution.py:392
  39.2 5.5 %collective-permute-start.7 = (f32[32,8,256]{2,1,0:T(8,128)S(1)}, f32[32,8,256]{2,1,0:T(8,128)S(1)}, u32[]{:S(2)}, u32[]{:S(2)}) collective-permute-start(f32[32,8,256]{2,1,0:T(8,128)S(1)} %get-tuple-element.47), channel_id=1, source_target_pairs={{1,2},{2,1},{3,4},{4,3},{5,6},{6,5},{7,8},{8,7},{9,10},{10,9},{11,... | collective-permute-start | bytes 786440 | tf_op jit(solution)/shard_map/ppermute | solution.py:21
  44.7 1.9 %collective-permute-start.8 = (f32[32,8,256]{2,1,0:T(8,128)S(1)}, f32[32,8,256]{2,1,0:T(8,128)S(1)}, u32[]{:S(2)}, u32[]{:S(2)}) collective-permute-start(f32[32,8,256]{2,1,0:T(8,128)S(1)} %get-tuple-element.48), channel_id=1, source_target_pairs={{0,1},{1,0},{2,3},{3,2},{4,5},{5,4},{6,7},{7,6},{8,9},{9,8},{10,11... | collective-permute-start | bytes 786440 | tf_op jit(solution)/shard_map/ppermute | solution.py:21
  46.7 2.8 %collective-permute-start.9 = (f32[8,16,256]{2,1,0:T(8,128)S(1)}, f32[8,16,256]{2,1,0:T(8,128)S(1)}, u32[]{:S(2)}, u32[]{:S(2)}) collective-permute-start(f32[8,16,256]{2,1,0:T(8,128)S(1)} %get-tuple-element.49), channel_id=1, source_target_pairs={{32,64},{64,32},{33,65},{65,33},{34,66},{66,34},{35,67},{67,35},{3... | collective-permute-start | bytes 393224 | tf_op jit(solution)/shard_map/ppermute | solution.py:21
  49.4 1.9 %collective-permute-start.10 = (f32[8,16,256]{2,1,0:T(8,128)S(1)}, f32[8,16,256]{2,1,0:T(8,128)S(1)}, u32[]{:S(2)}, u32[]{:S(2)}) collective-permute-start(f32[8,16,256]{2,1,0:T(8,128)S(1)} %get-tuple-element.50), channel_id=1, source_target_pairs={{0,32},{32,0},{64,96},{96,64},{1,33},{33,1},{65,97},{97,65},{2,34}... | collective-permute-start | bytes 393224 | tf_op jit(solution)/shard_map/ppermute | solution.py:21
  51.4 1.5 %shard_map.118 = (f32[32,16,256]{2,1,0:T(8,128)S(1)}, f32[32,16,256]{2,1,0:T(8,128)S(1)}, f32[32,16,256]{2,1,0:T(8,128)S(1)}) custom-call(f32[32,16,256]{2,1,0:T(8,128)S(1)} %bitcast.16, f32[32,16,256]{2,1,0:T(8,128)S(1)} %get-tuple-element.51.wave2, f32[32,16,256]{2,1,0:T(8,128)S(1)} %bitcast.18, f32[32,16,256]{2,1,0:T(8,128)S(1)} %bitcast.21, ...), custom_call_target="tpu_custom_call" | custom-call | tf_op jit(solution)/shard_map/pallas_call | solution.py:397
  53.4 1.6 %collective-permute-done.8.ya = f32[32,8,256]{2,1,0:T(8,128)S(1)} collective-permute-done((f32[32,8,256]{2,1,0:T(8,128)S(1)}, f32[32,8,256]{2,1,0:T(8,128)S(1)}, u32[]{:S(2)}, u32[]{:S(2)}) %collective-permute-start.8) | collective-permute-done | bytes 262176 | tf_op jit(solution)/shard_map/ppermute | solution.py:21
  55.0 1.1 %shard_map.119 = (f32[32,16,256]{2,1,0:T(8,128)S(1)}, f32[32,16,256]{2,1,0:T(8,128)S(1)}, f32[32,16,256]{2,1,0:T(8,128)S(1)}, f32[32,16,256]{2,1,0:T(8,128)S(1)}...) custom-call(f32[32,8,256]{2,1,0:T(8,128)S(1)} %collective-permute-do, ...), custom_call_target="tpu_custom_call", output_to_operand_aliasing={{0}: (4, {}), {1}: (5, {}), {2}: (6, {})} | custom-call | tf_op jit(solution)/shard_map/pallas_call | solution.py:400
  56.1 4.0 %collective-permute-start.11 = (f32[32,8,256]{2,1,0:T(8,128)S(1)}, f32[32,8,256]{2,1,0:T(8,128)S(1)}, u32[]{:S(2)}, u32[]{:S(2)}) collective-permute-start(f32[32,8,256]{2,1,0:T(8,128)S(1)} %get-tuple-element.59), channel_id=1, source_target_pairs={{1,2},{2,1},{3,4},{4,3},{5,6},{6,5},{7,8},{8,7},{9,10},{10,9},{11,... | collective-permute-start | bytes 786440 | tf_op jit(solution)/shard_map/ppermute | solution.py:21
  60.1 1.9 %collective-permute-start.12 = (f32[32,8,256]{2,1,0:T(8,128)S(1)}, f32[32,8,256]{2,1,0:T(8,128)S(1)}, u32[]{:S(2)}, u32[]{:S(2)}) collective-permute-start(f32[32,8,256]{2,1,0:T(8,128)S(1)} %get-tuple-element.60), channel_id=1, source_target_pairs={{0,1},{1,0},{2,3},{3,2},{4,5},{5,4},{6,7},{7,6},{8,9},{9,8},{10,11... | collective-permute-start | bytes 786440 | tf_op jit(solution)/shard_map/ppermute | solution.py:21
  62.1 1.9 %collective-permute-start.13 = (f32[8,16,256]{2,1,0:T(8,128)S(1)}, f32[8,16,256]{2,1,0:T(8,128)S(1)}, u32[]{:S(2)}, u32[]{:S(2)}) collective-permute-start(f32[8,16,256]{2,1,0:T(8,128)S(1)} %get-tuple-element.61), channel_id=1, source_target_pairs={{32,64},{64,32},{33,65},{65,33},{34,66},{66,34},{35,67},{67,35},{3... | collective-permute-start | bytes 393224 | tf_op jit(solution)/shard_map/ppermute | solution.py:21
  64.0 1.9 %collective-permute-start.14 = (f32[8,16,256]{2,1,0:T(8,128)S(1)}, f32[8,16,256]{2,1,0:T(8,128)S(1)}, u32[]{:S(2)}, u32[]{:S(2)}) collective-permute-start(f32[8,16,256]{2,1,0:T(8,128)S(1)} %get-tuple-element.62), channel_id=1, source_target_pairs={{0,32},{32,0},{64,96},{96,64},{1,33},{33,1},{65,97},{97,65},{2,34}... | collective-permute-start | bytes 393224 | tf_op jit(solution)/shard_map/ppermute | solution.py:21
  65.9 1.5 %shard_map.120 = (f32[32,16,256]{2,1,0:T(8,128)S(1)}, f32[32,16,256]{2,1,0:T(8,128)S(1)}) custom-call(f32[32,16,256]{2,1,0:T(8,128)S(1)} %get-tuple-element.63.wave3, f32[32,16,256]{2,1,0:T(8,128)S(1)} %get-tuple-element.64.image3, f32[32,16,256]{2,1,0:T(8,128)S(1)} %get-tuple-element.65.adj3, f32[32,16,256]{2,1,0:T(8,128)S(1)} %bitcast.19, ...), custom_call_target="tpu_custom_call" | custom-call | tf_op jit(solution)/shard_map/pallas_call | solution.py:405
  67.4 0.9 %collective-permute-done.13.xb = f32[8,16,256]{2,1,0:T(8,128)S(1)} collective-permute-done((f32[8,16,256]{2,1,0:T(8,128)S(1)}, f32[8,16,256]{2,1,0:T(8,128)S(1)}, u32[]{:S(2)}, u32[]{:S(2)}) %collective-permute-start.13) | collective-permute-done | bytes 131104 | tf_op jit(solution)/shard_map/ppermute | solution.py:21
  69.6 1.4 %shard_map.121 = (f32[16,16,128]{2,1,0:T(8,128)S(1)}, f32[16,16,128]{2,1,0:T(8,128)S(1)}, f32[32,16,128]{2,1,0:T(8,128)S(1)}, f32[32,16,128]{2,1,0:T(8,128)S(1)}...) custom-call(s32[1]{0:T(128)S(6)} %copy.27.offsets, f32[32,8,256]{2,1,0:T(8,128)S(1)} %collective-permute-done.11.yb, ...), custom_call_target="tpu_custom_call" | custom-call | tf_op jit(solution)/shard_map/pallas_call | solution.py:408
  71.0 2.2 %collective-permute-start.17 = (f32[16,16,128]{2,1,0:T(8,128)S(1)}, f32[16,16,128]{2,1,0:T(8,128)S(1)}, u32[]{:S(2)}, u32[]{:S(2)}) collective-permute-start(f32[16,16,128]{2,1,0:T(8,128)S(1)} %get-tuple-element.73), channel_id=1, source_target_pairs={{0,128},{128,0},{256,384},{384,256},{1,129},{129,1},{257,385},{385... | collective-permute-start | bytes 393224 | tf_op jit(solution)/shard_map/ppermute | solution.py:29
  73.2 4.4 %collective-permute-start.15 = (f32[16,16,128]{2,1,0:T(8,128)S(1)}, f32[16,16,128]{2,1,0:T(8,128)S(1)}, u32[]{:S(2)}, u32[]{:S(2)}) collective-permute-start(f32[16,16,128]{2,1,0:T(8,128)S(1)} %get-tuple-element.71), channel_id=1, source_target_pairs={{128,256},{256,128},{384,0},{0,384},{129,257},{257,129},{385,1},{1... | collective-permute-start | bytes 393224 | tf_op jit(solution)/shard_map/ppermute | solution.py:29
  77.9 4.7 %collective-permute-start.18 = (f32[32,16,128]{2,1,0:T(8,128)S(1)}, f32[32,16,128]{2,1,0:T(8,128)S(1)}, u32[]{:S(2)}, u32[]{:S(2)}) collective-permute-start(f32[32,16,128]{2,1,0:T(8,128)S(1)} %shard_map.123), channel_id=1, source_target_pairs={{128,256},{256,128},{384,0},{0,384},{129,257},{257,129},{385,1},{1... | collective-permute-start | bytes 786440 | tf_op jit(solution)/shard_map/ppermute | solution.py:29
  82.7 2.1 %collective-permute-start.16 = (f32[32,16,128]{2,1,0:T(8,128)S(1)}, f32[32,16,128]{2,1,0:T(8,128)S(1)}, u32[]{:S(2)}, u32[]{:S(2)}) collective-permute-start(f32[32,16,128]{2,1,0:T(8,128)S(1)} %shard_map.122), channel_id=1, source_target_pairs={{0,128},{128,0},{256,384},{384,256},{1,129},{129,1},{257,385},{385... | collective-permute-start | bytes 786440 | tf_op jit(solution)/shard_map/ppermute | solution.py:29
  85.6 1.8 %collective-permute-done.18.b = f32[32,16,128]{2,1,0:T(8,128)S(1)} collective-permute-done((f32[32,16,128]{2,1,0:T(8,128)S(1)}, f32[32,16,128]{2,1,0:T(8,128)S(1)}, u32[]{:S(2)}, u32[]{:S(2)}) %collective-permute-start.18) | collective-permute-done | bytes 262176 | tf_op jit(solution)/shard_map/ppermute | solution.py:29
  87.4 3.5 %collective-permute-done.16.a = f32[32,16,128]{2,1,0:T(8,128)S(1)} collective-permute-done((f32[32,16,128]{2,1,0:T(8,128)S(1)}, f32[32,16,128]{2,1,0:T(8,128)S(1)}, u32[]{:S(2)}, u32[]{:S(2)}) %collective-permute-start.16) | collective-permute-done | bytes 262176 | tf_op jit(solution)/shard_map/ppermute | solution.py:29
  (40 shorter events, 6.5 us)
Async XLA Ops:
  0.6 36.4 %collective-permute-start.1 = (f32[32,16,128]{2,1,0:T(8,128)}, f32[32,16,128]{2,1,0:T(8,128)S(1)}, u32[]{:S(2)}, u32[]{:S(2)}) collective-permute-start(f32[32,16,128]{2,1,0:T(8,128)} %tile.1), channel_id=1, source_target_pairs={{128,256},{256,128},{384,0},{0,384},{129,257},{257,129},{385,1},{1... | collective-permute-start | bytes 786440 | tf_op jit(solution)/shard_map/ppermute | solution.py:29
  5.3 31.8 %collective-permute-start = (f32[32,16,128]{2,1,0:T(8,128)}, f32[32,16,128]{2,1,0:T(8,128)S(1)}, u32[]{:S(2)}, u32[]{:S(2)}) collective-permute-start(f32[32,16,128]{2,1,0:T(8,128)} %tile.1), channel_id=1, source_target_pairs={{0,128},{128,0},{256,384},{384,256},{1,129},{129,1},{257,385},{385... | collective-permute-start | bytes 786440 | tf_op jit(solution)/shard_map/ppermute | solution.py:29
  7.4 29.6 %collective-permute-start.2 = (f32[32,16,128]{2,1,0:T(8,128)}, f32[32,16,128]{2,1,0:T(8,128)S(1)}, u32[]{:S(2)}, u32[]{:S(2)}) collective-permute-start(f32[32,16,128]{2,1,0:T(8,128)} %tile.1), channel_id=1, source_target_pairs={{0,256},{128,384},{256,0},{384,128},{1,257},{129,385},{257,1},{385... | collective-permute-start | bytes 786440 | tf_op jit(solution)/shard_map/ppermute | solution.py:34
  11.1 1.0 %copy-start = (f32[1,32,16,256]{3,2,1,0:T(8,128)S(1)}, f32[1,32,16,256]{3,2,1,0:T(8,128)}, u32[]{:S(2)}) copy-start(f32[1,32,16,256]{3,2,1,0:T(8,128)} %param.13) | copy-start | bytes 1572868
  12.1 23.9 %copy-start.1 = (f32[1,32,16,256]{3,2,1,0:T(8,128)S(1)}, f32[1,32,16,256]{3,2,1,0:T(8,128)}, u32[]{:S(2)}) copy-start(f32[1,32,16,256]{3,2,1,0:T(8,128)} %param.13) | copy-start | bytes 1572868
  12.2 15.2 %collective-permute-start.3 = (f32[16,8,256]{2,1,0:T(8,128)S(1)}, f32[16,8,256]{2,1,0:T(8,128)S(1)}, u32[]{:S(2)}, u32[]{:S(2)}) collective-permute-start(f32[16,8,256]{2,1,0:T(8,128)S(1)} %get-tuple-element.39), channel_id=1, source_target_pairs={{1,2},{2,1},{3,4},{4,3},{5,6},{6,5},{7,8},{8,7},{9,10},{10,9},{11,... | collective-permute-start | bytes 393224 | tf_op jit(solution)/shard_map/ppermute | solution.py:21
  24.4 9.4 %copy-start.9 = (s32[1,256,3]{1,0,2:T(1,128)S(1)}, s32[1,256,3]{1,0,2:T(1,128)}, u32[]{:S(2)}) copy-start(s32[1,256,3]{1,0,2:T(1,128)} %param.18) | copy-start | bytes 9220
  24.4 6.9 %collective-permute-start.4 = (f32[16,8,256]{2,1,0:T(8,128)S(1)}, f32[16,8,256]{2,1,0:T(8,128)S(1)}, u32[]{:S(2)}, u32[]{:S(2)}) collective-permute-start(f32[16,8,256]{2,1,0:T(8,128)S(1)} %get-tuple-element.40), channel_id=1, source_target_pairs={{0,1},{1,0},{2,3},{3,2},{4,5},{5,4},{6,7},{7,6},{8,9},{9,8},{10,11... | collective-permute-start | bytes 393224 | tf_op jit(solution)/shard_map/ppermute | solution.py:21
  27.4 9.6 %collective-permute-start.5 = (f32[4,16,256]{2,1,0:T(8,128)S(1)}, f32[4,16,256]{2,1,0:T(8,128)S(1)}, u32[]{:S(2)}, u32[]{:S(2)}) collective-permute-start(f32[4,16,256]{2,1,0:T(8,128)S(1)} %get-tuple-element.44), channel_id=1, source_target_pairs={{32,64},{64,32},{33,65},{65,33},{34,66},{66,34},{35,67},{67,35},{3... | collective-permute-start | bytes 196616 | tf_op jit(solution)/shard_map/ppermute | solution.py:21
  31.3 5.7 %collective-permute-start.6 = (f32[4,16,256]{2,1,0:T(8,128)S(1)}, f32[4,16,256]{2,1,0:T(8,128)S(1)}, u32[]{:S(2)}, u32[]{:S(2)}) collective-permute-start(f32[4,16,256]{2,1,0:T(8,128)S(1)} %get-tuple-element.45), channel_id=1, source_target_pairs={{0,32},{32,0},{64,96},{96,64},{1,33},{33,1},{65,97},{97,65},{2,34}... | collective-permute-start | bytes 196616 | tf_op jit(solution)/shard_map/ppermute | solution.py:21
  33.9 0.7 copy-start.6
  33.9 0.7 copy-start.7
  33.9 0.7 copy-start.8
  36.0 1.1 %copy-start.5 = (f32[32,16,128]{2,1,0:T(8,128)S(1)}, f32[32,16,128]{2,1,0:T(8,128)}, u32[]{:S(2)}) copy-start(f32[32,16,128]{2,1,0:T(8,128)} %tile.1) | copy-start | bytes 786436
  37.0 1.0 %copy-start.2 = (f32[1,32,16,256]{3,2,1,0:T(8,128)S(1)}, f32[1,32,16,256]{3,2,1,0:T(8,128)}, u32[]{:S(2)}) copy-start(f32[1,32,16,256]{3,2,1,0:T(8,128)} %param.14) | copy-start | bytes 1572868
  37.0 1.2 %copy-start.4 = (f32[1,32,16,256]{3,2,1,0:T(8,128)S(1)}, f32[1,32,16,256]{3,2,1,0:T(8,128)}, u32[]{:S(2)}) copy-start(f32[1,32,16,256]{3,2,1,0:T(8,128)} %param.12) | copy-start | bytes 1572868
  38.2 13.2 %copy-start.3 = (f32[1,32,16,256]{3,2,1,0:T(8,128)S(1)}, f32[1,32,16,256]{3,2,1,0:T(8,128)}, u32[]{:S(2)}) copy-start(f32[1,32,16,256]{3,2,1,0:T(8,128)} %param.15) | copy-start | bytes 1572868
  39.2 14.2 %collective-permute-start.7 = (f32[32,8,256]{2,1,0:T(8,128)S(1)}, f32[32,8,256]{2,1,0:T(8,128)S(1)}, u32[]{:S(2)}, u32[]{:S(2)}) collective-permute-start(f32[32,8,256]{2,1,0:T(8,128)S(1)} %get-tuple-element.47), channel_id=1, source_target_pairs={{1,2},{2,1},{3,4},{4,3},{5,6},{6,5},{7,8},{8,7},{9,10},{10,9},{11,... | collective-permute-start | bytes 786440 | tf_op jit(solution)/shard_map/ppermute | solution.py:21
  44.7 10.3 %collective-permute-start.8 = (f32[32,8,256]{2,1,0:T(8,128)S(1)}, f32[32,8,256]{2,1,0:T(8,128)S(1)}, u32[]{:S(2)}, u32[]{:S(2)}) collective-permute-start(f32[32,8,256]{2,1,0:T(8,128)S(1)} %get-tuple-element.48), channel_id=1, source_target_pairs={{0,1},{1,0},{2,3},{3,2},{4,5},{5,4},{6,7},{7,6},{8,9},{9,8},{10,11... | collective-permute-start | bytes 786440 | tf_op jit(solution)/shard_map/ppermute | solution.py:21
  46.7 6.3 %collective-permute-start.9 = (f32[8,16,256]{2,1,0:T(8,128)S(1)}, f32[8,16,256]{2,1,0:T(8,128)S(1)}, u32[]{:S(2)}, u32[]{:S(2)}) collective-permute-start(f32[8,16,256]{2,1,0:T(8,128)S(1)} %get-tuple-element.49), channel_id=1, source_target_pairs={{32,64},{64,32},{33,65},{65,33},{34,66},{66,34},{35,67},{67,35},{3... | collective-permute-start | bytes 393224 | tf_op jit(solution)/shard_map/ppermute | solution.py:21
  49.4 3.5 %collective-permute-start.10 = (f32[8,16,256]{2,1,0:T(8,128)S(1)}, f32[8,16,256]{2,1,0:T(8,128)S(1)}, u32[]{:S(2)}, u32[]{:S(2)}) collective-permute-start(f32[8,16,256]{2,1,0:T(8,128)S(1)} %get-tuple-element.50), channel_id=1, source_target_pairs={{0,32},{32,0},{64,96},{96,64},{1,33},{33,1},{65,97},{97,65},{2,34}... | collective-permute-start | bytes 393224 | tf_op jit(solution)/shard_map/ppermute | solution.py:21
  56.1 13.1 %collective-permute-start.11 = (f32[32,8,256]{2,1,0:T(8,128)S(1)}, f32[32,8,256]{2,1,0:T(8,128)S(1)}, u32[]{:S(2)}, u32[]{:S(2)}) collective-permute-start(f32[32,8,256]{2,1,0:T(8,128)S(1)} %get-tuple-element.59), channel_id=1, source_target_pairs={{1,2},{2,1},{3,4},{4,3},{5,6},{6,5},{7,8},{8,7},{9,10},{10,9},{11,... | collective-permute-start | bytes 786440 | tf_op jit(solution)/shard_map/ppermute | solution.py:21
  60.1 9.5 %collective-permute-start.12 = (f32[32,8,256]{2,1,0:T(8,128)S(1)}, f32[32,8,256]{2,1,0:T(8,128)S(1)}, u32[]{:S(2)}, u32[]{:S(2)}) collective-permute-start(f32[32,8,256]{2,1,0:T(8,128)S(1)} %get-tuple-element.60), channel_id=1, source_target_pairs={{0,1},{1,0},{2,3},{3,2},{4,5},{5,4},{6,7},{7,6},{8,9},{9,8},{10,11... | collective-permute-start | bytes 786440 | tf_op jit(solution)/shard_map/ppermute | solution.py:21
  62.1 6.3 %collective-permute-start.13 = (f32[8,16,256]{2,1,0:T(8,128)S(1)}, f32[8,16,256]{2,1,0:T(8,128)S(1)}, u32[]{:S(2)}, u32[]{:S(2)}) collective-permute-start(f32[8,16,256]{2,1,0:T(8,128)S(1)} %get-tuple-element.61), channel_id=1, source_target_pairs={{32,64},{64,32},{33,65},{65,33},{34,66},{66,34},{35,67},{67,35},{3... | collective-permute-start | bytes 393224 | tf_op jit(solution)/shard_map/ppermute | solution.py:21
  64.0 4.4 %collective-permute-start.14 = (f32[8,16,256]{2,1,0:T(8,128)S(1)}, f32[8,16,256]{2,1,0:T(8,128)S(1)}, u32[]{:S(2)}, u32[]{:S(2)}) collective-permute-start(f32[8,16,256]{2,1,0:T(8,128)S(1)} %get-tuple-element.62), channel_id=1, source_target_pairs={{0,32},{32,0},{64,96},{96,64},{1,33},{33,1},{65,97},{97,65},{2,34}... | collective-permute-start | bytes 393224 | tf_op jit(solution)/shard_map/ppermute | solution.py:21
  71.0 6.9 %collective-permute-start.17 = (f32[16,16,128]{2,1,0:T(8,128)S(1)}, f32[16,16,128]{2,1,0:T(8,128)S(1)}, u32[]{:S(2)}, u32[]{:S(2)}) collective-permute-start(f32[16,16,128]{2,1,0:T(8,128)S(1)} %get-tuple-element.73), channel_id=1, source_target_pairs={{0,128},{128,0},{256,384},{384,256},{1,129},{129,1},{257,385},{385... | collective-permute-start | bytes 393224 | tf_op jit(solution)/shard_map/ppermute | solution.py:29
  73.2 9.4 %collective-permute-start.15 = (f32[16,16,128]{2,1,0:T(8,128)S(1)}, f32[16,16,128]{2,1,0:T(8,128)S(1)}, u32[]{:S(2)}, u32[]{:S(2)}) collective-permute-start(f32[16,16,128]{2,1,0:T(8,128)S(1)} %get-tuple-element.71), channel_id=1, source_target_pairs={{128,256},{256,128},{384,0},{0,384},{129,257},{257,129},{385,1},{1... | collective-permute-start | bytes 393224 | tf_op jit(solution)/shard_map/ppermute | solution.py:29
  77.9 9.5 %collective-permute-start.18 = (f32[32,16,128]{2,1,0:T(8,128)S(1)}, f32[32,16,128]{2,1,0:T(8,128)S(1)}, u32[]{:S(2)}, u32[]{:S(2)}) collective-permute-start(f32[32,16,128]{2,1,0:T(8,128)S(1)} %shard_map.123), channel_id=1, source_target_pairs={{128,256},{256,128},{384,0},{0,384},{129,257},{257,129},{385,1},{1... | collective-permute-start | bytes 786440 | tf_op jit(solution)/shard_map/ppermute | solution.py:29
  82.7 8.3 %collective-permute-start.16 = (f32[32,16,128]{2,1,0:T(8,128)S(1)}, f32[32,16,128]{2,1,0:T(8,128)S(1)}, u32[]{:S(2)}, u32[]{:S(2)}) collective-permute-start(f32[32,16,128]{2,1,0:T(8,128)S(1)} %shard_map.122), channel_id=1, source_target_pairs={{0,128},{128,0},{256,384},{384,256},{1,129},{129,1},{257,385},{385... | collective-permute-start | bytes 786440 | tf_op jit(solution)/shard_map/ppermute | solution.py:29

commit v4 on v3

--- a/solution.py
+++ b/solution.py
@@ -27,11 +27,6 @@
     for i in range(odd, size, 2):
         pairs += [(i, (i + 1) % size), ((i + 1) % size, i)]
     return lax.ppermute(value, "shot", pairs)
-
-
-def swap_across(value):
-    size = lax.axis_size("shot")
-    return lax.ppermute(value, "shot", [(i, (i + size // 2) % size) for i in range(size)])
 
 
 def exchange(payload):
@@ -150,6 +145,10 @@
     top = size_x - 4
     xa[plane : plane + 4] = field[pl.ds(jnp.where(even_x, top, 0), 4)]
     xb[plane : plane + 4] = field[pl.ds(jnp.where(even_x, 0, top), 4)]
+
+
+def after_kernel(value, other, out):
+    out[...] = value[...]
 
 
 def edges_kernel(field, ya, yb, xa, xb):
@@ -318,7 +317,7 @@
 
 def fourth_kernel(
     offsets, yb, ya, xb, xa, grad_in, adj4, lap1, outer,
-    far0, far1, near_a, near_b, own, extra2, side, side2, extra,
+    far0, far1, near_a0, near_a1, near_b, own, extra2, side, side2, extra,
 ):
     size_x, size_y = adj4.shape[0], adj4.shape[1]
     outer_parts(ya, yb, xa, xb, outer, size_x, size_y, (side, side2), (extra, extra2))
@@ -330,7 +329,7 @@
     which = [lax.rem(me + away, 4) - low for away in (2, turn, 4 - turn, 0)]
     half = size_x // 2
 
-    def body(x, far, at):
+    def body(x, far, near_a, at):
         lane = lax.broadcasted_iota(jnp.int32, (size_y, HALF), 1)
         rolled = []
         for z in halves():
@@ -340,26 +339,32 @@
         first = jnp.where(high, rolled[0], 0.0)
         second = jnp.where(high, rolled[1], rolled[0])
         third = jnp.where(high, 0.0, rolled[1])
-        for n, (out, place) in zip(which, ((far, at), (near_a, x), (near_b, x), (own, x))):
+        for n, (out, place) in zip(which, ((far, at), (near_a, at), (near_b, x), (own, x))):
             value = jnp.where(n == 0, first, jnp.where(n == 1, second, third))
             out[place] = jnp.where((n >= 0) & (n <= 2), value, 0.0)
         return 0
 
-    lax.fori_loop(0, half, lambda x, _: body(x, far0, x), 0, unroll=4)
-    lax.fori_loop(half, size_x, lambda x, _: body(x, far1, x - half), 0, unroll=4)
+    lax.fori_loop(0, half, lambda x, _: body(x, far0, near_a0, x), 0, unroll=4)
+    lax.fori_loop(half, size_x, lambda x, _: body(x, far1, near_a1, x - half), 0, unroll=4)
 
 
 def adjoint_kernel(adj2_in, extra, adj2):
     adj2[...] = adj2_in[...] + extra[...]
 
 
-def pass_kernel(first, near_in, far, near):
-    planes = pl.ds(first, far.shape[0])
+def pass_lower_kernel(near_in, far, near):
+    planes = pl.ds(0, far.shape[0])
     near[planes] = near_in[planes] + far[...]
 
 
-def sum_kernel(own, a, b, out):
-    out[...] = own[...] + (a[...] + b[...])
+def pass_kernel(near, far, out):
+    out[...] = near[...] + far[...]
+
+
+def sum_kernel(own, a0, a1, b, out):
+    half = a0.shape[0]
+    out[0:half] = own[0:half] + (a0[...] + b[0:half])
+    out[half:] = own[half:] + (a1[...] + b[half:])
 
 
 def local(model_vel2, offsets, wave_prev, wave_cur, adj_cur, adj_next, src_cell, src_amp, rec_cell, rec_res):
@@ -377,7 +382,7 @@
     ]
 
     tile_a, tile_b = swap_shot(model_vel2, 0), swap_shot(model_vel2, 1)
-    tile_ab = swap_across(model_vel2)
+    tile_ab = swap_shot(call(after_kernel, tile, n_in=2, room=2)(tile_b, tile_a), 0)
     edges = call(
         edges_kernel, (shaped(size_x // 2, 8, depth),) * 2 + (shaped(4, size_y, depth),) * 2, n_in=1
     )(wave1)
@@ -387,7 +392,7 @@
         smem=2, n_in=2, room=8,
     )(src_cell, src_amp, jnp.transpose(rec_cell[0]), jnp.transpose(rec_res[0]))
     yb, ya, xb, xa = halos
-    lap1 = call(first_inner_kernel, block, (whole,), n_in=6, room=6)(wave1, yb, ya, along_y, along_z, outer)
+    lap1 = call(first_inner_kernel, block, (whole,), n_in=6, room=6, flops=2000000000)(wave1, yb, ya, along_y, along_z, outer)
     lap1 = call(first_kernel, block, (side,), n_in=3, aliases={0: 0})(lap1, xb, xa)
     vel, wave2, image, *edges = call(
         second_kernel, (block,) * 3 + (edge_y,) * 2 + (edge_x,) * 2,
@@ -405,15 +410,15 @@
     inner_adj2, inner_grad = call(fourth_inner_kernel, (block,) * 2, (whole,) * 2, n_in=9, room=10)(
         wave3, image3, adj3, adj4, lap1, lap2, inject1, along_y, along_z
     )
-    far0, far1, near_a, near_b, own, extra = call(
-        fourth_kernel, (half, half, tile, tile, tile, block), (side, side, whole), smem=1, n_in=8, room=10
+    far0, far1, near_a0, near_a1, near_b, own, extra = call(
+        fourth_kernel, (half, half, half, half, tile, tile, block), (side, side, whole), smem=1, n_in=8, room=10
     )(offsets, *halos, inner_grad, adj4, lap1, outer)
     from_a, from_b = swap_shot(far0, 0), swap_shot(far1, 1)
-    near_b = call(functools.partial(pass_kernel, 0), tile, n_in=2, aliases={0: 0})(near_b, from_a)
-    near_a = call(functools.partial(pass_kernel, size_x // 2), tile, n_in=2, aliases={0: 0})(near_a, from_b)
-    got_b, got_a = swap_shot(near_b, 1), swap_shot(near_a, 0)
+    got_a0 = swap_shot(near_a0, 0)
+    got_b = swap_shot(call(pass_lower_kernel, tile, n_in=2, aliases={0: 0})(near_b, from_a), 1)
+    got_a1 = swap_shot(call(pass_kernel, half, n_in=2)(near_a1, from_b), 0)
     adj2 = call(adjoint_kernel, block, n_in=2)(inner_adj2, extra)
-    owned = call(sum_kernel, tile, n_in=3)(own, got_a, got_b)
+    owned = call(sum_kernel, tile, n_in=4)(own, got_a0, got_a1, got_b)
     return owned, adj2[None]
 
 

time: 92.9 us -> 88.9 us (0.957)
  waiting for transfers between devices: 13 us -> 6.88 us
  starting transfers between devices: 63.7 us -> 65.9 us
    ppermute x6 -> x8, starting transfers between devices: 20.2 us -> 25.6 us  [swap_shot(): return lax.ppermute(value, 'shot', pairs)]
    ppermute x12, waiting for transfers between devices: 7.43 us -> 3.8 us  [swap(): return lax.ppermute(value, axis, pairs)]
    ppermute x1 -> x0, starting transfers between devices: 3.63 us -> none  [swap_across(): lax.ppermute(value, 'shot', [(i, (i + size // 2) % size) for i in range(s...]
    ppermute x6 -> x8, waiting for transfers between devices: 5.53 us -> 3.08 us  [swap_shot(): return lax.ppermute(value, 'shot', pairs)]
    pallas_call x5 -> x6, Pallas kernels: 3.12 us -> 3.14 us  [the longest x1 1.42 us: local(): call(fourth_kernel, (half, half, half, half, tile, tile, block), (side, s...]
  transfers between devices with their start and end apart: 19 -> 20, of which waited for: 11 -> 7; matrix products, arithmetic and copies ran while one was open for 0% -> 0% of each run, Pallas kernels for 7% -> 7%
where the time goes in v4:
time: 88.9 us; the launch traced here: 87.9 us
  starting transfers between devices  65.9 us (74%)
  Pallas kernels  10.6 us (12%)
  waiting for transfers between devices  6.88 us (8%)
  local copies, waits for them, and re-layouts  2.8 us (3%)
  between operations  1.7 us (2%)
    ppermute x12, starting transfers between devices, swap(): return lax.ppermute(value, axis, pairs)  40.3 us
    ppermute x8, starting transfers between devices, swap_shot(): return lax.ppermute(value, 'shot', pairs)  25.6 us
    ppermute x12, waiting for transfers between devices, swap(): return lax.ppermute(value, axis, pairs)  3.8 us
    ppermute x8, waiting for transfers between devices, swap_shot(): return lax.ppermute(value, 'shot', pairs)  3.08 us
    unnamed x21, local copies, waits for them, and re-layouts  2.8 us
  transfers between devices with their start and end apart: 20, of which 7 were waited for; matrix products, arithmetic and copies ran while one was open for 0% of the time, Pallas kernels for 7%

profile of v4, /device:TPU:24, one launch (start us, length us, event | category | flops | bytes accessed | tf_op | source)
XLA Modules:
  0.0 87.9 jit_solution(1566896216408231845)
XLA Ops:
  0.6 3.4 %collective-permute-start = (f32[32,16,128]{2,1,0:T(8,128)}, f32[32,16,128]{2,1,0:T(8,128)S(1)}, u32[]{:S(2)}, u32[]{:S(2)}) collective-permute-start(f32[32,16,128]{2,1,0:T(8,128)} %tile.1), channel_id=1, source_target_pairs={{0,128},{128,0},{256,384},{384,256},{1,129},{129,1},{257,385},{385... | collective-permute-start | bytes 786440 | tf_op jit(solution)/shard_map/ppermute | solution.py:29
  4.0 4.0 %collective-permute-start.1 = (f32[32,16,128]{2,1,0:T(8,128)}, f32[32,16,128]{2,1,0:T(8,128)S(1)}, u32[]{:S(2)}, u32[]{:S(2)}) collective-permute-start(f32[32,16,128]{2,1,0:T(8,128)} %tile.1), channel_id=1, source_target_pairs={{128,256},{256,128},{384,0},{0,384},{129,257},{257,129},{385,1},{1... | collective-permute-start | bytes 786440 | tf_op jit(solution)/shard_map/ppermute | solution.py:29
  8.1 1.0 %copy-done.1 = f32[1,32,16,256]{3,2,1,0:T(8,128)S(1)} copy-done((f32[1,32,16,256]{3,2,1,0:T(8,128)S(1)}, f32[1,32,16,256]{3,2,1,0:T(8,128)}, u32[]{:S(2)}) %copy-start.1) | copy-done | bytes 524312
  9.2 12.2 %collective-permute-start.3 = (f32[16,8,256]{2,1,0:T(8,128)S(1)}, f32[16,8,256]{2,1,0:T(8,128)S(1)}, u32[]{:S(2)}, u32[]{:S(2)}) collective-permute-start(f32[16,8,256]{2,1,0:T(8,128)S(1)} %get-tuple-element.40), channel_id=1, source_target_pairs={{1,2},{2,1},{3,4},{4,3},{5,6},{6,5},{7,8},{8,7},{9,10},{10,9},{11,... | collective-permute-start | bytes 393224 | tf_op jit(solution)/shard_map/ppermute | solution.py:21
  21.4 1.9 %collective-permute-start.4 = (f32[16,8,256]{2,1,0:T(8,128)S(1)}, f32[16,8,256]{2,1,0:T(8,128)S(1)}, u32[]{:S(2)}, u32[]{:S(2)}) collective-permute-start(f32[16,8,256]{2,1,0:T(8,128)S(1)} %get-tuple-element.41), channel_id=1, source_target_pairs={{0,1},{1,0},{2,3},{3,2},{4,5},{5,4},{6,7},{7,6},{8,9},{9,8},{10,11... | collective-permute-start | bytes 393224 | tf_op jit(solution)/shard_map/ppermute | solution.py:21
  23.4 2.5 %collective-permute-start.2 = (f32[32,16,128]{2,1,0:T(8,128)S(1)}, f32[32,16,128]{2,1,0:T(8,128)S(1)}, u32[]{:S(2)}, u32[]{:S(2)}) collective-permute-start(f32[32,16,128]{2,1,0:T(8,128)S(1)} %shard_map.113), channel_id=1, source_target_pairs={{0,128},{128,0},{256,384},{384,256},{1,129},{129,1},{257,385},{385... | collective-permute-start | bytes 786440 | tf_op jit(solution)/shard_map/ppermute | solution.py:29
  25.9 1.9 %collective-permute-start.5 = (f32[4,16,256]{2,1,0:T(8,128)S(1)}, f32[4,16,256]{2,1,0:T(8,128)S(1)}, u32[]{:S(2)}, u32[]{:S(2)}) collective-permute-start(f32[4,16,256]{2,1,0:T(8,128)S(1)} %get-tuple-element.45), channel_id=1, source_target_pairs={{32,64},{64,32},{33,65},{65,33},{34,66},{66,34},{35,67},{67,35},{3... | collective-permute-start | bytes 196616 | tf_op jit(solution)/shard_map/ppermute | solution.py:21
  27.8 1.9 %collective-permute-start.6 = (f32[4,16,256]{2,1,0:T(8,128)S(1)}, f32[4,16,256]{2,1,0:T(8,128)S(1)}, u32[]{:S(2)}, u32[]{:S(2)}) collective-permute-start(f32[4,16,256]{2,1,0:T(8,128)S(1)} %get-tuple-element.46), channel_id=1, source_target_pairs={{0,32},{32,0},{64,96},{96,64},{1,33},{33,1},{65,97},{97,65},{2,34}... | collective-permute-start | bytes 196616 | tf_op jit(solution)/shard_map/ppermute | solution.py:21
  31.1 1.4 %shard_map.115 = (bf16[256,256]{1,0:T(8,128)(2,1)S(1)}, bf16[256,256]{1,0:T(8,128)(2,1)S(1)}, bf16[2,256,256]{2,1,0:T(8,128)(2,1)S(1)}, f32[32,16,256]{2,1,0:T(8...) custom-call(s32[1,3]{1,0:T(1,128)S(1)} %copy-done.7, ...), custom_call_target="tpu_custom_call" | custom-call | tf_op jit(solution)/shard_map/pallas_call | solution.py:390
  33.7 0.9 %copy-done = f32[1,32,16,256]{3,2,1,0:T(8,128)S(1)} copy-done((f32[1,32,16,256]{3,2,1,0:T(8,128)S(1)}, f32[1,32,16,256]{3,2,1,0:T(8,128)}, u32[]{:S(2)}) %copy-start) | copy-done | bytes 524312
  34.7 1.0 %shard_map.118 = (f32[32,16,256]{2,1,0:T(8,128)S(1)}, f32[32,16,256]{2,1,0:T(8,128)S(1)}, f32[32,16,256]{2,1,0:T(8,128)S(1)}, f32[32,8,256]{2,1,0:T(8,128)S(1)},...) custom-call(s32[1]{0:T(128)S(6)} %copy.25.offsets, f32[32,16,128]{2,1,0:T(8,128)S(1)} %copy-done.5, ...), custom_call_target="tpu_custom_call" | custom-call | tf_op jit(solution)/shard_map/pallas_call | solution.py:397
  35.8 3.9 %collective-permute-start.7 = (f32[32,8,256]{2,1,0:T(8,128)S(1)}, f32[32,8,256]{2,1,0:T(8,128)S(1)}, u32[]{:S(2)}, u32[]{:S(2)}) collective-permute-start(f32[32,8,256]{2,1,0:T(8,128)S(1)} %get-tuple-element.48), channel_id=1, source_target_pairs={{1,2},{2,1},{3,4},{4,3},{5,6},{6,5},{7,8},{8,7},{9,10},{10,9},{11,... | collective-permute-start | bytes 786440 | tf_op jit(solution)/shard_map/ppermute | solution.py:21
  39.7 1.9 %collective-permute-start.8 = (f32[32,8,256]{2,1,0:T(8,128)S(1)}, f32[32,8,256]{2,1,0:T(8,128)S(1)}, u32[]{:S(2)}, u32[]{:S(2)}) collective-permute-start(f32[32,8,256]{2,1,0:T(8,128)S(1)} %get-tuple-element.49), channel_id=1, source_target_pairs={{0,1},{1,0},{2,3},{3,2},{4,5},{5,4},{6,7},{7,6},{8,9},{9,8},{10,11... | collective-permute-start | bytes 786440 | tf_op jit(solution)/shard_map/ppermute | solution.py:21
  41.6 3.4 %collective-permute-start.9 = (f32[8,16,256]{2,1,0:T(8,128)S(1)}, f32[8,16,256]{2,1,0:T(8,128)S(1)}, u32[]{:S(2)}, u32[]{:S(2)}) collective-permute-start(f32[8,16,256]{2,1,0:T(8,128)S(1)} %get-tuple-element.50), channel_id=1, source_target_pairs={{32,64},{64,32},{33,65},{65,33},{34,66},{66,34},{35,67},{67,35},{3... | collective-permute-start | bytes 393224 | tf_op jit(solution)/shard_map/ppermute | solution.py:21
  45.0 1.9 %collective-permute-start.10 = (f32[8,16,256]{2,1,0:T(8,128)S(1)}, f32[8,16,256]{2,1,0:T(8,128)S(1)}, u32[]{:S(2)}, u32[]{:S(2)}) collective-permute-start(f32[8,16,256]{2,1,0:T(8,128)S(1)} %get-tuple-element.51), channel_id=1, source_target_pairs={{0,32},{32,0},{64,96},{96,64},{1,33},{33,1},{65,97},{97,65},{2,34}... | collective-permute-start | bytes 393224 | tf_op jit(solution)/shard_map/ppermute | solution.py:21
  46.9 1.5 %shard_map.119 = (f32[32,16,256]{2,1,0:T(8,128)S(1)}, f32[32,16,256]{2,1,0:T(8,128)S(1)}, f32[32,16,256]{2,1,0:T(8,128)S(1)}) custom-call(f32[32,16,256]{2,1,0:T(8,128)S(1)} %bitcast.20, f32[32,16,256]{2,1,0:T(8,128)S(1)} %get-tuple-element.52.wave2, f32[32,16,256]{2,1,0:T(8,128)S(1)} %bitcast.14, f32[32,16,256]{2,1,0:T(8,128)S(1)} %bitcast.21, ...), custom_call_target="tpu_custom_call" | custom-call | tf_op jit(solution)/shard_map/pallas_call | solution.py:402
  48.4 1.7 %collective-permute-done.7.yb = f32[32,8,256]{2,1,0:T(8,128)S(1)} collective-permute-done((f32[32,8,256]{2,1,0:T(8,128)S(1)}, f32[32,8,256]{2,1,0:T(8,128)S(1)}, u32[]{:S(2)}, u32[]{:S(2)}) %collective-permute-start.7) | collective-permute-done | bytes 262176 | tf_op jit(solution)/shard_map/ppermute | solution.py:21
  50.1 1.1 %shard_map.120 = (f32[32,16,256]{2,1,0:T(8,128)S(1)}, f32[32,16,256]{2,1,0:T(8,128)S(1)}, f32[32,16,256]{2,1,0:T(8,128)S(1)}, f32[32,16,256]{2,1,0:T(8,128)S(1)}...) custom-call(f32[32,8,256]{2,1,0:T(8,128)S(1)} %collective-permute-do, ...), custom_call_target="tpu_custom_call", output_to_operand_aliasing={{0}: (4, {}), {1}: (5, {}), {2}: (6, {})} | custom-call | tf_op jit(solution)/shard_map/pallas_call | solution.py:405
  51.2 5.5 %collective-permute-start.11 = (f32[32,8,256]{2,1,0:T(8,128)S(1)}, f32[32,8,256]{2,1,0:T(8,128)S(1)}, u32[]{:S(2)}, u32[]{:S(2)}) collective-permute-start(f32[32,8,256]{2,1,0:T(8,128)S(1)} %get-tuple-element.60), channel_id=1, source_target_pairs={{1,2},{2,1},{3,4},{4,3},{5,6},{6,5},{7,8},{8,7},{9,10},{10,9},{11,... | collective-permute-start | bytes 786440 | tf_op jit(solution)/shard_map/ppermute | solution.py:21
  56.6 1.9 %collective-permute-start.12 = (f32[32,8,256]{2,1,0:T(8,128)S(1)}, f32[32,8,256]{2,1,0:T(8,128)S(1)}, u32[]{:S(2)}, u32[]{:S(2)}) collective-permute-start(f32[32,8,256]{2,1,0:T(8,128)S(1)} %get-tuple-element.61), channel_id=1, source_target_pairs={{0,1},{1,0},{2,3},{3,2},{4,5},{5,4},{6,7},{7,6},{8,9},{9,8},{10,11... | collective-permute-start | bytes 786440 | tf_op jit(solution)/shard_map/ppermute | solution.py:21
  58.6 1.9 %collective-permute-start.13 = (f32[8,16,256]{2,1,0:T(8,128)S(1)}, f32[8,16,256]{2,1,0:T(8,128)S(1)}, u32[]{:S(2)}, u32[]{:S(2)}) collective-permute-start(f32[8,16,256]{2,1,0:T(8,128)S(1)} %get-tuple-element.62), channel_id=1, source_target_pairs={{32,64},{64,32},{33,65},{65,33},{34,66},{66,34},{35,67},{67,35},{3... | collective-permute-start | bytes 393224 | tf_op jit(solution)/shard_map/ppermute | solution.py:21
  60.5 1.9 %collective-permute-start.14 = (f32[8,16,256]{2,1,0:T(8,128)S(1)}, f32[8,16,256]{2,1,0:T(8,128)S(1)}, u32[]{:S(2)}, u32[]{:S(2)}) collective-permute-start(f32[8,16,256]{2,1,0:T(8,128)S(1)} %get-tuple-element.63), channel_id=1, source_target_pairs={{0,32},{32,0},{64,96},{96,64},{1,33},{33,1},{65,97},{97,65},{2,34}... | collective-permute-start | bytes 393224 | tf_op jit(solution)/shard_map/ppermute | solution.py:21
  62.4 1.5 %shard_map.121 = (f32[32,16,256]{2,1,0:T(8,128)S(1)}, f32[32,16,256]{2,1,0:T(8,128)S(1)}) custom-call(f32[32,16,256]{2,1,0:T(8,128)S(1)} %get-tuple-element.64.wave3, f32[32,16,256]{2,1,0:T(8,128)S(1)} %get-tuple-element.65.image3, f32[32,16,256]{2,1,0:T(8,128)S(1)} %get-tuple-element.66.adj3, f32[32,16,256]{2,1,0:T(8,128)S(1)} %bitcast.15, ...), custom_call_target="tpu_custom_call" | custom-call | tf_op jit(solution)/shard_map/pallas_call | solution.py:410
  63.9 1.0 %collective-permute-done.13.xb = f32[8,16,256]{2,1,0:T(8,128)S(1)} collective-permute-done((f32[8,16,256]{2,1,0:T(8,128)S(1)}, f32[8,16,256]{2,1,0:T(8,128)S(1)}, u32[]{:S(2)}, u32[]{:S(2)}) %collective-permute-start.13) | collective-permute-done | bytes 131104 | tf_op jit(solution)/shard_map/ppermute | solution.py:21
  64.9 1.2 %collective-permute-done.12.ya = f32[32,8,256]{2,1,0:T(8,128)S(1)} collective-permute-done((f32[32,8,256]{2,1,0:T(8,128)S(1)}, f32[32,8,256]{2,1,0:T(8,128)S(1)}, u32[]{:S(2)}, u32[]{:S(2)}) %collective-permute-start.12) | collective-permute-done | bytes 262176 | tf_op jit(solution)/shard_map/ppermute | solution.py:21
  66.0 1.4 %shard_map.122 = (f32[16,16,128]{2,1,0:T(8,128)S(1)}, f32[16,16,128]{2,1,0:T(8,128)S(1)}, f32[16,16,128]{2,1,0:T(8,128)S(1)}, f32[16,16,128]{2,1,0:T(8,128)S(1)}...) custom-call(s32[1]{0:T(128)S(6)} %copy.25.offsets, ...), custom_call_target="tpu_custom_call" | custom-call | tf_op jit(solution)/shard_map/pallas_call | solution.py:413
  67.4 3.3 %collective-permute-start.18 = (f32[16,16,128]{2,1,0:T(8,128)S(1)}, f32[16,16,128]{2,1,0:T(8,128)S(1)}, u32[]{:S(2)}, u32[]{:S(2)}) collective-permute-start(f32[16,16,128]{2,1,0:T(8,128)S(1)} %get-tuple-element.75), channel_id=1, source_target_pairs={{0,128},{128,0},{256,384},{384,256},{1,129},{129,1},{257,385},{385... | collective-permute-start | bytes 393224 | tf_op jit(solution)/shard_map/ppermute | solution.py:29
  70.8 3.1 %collective-permute-start.16 = (f32[16,16,128]{2,1,0:T(8,128)S(1)}, f32[16,16,128]{2,1,0:T(8,128)S(1)}, u32[]{:S(2)}, u32[]{:S(2)}) collective-permute-start(f32[16,16,128]{2,1,0:T(8,128)S(1)} %get-tuple-element.73), channel_id=1, source_target_pairs={{128,256},{256,128},{384,0},{0,384},{129,257},{257,129},{385,1},{1... | collective-permute-start | bytes 393224 | tf_op jit(solution)/shard_map/ppermute | solution.py:29
  74.3 3.6 %collective-permute-start.19 = (f32[32,16,128]{2,1,0:T(8,128)S(1)}, f32[32,16,128]{2,1,0:T(8,128)S(1)}, u32[]{:S(2)}, u32[]{:S(2)}) collective-permute-start(f32[32,16,128]{2,1,0:T(8,128)S(1)} %shard_map.124), channel_id=1, source_target_pairs={{128,256},{256,128},{384,0},{0,384},{129,257},{257,129},{385,1},{1... | collective-permute-start | bytes 786440 | tf_op jit(solution)/shard_map/ppermute | solution.py:29
  77.9 2.2 %collective-permute-start.15 = (f32[16,16,128]{2,1,0:T(8,128)S(1)}, f32[16,16,128]{2,1,0:T(8,128)S(1)}, u32[]{:S(2)}, u32[]{:S(2)}) collective-permute-start(f32[16,16,128]{2,1,0:T(8,128)S(1)} %get-tuple-element.71), channel_id=1, source_target_pairs={{0,128},{128,0},{256,384},{384,256},{1,129},{129,1},{257,385},{385... | collective-permute-start | bytes 393224 | tf_op jit(solution)/shard_map/ppermute | solution.py:29
  80.3 3.5 %collective-permute-start.17 = (f32[16,16,128]{2,1,0:T(8,128)S(1)}, f32[16,16,128]{2,1,0:T(8,128)S(1)}, u32[]{:S(2)}, u32[]{:S(2)}) collective-permute-start(f32[16,16,128]{2,1,0:T(8,128)S(1)} %shard_map.123), channel_id=1, source_target_pairs={{0,128},{128,0},{256,384},{384,256},{1,129},{129,1},{257,385},{385... | collective-permute-start | bytes 393224 | tf_op jit(solution)/shard_map/ppermute | solution.py:29
  84.8 2.4 %collective-permute-done.17.a1 = f32[16,16,128]{2,1,0:T(8,128)S(1)} collective-permute-done((f32[16,16,128]{2,1,0:T(8,128)S(1)}, f32[16,16,128]{2,1,0:T(8,128)S(1)}, u32[]{:S(2)}, u32[]{:S(2)}) %collective-permute-start.17) | collective-permute-done | bytes 131104 | tf_op jit(solution)/shard_map/ppermute | solution.py:29
  (43 shorter events, 4.3 us)
Async XLA Ops:
  0.6 22.7 %collective-permute-start = (f32[32,16,128]{2,1,0:T(8,128)}, f32[32,16,128]{2,1,0:T(8,128)S(1)}, u32[]{:S(2)}, u32[]{:S(2)}) collective-permute-start(f32[32,16,128]{2,1,0:T(8,128)} %tile.1), channel_id=1, source_target_pairs={{0,128},{128,0},{256,384},{384,256},{1,129},{129,1},{257,385},{385... | collective-permute-start | bytes 786440 | tf_op jit(solution)/shard_map/ppermute | solution.py:29
  4.0 19.3 %collective-permute-start.1 = (f32[32,16,128]{2,1,0:T(8,128)}, f32[32,16,128]{2,1,0:T(8,128)S(1)}, u32[]{:S(2)}, u32[]{:S(2)}) collective-permute-start(f32[32,16,128]{2,1,0:T(8,128)} %tile.1), channel_id=1, source_target_pairs={{128,256},{256,128},{384,0},{0,384},{129,257},{257,129},{385,1},{1... | collective-permute-start | bytes 786440 | tf_op jit(solution)/shard_map/ppermute | solution.py:29
  8.1 1.0 %copy-start.1 = (f32[1,32,16,256]{3,2,1,0:T(8,128)S(1)}, f32[1,32,16,256]{3,2,1,0:T(8,128)}, u32[]{:S(2)}) copy-start(f32[1,32,16,256]{3,2,1,0:T(8,128)} %param.13) | copy-start | bytes 1572868
  9.2 23.4 %copy-start.2 = (f32[1,32,16,256]{3,2,1,0:T(8,128)S(1)}, f32[1,32,16,256]{3,2,1,0:T(8,128)}, u32[]{:S(2)}) copy-start(f32[1,32,16,256]{3,2,1,0:T(8,128)} %param.13) | copy-start | bytes 1572868
  9.2 23.4 %collective-permute-start.3 = (f32[16,8,256]{2,1,0:T(8,128)S(1)}, f32[16,8,256]{2,1,0:T(8,128)S(1)}, u32[]{:S(2)}, u32[]{:S(2)}) collective-permute-start(f32[16,8,256]{2,1,0:T(8,128)S(1)} %get-tuple-element.40), channel_id=1, source_target_pairs={{1,2},{2,1},{3,4},{4,3},{5,6},{6,5},{7,8},{8,7},{9,10},{10,9},{11,... | collective-permute-start | bytes 393224 | tf_op jit(solution)/shard_map/ppermute | solution.py:21
  21.4 11.2 %collective-permute-start.4 = (f32[16,8,256]{2,1,0:T(8,128)S(1)}, f32[16,8,256]{2,1,0:T(8,128)S(1)}, u32[]{:S(2)}, u32[]{:S(2)}) collective-permute-start(f32[16,8,256]{2,1,0:T(8,128)S(1)} %get-tuple-element.41), channel_id=1, source_target_pairs={{0,1},{1,0},{2,3},{3,2},{4,5},{5,4},{6,7},{7,6},{8,9},{9,8},{10,11... | collective-permute-start | bytes 393224 | tf_op jit(solution)/shard_map/ppermute | solution.py:21
  23.4 7.0 %copy-start.9 = (s32[1,256,3]{1,0,2:T(1,128)S(1)}, s32[1,256,3]{1,0,2:T(1,128)}, u32[]{:S(2)}) copy-start(s32[1,256,3]{1,0,2:T(1,128)} %param.18) | copy-start | bytes 9220
  23.4 10.3 %collective-permute-start.2 = (f32[32,16,128]{2,1,0:T(8,128)S(1)}, f32[32,16,128]{2,1,0:T(8,128)S(1)}, u32[]{:S(2)}, u32[]{:S(2)}) collective-permute-start(f32[32,16,128]{2,1,0:T(8,128)S(1)} %shard_map.113), channel_id=1, source_target_pairs={{0,128},{128,0},{256,384},{384,256},{1,129},{129,1},{257,385},{385... | collective-permute-start | bytes 786440 | tf_op jit(solution)/shard_map/ppermute | solution.py:29
  25.9 7.6 %collective-permute-start.5 = (f32[4,16,256]{2,1,0:T(8,128)S(1)}, f32[4,16,256]{2,1,0:T(8,128)S(1)}, u32[]{:S(2)}, u32[]{:S(2)}) collective-permute-start(f32[4,16,256]{2,1,0:T(8,128)S(1)} %get-tuple-element.45), channel_id=1, source_target_pairs={{32,64},{64,32},{33,65},{65,33},{34,66},{66,34},{35,67},{67,35},{3... | collective-permute-start | bytes 196616 | tf_op jit(solution)/shard_map/ppermute | solution.py:21
  27.8 5.7 %collective-permute-start.6 = (f32[4,16,256]{2,1,0:T(8,128)S(1)}, f32[4,16,256]{2,1,0:T(8,128)S(1)}, u32[]{:S(2)}, u32[]{:S(2)}) collective-permute-start(f32[4,16,256]{2,1,0:T(8,128)S(1)} %get-tuple-element.46), channel_id=1, source_target_pairs={{0,32},{32,0},{64,96},{96,64},{1,33},{33,1},{65,97},{97,65},{2,34}... | collective-permute-start | bytes 196616 | tf_op jit(solution)/shard_map/ppermute | solution.py:21
  30.4 0.7 copy-start.6
  30.4 0.7 copy-start.7
  30.5 0.7 copy-start.8
  32.6 1.1 %copy-start.5 = (f32[32,16,128]{2,1,0:T(8,128)S(1)}, f32[32,16,128]{2,1,0:T(8,128)}, u32[]{:S(2)}) copy-start(f32[32,16,128]{2,1,0:T(8,128)} %tile.1) | copy-start | bytes 786436
  33.5 1.0 %copy-start = (f32[1,32,16,256]{3,2,1,0:T(8,128)S(1)}, f32[1,32,16,256]{3,2,1,0:T(8,128)}, u32[]{:S(2)}) copy-start(f32[1,32,16,256]{3,2,1,0:T(8,128)} %param.14) | copy-start | bytes 1572868
  33.5 1.2 %copy-start.4 = (f32[1,32,16,256]{3,2,1,0:T(8,128)S(1)}, f32[1,32,16,256]{3,2,1,0:T(8,128)}, u32[]{:S(2)}) copy-start(f32[1,32,16,256]{3,2,1,0:T(8,128)} %param.12) | copy-start | bytes 1572868
  34.7 12.2 %copy-start.3 = (f32[1,32,16,256]{3,2,1,0:T(8,128)S(1)}, f32[1,32,16,256]{3,2,1,0:T(8,128)}, u32[]{:S(2)}) copy-start(f32[1,32,16,256]{3,2,1,0:T(8,128)} %param.15) | copy-start | bytes 1572868
  35.8 14.3 %collective-permute-start.7 = (f32[32,8,256]{2,1,0:T(8,128)S(1)}, f32[32,8,256]{2,1,0:T(8,128)S(1)}, u32[]{:S(2)}, u32[]{:S(2)}) collective-permute-start(f32[32,8,256]{2,1,0:T(8,128)S(1)} %get-tuple-element.48), channel_id=1, source_target_pairs={{1,2},{2,1},{3,4},{4,3},{5,6},{6,5},{7,8},{8,7},{9,10},{10,9},{11,... | collective-permute-start | bytes 786440 | tf_op jit(solution)/shard_map/ppermute | solution.py:21
  39.7 10.4 %collective-permute-start.8 = (f32[32,8,256]{2,1,0:T(8,128)S(1)}, f32[32,8,256]{2,1,0:T(8,128)S(1)}, u32[]{:S(2)}, u32[]{:S(2)}) collective-permute-start(f32[32,8,256]{2,1,0:T(8,128)S(1)} %get-tuple-element.49), channel_id=1, source_target_pairs={{0,1},{1,0},{2,3},{3,2},{4,5},{5,4},{6,7},{7,6},{8,9},{9,8},{10,11... | collective-permute-start | bytes 786440 | tf_op jit(solution)/shard_map/ppermute | solution.py:21
  41.6 6.8 %collective-permute-start.9 = (f32[8,16,256]{2,1,0:T(8,128)S(1)}, f32[8,16,256]{2,1,0:T(8,128)S(1)}, u32[]{:S(2)}, u32[]{:S(2)}) collective-permute-start(f32[8,16,256]{2,1,0:T(8,128)S(1)} %get-tuple-element.50), channel_id=1, source_target_pairs={{32,64},{64,32},{33,65},{65,33},{34,66},{66,34},{35,67},{67,35},{3... | collective-permute-start | bytes 393224 | tf_op jit(solution)/shard_map/ppermute | solution.py:21
  45.0 3.4 %collective-permute-start.10 = (f32[8,16,256]{2,1,0:T(8,128)S(1)}, f32[8,16,256]{2,1,0:T(8,128)S(1)}, u32[]{:S(2)}, u32[]{:S(2)}) collective-permute-start(f32[8,16,256]{2,1,0:T(8,128)S(1)} %get-tuple-element.51), channel_id=1, source_target_pairs={{0,32},{32,0},{64,96},{96,64},{1,33},{33,1},{65,97},{97,65},{2,34}... | collective-permute-start | bytes 393224 | tf_op jit(solution)/shard_map/ppermute | solution.py:21
  51.2 13.7 %collective-permute-start.11 = (f32[32,8,256]{2,1,0:T(8,128)S(1)}, f32[32,8,256]{2,1,0:T(8,128)S(1)}, u32[]{:S(2)}, u32[]{:S(2)}) collective-permute-start(f32[32,8,256]{2,1,0:T(8,128)S(1)} %get-tuple-element.60), channel_id=1, source_target_pairs={{1,2},{2,1},{3,4},{4,3},{5,6},{6,5},{7,8},{8,7},{9,10},{10,9},{11,... | collective-permute-start | bytes 786440 | tf_op jit(solution)/shard_map/ppermute | solution.py:21
  56.6 9.4 %collective-permute-start.12 = (f32[32,8,256]{2,1,0:T(8,128)S(1)}, f32[32,8,256]{2,1,0:T(8,128)S(1)}, u32[]{:S(2)}, u32[]{:S(2)}) collective-permute-start(f32[32,8,256]{2,1,0:T(8,128)S(1)} %get-tuple-element.61), channel_id=1, source_target_pairs={{0,1},{1,0},{2,3},{3,2},{4,5},{5,4},{6,7},{7,6},{8,9},{9,8},{10,11... | collective-permute-start | bytes 786440 | tf_op jit(solution)/shard_map/ppermute | solution.py:21
  58.6 6.3 %collective-permute-start.13 = (f32[8,16,256]{2,1,0:T(8,128)S(1)}, f32[8,16,256]{2,1,0:T(8,128)S(1)}, u32[]{:S(2)}, u32[]{:S(2)}) collective-permute-start(f32[8,16,256]{2,1,0:T(8,128)S(1)} %get-tuple-element.62), channel_id=1, source_target_pairs={{32,64},{64,32},{33,65},{65,33},{34,66},{66,34},{35,67},{67,35},{3... | collective-permute-start | bytes 393224 | tf_op jit(solution)/shard_map/ppermute | solution.py:21
  60.5 4.4 %collective-permute-start.14 = (f32[8,16,256]{2,1,0:T(8,128)S(1)}, f32[8,16,256]{2,1,0:T(8,128)S(1)}, u32[]{:S(2)}, u32[]{:S(2)}) collective-permute-start(f32[8,16,256]{2,1,0:T(8,128)S(1)} %get-tuple-element.63), channel_id=1, source_target_pairs={{0,32},{32,0},{64,96},{96,64},{1,33},{33,1},{65,97},{97,65},{2,34}... | collective-permute-start | bytes 393224 | tf_op jit(solution)/shard_map/ppermute | solution.py:21
  67.4 6.9 %collective-permute-start.18 = (f32[16,16,128]{2,1,0:T(8,128)S(1)}, f32[16,16,128]{2,1,0:T(8,128)S(1)}, u32[]{:S(2)}, u32[]{:S(2)}) collective-permute-start(f32[16,16,128]{2,1,0:T(8,128)S(1)} %get-tuple-element.75), channel_id=1, source_target_pairs={{0,128},{128,0},{256,384},{384,256},{1,129},{129,1},{257,385},{385... | collective-permute-start | bytes 393224 | tf_op jit(solution)/shard_map/ppermute | solution.py:29
  70.8 9.5 %collective-permute-start.16 = (f32[16,16,128]{2,1,0:T(8,128)S(1)}, f32[16,16,128]{2,1,0:T(8,128)S(1)}, u32[]{:S(2)}, u32[]{:S(2)}) collective-permute-start(f32[16,16,128]{2,1,0:T(8,128)S(1)} %get-tuple-element.73), channel_id=1, source_target_pairs={{128,256},{256,128},{384,0},{0,384},{129,257},{257,129},{385,1},{1... | collective-permute-start | bytes 393224 | tf_op jit(solution)/shard_map/ppermute | solution.py:29
  74.3 12.8 %collective-permute-start.19 = (f32[32,16,128]{2,1,0:T(8,128)S(1)}, f32[32,16,128]{2,1,0:T(8,128)S(1)}, u32[]{:S(2)}, u32[]{:S(2)}) collective-permute-start(f32[32,16,128]{2,1,0:T(8,128)S(1)} %shard_map.124), channel_id=1, source_target_pairs={{128,256},{256,128},{384,0},{0,384},{129,257},{257,129},{385,1},{1... | collective-permute-start | bytes 786440 | tf_op jit(solution)/shard_map/ppermute | solution.py:29
  77.9 6.9 %collective-permute-start.15 = (f32[16,16,128]{2,1,0:T(8,128)S(1)}, f32[16,16,128]{2,1,0:T(8,128)S(1)}, u32[]{:S(2)}, u32[]{:S(2)}) collective-permute-start(f32[16,16,128]{2,1,0:T(8,128)S(1)} %get-tuple-element.71), channel_id=1, source_target_pairs={{0,128},{128,0},{256,384},{384,256},{1,129},{129,1},{257,385},{385... | collective-permute-start | bytes 393224 | tf_op jit(solution)/shard_map/ppermute | solution.py:29
  80.3 6.9 %collective-permute-start.17 = (f32[16,16,128]{2,1,0:T(8,128)S(1)}, f32[16,16,128]{2,1,0:T(8,128)S(1)}, u32[]{:S(2)}, u32[]{:S(2)}) collective-permute-start(f32[16,16,128]{2,1,0:T(8,128)S(1)} %shard_map.123), channel_id=1, source_target_pairs={{0,128},{128,0},{256,384},{384,256},{1,129},{129,1},{257,385},{385... | collective-permute-start | bytes 393224 | tf_op jit(solution)/shard_map/ppermute | solution.py:29

commit v5 on v3

--- a/solution.py
+++ b/solution.py
@@ -27,11 +27,6 @@
     for i in range(odd, size, 2):
         pairs += [(i, (i + 1) % size), ((i + 1) % size, i)]
     return lax.ppermute(value, "shot", pairs)
-
-
-def swap_across(value):
-    size = lax.axis_size("shot")
-    return lax.ppermute(value, "shot", [(i, (i + size // 2) % size) for i in range(size)])
 
 
 def exchange(payload):
@@ -150,6 +145,12 @@
     top = size_x - 4
     xa[plane : plane + 4] = field[pl.ds(jnp.where(even_x, top, 0), 4)]
     xb[plane : plane + 4] = field[pl.ds(jnp.where(even_x, 0, top), 4)]
+
+
+def pair_kernel(first, second, out):
+    half = first.shape[0]
+    out[0:half] = first[...]
+    out[half:] = second[...]
 
 
 def edges_kernel(field, ya, yb, xa, xb):
@@ -235,14 +236,16 @@
 
 
 def second_kernel(
-    offsets, tile, tile_a, tile_b, tile_ab, lap1, wave0, wave1, adj4, source,
+    offsets, tile, tile_a, pair, lap1, wave0, wave1, adj4, source,
     vel, wave2, image, ya, yb, xa, xb, column,
 ):
     size_x, size_y = wave1.shape[0], wave1.shape[1]
     me = lax.axis_index("shot")
     turn = jnp.where(even("shot"), 1, 3)
-    for part, away in ((tile, 0), (tile_a, turn), (tile_ab, 2), (tile_b, 4 - turn)):
-        column[lax.rem(me + away, 4)] = part[...]
+    column[me] = tile[...]
+    column[lax.rem(me + turn, 4)] = tile_a[...]
+    column[lax.rem(me + 4 - turn, 4)] = pair[0:size_x]
+    column[lax.rem(me + 2, 4)] = pair[size_x:]
     start = offsets[0]
     low = start // HALF
     shift_by = lax.rem(start, HALF)
@@ -318,19 +321,15 @@
 
 def fourth_kernel(
     offsets, yb, ya, xb, xa, grad_in, adj4, lap1, outer,
-    far0, far1, near_a, near_b, own, extra2, side, side2, extra,
+    placed, extra2, side, side2, extra,
 ):
     size_x, size_y = adj4.shape[0], adj4.shape[1]
     outer_parts(ya, yb, xa, xb, outer, size_x, size_y, (side, side2), (extra, extra2))
     start = offsets[0]
     low = start // HALF
     shift_by = lax.rem(start, HALF)
-    me = lax.axis_index("shot")
-    turn = jnp.where(even("shot"), 1, 3)
-    which = [lax.rem(me + away, 4) - low for away in (2, turn, 4 - turn, 0)]
-    half = size_x // 2
-
-    def body(x, far, at):
+
+    def body(x, _):
         lane = lax.broadcasted_iota(jnp.int32, (size_y, HALF), 1)
         rolled = []
         for z in halves():
@@ -340,26 +339,17 @@
         first = jnp.where(high, rolled[0], 0.0)
         second = jnp.where(high, rolled[1], rolled[0])
         third = jnp.where(high, 0.0, rolled[1])
-        for n, (out, place) in zip(which, ((far, at), (near_a, x), (near_b, x), (own, x))):
-            value = jnp.where(n == 0, first, jnp.where(n == 1, second, third))
-            out[place] = jnp.where((n >= 0) & (n <= 2), value, 0.0)
+        for n in range(4):
+            value = jnp.where(low == n, first, jnp.where(low + 1 == n, second, third))
+            placed[n, x] = jnp.where((low <= n) & (n <= low + 2), value, 0.0)
         return 0
 
-    lax.fori_loop(0, half, lambda x, _: body(x, far0, x), 0, unroll=4)
-    lax.fori_loop(half, size_x, lambda x, _: body(x, far1, x - half), 0, unroll=4)
-
-
-def adjoint_kernel(adj2_in, extra, adj2):
+    lax.fori_loop(0, size_x, body, 0, unroll=4)
+
+
+def last_kernel(parts, adj2_in, extra, out, adj2):
+    out[...] = (parts[0] + parts[1]) + (parts[2] + parts[3])
     adj2[...] = adj2_in[...] + extra[...]
-
-
-def pass_kernel(first, near_in, far, near):
-    planes = pl.ds(first, far.shape[0])
-    near[planes] = near_in[planes] + far[...]
-
-
-def sum_kernel(own, a, b, out):
-    out[...] = own[...] + (a[...] + b[...])
 
 
 def local(model_vel2, offsets, wave_prev, wave_cur, adj_cur, adj_next, src_cell, src_amp, rec_cell, rec_res):
@@ -367,7 +357,7 @@
     wave0, wave1, adj4, adj5 = wave_prev[0], wave_cur[0], adj_cur[0], adj_next[0]
     block = shaped(size_x, size_y, depth)
     edge_y, edge_x = shaped(size_x, 8, depth), shaped(8, size_y, depth)
-    tile, half = shaped(size_x, size_y, HALF), shaped(size_x // 2, size_y, HALF)
+    tile = shaped(size_x, size_y, HALF)
     whole = pltpu.VMEM((size_x, size_y, depth), F32)
     side = pltpu.VMEM((8, size_y, depth), F32)
     rows, bf16 = size_x // 2 * size_y, jnp.bfloat16
@@ -376,8 +366,8 @@
         for dims in ((rows, rows), (depth, depth), (2, rows, size_x // 2 * 16))
     ]
 
-    tile_a, tile_b = swap_shot(model_vel2, 0), swap_shot(model_vel2, 1)
-    tile_ab = swap_across(model_vel2)
+    tile_a = swap_shot(model_vel2, 0)
+    pair = swap_shot(call(pair_kernel, shaped(2 * size_x, size_y, HALF), n_in=2)(model_vel2, tile_a), 1)
     edges = call(
         edges_kernel, (shaped(size_x // 2, 8, depth),) * 2 + (shaped(4, size_y, depth),) * 2, n_in=1
     )(wave1)
@@ -387,12 +377,12 @@
         smem=2, n_in=2, room=8,
     )(src_cell, src_amp, jnp.transpose(rec_cell[0]), jnp.transpose(rec_res[0]))
     yb, ya, xb, xa = halos
-    lap1 = call(first_inner_kernel, block, (whole,), n_in=6, room=6)(wave1, yb, ya, along_y, along_z, outer)
+    lap1 = call(first_inner_kernel, block, (whole,), n_in=6, room=6, flops=5000000000)(wave1, yb, ya, along_y, along_z, outer)
     lap1 = call(first_kernel, block, (side,), n_in=3, aliases={0: 0})(lap1, xb, xa)
     vel, wave2, image, *edges = call(
         second_kernel, (block,) * 3 + (edge_y,) * 2 + (edge_x,) * 2,
-        (pltpu.VMEM((4, size_x, size_y, HALF), F32),), smem=1, n_in=9, room=8,
-    )(offsets, model_vel2, tile_a, tile_b, tile_ab, lap1, wave0, wave1, adj4, source0)
+        (pltpu.VMEM((4, size_x, size_y, HALF), F32),), smem=1, n_in=8, room=8,
+    )(offsets, model_vel2, tile_a, pair, lap1, wave0, wave1, adj4, source0)
     halos = exchange(edges)
     inner = call(third_inner_kernel, (block,) * 3, (whole,) * 2, n_in=10, room=10)(
         wave1, wave2, adj4, adj5, vel, image, source1, inject0, along_y, along_z
@@ -405,15 +395,11 @@
     inner_adj2, inner_grad = call(fourth_inner_kernel, (block,) * 2, (whole,) * 2, n_in=9, room=10)(
         wave3, image3, adj3, adj4, lap1, lap2, inject1, along_y, along_z
     )
-    far0, far1, near_a, near_b, own, extra = call(
-        fourth_kernel, (half, half, tile, tile, tile, block), (side, side, whole), smem=1, n_in=8, room=10
+    placed, extra = call(
+        fourth_kernel, (shaped(4, size_x, size_y, HALF), block), (side, side, whole), smem=1, n_in=8, room=10
     )(offsets, *halos, inner_grad, adj4, lap1, outer)
-    from_a, from_b = swap_shot(far0, 0), swap_shot(far1, 1)
-    near_b = call(functools.partial(pass_kernel, 0), tile, n_in=2, aliases={0: 0})(near_b, from_a)
-    near_a = call(functools.partial(pass_kernel, size_x // 2), tile, n_in=2, aliases={0: 0})(near_a, from_b)
-    got_b, got_a = swap_shot(near_b, 1), swap_shot(near_a, 0)
-    adj2 = call(adjoint_kernel, block, n_in=2)(inner_adj2, extra)
-    owned = call(sum_kernel, tile, n_in=3)(own, got_a, got_b)
+    parts = lax.all_to_all(placed, "shot", 0, 0)
+    owned, adj2 = call(last_kernel, (tile, block), n_in=3)(parts, inner_adj2, extra)
     return owned, adj2[None]
 
 

time: 92.9 us -> 85.7 us (0.922)
  starting transfers between devices: 63.7 us -> 46.1 us
  blocking collectives: 0 us -> 16.9 us
  waiting for transfers between devices: 13 us -> 7.87 us
  local copies, waits for them, and re-layouts: 2.78 us -> 1.74 us
    all_to_all x0 -> x1, blocking collectives: none -> 16.9 us  [local(): parts = lax.all_to_all(placed, 'shot', 0, 0)]
    ppermute x6 -> x2, starting transfers between devices: 20.2 us -> 7.4 us  [swap_shot(): return lax.ppermute(value, 'shot', pairs)]
    ppermute x12, waiting for transfers between devices: 7.43 us -> 3.38 us  [swap(): return lax.ppermute(value, axis, pairs)]
    ppermute x1 -> x0, starting transfers between devices: 3.63 us -> none  [swap_across(): lax.ppermute(value, 'shot', [(i, (i + size // 2) % size) for i in range(s...]
    ppermute x12, starting transfers between devices: 39.8 us -> 38.7 us  [swap(): return lax.ppermute(value, axis, pairs)]
    unnamed x21, local copies, waits for them, and re-layouts: 2.78 us -> 1.74 us
    ppermute x6 -> x2, waiting for transfers between devices: 5.53 us -> 4.49 us  [swap_shot(): return lax.ppermute(value, 'shot', pairs)]
    pallas_call x6 -> x4, Pallas kernels: 3.97 us -> 3.36 us  [the longest x1 1.43 us: local(): call(fourth_kernel, (shaped(4, size_x, size_y, HALF), block), (side, side...]
  transfers between devices with their start and end apart: 19 -> 14, of which waited for: 11 -> 5; matrix products, arithmetic and copies ran while one was open for 0% -> 0% of each run, Pallas kernels for 7% -> 6%
where the time goes in v5:
time: 85.7 us; the launch traced here: 84.1 us
  starting transfers between devices  46.1 us (54%)
  blocking collectives  16.9 us (20%)
  Pallas kernels  9.97 us (12%)
  waiting for transfers between devices  7.87 us (9%)
  local copies, waits for them, and re-layouts  1.74 us (2%)
  between operations  1.61 us (2%)
    ppermute x12, starting transfers between devices, swap(): return lax.ppermute(value, axis, pairs)  38.7 us
    all_to_all x1, blocking collectives, local(): parts = lax.all_to_all(placed, 'shot', 0, 0)  16.9 us
    ppermute x2, starting transfers between devices, swap_shot(): return lax.ppermute(value, 'shot', pairs)  7.4 us
    ppermute x2, waiting for transfers between devices, swap_shot(): return lax.ppermute(value, 'shot', pairs)  4.49 us
    ppermute x12, waiting for transfers between devices, swap(): return lax.ppermute(value, axis, pairs)  3.38 us
    unnamed x21, local copies, waits for them, and re-layouts  1.74 us
  transfers between devices with their start and end apart: 14, of which 5 were waited for; matrix products, arithmetic and copies ran while one was open for 0% of the time, Pallas kernels for 6%

profile of v5, /device:TPU:24, one launch (start us, length us, event | category | flops | bytes accessed | tf_op | source)
XLA Modules:
  0.0 84.1 jit_solution(13808784970164128038)
XLA Ops:
  0.6 3.4 %collective-permute-start = (f32[32,16,128]{2,1,0:T(8,128)}, f32[32,16,128]{2,1,0:T(8,128)S(1)}, u32[]{:S(2)}, u32[]{:S(2)}) collective-permute-start(f32[32,16,128]{2,1,0:T(8,128)} %tile.1), channel_id=1, source_target_pairs={{0,128},{128,0},{256,384},{384,256},{1,129},{129,1},{257,385},{385... | collective-permute-start | bytes 786440 | tf_op jit(solution)/shard_map/ppermute | solution.py:29
  4.0 1.0 %copy-done.1 = f32[1,32,16,256]{3,2,1,0:T(8,128)S(1)} copy-done((f32[1,32,16,256]{3,2,1,0:T(8,128)S(1)}, f32[1,32,16,256]{3,2,1,0:T(8,128)}, u32[]{:S(2)}) %copy-start.1) | copy-done | bytes 524312
  5.1 0.1 shard_map.114
  5.2 12.1 %collective-permute-start.2 = (f32[16,8,256]{2,1,0:T(8,128)S(1)}, f32[16,8,256]{2,1,0:T(8,128)S(1)}, u32[]{:S(2)}, u32[]{:S(2)}) collective-permute-start(f32[16,8,256]{2,1,0:T(8,128)S(1)} %get-tuple-element.37), channel_id=1, source_target_pairs={{1,2},{2,1},{3,4},{4,3},{5,6},{6,5},{7,8},{8,7},{9,10},{10,9},{11,... | collective-permute-start | bytes 393224 | tf_op jit(solution)/shard_map/ppermute | solution.py:21
  17.3 2.1 %collective-permute-start.3 = (f32[16,8,256]{2,1,0:T(8,128)S(1)}, f32[16,8,256]{2,1,0:T(8,128)S(1)}, u32[]{:S(2)}, u32[]{:S(2)}) collective-permute-start(f32[16,8,256]{2,1,0:T(8,128)S(1)} %get-tuple-element.38), channel_id=1, source_target_pairs={{0,1},{1,0},{2,3},{3,2},{4,5},{5,4},{6,7},{7,6},{8,9},{9,8},{10,11... | collective-permute-start | bytes 393224 | tf_op jit(solution)/shard_map/ppermute | solution.py:21
  19.4 4.0 %collective-permute-start.1 = (f32[64,16,128]{2,1,0:T(8,128)S(1)}, f32[64,16,128]{2,1,0:T(8,128)S(1)}, u32[]{:S(2)}, u32[]{:S(2)}) collective-permute-start(f32[64,16,128]{2,1,0:T(8,128)S(1)} %shard_map.113), channel_id=1, source_target_pairs={{128,256},{256,128},{384,0},{0,384},{129,257},{257,129},{385,1},{1... | collective-permute-start | bytes 1572872 | tf_op jit(solution)/shard_map/ppermute | solution.py:29
  23.4 1.9 %collective-permute-start.4 = (f32[4,16,256]{2,1,0:T(8,128)S(1)}, f32[4,16,256]{2,1,0:T(8,128)S(1)}, u32[]{:S(2)}, u32[]{:S(2)}) collective-permute-start(f32[4,16,256]{2,1,0:T(8,128)S(1)} %get-tuple-element.42), channel_id=1, source_target_pairs={{32,64},{64,32},{33,65},{65,33},{34,66},{66,34},{35,67},{67,35},{3... | collective-permute-start | bytes 196616 | tf_op jit(solution)/shard_map/ppermute | solution.py:21
  25.3 1.9 %collective-permute-start.5 = (f32[4,16,256]{2,1,0:T(8,128)S(1)}, f32[4,16,256]{2,1,0:T(8,128)S(1)}, u32[]{:S(2)}, u32[]{:S(2)}) collective-permute-start(f32[4,16,256]{2,1,0:T(8,128)S(1)} %get-tuple-element.43), channel_id=1, source_target_pairs={{0,32},{32,0},{64,96},{96,64},{1,33},{33,1},{65,97},{97,65},{2,34}... | collective-permute-start | bytes 196616 | tf_op jit(solution)/shard_map/ppermute | solution.py:21
  28.0 0.6 copy-done.6
  28.6 1.4 %shard_map.115 = (bf16[256,256]{1,0:T(8,128)(2,1)S(1)}, bf16[256,256]{1,0:T(8,128)(2,1)S(1)}, bf16[2,256,256]{2,1,0:T(8,128)(2,1)S(1)}, f32[32,16,256]{2,1,0:T(8...) custom-call(s32[1,3]{1,0:T(1,128)S(1)} %copy-done.7, ...), custom_call_target="tpu_custom_call" | custom-call | tf_op jit(solution)/shard_map/pallas_call | solution.py:375
  30.1 0.9 %shard_map.116.inner = f32[32,16,256]{2,1,0:T(8,128)S(1)} custom-call(f32[32,16,256]{2,1,0:T(8,128)S(1)} %bitcast.18, f32[16,8,256]{2,1,0:T(8,128)S(1)} %collective-permute-done.2.yb, f32[16,8,256]{2,1,0:T(8,128)S(1)} %collective-permute-done.3.ya, bf16[256,256]{1,0:T(8,128)(2,1)S(1)} %get-tuple-element.39.along_y, ...), custom_call_target="tpu_custom_call" | custom-call | flops 5000000000 | tf_op jit(solution)/shard_map/pallas_call | solution.py:380
  31.0 0.1 shard_map.117.lap1
  31.1 4.5 %collective-permute-done.1.pair = f32[64,16,128]{2,1,0:T(8,128)S(1)} collective-permute-done((f32[64,16,128]{2,1,0:T(8,128)S(1)}, f32[64,16,128]{2,1,0:T(8,128)S(1)}, u32[]{:S(2)}, u32[]{:S(2)}) %collective-permute-start.1) | collective-permute-done | bytes 524320 | tf_op jit(solution)/shard_map/ppermute | solution.py:29
  35.6 1.0 %shard_map.118 = (f32[32,16,256]{2,1,0:T(8,128)S(1)}, f32[32,16,256]{2,1,0:T(8,128)S(1)}, f32[32,16,256]{2,1,0:T(8,128)S(1)}, f32[32,8,256]{2,1,0:T(8,128)S(1)},...) custom-call(s32[1]{0:T(128)S(6)} %copy.23.offsets, f32[32,16,128]{2,1,0:T(8,128)S(1)} %copy-done.3, ...), custom_call_target="tpu_custom_call" | custom-call | tf_op jit(solution)/shard_map/pallas_call | solution.py:382
  36.6 3.6 %collective-permute-start.6 = (f32[32,8,256]{2,1,0:T(8,128)S(1)}, f32[32,8,256]{2,1,0:T(8,128)S(1)}, u32[]{:S(2)}, u32[]{:S(2)}) collective-permute-start(f32[32,8,256]{2,1,0:T(8,128)S(1)} %get-tuple-element.45), channel_id=1, source_target_pairs={{1,2},{2,1},{3,4},{4,3},{5,6},{6,5},{7,8},{8,7},{9,10},{10,9},{11,... | collective-permute-start | bytes 786440 | tf_op jit(solution)/shard_map/ppermute | solution.py:21
  40.3 1.9 %collective-permute-start.7 = (f32[32,8,256]{2,1,0:T(8,128)S(1)}, f32[32,8,256]{2,1,0:T(8,128)S(1)}, u32[]{:S(2)}, u32[]{:S(2)}) collective-permute-start(f32[32,8,256]{2,1,0:T(8,128)S(1)} %get-tuple-element.46), channel_id=1, source_target_pairs={{0,1},{1,0},{2,3},{3,2},{4,5},{5,4},{6,7},{7,6},{8,9},{9,8},{10,11... | collective-permute-start | bytes 786440 | tf_op jit(solution)/shard_map/ppermute | solution.py:21
  42.2 1.9 %collective-permute-start.8 = (f32[8,16,256]{2,1,0:T(8,128)S(1)}, f32[8,16,256]{2,1,0:T(8,128)S(1)}, u32[]{:S(2)}, u32[]{:S(2)}) collective-permute-start(f32[8,16,256]{2,1,0:T(8,128)S(1)} %get-tuple-element.47), channel_id=1, source_target_pairs={{32,64},{64,32},{33,65},{65,33},{34,66},{66,34},{35,67},{67,35},{3... | collective-permute-start | bytes 393224 | tf_op jit(solution)/shard_map/ppermute | solution.py:21
  44.1 1.9 %collective-permute-start.9 = (f32[8,16,256]{2,1,0:T(8,128)S(1)}, f32[8,16,256]{2,1,0:T(8,128)S(1)}, u32[]{:S(2)}, u32[]{:S(2)}) collective-permute-start(f32[8,16,256]{2,1,0:T(8,128)S(1)} %get-tuple-element.48), channel_id=1, source_target_pairs={{0,32},{32,0},{64,96},{96,64},{1,33},{33,1},{65,97},{97,65},{2,34}... | collective-permute-start | bytes 393224 | tf_op jit(solution)/shard_map/ppermute | solution.py:21
  46.1 1.5 %shard_map.119 = (f32[32,16,256]{2,1,0:T(8,128)S(1)}, f32[32,16,256]{2,1,0:T(8,128)S(1)}, f32[32,16,256]{2,1,0:T(8,128)S(1)}) custom-call(f32[32,16,256]{2,1,0:T(8,128)S(1)} %bitcast.20, f32[32,16,256]{2,1,0:T(8,128)S(1)} %get-tuple-element.49.wave2, f32[32,16,256]{2,1,0:T(8,128)S(1)} %bitcast.14, f32[32,16,256]{2,1,0:T(8,128)S(1)} %bitcast.21, ...), custom_call_target="tpu_custom_call" | custom-call | tf_op jit(solution)/shard_map/pallas_call | solution.py:387
  47.6 0.9 %collective-permute-done.8.xb = f32[8,16,256]{2,1,0:T(8,128)S(1)} collective-permute-done((f32[8,16,256]{2,1,0:T(8,128)S(1)}, f32[8,16,256]{2,1,0:T(8,128)S(1)}, u32[]{:S(2)}, u32[]{:S(2)}) %collective-permute-start.8) | collective-permute-done | bytes 131104 | tf_op jit(solution)/shard_map/ppermute | solution.py:21
  48.5 0.3 collective-permute-done.6.yb
  48.8 1.1 %shard_map.120 = (f32[32,16,256]{2,1,0:T(8,128)S(1)}, f32[32,16,256]{2,1,0:T(8,128)S(1)}, f32[32,16,256]{2,1,0:T(8,128)S(1)}, f32[32,16,256]{2,1,0:T(8,128)S(1)}...) custom-call(f32[32,8,256]{2,1,0:T(8,128)S(1)} %collective-permute-do, ...), custom_call_target="tpu_custom_call", output_to_operand_aliasing={{0}: (4, {}), {1}: (5, {}), {2}: (6, {})} | custom-call | tf_op jit(solution)/shard_map/pallas_call | solution.py:390
  49.9 5.6 %collective-permute-start.10 = (f32[32,8,256]{2,1,0:T(8,128)S(1)}, f32[32,8,256]{2,1,0:T(8,128)S(1)}, u32[]{:S(2)}, u32[]{:S(2)}) collective-permute-start(f32[32,8,256]{2,1,0:T(8,128)S(1)} %get-tuple-element.57), channel_id=1, source_target_pairs={{1,2},{2,1},{3,4},{4,3},{5,6},{6,5},{7,8},{8,7},{9,10},{10,9},{11,... | collective-permute-start | bytes 786440 | tf_op jit(solution)/shard_map/ppermute | solution.py:21
  55.5 1.9 %collective-permute-start.11 = (f32[32,8,256]{2,1,0:T(8,128)S(1)}, f32[32,8,256]{2,1,0:T(8,128)S(1)}, u32[]{:S(2)}, u32[]{:S(2)}) collective-permute-start(f32[32,8,256]{2,1,0:T(8,128)S(1)} %get-tuple-element.58), channel_id=1, source_target_pairs={{0,1},{1,0},{2,3},{3,2},{4,5},{5,4},{6,7},{7,6},{8,9},{9,8},{10,11... | collective-permute-start | bytes 786440 | tf_op jit(solution)/shard_map/ppermute | solution.py:21
  57.4 1.9 %collective-permute-start.12 = (f32[8,16,256]{2,1,0:T(8,128)S(1)}, f32[8,16,256]{2,1,0:T(8,128)S(1)}, u32[]{:S(2)}, u32[]{:S(2)}) collective-permute-start(f32[8,16,256]{2,1,0:T(8,128)S(1)} %get-tuple-element.59), channel_id=1, source_target_pairs={{32,64},{64,32},{33,65},{65,33},{34,66},{66,34},{35,67},{67,35},{3... | collective-permute-start | bytes 393224 | tf_op jit(solution)/shard_map/ppermute | solution.py:21
  59.3 1.9 %collective-permute-start.13 = (f32[8,16,256]{2,1,0:T(8,128)S(1)}, f32[8,16,256]{2,1,0:T(8,128)S(1)}, u32[]{:S(2)}, u32[]{:S(2)}) collective-permute-start(f32[8,16,256]{2,1,0:T(8,128)S(1)} %get-tuple-element.60), channel_id=1, source_target_pairs={{0,32},{32,0},{64,96},{96,64},{1,33},{33,1},{65,97},{97,65},{2,34}... | collective-permute-start | bytes 393224 | tf_op jit(solution)/shard_map/ppermute | solution.py:21
  61.2 1.5 %shard_map.121 = (f32[32,16,256]{2,1,0:T(8,128)S(1)}, f32[32,16,256]{2,1,0:T(8,128)S(1)}) custom-call(f32[32,16,256]{2,1,0:T(8,128)S(1)} %get-tuple-element.61.wave3, f32[32,16,256]{2,1,0:T(8,128)S(1)} %get-tuple-element.62.image3, f32[32,16,256]{2,1,0:T(8,128)S(1)} %get-tuple-element.63.adj3, f32[32,16,256]{2,1,0:T(8,128)S(1)} %bitcast.15, ...), custom_call_target="tpu_custom_call" | custom-call | tf_op jit(solution)/shard_map/pallas_call | solution.py:395
  62.7 1.0 %collective-permute-done.12.xb = f32[8,16,256]{2,1,0:T(8,128)S(1)} collective-permute-done((f32[8,16,256]{2,1,0:T(8,128)S(1)}, f32[8,16,256]{2,1,0:T(8,128)S(1)}, u32[]{:S(2)}, u32[]{:S(2)}) %collective-permute-start.12) | collective-permute-done | bytes 131104 | tf_op jit(solution)/shard_map/ppermute | solution.py:21
  63.7 1.2 %collective-permute-done.11.ya = f32[32,8,256]{2,1,0:T(8,128)S(1)} collective-permute-done((f32[32,8,256]{2,1,0:T(8,128)S(1)}, f32[32,8,256]{2,1,0:T(8,128)S(1)}, u32[]{:S(2)}, u32[]{:S(2)}) %collective-permute-start.11) | collective-permute-done | bytes 262176 | tf_op jit(solution)/shard_map/ppermute | solution.py:21
  64.9 1.4 %shard_map.122 = (f32[4,32,16,128]{3,2,1,0:T(8,128)S(1)}, f32[32,16,256]{2,1,0:T(8,128)S(1)}) custom-call(s32[1]{0:T(128)S(6)} %copy.23.offsets, f32[32,8,256]{2,1,0:T(8,128)S(1)} %collective-permute-done.10.yb, f32[32,8,256]{2,1,0:T(8,128)S(1)} %collective-permute-done.11.ya, f32[8,16,256]{2,1,0:T(8,128)S(1)} %collective-permute-done.12.xb, ...), custom_call_target="tpu_custom_call" | custom-call | tf_op jit(solution)/shard_map/pallas_call | solution.py:398
  66.3 16.9 %all_to_all.5.parts = f32[4,32,16,128]{3,2,1,0:T(8,128)S(1)} all-to-all(f32[4,32,16,128]{3,2,1,0:T(8,128)S(1)} %get-tuple-element.67), channel_id=1, replica_groups=mesh['shot'=4,'gx'=4,'gy'=32] {'shot'}, dimensions={0} | all-to-all | bytes 2097152 | tf_op jit(solution)/shard_map/all_to_all | solution.py:401
  83.1 1.0 %shard_map.123 = (f32[32,16,128]{2,1,0:T(8,128)}, f32[32,16,256]{2,1,0:T(8,128)}) custom-call(f32[4,32,16,128]{3,2,1,0:T(8,128)S(1)} %all_to_all.5.parts, f32[32,16,256]{2,1,0:T(8,128)S(1)} %get-tuple-element.68.adj2_in, f32[32,16,256]{2,1,0:T(8,128)S(1)} %get-tuple-element.69.extra), custom_call_target="tpu_custom_call" | custom-call | tf_op jit(solution)/shard_map/pallas_call | solution.py:402
  (29 shorter events, 0.1 us)
Async XLA Ops:
  0.6 18.7 %collective-permute-start = (f32[32,16,128]{2,1,0:T(8,128)}, f32[32,16,128]{2,1,0:T(8,128)S(1)}, u32[]{:S(2)}, u32[]{:S(2)}) collective-permute-start(f32[32,16,128]{2,1,0:T(8,128)} %tile.1), channel_id=1, source_target_pairs={{0,128},{128,0},{256,384},{384,256},{1,129},{129,1},{257,385},{385... | collective-permute-start | bytes 786440 | tf_op jit(solution)/shard_map/ppermute | solution.py:29
  4.0 1.0 %copy-start.1 = (f32[1,32,16,256]{3,2,1,0:T(8,128)S(1)}, f32[1,32,16,256]{3,2,1,0:T(8,128)}, u32[]{:S(2)}) copy-start(f32[1,32,16,256]{3,2,1,0:T(8,128)} %param.13) | copy-start | bytes 1572868
  5.1 14.3 %copy-start.3 = (f32[32,16,128]{2,1,0:T(8,128)S(1)}, f32[32,16,128]{2,1,0:T(8,128)}, u32[]{:S(2)}) copy-start(f32[32,16,128]{2,1,0:T(8,128)} %tile.1) | copy-start | bytes 786436
  5.2 24.9 %collective-permute-start.2 = (f32[16,8,256]{2,1,0:T(8,128)S(1)}, f32[16,8,256]{2,1,0:T(8,128)S(1)}, u32[]{:S(2)}, u32[]{:S(2)}) collective-permute-start(f32[16,8,256]{2,1,0:T(8,128)S(1)} %get-tuple-element.37), channel_id=1, source_target_pairs={{1,2},{2,1},{3,4},{4,3},{5,6},{6,5},{7,8},{8,7},{9,10},{10,9},{11,... | collective-permute-start | bytes 393224 | tf_op jit(solution)/shard_map/ppermute | solution.py:21
  17.2 12.8 %copy-start.2 = (f32[1,32,16,256]{3,2,1,0:T(8,128)S(1)}, f32[1,32,16,256]{3,2,1,0:T(8,128)}, u32[]{:S(2)}) copy-start(f32[1,32,16,256]{3,2,1,0:T(8,128)} %param.13) | copy-start | bytes 1572868
  17.3 12.8 %collective-permute-start.3 = (f32[16,8,256]{2,1,0:T(8,128)S(1)}, f32[16,8,256]{2,1,0:T(8,128)S(1)}, u32[]{:S(2)}, u32[]{:S(2)}) collective-permute-start(f32[16,8,256]{2,1,0:T(8,128)S(1)} %get-tuple-element.38), channel_id=1, source_target_pairs={{0,1},{1,0},{2,3},{3,2},{4,5},{5,4},{6,7},{7,6},{8,9},{9,8},{10,11... | collective-permute-start | bytes 393224 | tf_op jit(solution)/shard_map/ppermute | solution.py:21
  19.4 8.5 %copy-start.9 = (s32[1,256,3]{1,0,2:T(1,128)S(1)}, s32[1,256,3]{1,0,2:T(1,128)}, u32[]{:S(2)}) copy-start(s32[1,256,3]{1,0,2:T(1,128)} %param.18) | copy-start | bytes 9220
  19.4 16.2 %collective-permute-start.1 = (f32[64,16,128]{2,1,0:T(8,128)S(1)}, f32[64,16,128]{2,1,0:T(8,128)S(1)}, u32[]{:S(2)}, u32[]{:S(2)}) collective-permute-start(f32[64,16,128]{2,1,0:T(8,128)S(1)} %shard_map.113), channel_id=1, source_target_pairs={{128,256},{256,128},{384,0},{0,384},{129,257},{257,129},{385,1},{1... | collective-permute-start | bytes 1572872 | tf_op jit(solution)/shard_map/ppermute | solution.py:29
  23.4 7.6 %collective-permute-start.4 = (f32[4,16,256]{2,1,0:T(8,128)S(1)}, f32[4,16,256]{2,1,0:T(8,128)S(1)}, u32[]{:S(2)}, u32[]{:S(2)}) collective-permute-start(f32[4,16,256]{2,1,0:T(8,128)S(1)} %get-tuple-element.42), channel_id=1, source_target_pairs={{32,64},{64,32},{33,65},{65,33},{34,66},{66,34},{35,67},{67,35},{3... | collective-permute-start | bytes 196616 | tf_op jit(solution)/shard_map/ppermute | solution.py:21
  25.3 5.7 %collective-permute-start.5 = (f32[4,16,256]{2,1,0:T(8,128)S(1)}, f32[4,16,256]{2,1,0:T(8,128)S(1)}, u32[]{:S(2)}, u32[]{:S(2)}) collective-permute-start(f32[4,16,256]{2,1,0:T(8,128)S(1)} %get-tuple-element.43), channel_id=1, source_target_pairs={{0,32},{32,0},{64,96},{96,64},{1,33},{33,1},{65,97},{97,65},{2,34}... | collective-permute-start | bytes 196616 | tf_op jit(solution)/shard_map/ppermute | solution.py:21
  27.9 0.7 copy-start.6
  27.9 0.7 copy-start.7
  28.0 0.7 copy-start.8
  31.0 4.6 %copy-start = (f32[1,32,16,256]{3,2,1,0:T(8,128)S(1)}, f32[1,32,16,256]{3,2,1,0:T(8,128)}, u32[]{:S(2)}) copy-start(f32[1,32,16,256]{3,2,1,0:T(8,128)} %param.14) | copy-start | bytes 1572868
  31.0 4.6 %copy-start.5 = (f32[1,32,16,256]{3,2,1,0:T(8,128)S(1)}, f32[1,32,16,256]{3,2,1,0:T(8,128)}, u32[]{:S(2)}) copy-start(f32[1,32,16,256]{3,2,1,0:T(8,128)} %param.12) | copy-start | bytes 1572868
  35.6 10.5 %copy-start.4 = (f32[1,32,16,256]{3,2,1,0:T(8,128)S(1)}, f32[1,32,16,256]{3,2,1,0:T(8,128)}, u32[]{:S(2)}) copy-start(f32[1,32,16,256]{3,2,1,0:T(8,128)} %param.15) | copy-start | bytes 1572868
  36.6 12.2 %collective-permute-start.6 = (f32[32,8,256]{2,1,0:T(8,128)S(1)}, f32[32,8,256]{2,1,0:T(8,128)S(1)}, u32[]{:S(2)}, u32[]{:S(2)}) collective-permute-start(f32[32,8,256]{2,1,0:T(8,128)S(1)} %get-tuple-element.45), channel_id=1, source_target_pairs={{1,2},{2,1},{3,4},{4,3},{5,6},{6,5},{7,8},{8,7},{9,10},{10,9},{11,... | collective-permute-start | bytes 786440 | tf_op jit(solution)/shard_map/ppermute | solution.py:21
  40.3 8.5 %collective-permute-start.7 = (f32[32,8,256]{2,1,0:T(8,128)S(1)}, f32[32,8,256]{2,1,0:T(8,128)S(1)}, u32[]{:S(2)}, u32[]{:S(2)}) collective-permute-start(f32[32,8,256]{2,1,0:T(8,128)S(1)} %get-tuple-element.46), channel_id=1, source_target_pairs={{0,1},{1,0},{2,3},{3,2},{4,5},{5,4},{6,7},{7,6},{8,9},{9,8},{10,11... | collective-permute-start | bytes 786440 | tf_op jit(solution)/shard_map/ppermute | solution.py:21
  42.2 6.3 %collective-permute-start.8 = (f32[8,16,256]{2,1,0:T(8,128)S(1)}, f32[8,16,256]{2,1,0:T(8,128)S(1)}, u32[]{:S(2)}, u32[]{:S(2)}) collective-permute-start(f32[8,16,256]{2,1,0:T(8,128)S(1)} %get-tuple-element.47), channel_id=1, source_target_pairs={{32,64},{64,32},{33,65},{65,33},{34,66},{66,34},{35,67},{67,35},{3... | collective-permute-start | bytes 393224 | tf_op jit(solution)/shard_map/ppermute | solution.py:21
  44.1 4.4 %collective-permute-start.9 = (f32[8,16,256]{2,1,0:T(8,128)S(1)}, f32[8,16,256]{2,1,0:T(8,128)S(1)}, u32[]{:S(2)}, u32[]{:S(2)}) collective-permute-start(f32[8,16,256]{2,1,0:T(8,128)S(1)} %get-tuple-element.48), channel_id=1, source_target_pairs={{0,32},{32,0},{64,96},{96,64},{1,33},{33,1},{65,97},{97,65},{2,34}... | collective-permute-start | bytes 393224 | tf_op jit(solution)/shard_map/ppermute | solution.py:21
  49.9 13.8 %collective-permute-start.10 = (f32[32,8,256]{2,1,0:T(8,128)S(1)}, f32[32,8,256]{2,1,0:T(8,128)S(1)}, u32[]{:S(2)}, u32[]{:S(2)}) collective-permute-start(f32[32,8,256]{2,1,0:T(8,128)S(1)} %get-tuple-element.57), channel_id=1, source_target_pairs={{1,2},{2,1},{3,4},{4,3},{5,6},{6,5},{7,8},{8,7},{9,10},{10,9},{11,... | collective-permute-start | bytes 786440 | tf_op jit(solution)/shard_map/ppermute | solution.py:21
  55.5 9.4 %collective-permute-start.11 = (f32[32,8,256]{2,1,0:T(8,128)S(1)}, f32[32,8,256]{2,1,0:T(8,128)S(1)}, u32[]{:S(2)}, u32[]{:S(2)}) collective-permute-start(f32[32,8,256]{2,1,0:T(8,128)S(1)} %get-tuple-element.58), channel_id=1, source_target_pairs={{0,1},{1,0},{2,3},{3,2},{4,5},{5,4},{6,7},{7,6},{8,9},{9,8},{10,11... | collective-permute-start | bytes 786440 | tf_op jit(solution)/shard_map/ppermute | solution.py:21
  57.4 6.3 %collective-permute-start.12 = (f32[8,16,256]{2,1,0:T(8,128)S(1)}, f32[8,16,256]{2,1,0:T(8,128)S(1)}, u32[]{:S(2)}, u32[]{:S(2)}) collective-permute-start(f32[8,16,256]{2,1,0:T(8,128)S(1)} %get-tuple-element.59), channel_id=1, source_target_pairs={{32,64},{64,32},{33,65},{65,33},{34,66},{66,34},{35,67},{67,35},{3... | collective-permute-start | bytes 393224 | tf_op jit(solution)/shard_map/ppermute | solution.py:21
  59.3 4.4 %collective-permute-start.13 = (f32[8,16,256]{2,1,0:T(8,128)S(1)}, f32[8,16,256]{2,1,0:T(8,128)S(1)}, u32[]{:S(2)}, u32[]{:S(2)}) collective-permute-start(f32[8,16,256]{2,1,0:T(8,128)S(1)} %get-tuple-element.60), channel_id=1, source_target_pairs={{0,32},{32,0},{64,96},{96,64},{1,33},{33,1},{65,97},{97,65},{2,34}... | collective-permute-start | bytes 393224 | tf_op jit(solution)/shard_map/ppermute | solution.py:21

commit v6 on v5

--- a/solution.py
+++ b/solution.py
@@ -27,6 +27,11 @@
     for i in range(odd, size, 2):
         pairs += [(i, (i + 1) % size), ((i + 1) % size, i)]
     return lax.ppermute(value, "shot", pairs)
+
+
+def swap_across(value):
+    size = lax.axis_size("shot")
+    return lax.ppermute(value, "shot", [(i, (i + size // 2) % size) for i in range(size)])
 
 
 def exchange(payload):
@@ -147,10 +152,12 @@
     xb[plane : plane + 4] = field[pl.ds(jnp.where(even_x, 0, top), 4)]
 
 
-def pair_kernel(first, second, out):
-    half = first.shape[0]
-    out[0:half] = first[...]
-    out[half:] = second[...]
+def copies_kernel(tile, out, sems):
+    moves = [pltpu.make_async_copy(tile, out.at[n], sems.at[n]) for n in range(4)]
+    for move in moves:
+        move.start()
+    for move in moves:
+        move.wait()
 
 
 def edges_kernel(field, ya, yb, xa, xb):
@@ -167,16 +174,14 @@
     xb[...] = field[pl.ds(jnp.where(even_x, 0, top), 4)]
 
 
-def tables_kernel(
-    size_x, size_y, cell, amp, cells, res, along_y, along_z, outer, source0, source1, inject0, inject1
-):
-    depth = inject0.shape[2]
+def index(shape, dim):
+    return lax.broadcasted_iota(jnp.int32, shape, dim)
+
+
+def matrices_kernel(size_x, size_y, along_y, along_z, outer):
+    depth = along_z.shape[0]
     half = size_x // 2
     rows = half * size_y
-
-    def index(shape, dim):
-        return lax.broadcasted_iota(jnp.int32, shape, dim)
-
     along_z[...] = weight(index((depth, depth), 0) - index((depth, depth), 1)).astype(jnp.bfloat16)
     here, there = index((rows, rows), 0), index((rows, rows), 1)
     near = jnp.where(here // size_y == there // size_y, weight(here - there), 0.0)
@@ -189,6 +194,11 @@
         both = jnp.concatenate([jnp.where(use, below, 0.0), jnp.where(use, above, 0.0)], axis=1)
         outer[field] = both.astype(jnp.bfloat16)
 
+
+def inject_kernel(size_x, size_y, cell, amp, cells, res, other, source0, source1, inject0, inject1):
+    depth = inject0.shape[2]
+    half = size_x // 2
+    rows = half * size_y
     base_x, base_y = lax.axis_index("gx") * size_x, lax.axis_index("gy") * size_y
     x, y = cell[0, 0] - base_x, cell[0, 1] - base_y
     source0[...] = jnp.zeros_like(source0)
@@ -236,16 +246,9 @@
 
 
 def second_kernel(
-    offsets, tile, tile_a, pair, lap1, wave0, wave1, adj4, source,
-    vel, wave2, image, ya, yb, xa, xb, column,
+    offsets, column, lap1, wave0, wave1, adj4, source, vel, wave2, image, ya, yb, xa, xb
 ):
     size_x, size_y = wave1.shape[0], wave1.shape[1]
-    me = lax.axis_index("shot")
-    turn = jnp.where(even("shot"), 1, 3)
-    column[me] = tile[...]
-    column[lax.rem(me + turn, 4)] = tile_a[...]
-    column[lax.rem(me + 4 - turn, 4)] = pair[0:size_x]
-    column[lax.rem(me + 2, 4)] = pair[size_x:]
     start = offsets[0]
     low = start // HALF
     shift_by = lax.rem(start, HALF)
@@ -321,13 +324,17 @@
 
 def fourth_kernel(
     offsets, yb, ya, xb, xa, grad_in, adj4, lap1, outer,
-    placed, extra2, side, side2, extra,
+    far, near_b, near_a, own, extra2, side, side2, extra,
 ):
     size_x, size_y = adj4.shape[0], adj4.shape[1]
     outer_parts(ya, yb, xa, xb, outer, size_x, size_y, (side, side2), (extra, extra2))
     start = offsets[0]
     low = start // HALF
     shift_by = lax.rem(start, HALF)
+
+    me = lax.axis_index("shot")
+    turn = jnp.where(even("shot"), 1, 3)
+    which = [(lax.rem(me + away, 4) - low, tile) for away, tile in ((2, far), (turn, near_a), (4 - turn, near_b), (0, own))]
 
     def body(x, _):
         lane = lax.broadcasted_iota(jnp.int32, (size_y, HALF), 1)
@@ -339,16 +346,16 @@
         first = jnp.where(high, rolled[0], 0.0)
         second = jnp.where(high, rolled[1], rolled[0])
         third = jnp.where(high, 0.0, rolled[1])
-        for n in range(4):
-            value = jnp.where(low == n, first, jnp.where(low + 1 == n, second, third))
-            placed[n, x] = jnp.where((low <= n) & (n <= low + 2), value, 0.0)
+        for n, tile in which:
+            value = jnp.where(n == 0, first, jnp.where(n == 1, second, third))
+            tile[x] = jnp.where((n >= 0) & (n <= 2), value, 0.0)
         return 0
 
     lax.fori_loop(0, size_x, body, 0, unroll=4)
 
 
-def last_kernel(parts, adj2_in, extra, out, adj2):
-    out[...] = (parts[0] + parts[1]) + (parts[2] + parts[3])
+def last_kernel(own, far, b, a, adj2_in, extra, out, adj2):
+    out[...] = (own[...] + far[...]) + (a[...] + b[...])
     adj2[...] = adj2_in[...] + extra[...]
 
 
@@ -366,23 +373,37 @@
         for dims in ((rows, rows), (depth, depth), (2, rows, size_x // 2 * 16))
     ]
 
-    tile_a = swap_shot(model_vel2, 0)
-    pair = swap_shot(call(pair_kernel, shaped(2 * size_x, size_y, HALF), n_in=2)(model_vel2, tile_a), 1)
+    copies = pl.pallas_call(
+        copies_kernel,
+        out_shape=shaped(4, size_x, size_y, HALF),
+        in_specs=[pl.BlockSpec(memory_space=pltpu.HBM)],
+        out_specs=pl.BlockSpec(memory_space=pltpu.HBM),
+        scratch_shapes=[pltpu.SemaphoreType.DMA((4,))],
+        compiler_params=pltpu.CompilerParams(vmem_limit_bytes=1 << 20),
+    )(model_vel2)
+    column = lax.all_to_all(copies, "shot", 0, 0)
     edges = call(
-        edges_kernel, (shaped(size_x // 2, 8, depth),) * 2 + (shaped(4, size_y, depth),) * 2, n_in=1
+        edges_kernel, (shaped(size_x // 2, 8, depth),) * 2 + (shaped(4, size_y, depth),) * 2, n_in=1, room=1
     )(wave1)
     halos = exchange(edges)
-    along_y, along_z, outer, source0, source1, inject0, inject1 = call(
-        functools.partial(tables_kernel, size_x, size_y), (*matrices, block, block, block, block),
-        smem=2, n_in=2, room=8,
-    )(src_cell, src_amp, jnp.transpose(rec_cell[0]), jnp.transpose(rec_res[0]))
+    along_y, along_z, outer = call(
+        functools.partial(matrices_kernel, size_x, size_y), tuple(matrices), n_in=0, room=1
+    )()
     yb, ya, xb, xa = halos
-    lap1 = call(first_inner_kernel, block, (whole,), n_in=6, room=6, flops=5000000000)(wave1, yb, ya, along_y, along_z, outer)
-    lap1 = call(first_kernel, block, (side,), n_in=3, aliases={0: 0})(lap1, xb, xa)
+    lap1 = call(first_inner_kernel, block, (whole,), n_in=6, room=2, flops=0)(wave1, yb, ya, along_y, along_z, outer)
+    lap1 = call(first_kernel, block, (side,), n_in=3, room=1, aliases={0: 0})(lap1, xb, xa)
+    source0, source1, inject0, inject1 = pl.pallas_call(
+        functools.partial(inject_kernel, size_x, size_y),
+        out_shape=(block,) * 4,
+        in_specs=[pl.BlockSpec(memory_space=pltpu.SMEM)] * 2 + [pl.BlockSpec(memory_space=pltpu.VMEM)] * 2
+        + [pl.BlockSpec(memory_space=pl.ANY)],
+        out_specs=(pl.BlockSpec(memory_space=pltpu.VMEM),) * 4,
+        compiler_params=pltpu.CompilerParams(vmem_limit_bytes=4 << 20),
+    )(src_cell, src_amp, jnp.transpose(rec_cell[0]), jnp.transpose(rec_res[0]), column)
     vel, wave2, image, *edges = call(
         second_kernel, (block,) * 3 + (edge_y,) * 2 + (edge_x,) * 2,
-        (pltpu.VMEM((4, size_x, size_y, HALF), F32),), smem=1, n_in=8, room=8,
-    )(offsets, model_vel2, tile_a, pair, lap1, wave0, wave1, adj4, source0)
+        smem=1, n_in=6, room=4,
+    )(offsets, column, lap1, wave0, wave1, adj4, source0)
     halos = exchange(edges)
     inner = call(third_inner_kernel, (block,) * 3, (whole,) * 2, n_in=10, room=10)(
         wave1, wave2, adj4, adj5, vel, image, source1, inject0, along_y, along_z
@@ -395,11 +416,11 @@
     inner_adj2, inner_grad = call(fourth_inner_kernel, (block,) * 2, (whole,) * 2, n_in=9, room=10)(
         wave3, image3, adj3, adj4, lap1, lap2, inject1, along_y, along_z
     )
-    placed, extra = call(
-        fourth_kernel, (shaped(4, size_x, size_y, HALF), block), (side, side, whole), smem=1, n_in=8, room=10
+    far, near_b, near_a, own, extra = call(
+        fourth_kernel, (tile, tile, tile, tile, block), (side, side, whole), smem=1, n_in=8, room=10
     )(offsets, *halos, inner_grad, adj4, lap1, outer)
-    parts = lax.all_to_all(placed, "shot", 0, 0)
-    owned, adj2 = call(last_kernel, (tile, block), n_in=3)(parts, inner_adj2, extra)
+    far, b, a = swap_across(far), swap_shot(near_b, 1), swap_shot(near_a, 0)
+    owned, adj2 = call(last_kernel, (tile, block), n_in=6)(own, far, b, a, inner_adj2, extra)
     return owned, adj2[None]
 
 

time: 85.7 us -> 80.7 us (0.942)
  blocking collectives: 16.9 us -> 0 us
  starting transfers between devices: 46.1 us -> 55.6 us
  waiting for transfers between devices: 7.87 us -> 9.65 us
  Pallas kernels: 9.97 us -> 10.9 us
    all_to_all x1 -> x0, blocking collectives: 16.9 us -> none  [local(): parts = lax.all_to_all(placed, 'shot', 0, 0)]
    ppermute x0 -> x1, starting transfers between devices: none -> 5.43 us  [swap_across(): lax.ppermute(value, 'shot', [(i, (i + size // 2) % size) for i in range(s...]
    all_to_all x0 -> x1, starting transfers between devices: none -> 4.44 us  [local(): column = lax.all_to_all(copies, 'shot', 0, 0)]
    ppermute x2, starting transfers between devices: 7.4 us -> 5 us  [swap_shot(): return lax.ppermute(value, 'shot', pairs)]
    ppermute x12, starting transfers between devices: 38.7 us -> 40.7 us  [swap(): return lax.ppermute(value, axis, pairs)]
    ppermute x2, waiting for transfers between devices: 4.49 us -> 6.27 us  [swap_shot(): return lax.ppermute(value, 'shot', pairs)]
    pallas_call x7 -> x8, Pallas kernels: 5.86 us -> 6.81 us  [the longest x1 1.43 us: local(): call(fourth_kernel, (tile, tile, tile, tile, block), (side, side, whole),...]
    unnamed x21 -> x19, local copies, waits for them, and re-layouts: 1.74 us -> 1.63 us
  transfers between devices with their start and end apart: 14 -> 16, of which waited for: 5 -> 9; matrix products, arithmetic and copies ran while one was open for 0% -> 0% of each run, Pallas kernels for 6% -> 5%
where the time goes in v6:
time: 80.7 us; the launch traced here: 79.4 us
  starting transfers between devices  55.6 us (69%)
  Pallas kernels  10.9 us (14%)
  waiting for transfers between devices  9.65 us (12%)
  local copies, waits for them, and re-layouts  1.63 us (2%)
  between operations  1.61 us (2%)
    ppermute x12, starting transfers between devices, swap(): return lax.ppermute(value, axis, pairs)  40.7 us
    ppermute x2, waiting for transfers between devices, swap_shot(): return lax.ppermute(value, 'shot', pairs)  6.27 us
    ppermute x1, starting transfers between devices, swap_across(): lax.ppermute(value, 'shot', [(i, (i + size // 2) % size) for i in range(s...  5.43 us
    ppermute x2, starting transfers between devices, swap_shot(): return lax.ppermute(value, 'shot', pairs)  5 us
    all_to_all x1, starting transfers between devices, local(): column = lax.all_to_all(copies, 'shot', 0, 0)  4.44 us
    ppermute x12, waiting for transfers between devices, swap(): return lax.ppermute(value, axis, pairs)  3.31 us
    unnamed x19, local copies, waits for them, and re-layouts  1.63 us
  transfers between devices with their start and end apart: 16, of which 9 were waited for; matrix products, arithmetic and copies ran while one was open for 0% of the time, Pallas kernels for 5%

profile of v6, /device:TPU:24, one launch (start us, length us, event | category | flops | bytes accessed | tf_op | source)
XLA Modules:
  0.0 79.4 jit_solution(17883584210768484290)
XLA Ops:
  0.6 0.9 %copy-done.4 = f32[32,16,128]{2,1,0:T(8,128)S(1)} copy-done((f32[32,16,128]{2,1,0:T(8,128)S(1)}, f32[32,16,128]{2,1,0:T(8,128)}, u32[]{:S(2)}) %copy-start.4) | copy-done | bytes 262168
  1.6 1.0 %shard_map.113 = f32[4,32,16,128]{3,2,1,0:T(8,128)} custom-call(f32[32,16,128]{2,1,0:T(8,128)S(1)} %copy-done.4), custom_call_target="tpu_custom_call" | custom-call | tf_op jit(solution)/shard_map/pallas_call | solution.py:376
  2.6 4.4 %all-to-all-start = ((f32[4,32,16,128]{3,2,1,0:T(8,128)}), f32[4,32,16,128]{3,2,1,0:T(8,128)S(1)}, u32[]{:S(2)}, u32[]{:S(2)}) async-start(f32[4,32,16,128]{3,2,1,0:T(8,128)} %shard_map.113), calls=%async_computation | async-start | bytes 2097152 | tf_op jit(solution)/shard_map/all_to_all | solution.py:384
  7.1 12.1 %collective-permute-start = (f32[16,8,256]{2,1,0:T(8,128)S(1)}, f32[16,8,256]{2,1,0:T(8,128)S(1)}, u32[]{:S(2)}, u32[]{:S(2)}) collective-permute-start(f32[16,8,256]{2,1,0:T(8,128)S(1)} %get-tuple-element.40), channel_id=1, source_target_pairs={{1,2},{2,1},{3,4},{4,3},{5,6},{6,5},{7,8},{8,7},{9,10},{10,9},{11,... | collective-permute-start | bytes 393224 | tf_op jit(solution)/shard_map/ppermute | solution.py:21
  19.2 1.9 %collective-permute-start.1 = (f32[16,8,256]{2,1,0:T(8,128)S(1)}, f32[16,8,256]{2,1,0:T(8,128)S(1)}, u32[]{:S(2)}, u32[]{:S(2)}) collective-permute-start(f32[16,8,256]{2,1,0:T(8,128)S(1)} %get-tuple-element.41), channel_id=1, source_target_pairs={{0,1},{1,0},{2,3},{3,2},{4,5},{5,4},{6,7},{7,6},{8,9},{9,8},{10,11... | collective-permute-start | bytes 393224 | tf_op jit(solution)/shard_map/ppermute | solution.py:21
  21.2 1.9 %collective-permute-start.2 = (f32[4,16,256]{2,1,0:T(8,128)S(1)}, f32[4,16,256]{2,1,0:T(8,128)S(1)}, u32[]{:S(2)}, u32[]{:S(2)}) collective-permute-start(f32[4,16,256]{2,1,0:T(8,128)S(1)} %get-tuple-element.45), channel_id=1, source_target_pairs={{32,64},{64,32},{33,65},{65,33},{34,66},{66,34},{35,67},{67,35},{3... | collective-permute-start | bytes 196616 | tf_op jit(solution)/shard_map/ppermute | solution.py:21
  23.1 1.9 %collective-permute-start.3 = (f32[4,16,256]{2,1,0:T(8,128)S(1)}, f32[4,16,256]{2,1,0:T(8,128)S(1)}, u32[]{:S(2)}, u32[]{:S(2)}) collective-permute-start(f32[4,16,256]{2,1,0:T(8,128)S(1)} %get-tuple-element.46), channel_id=1, source_target_pairs={{0,32},{32,0},{64,96},{96,64},{1,33},{33,1},{65,97},{97,65},{2,34}... | collective-permute-start | bytes 196616 | tf_op jit(solution)/shard_map/ppermute | solution.py:21
  26.1 0.9 %shard_map.116.inner = f32[32,16,256]{2,1,0:T(8,128)S(1)} custom-call(f32[32,16,256]{2,1,0:T(8,128)S(1)} %bitcast.14, f32[16,8,256]{2,1,0:T(8,128)S(1)} %collective-permute-done.yb, f32[16,8,256]{2,1,0:T(8,128)S(1)} %collective-permute-done.1.ya, bf16[256,256]{1,0:T(8,128)(2,1)S(1)} %get-tuple-element.42.along_y, ...), custom_call_target="tpu_custom_call" | custom-call | tf_op jit(solution)/shard_map/pallas_call | solution.py:393
  27.1 0.6 copy-done.5
  27.8 1.3 %shard_map.118 = (f32[32,16,256]{2,1,0:T(8,128)S(1)}, f32[32,16,256]{2,1,0:T(8,128)S(1)}, f32[32,16,256]{2,1,0:T(8,128)S(1)}, f32[32,16,256]{2,1,0:T(8,128)S(1)}) custom-call(s32[1,3]{1,0:T(1,128)S(1)} %copy-done.6, f32[1,2]{1,0:T(1,128)S(1)} %copy-done.7, s32[3,256]{1,0:T(4,128)S(1)} %bitcast.23, f32[2,256]{1,0:T(2,128)S(1)} %bitcast.24, ...), custom_call_target="tpu_custom_call" | custom-call | tf_op jit(solution)/shard_map/pallas_call | solution.py:395
  29.1 0.9 %shard_map.119 = (f32[32,16,256]{2,1,0:T(8,128)S(1)}, f32[32,16,256]{2,1,0:T(8,128)S(1)}, f32[32,16,256]{2,1,0:T(8,128)S(1)}, f32[32,8,256]{2,1,0:T(8,128)S(1)},...) custom-call(s32[1]{0:T(128)S(6)} %copy.23.offsets, ...), custom_call_target="tpu_custom_call" | custom-call | tf_op jit(solution)/shard_map/pallas_call | solution.py:403
  30.0 7.1 %collective-permute-start.4 = (f32[32,8,256]{2,1,0:T(8,128)S(1)}, f32[32,8,256]{2,1,0:T(8,128)S(1)}, u32[]{:S(2)}, u32[]{:S(2)}) collective-permute-start(f32[32,8,256]{2,1,0:T(8,128)S(1)} %get-tuple-element.48), channel_id=1, source_target_pairs={{1,2},{2,1},{3,4},{4,3},{5,6},{6,5},{7,8},{8,7},{9,10},{10,9},{11,... | collective-permute-start | bytes 786440 | tf_op jit(solution)/shard_map/ppermute | solution.py:21
  37.2 1.9 %collective-permute-start.5 = (f32[32,8,256]{2,1,0:T(8,128)S(1)}, f32[32,8,256]{2,1,0:T(8,128)S(1)}, u32[]{:S(2)}, u32[]{:S(2)}) collective-permute-start(f32[32,8,256]{2,1,0:T(8,128)S(1)} %get-tuple-element.49), channel_id=1, source_target_pairs={{0,1},{1,0},{2,3},{3,2},{4,5},{5,4},{6,7},{7,6},{8,9},{9,8},{10,11... | collective-permute-start | bytes 786440 | tf_op jit(solution)/shard_map/ppermute | solution.py:21
  39.1 1.9 %collective-permute-start.6 = (f32[8,16,256]{2,1,0:T(8,128)S(1)}, f32[8,16,256]{2,1,0:T(8,128)S(1)}, u32[]{:S(2)}, u32[]{:S(2)}) collective-permute-start(f32[8,16,256]{2,1,0:T(8,128)S(1)} %get-tuple-element.50), channel_id=1, source_target_pairs={{32,64},{64,32},{33,65},{65,33},{34,66},{66,34},{35,67},{67,35},{3... | collective-permute-start | bytes 393224 | tf_op jit(solution)/shard_map/ppermute | solution.py:21
  41.0 1.9 %collective-permute-start.7 = (f32[8,16,256]{2,1,0:T(8,128)S(1)}, f32[8,16,256]{2,1,0:T(8,128)S(1)}, u32[]{:S(2)}, u32[]{:S(2)}) collective-permute-start(f32[8,16,256]{2,1,0:T(8,128)S(1)} %get-tuple-element.51), channel_id=1, source_target_pairs={{0,32},{32,0},{64,96},{96,64},{1,33},{33,1},{65,97},{97,65},{2,34}... | collective-permute-start | bytes 393224 | tf_op jit(solution)/shard_map/ppermute | solution.py:21
  43.0 1.5 %shard_map.120 = (f32[32,16,256]{2,1,0:T(8,128)S(1)}, f32[32,16,256]{2,1,0:T(8,128)S(1)}, f32[32,16,256]{2,1,0:T(8,128)S(1)}) custom-call(f32[32,16,256]{2,1,0:T(8,128)S(1)} %bitcast.16, f32[32,16,256]{2,1,0:T(8,128)S(1)} %get-tuple-element.52.wave2, f32[32,16,256]{2,1,0:T(8,128)S(1)} %bitcast.18, f32[32,16,256]{2,1,0:T(8,128)S(1)} %bitcast.21, ...), custom_call_target="tpu_custom_call" | custom-call | tf_op jit(solution)/shard_map/pallas_call | solution.py:408
  44.4 0.9 %collective-permute-done.6.xb = f32[8,16,256]{2,1,0:T(8,128)S(1)} collective-permute-done((f32[8,16,256]{2,1,0:T(8,128)S(1)}, f32[8,16,256]{2,1,0:T(8,128)S(1)}, u32[]{:S(2)}, u32[]{:S(2)}) %collective-permute-start.6) | collective-permute-done | bytes 131104 | tf_op jit(solution)/shard_map/ppermute | solution.py:21
  45.6 1.1 %shard_map.121 = (f32[32,16,256]{2,1,0:T(8,128)S(1)}, f32[32,16,256]{2,1,0:T(8,128)S(1)}, f32[32,16,256]{2,1,0:T(8,128)S(1)}, f32[32,16,256]{2,1,0:T(8,128)S(1)}...) custom-call(f32[32,8,256]{2,1,0:T(8,128)S(1)} %collective-permute-do, ...), custom_call_target="tpu_custom_call", output_to_operand_aliasing={{0}: (4, {}), {1}: (5, {}), {2}: (6, {})} | custom-call | tf_op jit(solution)/shard_map/pallas_call | solution.py:411
  46.7 4.0 %collective-permute-start.8 = (f32[32,8,256]{2,1,0:T(8,128)S(1)}, f32[32,8,256]{2,1,0:T(8,128)S(1)}, u32[]{:S(2)}, u32[]{:S(2)}) collective-permute-start(f32[32,8,256]{2,1,0:T(8,128)S(1)} %get-tuple-element.60), channel_id=1, source_target_pairs={{1,2},{2,1},{3,4},{4,3},{5,6},{6,5},{7,8},{8,7},{9,10},{10,9},{11,... | collective-permute-start | bytes 786440 | tf_op jit(solution)/shard_map/ppermute | solution.py:21
  50.8 1.9 %collective-permute-start.9 = (f32[32,8,256]{2,1,0:T(8,128)S(1)}, f32[32,8,256]{2,1,0:T(8,128)S(1)}, u32[]{:S(2)}, u32[]{:S(2)}) collective-permute-start(f32[32,8,256]{2,1,0:T(8,128)S(1)} %get-tuple-element.61), channel_id=1, source_target_pairs={{0,1},{1,0},{2,3},{3,2},{4,5},{5,4},{6,7},{7,6},{8,9},{9,8},{10,11... | collective-permute-start | bytes 786440 | tf_op jit(solution)/shard_map/ppermute | solution.py:21
  52.7 2.1 %collective-permute-start.10 = (f32[8,16,256]{2,1,0:T(8,128)S(1)}, f32[8,16,256]{2,1,0:T(8,128)S(1)}, u32[]{:S(2)}, u32[]{:S(2)}) collective-permute-start(f32[8,16,256]{2,1,0:T(8,128)S(1)} %get-tuple-element.62), channel_id=1, source_target_pairs={{32,64},{64,32},{33,65},{65,33},{34,66},{66,34},{35,67},{67,35},{3... | collective-permute-start | bytes 393224 | tf_op jit(solution)/shard_map/ppermute | solution.py:21
  54.8 1.9 %collective-permute-start.11 = (f32[8,16,256]{2,1,0:T(8,128)S(1)}, f32[8,16,256]{2,1,0:T(8,128)S(1)}, u32[]{:S(2)}, u32[]{:S(2)}) collective-permute-start(f32[8,16,256]{2,1,0:T(8,128)S(1)} %get-tuple-element.63), channel_id=1, source_target_pairs={{0,32},{32,0},{64,96},{96,64},{1,33},{33,1},{65,97},{97,65},{2,34}... | collective-permute-start | bytes 393224 | tf_op jit(solution)/shard_map/ppermute | solution.py:21
  56.7 1.5 %shard_map.122 = (f32[32,16,256]{2,1,0:T(8,128)S(1)}, f32[32,16,256]{2,1,0:T(8,128)S(1)}) custom-call(f32[32,16,256]{2,1,0:T(8,128)S(1)} %get-tuple-element.64.wave3, f32[32,16,256]{2,1,0:T(8,128)S(1)} %get-tuple-element.65.image3, f32[32,16,256]{2,1,0:T(8,128)S(1)} %get-tuple-element.66.adj3, f32[32,16,256]{2,1,0:T(8,128)S(1)} %bitcast.19, ...), custom_call_target="tpu_custom_call" | custom-call | tf_op jit(solution)/shard_map/pallas_call | solution.py:416
  58.2 0.8 collective-permute-done.10.xb
  59.0 0.9 %collective-permute-done.8.yb = f32[32,8,256]{2,1,0:T(8,128)S(1)} collective-permute-done((f32[32,8,256]{2,1,0:T(8,128)S(1)}, f32[32,8,256]{2,1,0:T(8,128)S(1)}, u32[]{:S(2)}, u32[]{:S(2)}) %collective-permute-start.8) | collective-permute-done | bytes 262176 | tf_op jit(solution)/shard_map/ppermute | solution.py:21
  60.1 1.4 %shard_map.123 = (f32[32,16,128]{2,1,0:T(8,128)S(1)}, f32[32,16,128]{2,1,0:T(8,128)S(1)}, f32[32,16,128]{2,1,0:T(8,128)S(1)}, f32[32,16,128]{2,1,0:T(8,128)S(1)}, f32[32,16,256]{2,1,0:T(8,128)S(1)}) custom-call(s32[1]{0:T(128)S(6)} %copy.23.offsets, f32[32,8,256]{2,1,0:T(8,128)S(1)} %collective-permute-done.8.yb, ...), custom_call_target="tpu_custom_call" | custom-call | tf_op jit(solution)/shard_map/pallas_call | solution.py:419
  61.6 5.4 %collective-permute-start.12 = (f32[32,16,128]{2,1,0:T(8,128)S(1)}, f32[32,16,128]{2,1,0:T(8,128)S(1)}, u32[]{:S(2)}, u32[]{:S(2)}) collective-permute-start(f32[32,16,128]{2,1,0:T(8,128)S(1)} %get-tuple-element.71), channel_id=1, source_target_pairs={{0,256},{128,384},{256,0},{384,128},{1,257},{129,385},{257,1},{385... | collective-permute-start | bytes 786440 | tf_op jit(solution)/shard_map/ppermute | solution.py:34
  67.0 3.1 %collective-permute-start.13 = (f32[32,16,128]{2,1,0:T(8,128)S(1)}, f32[32,16,128]{2,1,0:T(8,128)S(1)}, u32[]{:S(2)}, u32[]{:S(2)}) collective-permute-start(f32[32,16,128]{2,1,0:T(8,128)S(1)} %get-tuple-element.72), channel_id=1, source_target_pairs={{128,256},{256,128},{384,0},{0,384},{129,257},{257,129},{385,1},{1... | collective-permute-start | bytes 786440 | tf_op jit(solution)/shard_map/ppermute | solution.py:29
  70.1 1.9 %collective-permute-start.14 = (f32[32,16,128]{2,1,0:T(8,128)S(1)}, f32[32,16,128]{2,1,0:T(8,128)S(1)}, u32[]{:S(2)}, u32[]{:S(2)}) collective-permute-start(f32[32,16,128]{2,1,0:T(8,128)S(1)} %get-tuple-element.73), channel_id=1, source_target_pairs={{0,128},{128,0},{256,384},{384,256},{1,129},{129,1},{257,385},{385... | collective-permute-start | bytes 786440 | tf_op jit(solution)/shard_map/ppermute | solution.py:29
  72.1 5.4 %collective-permute-done.13.b = f32[32,16,128]{2,1,0:T(8,128)S(1)} collective-permute-done((f32[32,16,128]{2,1,0:T(8,128)S(1)}, f32[32,16,128]{2,1,0:T(8,128)S(1)}, u32[]{:S(2)}, u32[]{:S(2)}) %collective-permute-start.13) | collective-permute-done | bytes 262176 | tf_op jit(solution)/shard_map/ppermute | solution.py:29
  77.5 0.8 %collective-permute-done.14.a = f32[32,16,128]{2,1,0:T(8,128)S(1)} collective-permute-done((f32[32,16,128]{2,1,0:T(8,128)S(1)}, f32[32,16,128]{2,1,0:T(8,128)S(1)}, u32[]{:S(2)}, u32[]{:S(2)}) %collective-permute-start.14) | collective-permute-done | bytes 262176 | tf_op jit(solution)/shard_map/ppermute | solution.py:29
  78.4 1.0 %shard_map.124 = (f32[32,16,128]{2,1,0:T(8,128)}, f32[32,16,256]{2,1,0:T(8,128)}) custom-call(f32[32,16,128]{2,1,0:T(8,128)S(1)} %get-tuple-element.70.own, f32[32,16,128]{2,1,0:T(8,128)S(1)} %collective-permute-done.12.far, f32[32,16,128]{2,1,0:T(8,128)S(1)} %collective-permute-done.13.b, f32[32,16,128]{2,1,0:T(8,128)S(1)} %collective-permute-done.14.a, ...), custom_call_target="tpu_custom_call" | custom-call | tf_op jit(solution)/shard_map/pallas_call | solution.py:423
  (31 shorter events, 1.2 us)
Async XLA Ops:
  0.6 1.0 %copy-start.4 = (f32[32,16,128]{2,1,0:T(8,128)S(1)}, f32[32,16,128]{2,1,0:T(8,128)}, u32[]{:S(2)}) copy-start(f32[32,16,128]{2,1,0:T(8,128)} %tile.1) | copy-start | bytes 786436
  2.6 4.5 %copy-start = (f32[1,32,16,256]{3,2,1,0:T(8,128)S(1)}, f32[1,32,16,256]{3,2,1,0:T(8,128)}, u32[]{:S(2)}) copy-start(f32[1,32,16,256]{3,2,1,0:T(8,128)} %param.13) | copy-start | bytes 1572868
  2.6 24.5 %all-to-all-start = ((f32[4,32,16,128]{3,2,1,0:T(8,128)}), f32[4,32,16,128]{3,2,1,0:T(8,128)S(1)}, u32[]{:S(2)}, u32[]{:S(2)}) async-start(f32[4,32,16,128]{3,2,1,0:T(8,128)} %shard_map.113), calls=%async_computation | async-start | bytes 2097152 | tf_op jit(solution)/shard_map/all_to_all | solution.py:384
  7.1 18.8 %collective-permute-start = (f32[16,8,256]{2,1,0:T(8,128)S(1)}, f32[16,8,256]{2,1,0:T(8,128)S(1)}, u32[]{:S(2)}, u32[]{:S(2)}) collective-permute-start(f32[16,8,256]{2,1,0:T(8,128)S(1)} %get-tuple-element.40), channel_id=1, source_target_pairs={{1,2},{2,1},{3,4},{4,3},{5,6},{6,5},{7,8},{8,7},{9,10},{10,9},{11,... | collective-permute-start | bytes 393224 | tf_op jit(solution)/shard_map/ppermute | solution.py:21
  19.2 6.9 %collective-permute-start.1 = (f32[16,8,256]{2,1,0:T(8,128)S(1)}, f32[16,8,256]{2,1,0:T(8,128)S(1)}, u32[]{:S(2)}, u32[]{:S(2)}) collective-permute-start(f32[16,8,256]{2,1,0:T(8,128)S(1)} %get-tuple-element.41), channel_id=1, source_target_pairs={{0,1},{1,0},{2,3},{3,2},{4,5},{5,4},{6,7},{7,6},{8,9},{9,8},{10,11... | collective-permute-start | bytes 393224 | tf_op jit(solution)/shard_map/ppermute | solution.py:21
  21.2 4.7 %copy-start.8 = (s32[1,256,3]{1,0,2:T(1,128)S(1)}, s32[1,256,3]{1,0,2:T(1,128)}, u32[]{:S(2)}) copy-start(s32[1,256,3]{1,0,2:T(1,128)} %param.18) | copy-start | bytes 9220
  21.2 5.8 %collective-permute-start.2 = (f32[4,16,256]{2,1,0:T(8,128)S(1)}, f32[4,16,256]{2,1,0:T(8,128)S(1)}, u32[]{:S(2)}, u32[]{:S(2)}) collective-permute-start(f32[4,16,256]{2,1,0:T(8,128)S(1)} %get-tuple-element.45), channel_id=1, source_target_pairs={{32,64},{64,32},{33,65},{65,33},{34,66},{66,34},{35,67},{67,35},{3... | collective-permute-start | bytes 196616 | tf_op jit(solution)/shard_map/ppermute | solution.py:21
  23.1 3.9 %collective-permute-start.3 = (f32[4,16,256]{2,1,0:T(8,128)S(1)}, f32[4,16,256]{2,1,0:T(8,128)S(1)}, u32[]{:S(2)}, u32[]{:S(2)}) collective-permute-start(f32[4,16,256]{2,1,0:T(8,128)S(1)} %get-tuple-element.46), channel_id=1, source_target_pairs={{0,32},{32,0},{64,96},{96,64},{1,33},{33,1},{65,97},{97,65},{2,34}... | collective-permute-start | bytes 196616 | tf_op jit(solution)/shard_map/ppermute | solution.py:21
  27.1 0.7 copy-start.5
  27.1 0.7 copy-start.6
  27.1 0.7 copy-start.7
  27.8 1.3 %copy-start.1 = (f32[1,32,16,256]{3,2,1,0:T(8,128)S(1)}, f32[1,32,16,256]{3,2,1,0:T(8,128)}, u32[]{:S(2)}) copy-start(f32[1,32,16,256]{3,2,1,0:T(8,128)} %param.14) | copy-start | bytes 1572868
  27.8 1.3 %copy-start.3 = (f32[1,32,16,256]{3,2,1,0:T(8,128)S(1)}, f32[1,32,16,256]{3,2,1,0:T(8,128)}, u32[]{:S(2)}) copy-start(f32[1,32,16,256]{3,2,1,0:T(8,128)} %param.12) | copy-start | bytes 1572868
  29.1 13.9 %copy-start.2 = (f32[1,32,16,256]{3,2,1,0:T(8,128)S(1)}, f32[1,32,16,256]{3,2,1,0:T(8,128)}, u32[]{:S(2)}) copy-start(f32[1,32,16,256]{3,2,1,0:T(8,128)} %param.15) | copy-start | bytes 1572868
  30.0 15.3 %collective-permute-start.4 = (f32[32,8,256]{2,1,0:T(8,128)S(1)}, f32[32,8,256]{2,1,0:T(8,128)S(1)}, u32[]{:S(2)}, u32[]{:S(2)}) collective-permute-start(f32[32,8,256]{2,1,0:T(8,128)S(1)} %get-tuple-element.48), channel_id=1, source_target_pairs={{1,2},{2,1},{3,4},{4,3},{5,6},{6,5},{7,8},{8,7},{9,10},{10,9},{11,... | collective-permute-start | bytes 786440 | tf_op jit(solution)/shard_map/ppermute | solution.py:21
  37.2 8.5 %collective-permute-start.5 = (f32[32,8,256]{2,1,0:T(8,128)S(1)}, f32[32,8,256]{2,1,0:T(8,128)S(1)}, u32[]{:S(2)}, u32[]{:S(2)}) collective-permute-start(f32[32,8,256]{2,1,0:T(8,128)S(1)} %get-tuple-element.49), channel_id=1, source_target_pairs={{0,1},{1,0},{2,3},{3,2},{4,5},{5,4},{6,7},{7,6},{8,9},{9,8},{10,11... | collective-permute-start | bytes 786440 | tf_op jit(solution)/shard_map/ppermute | solution.py:21
  39.1 6.3 %collective-permute-start.6 = (f32[8,16,256]{2,1,0:T(8,128)S(1)}, f32[8,16,256]{2,1,0:T(8,128)S(1)}, u32[]{:S(2)}, u32[]{:S(2)}) collective-permute-start(f32[8,16,256]{2,1,0:T(8,128)S(1)} %get-tuple-element.50), channel_id=1, source_target_pairs={{32,64},{64,32},{33,65},{65,33},{34,66},{66,34},{35,67},{67,35},{3... | collective-permute-start | bytes 393224 | tf_op jit(solution)/shard_map/ppermute | solution.py:21
  41.0 4.4 %collective-permute-start.7 = (f32[8,16,256]{2,1,0:T(8,128)S(1)}, f32[8,16,256]{2,1,0:T(8,128)S(1)}, u32[]{:S(2)}, u32[]{:S(2)}) collective-permute-start(f32[8,16,256]{2,1,0:T(8,128)S(1)} %get-tuple-element.51), channel_id=1, source_target_pairs={{0,32},{32,0},{64,96},{96,64},{1,33},{33,1},{65,97},{97,65},{2,34}... | collective-permute-start | bytes 393224 | tf_op jit(solution)/shard_map/ppermute | solution.py:21
  46.7 13.2 %collective-permute-start.8 = (f32[32,8,256]{2,1,0:T(8,128)S(1)}, f32[32,8,256]{2,1,0:T(8,128)S(1)}, u32[]{:S(2)}, u32[]{:S(2)}) collective-permute-start(f32[32,8,256]{2,1,0:T(8,128)S(1)} %get-tuple-element.60), channel_id=1, source_target_pairs={{1,2},{2,1},{3,4},{4,3},{5,6},{6,5},{7,8},{8,7},{9,10},{10,9},{11,... | collective-permute-start | bytes 786440 | tf_op jit(solution)/shard_map/ppermute | solution.py:21
  50.8 9.4 %collective-permute-start.9 = (f32[32,8,256]{2,1,0:T(8,128)S(1)}, f32[32,8,256]{2,1,0:T(8,128)S(1)}, u32[]{:S(2)}, u32[]{:S(2)}) collective-permute-start(f32[32,8,256]{2,1,0:T(8,128)S(1)} %get-tuple-element.61), channel_id=1, source_target_pairs={{0,1},{1,0},{2,3},{3,2},{4,5},{5,4},{6,7},{7,6},{8,9},{9,8},{10,11... | collective-permute-start | bytes 786440 | tf_op jit(solution)/shard_map/ppermute | solution.py:21
  52.7 6.3 %collective-permute-start.10 = (f32[8,16,256]{2,1,0:T(8,128)S(1)}, f32[8,16,256]{2,1,0:T(8,128)S(1)}, u32[]{:S(2)}, u32[]{:S(2)}) collective-permute-start(f32[8,16,256]{2,1,0:T(8,128)S(1)} %get-tuple-element.62), channel_id=1, source_target_pairs={{32,64},{64,32},{33,65},{65,33},{34,66},{66,34},{35,67},{67,35},{3... | collective-permute-start | bytes 393224 | tf_op jit(solution)/shard_map/ppermute | solution.py:21
  54.8 4.2 %collective-permute-start.11 = (f32[8,16,256]{2,1,0:T(8,128)S(1)}, f32[8,16,256]{2,1,0:T(8,128)S(1)}, u32[]{:S(2)}, u32[]{:S(2)}) collective-permute-start(f32[8,16,256]{2,1,0:T(8,128)S(1)} %get-tuple-element.63), channel_id=1, source_target_pairs={{0,32},{32,0},{64,96},{96,64},{1,33},{33,1},{65,97},{97,65},{2,34}... | collective-permute-start | bytes 393224 | tf_op jit(solution)/shard_map/ppermute | solution.py:21
  61.6 10.5 %collective-permute-start.12 = (f32[32,16,128]{2,1,0:T(8,128)S(1)}, f32[32,16,128]{2,1,0:T(8,128)S(1)}, u32[]{:S(2)}, u32[]{:S(2)}) collective-permute-start(f32[32,16,128]{2,1,0:T(8,128)S(1)} %get-tuple-element.71), channel_id=1, source_target_pairs={{0,256},{128,384},{256,0},{384,128},{1,257},{129,385},{257,1},{385... | collective-permute-start | bytes 786440 | tf_op jit(solution)/shard_map/ppermute | solution.py:34
  67.0 10.5 %collective-permute-start.13 = (f32[32,16,128]{2,1,0:T(8,128)S(1)}, f32[32,16,128]{2,1,0:T(8,128)S(1)}, u32[]{:S(2)}, u32[]{:S(2)}) collective-permute-start(f32[32,16,128]{2,1,0:T(8,128)S(1)} %get-tuple-element.72), channel_id=1, source_target_pairs={{128,256},{256,128},{384,0},{0,384},{129,257},{257,129},{385,1},{1... | collective-permute-start | bytes 786440 | tf_op jit(solution)/shard_map/ppermute | solution.py:29
  70.1 8.3 %collective-permute-start.14 = (f32[32,16,128]{2,1,0:T(8,128)S(1)}, f32[32,16,128]{2,1,0:T(8,128)S(1)}, u32[]{:S(2)}, u32[]{:S(2)}) collective-permute-start(f32[32,16,128]{2,1,0:T(8,128)S(1)} %get-tuple-element.73), channel_id=1, source_target_pairs={{0,128},{128,0},{256,384},{384,256},{1,129},{129,1},{257,385},{385... | collective-permute-start | bytes 786440 | tf_op jit(solution)/shard_map/ppermute | solution.py:29

commit v7 on v6

--- a/solution.py
+++ b/solution.py
@@ -90,14 +90,20 @@
         out[at : at + chunk] = total.reshape(chunk, size_y, depth)
 
 
-def outer_part(ya, yb, at, outer, field, size_y):
+def outer_part(ya, yb, at, outer, field):
     depth = ya.shape[2]
-    chunk = outer.shape[1] // size_y
+    chunk = outer.shape[1] // 8
     a, b = (m[at : at + chunk].reshape(chunk * 8, depth) for m in (ya, yb))
     even_y = even("gy")
     below, above = three(jnp.where(even_y, b, a)), three(jnp.where(even_y, a, b))
     total = sum(product(outer[field], jnp.concatenate(pair, axis=0)) for pair in zip(below, above))
-    return total.reshape(chunk, size_y, depth)
+    return total.reshape(chunk, 8, depth) * (1.0 / SCALE)
+
+
+def spread(rows, size_y):
+    first = lax.broadcasted_iota(jnp.int32, rows.shape, 0) < 4
+    middle = [jnp.zeros((size_y - 16, rows.shape[1]), F32)] if size_y > 16 else []
+    return jnp.concatenate([jnp.where(first, rows, 0.0)] + middle + [jnp.where(first, 0.0, rows)], axis=0)
 
 
 def outside_x(xa, xb, plane, out):
@@ -113,14 +119,22 @@
         out[7 - i] = last
 
 
-def outer_parts(ya, yb, xa, xb, outer, size_x, size_y, sides, extras):
-    chunk = outer.shape[1] // size_y
-    for field, (side, extra) in enumerate(zip(sides, extras)):
+def outer_parts(ya, yb, xa, xb, outer, sides, rows):
+    chunk = outer.shape[1] // 8
+    for field, (side, row) in enumerate(zip(sides, rows)):
         outside_x(xa, xb, 4 * field, side)
-        for at in range(0, size_x, chunk):
-            extra[at : at + chunk] = outer_part(ya, yb, at, outer, field, size_y) * (1.0 / SCALE)
-        extra[0:4] = extra[0:4] + side[0:4]
-        extra[size_x - 4 : size_x] = extra[size_x - 4 : size_x] + side[4:8]
+        for at in range(0, row.shape[0], chunk):
+            row[at : at + chunk] = outer_part(ya, yb, at, outer, field)
+
+
+def outer_of(side, row, x, z):
+    size_x, size_y = row.shape[0], side.shape[1]
+    extra = spread(row[x, :, z], size_y)
+    if x < 4:
+        extra = extra + side[x, :, z]
+    if x >= size_x - 4:
+        extra = extra + side[x - (size_x - 8), :, z]
+    return extra
 
 
 def across(plane, x, z):
@@ -174,44 +188,53 @@
     xb[...] = field[pl.ds(jnp.where(even_x, 0, top), 4)]
 
 
+def source_of(cell, amp, step, size_x, size_y):
+    shape = (size_y, HALF)
+
+    def one(array, n):
+        return jnp.broadcast_to(array[0:1, n : n + 1], shape)
+
+    x = one(cell, 0) - lax.axis_index("gx") * size_x
+    y = one(cell, 1) - lax.axis_index("gy") * size_y
+    at_y = lax.broadcasted_iota(jnp.int32, shape, 0) == y
+    z = lax.broadcasted_iota(jnp.int32, shape, 1)
+    return x, [jnp.where(at_y & (z + h * HALF == one(cell, 2)), one(amp, step), 0.0) for h in range(2)]
+
+
 def index(shape, dim):
     return lax.broadcasted_iota(jnp.int32, shape, dim)
 
 
-def matrices_kernel(size_x, size_y, along_y, along_z, outer):
+def matrices_kernel(size_x, size_y, along_y, along_z):
     depth = along_z.shape[0]
-    half = size_x // 2
-    rows = half * size_y
+    rows = size_x // 2 * size_y
     along_z[...] = weight(index((depth, depth), 0) - index((depth, depth), 1)).astype(jnp.bfloat16)
     here, there = index((rows, rows), 0), index((rows, rows), 1)
     near = jnp.where(here // size_y == there // size_y, weight(here - there), 0.0)
     along_y[...] = near.astype(jnp.bfloat16)
-    here, there = index((rows, half * 8), 0), index((rows, half * 8), 1)
-    y, row = lax.rem(here, size_y), lax.rem(there, 4)
+
+
+def outer_matrices(size_x, size_y, outer):
+    half = size_x // 2
+    shape = (half * 8, half * 8)
+    here, there = index(shape, 0), index(shape, 1)
+    y, row = lax.rem(here, 8), lax.rem(there, 4)
+    y = jnp.where(y < 4, y, y + size_y - 8)
     below, above = weight(y - row + 4), weight(row + size_y - y)
     for field in range(2):
-        use = (here // size_y == there // 8) & (lax.rem(there, 8) // 4 == field)
+        use = (here // 8 == there // 8) & (lax.rem(there, 8) // 4 == field)
         both = jnp.concatenate([jnp.where(use, below, 0.0), jnp.where(use, above, 0.0)], axis=1)
         outer[field] = both.astype(jnp.bfloat16)
 
 
-def inject_kernel(size_x, size_y, cell, amp, cells, res, other, source0, source1, inject0, inject1):
+def inject_kernel(size_x, size_y, cells, res, other, inject0, inject1, outer):
+    outer_matrices(size_x, size_y, outer)
     depth = inject0.shape[2]
     half = size_x // 2
     rows = half * size_y
-    base_x, base_y = lax.axis_index("gx") * size_x, lax.axis_index("gy") * size_y
-    x, y = cell[0, 0] - base_x, cell[0, 1] - base_y
-    source0[...] = jnp.zeros_like(source0)
-    source1[...] = jnp.zeros_like(source1)
-
-    @pl.when((x >= 0) & (x < size_x) & (y >= 0) & (y < size_y))
-    def _():
-        at = (index((size_y, depth), 0) == y) & (index((size_y, depth), 1) == cell[0, 2])
-        source0[x] = jnp.where(at, amp[0, 0], 0.0)
-        source1[x] = jnp.where(at, amp[0, 1], 0.0)
-
     count = cells.shape[1]
-    x, y = cells[0:1, :] - base_x, cells[1:2, :] - base_y
+    x = cells[0:1, :] - lax.axis_index("gx") * size_x
+    y = cells[1:2, :] - lax.axis_index("gy") * size_y
     inside = (x >= 0) & (x < size_x) & (y >= 0) & (y < size_y)
     place = jnp.where(inside, x * size_y + y, -1)
     deep = index((depth, count), 0) == cells[2:3, :]
@@ -226,16 +249,17 @@
             out[part * half : (part + 1) * half] = done.reshape(half, size_y, depth)
 
 
-def first_inner_kernel(wave1, yb, ya, along_y, along_z, outer, lap1, flat):
+def first_inner_kernel(wave1, yb, ya, along_y, along_z, lap1, flat, outer, row):
     size_x, size_y = wave1.shape[0], wave1.shape[1]
+    outer_matrices(size_x, size_y, outer)
     flat_part(wave1, along_y, along_z, flat)
     half = size_x // 2
     for part in range(2):
-        x = slice(part * half, (part + 1) * half)
-        flat[x] = flat[x] + outer_part(ya, yb, 0, outer, part, size_y)
+        row[part * half : (part + 1) * half] = outer_part(ya, yb, 0, outer, part)
     for x in range(size_x):
         for z in halves():
-            lap1[x, :, z] = across(within(wave1), x, z) + flat[x, :, z] * (1.0 / SCALE)
+            lap = across(within(wave1), x, z) + flat[x, :, z] * (1.0 / SCALE)
+            lap1[x, :, z] = lap + spread(row[x, :, z], size_y)
 
 
 def first_kernel(inner, xb, xa, lap1, side):
@@ -246,7 +270,7 @@
 
 
 def second_kernel(
-    offsets, column, lap1, wave0, wave1, adj4, source, vel, wave2, image, ya, yb, xa, xb
+    offsets, column, lap1, wave0, wave1, adj4, cell, amp, vel, wave2, image, ya, yb, xa, xb
 ):
     size_x, size_y = wave1.shape[0], wave1.shape[1]
     start = offsets[0]
@@ -255,6 +279,8 @@
     back = lax.rem(HALF - shift_by, HALF)
     third = jnp.minimum(low + 2, 3)
 
+    plane, amounts = source_of(cell, amp, 0, size_x, size_y)
+
     def body(x, _):
         lane = lax.broadcasted_iota(jnp.int32, (size_y, HALF), 1)
         rolled = [pltpu.roll(column[i, x], back, 1) for i in (low, low + 1, third)]
@@ -262,7 +288,8 @@
             v = jnp.where(lane < HALF - shift_by, rolled[h], rolled[h + 1])
             vel[x, :, z] = v
             image[x, :, z] = v * adj4[x, :, z]
-            wave2[x, :, z] = 2.0 * wave1[x, :, z] - wave0[x, :, z] + v * lap1[x, :, z] + source[x, :, z]
+            wave = 2.0 * wave1[x, :, z] - wave0[x, :, z] + v * lap1[x, :, z]
+            wave2[x, :, z] = wave + jnp.where(plane == x, amounts[h], 0.0)
         return 0
 
     lax.fori_loop(0, size_x, body, 0, unroll=4)
@@ -271,37 +298,36 @@
 
 
 def third_inner_kernel(
-    wave1, wave2, adj4, adj5, vel, image, source, inject, along_y, along_z,
+    wave1, wave2, adj4, adj5, vel, image, cell, amp, inject, along_y, along_z,
     lap2, wave3, adj3, flat, flat2,
 ):
     flat_part(wave2, along_y, along_z, flat)
     flat_part(image, along_y, along_z, flat2)
+    plane, amounts = source_of(cell, amp, 1, wave1.shape[0], wave1.shape[1])
     for x in range(wave1.shape[0]):
-        for z in halves():
+        for h, z in enumerate(halves()):
             lap = across(within(wave2), x, z) + flat[x, :, z] * (1.0 / SCALE)
             lap2[x, :, z] = lap
-            wave3[x, :, z] = 2.0 * wave2[x, :, z] - wave1[x, :, z] + vel[x, :, z] * lap + source[x, :, z]
+            wave = 2.0 * wave2[x, :, z] - wave1[x, :, z] + vel[x, :, z] * lap
+            wave3[x, :, z] = wave + jnp.where(plane == x, amounts[h], 0.0)
             adj = across(within(image), x, z) + flat2[x, :, z] * (1.0 / SCALE)
             adj3[x, :, z] = 2.0 * adj4[x, :, z] - adj5[x, :, z] + adj + inject[x, :, z]
 
 
 def third_kernel(
     yb, ya, xb, xa, lap2_in, wave3_in, adj3_in, vel, outer,
-    lap2, wave3, adj3, image3, pya, pyb, pxa, pxb, side, side2, extra, extra2,
+    lap2, wave3, adj3, image3, pya, pyb, pxa, pxb, side, side2, row, row2,
 ):
-    size_x, size_y = vel.shape[0], vel.shape[1]
-    outer_parts(ya, yb, xa, xb, outer, size_x, size_y, (side, side2), (extra, extra2))
-
-    def body(x, _):
-        v = vel[x]
-        lap2[x] = lap2_in[x] + extra[x]
-        wave3[x] = wave3_in[x] + v * extra[x]
-        adj = adj3_in[x] + extra2[x]
-        adj3[x] = adj
-        image3[x] = v * adj
-        return 0
-
-    lax.fori_loop(0, size_x, body, 0, unroll=4)
+    outer_parts(ya, yb, xa, xb, outer, (side, side2), (row, row2))
+    for x in range(vel.shape[0]):
+        for z in halves():
+            v = vel[x, :, z]
+            extra = outer_of(side, row, x, z)
+            lap2[x, :, z] = lap2_in[x, :, z] + extra
+            wave3[x, :, z] = wave3_in[x, :, z] + v * extra
+            adj = adj3_in[x, :, z] + outer_of(side2, row2, x, z)
+            adj3[x, :, z] = adj
+            image3[x, :, z] = v * adj
     put_edges(wave3, 0, pya, pyb, pxa, pxb, 0)
     put_edges(image3, 4, pya, pyb, pxa, pxb, 4)
 
@@ -324,10 +350,10 @@
 
 def fourth_kernel(
     offsets, yb, ya, xb, xa, grad_in, adj4, lap1, outer,
-    far, near_b, near_a, own, extra2, side, side2, extra,
+    far, near_b, near_a, own, extra2, side, side2, row, row2,
 ):
     size_x, size_y = adj4.shape[0], adj4.shape[1]
-    outer_parts(ya, yb, xa, xb, outer, size_x, size_y, (side, side2), (extra, extra2))
+    outer_parts(ya, yb, xa, xb, outer, (side, side2), (row, row2))
     start = offsets[0]
     low = start // HALF
     shift_by = lax.rem(start, HALF)
@@ -336,27 +362,29 @@
     turn = jnp.where(even("shot"), 1, 3)
     which = [(lax.rem(me + away, 4) - low, tile) for away, tile in ((2, far), (turn, near_a), (4 - turn, near_b), (0, own))]
 
-    def body(x, _):
-        lane = lax.broadcasted_iota(jnp.int32, (size_y, HALF), 1)
+    lane = lax.broadcasted_iota(jnp.int32, (size_y, HALF), 1)
+    high = lane >= shift_by
+    for x in range(size_x):
         rolled = []
         for z in halves():
-            grad = grad_in[x, :, z] + adj4[x, :, z] * extra[x, :, z] + lap1[x, :, z] * extra2[x, :, z]
+            more = outer_of(side2, row2, x, z)
+            extra2[x, :, z] = more
+            grad = grad_in[x, :, z] + adj4[x, :, z] * outer_of(side, row, x, z) + lap1[x, :, z] * more
             rolled.append(pltpu.roll(grad, shift_by, 1))
-        high = lane >= shift_by
         first = jnp.where(high, rolled[0], 0.0)
         second = jnp.where(high, rolled[1], rolled[0])
         third = jnp.where(high, 0.0, rolled[1])
         for n, tile in which:
             value = jnp.where(n == 0, first, jnp.where(n == 1, second, third))
             tile[x] = jnp.where((n >= 0) & (n <= 2), value, 0.0)
-        return 0
-
-    lax.fori_loop(0, size_x, body, 0, unroll=4)
-
-
-def last_kernel(own, far, b, a, adj2_in, extra, out, adj2):
+
+
+def adjoint_kernel(adj2_in, extra, adj2):
+    adj2[...] = adj2_in[...] + extra[...]
+
+
+def sum_kernel(own, far, b, a, out):
     out[...] = (own[...] + far[...]) + (a[...] + b[...])
-    adj2[...] = adj2_in[...] + extra[...]
 
 
 def local(model_vel2, offsets, wave_prev, wave_cur, adj_cur, adj_next, src_cell, src_amp, rec_cell, rec_res):
@@ -368,10 +396,8 @@
     whole = pltpu.VMEM((size_x, size_y, depth), F32)
     side = pltpu.VMEM((8, size_y, depth), F32)
     rows, bf16 = size_x // 2 * size_y, jnp.bfloat16
-    matrices = [
-        jax.ShapeDtypeStruct(dims, bf16)
-        for dims in ((rows, rows), (depth, depth), (2, rows, size_x // 2 * 16))
-    ]
+    outer_dims = (2, size_x // 2 * 8, size_x // 2 * 16)
+    rows8 = pltpu.VMEM((size_x, 8, depth), F32)
 
     copies = pl.pallas_call(
         copies_kernel,
@@ -386,30 +412,32 @@
         edges_kernel, (shaped(size_x // 2, 8, depth),) * 2 + (shaped(4, size_y, depth),) * 2, n_in=1, room=1
     )(wave1)
     halos = exchange(edges)
-    along_y, along_z, outer = call(
-        functools.partial(matrices_kernel, size_x, size_y), tuple(matrices), n_in=0, room=1
+    along_y, along_z = call(
+        functools.partial(matrices_kernel, size_x, size_y),
+        (jax.ShapeDtypeStruct((rows, rows), bf16), jax.ShapeDtypeStruct((depth, depth), bf16)), room=1,
     )()
     yb, ya, xb, xa = halos
-    lap1 = call(first_inner_kernel, block, (whole,), n_in=6, room=2, flops=0)(wave1, yb, ya, along_y, along_z, outer)
+    lap1 = call(first_inner_kernel, block, (whole, pltpu.VMEM(outer_dims, bf16), rows8), n_in=5, room=2)(
+        wave1, yb, ya, along_y, along_z
+    )
     lap1 = call(first_kernel, block, (side,), n_in=3, room=1, aliases={0: 0})(lap1, xb, xa)
-    source0, source1, inject0, inject1 = pl.pallas_call(
-        functools.partial(inject_kernel, size_x, size_y),
-        out_shape=(block,) * 4,
-        in_specs=[pl.BlockSpec(memory_space=pltpu.SMEM)] * 2 + [pl.BlockSpec(memory_space=pltpu.VMEM)] * 2
-        + [pl.BlockSpec(memory_space=pl.ANY)],
-        out_specs=(pl.BlockSpec(memory_space=pltpu.VMEM),) * 4,
-        compiler_params=pltpu.CompilerParams(vmem_limit_bytes=4 << 20),
-    )(src_cell, src_amp, jnp.transpose(rec_cell[0]), jnp.transpose(rec_res[0]), column)
     vel, wave2, image, *edges = call(
         second_kernel, (block,) * 3 + (edge_y,) * 2 + (edge_x,) * 2,
-        smem=1, n_in=6, room=4,
-    )(offsets, column, lap1, wave0, wave1, adj4, source0)
+        smem=1, n_in=7, room=4,
+    )(offsets, column, lap1, wave0, wave1, adj4, src_cell, src_amp)
+    inject0, inject1, outer = pl.pallas_call(
+        functools.partial(inject_kernel, size_x, size_y),
+        out_shape=(block, block, jax.ShapeDtypeStruct(outer_dims, bf16)),
+        in_specs=[pl.BlockSpec(memory_space=pltpu.VMEM)] * 2 + [pl.BlockSpec(memory_space=pl.ANY)],
+        out_specs=(pl.BlockSpec(memory_space=pltpu.VMEM),) * 3,
+        compiler_params=pltpu.CompilerParams(vmem_limit_bytes=4 << 20),
+    )(jnp.transpose(rec_cell[0]), jnp.transpose(rec_res[0]), vel)
     halos = exchange(edges)
-    inner = call(third_inner_kernel, (block,) * 3, (whole,) * 2, n_in=10, room=10)(
-        wave1, wave2, adj4, adj5, vel, image, source1, inject0, along_y, along_z
+    inner = call(third_inner_kernel, (block,) * 3, (whole,) * 2, n_in=11, room=10)(
+        wave1, wave2, adj4, adj5, vel, image, src_cell, src_amp, inject0, along_y, along_z
     )
     lap2, wave3, adj3, image3, *edges = call(
-        third_kernel, (block,) * 4 + (edge_y,) * 2 + (edge_x,) * 2, (side, side, whole, whole), n_in=9,
+        third_kernel, (block,) * 4 + (edge_y,) * 2 + (edge_x,) * 2, (side, side, rows8, rows8), n_in=9,
         room=10, aliases={4: 0, 5: 1, 6: 2},
     )(*halos, *inner, vel, outer)
     halos = exchange(edges)
@@ -417,10 +445,11 @@
         wave3, image3, adj3, adj4, lap1, lap2, inject1, along_y, along_z
     )
     far, near_b, near_a, own, extra = call(
-        fourth_kernel, (tile, tile, tile, tile, block), (side, side, whole), smem=1, n_in=8, room=10
+        fourth_kernel, (tile, tile, tile, tile, block), (side, side, rows8, rows8), smem=1, n_in=8, room=10
     )(offsets, *halos, inner_grad, adj4, lap1, outer)
     far, b, a = swap_across(far), swap_shot(near_b, 1), swap_shot(near_a, 0)
-    owned, adj2 = call(last_kernel, (tile, block), n_in=6)(own, far, b, a, inner_adj2, extra)
+    adj2 = call(adjoint_kernel, block, n_in=2)(inner_adj2, extra)
+    owned = call(sum_kernel, tile, n_in=4)(own, far, b, a)
     return owned, adj2[None]
 
 

time: 80.7 us -> 79.7 us (0.988)
    pallas_call x5 -> x6, Pallas kernels: 5 us -> 4.88 us  [the longest x1 1.62 us: local(): call(third_inner_kernel, (block,) * 3, (whole,) * 2, n_in=11, room=10)]
  transfers between devices with their start and end apart: 16 -> 16, of which waited for: 9 -> 8; matrix products, arithmetic and copies ran while one was open for 0% -> 0% of each run, Pallas kernels for 5% -> 7%
where the time goes in v7:
time: 79.7 us; the launch traced here: 79.1 us
  starting transfers between devices  56.2 us (71%)
  Pallas kernels  10.3 us (13%)
  waiting for transfers between devices  8.86 us (11%)
  local copies, waits for them, and re-layouts  2.04 us (3%)
  between operations  1.6 us (2%)
    ppermute x12, starting transfers between devices, swap(): return lax.ppermute(value, axis, pairs)  41.4 us
    ppermute x2, waiting for transfers between devices, swap_shot(): return lax.ppermute(value, 'shot', pairs)  6.03 us
    ppermute x1, starting transfers between devices, swap_across(): lax.ppermute(value, 'shot', [(i, (i + size // 2) % size) for i in range(s...  5.44 us
    ppermute x2, starting transfers between devices, swap_shot(): return lax.ppermute(value, 'shot', pairs)  5 us
    all_to_all x1, starting transfers between devices, local(): column = lax.all_to_all(copies, 'shot', 0, 0)  4.44 us
    ppermute x12, waiting for transfers between devices, swap(): return lax.ppermute(value, axis, pairs)  2.73 us
    unnamed x19, local copies, waits for them, and re-layouts  2.04 us
    pallas_call x1, Pallas kernels, local(): call(third_inner_kernel, (block,) * 3, (whole,) * 2, n_in=11, room=10)  1.62 us
  transfers between devices with their start and end apart: 16, of which 8 were waited for; matrix products, arithmetic and copies ran while one was open for 0% of the time, Pallas kernels for 7%

profile of v7, /device:TPU:24, one launch (start us, length us, event | category | flops | bytes accessed | tf_op | source)
XLA Modules:
  0.0 79.1 jit_solution(16929425416397747785)
XLA Ops:
  0.6 0.9 %copy-done.4 = f32[32,16,128]{2,1,0:T(8,128)S(1)} copy-done((f32[32,16,128]{2,1,0:T(8,128)S(1)}, f32[32,16,128]{2,1,0:T(8,128)}, u32[]{:S(2)}) %copy-start.4) | copy-done | bytes 262168
  1.6 1.0 %shard_map.113 = f32[4,32,16,128]{3,2,1,0:T(8,128)} custom-call(f32[32,16,128]{2,1,0:T(8,128)S(1)} %copy-done.4), custom_call_target="tpu_custom_call" | custom-call | tf_op jit(solution)/shard_map/pallas_call | solution.py:402
  2.6 4.4 %all-to-all-start = ((f32[4,32,16,128]{3,2,1,0:T(8,128)}), f32[4,32,16,128]{3,2,1,0:T(8,128)S(1)}, u32[]{:S(2)}, u32[]{:S(2)}) async-start(f32[4,32,16,128]{3,2,1,0:T(8,128)} %shard_map.113), calls=%async_computation | async-start | bytes 2097152 | tf_op jit(solution)/shard_map/all_to_all | solution.py:410
  7.1 12.1 %collective-permute-start = (f32[16,8,256]{2,1,0:T(8,128)S(1)}, f32[16,8,256]{2,1,0:T(8,128)S(1)}, u32[]{:S(2)}, u32[]{:S(2)}) collective-permute-start(f32[16,8,256]{2,1,0:T(8,128)S(1)} %get-tuple-element.36), channel_id=1, source_target_pairs={{1,2},{2,1},{3,4},{4,3},{5,6},{6,5},{7,8},{8,7},{9,10},{10,9},{11,... | collective-permute-start | bytes 393224 | tf_op jit(solution)/shard_map/ppermute | solution.py:21
  19.2 1.9 %collective-permute-start.1 = (f32[16,8,256]{2,1,0:T(8,128)S(1)}, f32[16,8,256]{2,1,0:T(8,128)S(1)}, u32[]{:S(2)}, u32[]{:S(2)}) collective-permute-start(f32[16,8,256]{2,1,0:T(8,128)S(1)} %get-tuple-element.37), channel_id=1, source_target_pairs={{0,1},{1,0},{2,3},{3,2},{4,5},{5,4},{6,7},{7,6},{8,9},{9,8},{10,11... | collective-permute-start | bytes 393224 | tf_op jit(solution)/shard_map/ppermute | solution.py:21
  21.1 1.9 %collective-permute-start.2 = (f32[4,16,256]{2,1,0:T(8,128)S(1)}, f32[4,16,256]{2,1,0:T(8,128)S(1)}, u32[]{:S(2)}, u32[]{:S(2)}) collective-permute-start(f32[4,16,256]{2,1,0:T(8,128)S(1)} %get-tuple-element.40), channel_id=1, source_target_pairs={{32,64},{64,32},{33,65},{65,33},{34,66},{66,34},{35,67},{67,35},{3... | collective-permute-start | bytes 196616 | tf_op jit(solution)/shard_map/ppermute | solution.py:21
  23.1 1.9 %collective-permute-start.3 = (f32[4,16,256]{2,1,0:T(8,128)S(1)}, f32[4,16,256]{2,1,0:T(8,128)S(1)}, u32[]{:S(2)}, u32[]{:S(2)}) collective-permute-start(f32[4,16,256]{2,1,0:T(8,128)S(1)} %get-tuple-element.41), channel_id=1, source_target_pairs={{0,32},{32,0},{64,96},{96,64},{1,33},{33,1},{65,97},{97,65},{2,34}... | collective-permute-start | bytes 196616 | tf_op jit(solution)/shard_map/ppermute | solution.py:21
  26.1 0.8 %shard_map.116.inner = f32[32,16,256]{2,1,0:T(8,128)S(1)} custom-call(f32[32,16,256]{2,1,0:T(8,128)S(1)} %bitcast.14, f32[16,8,256]{2,1,0:T(8,128)S(1)} %collective-permute-done.yb, f32[16,8,256]{2,1,0:T(8,128)S(1)} %collective-permute-done.1.ya, bf16[256,256]{1,0:T(8,128)(2,1)S(1)} %get-tuple-element.38.along_y, bf16[256,256]{1,0:T(8,128)(2,1)S(1)} %get-tuple-element.39.along_z), custom_call_target="tpu_custom_call" | custom-call | tf_op jit(solution)/shard_map/pallas_call | solution.py:420
  27.1 0.9 %copy-done.1 = f32[1,32,16,256]{3,2,1,0:T(8,128)S(1)} copy-done((f32[1,32,16,256]{3,2,1,0:T(8,128)S(1)}, f32[1,32,16,256]{3,2,1,0:T(8,128)}, u32[]{:S(2)}) %copy-start.1) | copy-done | bytes 524312
  28.1 1.0 %shard_map.118 = (f32[32,16,256]{2,1,0:T(8,128)S(1)}, f32[32,16,256]{2,1,0:T(8,128)S(1)}, f32[32,16,256]{2,1,0:T(8,128)S(1)}, f32[32,8,256]{2,1,0:T(8,128)S(1)},...) custom-call(s32[1]{0:T(128)S(6)} %copy.23.offsets, ...), custom_call_target="tpu_custom_call" | custom-call | tf_op jit(solution)/shard_map/pallas_call | solution.py:424
  29.2 6.9 %collective-permute-start.4 = (f32[32,8,256]{2,1,0:T(8,128)S(1)}, f32[32,8,256]{2,1,0:T(8,128)S(1)}, u32[]{:S(2)}, u32[]{:S(2)}) collective-permute-start(f32[32,8,256]{2,1,0:T(8,128)S(1)} %get-tuple-element.42), channel_id=1, source_target_pairs={{1,2},{2,1},{3,4},{4,3},{5,6},{6,5},{7,8},{8,7},{9,10},{10,9},{11,... | collective-permute-start | bytes 786440 | tf_op jit(solution)/shard_map/ppermute | solution.py:21
  36.0 1.9 %collective-permute-start.5 = (f32[32,8,256]{2,1,0:T(8,128)S(1)}, f32[32,8,256]{2,1,0:T(8,128)S(1)}, u32[]{:S(2)}, u32[]{:S(2)}) collective-permute-start(f32[32,8,256]{2,1,0:T(8,128)S(1)} %get-tuple-element.43), channel_id=1, source_target_pairs={{0,1},{1,0},{2,3},{3,2},{4,5},{5,4},{6,7},{7,6},{8,9},{9,8},{10,11... | collective-permute-start | bytes 786440 | tf_op jit(solution)/shard_map/ppermute | solution.py:21
  38.0 1.9 %collective-permute-start.6 = (f32[8,16,256]{2,1,0:T(8,128)S(1)}, f32[8,16,256]{2,1,0:T(8,128)S(1)}, u32[]{:S(2)}, u32[]{:S(2)}) collective-permute-start(f32[8,16,256]{2,1,0:T(8,128)S(1)} %get-tuple-element.44), channel_id=1, source_target_pairs={{32,64},{64,32},{33,65},{65,33},{34,66},{66,34},{35,67},{67,35},{3... | collective-permute-start | bytes 393224 | tf_op jit(solution)/shard_map/ppermute | solution.py:21
  39.9 1.9 %collective-permute-start.7 = (f32[8,16,256]{2,1,0:T(8,128)S(1)}, f32[8,16,256]{2,1,0:T(8,128)S(1)}, u32[]{:S(2)}, u32[]{:S(2)}) collective-permute-start(f32[8,16,256]{2,1,0:T(8,128)S(1)} %get-tuple-element.45), channel_id=1, source_target_pairs={{0,32},{32,0},{64,96},{96,64},{1,33},{33,1},{65,97},{97,65},{2,34}... | collective-permute-start | bytes 393224 | tf_op jit(solution)/shard_map/ppermute | solution.py:21
  41.9 0.7 shard_map.119
  42.6 1.6 %shard_map.120 = (f32[32,16,256]{2,1,0:T(8,128)S(1)}, f32[32,16,256]{2,1,0:T(8,128)S(1)}, f32[32,16,256]{2,1,0:T(8,128)S(1)}) custom-call(f32[32,16,256]{2,1,0:T(8,128)S(1)} %bitcast.16, f32[32,16,256]{2,1,0:T(8,128)S(1)} %get-tuple-element.46.wave2, f32[32,16,256]{2,1,0:T(8,128)S(1)} %bitcast.18, f32[32,16,256]{2,1,0:T(8,128)S(1)} %bitcast.22, ...), custom_call_target="tpu_custom_call" | custom-call | tf_op jit(solution)/shard_map/pallas_call | solution.py:436
  44.5 1.0 %shard_map.121 = (f32[32,16,256]{2,1,0:T(8,128)S(1)}, f32[32,16,256]{2,1,0:T(8,128)S(1)}, f32[32,16,256]{2,1,0:T(8,128)S(1)}, f32[32,16,256]{2,1,0:T(8,128)S(1)}...) custom-call(f32[32,8,256]{2,1,0:T(8,128)S(1)} %collective-permute-do, ...), custom_call_target="tpu_custom_call", output_to_operand_aliasing={{0}: (4, {}), {1}: (5, {}), {2}: (6, {})} | custom-call | tf_op jit(solution)/shard_map/pallas_call | solution.py:439
  45.6 4.3 %collective-permute-start.8 = (f32[32,8,256]{2,1,0:T(8,128)S(1)}, f32[32,8,256]{2,1,0:T(8,128)S(1)}, u32[]{:S(2)}, u32[]{:S(2)}) collective-permute-start(f32[32,8,256]{2,1,0:T(8,128)S(1)} %get-tuple-element.54), channel_id=1, source_target_pairs={{1,2},{2,1},{3,4},{4,3},{5,6},{6,5},{7,8},{8,7},{9,10},{10,9},{11,... | collective-permute-start | bytes 786440 | tf_op jit(solution)/shard_map/ppermute | solution.py:21
  49.8 1.9 %collective-permute-start.9 = (f32[32,8,256]{2,1,0:T(8,128)S(1)}, f32[32,8,256]{2,1,0:T(8,128)S(1)}, u32[]{:S(2)}, u32[]{:S(2)}) collective-permute-start(f32[32,8,256]{2,1,0:T(8,128)S(1)} %get-tuple-element.55), channel_id=1, source_target_pairs={{0,1},{1,0},{2,3},{3,2},{4,5},{5,4},{6,7},{7,6},{8,9},{9,8},{10,11... | collective-permute-start | bytes 786440 | tf_op jit(solution)/shard_map/ppermute | solution.py:21
  51.8 2.8 %collective-permute-start.10 = (f32[8,16,256]{2,1,0:T(8,128)S(1)}, f32[8,16,256]{2,1,0:T(8,128)S(1)}, u32[]{:S(2)}, u32[]{:S(2)}) collective-permute-start(f32[8,16,256]{2,1,0:T(8,128)S(1)} %get-tuple-element.56), channel_id=1, source_target_pairs={{32,64},{64,32},{33,65},{65,33},{34,66},{66,34},{35,67},{67,35},{3... | collective-permute-start | bytes 393224 | tf_op jit(solution)/shard_map/ppermute | solution.py:21
  54.6 1.9 %collective-permute-start.11 = (f32[8,16,256]{2,1,0:T(8,128)S(1)}, f32[8,16,256]{2,1,0:T(8,128)S(1)}, u32[]{:S(2)}, u32[]{:S(2)}) collective-permute-start(f32[8,16,256]{2,1,0:T(8,128)S(1)} %get-tuple-element.57), channel_id=1, source_target_pairs={{0,32},{32,0},{64,96},{96,64},{1,33},{33,1},{65,97},{97,65},{2,34}... | collective-permute-start | bytes 393224 | tf_op jit(solution)/shard_map/ppermute | solution.py:21
  56.5 1.5 %shard_map.122 = (f32[32,16,256]{2,1,0:T(8,128)S(1)}, f32[32,16,256]{2,1,0:T(8,128)S(1)}) custom-call(f32[32,16,256]{2,1,0:T(8,128)S(1)} %get-tuple-element.58.wave3, f32[32,16,256]{2,1,0:T(8,128)S(1)} %get-tuple-element.59.image3, f32[32,16,256]{2,1,0:T(8,128)S(1)} %get-tuple-element.60.adj3, f32[32,16,256]{2,1,0:T(8,128)S(1)} %bitcast.19, ...), custom_call_target="tpu_custom_call" | custom-call | tf_op jit(solution)/shard_map/pallas_call | solution.py:444
  58.1 1.6 %collective-permute-done.8.yb = f32[32,8,256]{2,1,0:T(8,128)S(1)} collective-permute-done((f32[32,8,256]{2,1,0:T(8,128)S(1)}, f32[32,8,256]{2,1,0:T(8,128)S(1)}, u32[]{:S(2)}, u32[]{:S(2)}) %collective-permute-start.8) | collective-permute-done | bytes 262176 | tf_op jit(solution)/shard_map/ppermute | solution.py:21
  59.7 0.5 collective-permute-done.9.ya
  60.1 0.7 shard_map.123
  60.9 5.4 %collective-permute-start.12 = (f32[32,16,128]{2,1,0:T(8,128)S(1)}, f32[32,16,128]{2,1,0:T(8,128)S(1)}, u32[]{:S(2)}, u32[]{:S(2)}) collective-permute-start(f32[32,16,128]{2,1,0:T(8,128)S(1)} %get-tuple-element.65), channel_id=1, source_target_pairs={{0,256},{128,384},{256,0},{384,128},{1,257},{129,385},{257,1},{385... | collective-permute-start | bytes 786440 | tf_op jit(solution)/shard_map/ppermute | solution.py:34
  66.3 3.1 %collective-permute-start.13 = (f32[32,16,128]{2,1,0:T(8,128)S(1)}, f32[32,16,128]{2,1,0:T(8,128)S(1)}, u32[]{:S(2)}, u32[]{:S(2)}) collective-permute-start(f32[32,16,128]{2,1,0:T(8,128)S(1)} %get-tuple-element.66), channel_id=1, source_target_pairs={{128,256},{256,128},{384,0},{0,384},{129,257},{257,129},{385,1},{1... | collective-permute-start | bytes 786440 | tf_op jit(solution)/shard_map/ppermute | solution.py:29
  69.4 1.9 %collective-permute-start.14 = (f32[32,16,128]{2,1,0:T(8,128)S(1)}, f32[32,16,128]{2,1,0:T(8,128)S(1)}, u32[]{:S(2)}, u32[]{:S(2)}) collective-permute-start(f32[32,16,128]{2,1,0:T(8,128)S(1)} %get-tuple-element.67), channel_id=1, source_target_pairs={{0,128},{128,0},{256,384},{384,256},{1,129},{129,1},{257,385},{385... | collective-permute-start | bytes 786440 | tf_op jit(solution)/shard_map/ppermute | solution.py:29
  71.3 0.8 %shard_map.125 = f32[32,16,256]{2,1,0:T(8,128)} custom-call(f32[32,16,256]{2,1,0:T(8,128)S(1)} %get-tuple-element.68.adj2_in, f32[32,16,256]{2,1,0:T(8,128)S(1)} %get-tuple-element.69.extra), custom_call_target="tpu_custom_call" | custom-call | tf_op jit(solution)/shard_map/pallas_call | solution.py:451
  72.3 5.5 %collective-permute-done.13.b = f32[32,16,128]{2,1,0:T(8,128)S(1)} collective-permute-done((f32[32,16,128]{2,1,0:T(8,128)S(1)}, f32[32,16,128]{2,1,0:T(8,128)S(1)}, u32[]{:S(2)}, u32[]{:S(2)}) %collective-permute-start.13) | collective-permute-done | bytes 262176 | tf_op jit(solution)/shard_map/ppermute | solution.py:29
  77.7 0.6 collective-permute-done.14.a
  78.3 0.8 shard_map.124
  (32 shorter events, 1.2 us)
Async XLA Ops:
  0.6 1.0 %copy-start.4 = (f32[32,16,128]{2,1,0:T(8,128)S(1)}, f32[32,16,128]{2,1,0:T(8,128)}, u32[]{:S(2)}) copy-start(f32[32,16,128]{2,1,0:T(8,128)} %tile.1) | copy-start | bytes 786436
  2.6 4.5 %copy-start = (f32[1,32,16,256]{3,2,1,0:T(8,128)S(1)}, f32[1,32,16,256]{3,2,1,0:T(8,128)}, u32[]{:S(2)}) copy-start(f32[1,32,16,256]{3,2,1,0:T(8,128)} %param.13) | copy-start | bytes 1572868
  2.6 24.4 %all-to-all-start = ((f32[4,32,16,128]{3,2,1,0:T(8,128)}), f32[4,32,16,128]{3,2,1,0:T(8,128)S(1)}, u32[]{:S(2)}, u32[]{:S(2)}) async-start(f32[4,32,16,128]{3,2,1,0:T(8,128)} %shard_map.113), calls=%async_computation | async-start | bytes 2097152 | tf_op jit(solution)/shard_map/all_to_all | solution.py:410
  7.1 18.6 %collective-permute-start = (f32[16,8,256]{2,1,0:T(8,128)S(1)}, f32[16,8,256]{2,1,0:T(8,128)S(1)}, u32[]{:S(2)}, u32[]{:S(2)}) collective-permute-start(f32[16,8,256]{2,1,0:T(8,128)S(1)} %get-tuple-element.36), channel_id=1, source_target_pairs={{1,2},{2,1},{3,4},{4,3},{5,6},{6,5},{7,8},{8,7},{9,10},{10,9},{11,... | collective-permute-start | bytes 393224 | tf_op jit(solution)/shard_map/ppermute | solution.py:21
  19.2 6.9 %collective-permute-start.1 = (f32[16,8,256]{2,1,0:T(8,128)S(1)}, f32[16,8,256]{2,1,0:T(8,128)S(1)}, u32[]{:S(2)}, u32[]{:S(2)}) collective-permute-start(f32[16,8,256]{2,1,0:T(8,128)S(1)} %get-tuple-element.37), channel_id=1, source_target_pairs={{0,1},{1,0},{2,3},{3,2},{4,5},{5,4},{6,7},{7,6},{8,9},{9,8},{10,11... | collective-permute-start | bytes 393224 | tf_op jit(solution)/shard_map/ppermute | solution.py:21
  21.1 5.8 %collective-permute-start.2 = (f32[4,16,256]{2,1,0:T(8,128)S(1)}, f32[4,16,256]{2,1,0:T(8,128)S(1)}, u32[]{:S(2)}, u32[]{:S(2)}) collective-permute-start(f32[4,16,256]{2,1,0:T(8,128)S(1)} %get-tuple-element.40), channel_id=1, source_target_pairs={{32,64},{64,32},{33,65},{65,33},{34,66},{66,34},{35,67},{67,35},{3... | collective-permute-start | bytes 196616 | tf_op jit(solution)/shard_map/ppermute | solution.py:21
  23.1 3.9 %collective-permute-start.3 = (f32[4,16,256]{2,1,0:T(8,128)S(1)}, f32[4,16,256]{2,1,0:T(8,128)S(1)}, u32[]{:S(2)}, u32[]{:S(2)}) collective-permute-start(f32[4,16,256]{2,1,0:T(8,128)S(1)} %get-tuple-element.41), channel_id=1, source_target_pairs={{0,32},{32,0},{64,96},{96,64},{1,33},{33,1},{65,97},{97,65},{2,34}... | collective-permute-start | bytes 196616 | tf_op jit(solution)/shard_map/ppermute | solution.py:21
  26.9 1.0 %copy-start.1 = (f32[1,32,16,256]{3,2,1,0:T(8,128)S(1)}, f32[1,32,16,256]{3,2,1,0:T(8,128)}, u32[]{:S(2)}) copy-start(f32[1,32,16,256]{3,2,1,0:T(8,128)} %param.14) | copy-start | bytes 1572868
  26.9 1.2 %copy-start.2 = (f32[1,32,16,256]{3,2,1,0:T(8,128)S(1)}, f32[1,32,16,256]{3,2,1,0:T(8,128)}, u32[]{:S(2)}) copy-start(f32[1,32,16,256]{3,2,1,0:T(8,128)} %param.12) | copy-start | bytes 1572868
  27.1 1.1 %copy-start.6 = (s32[1,3]{1,0:T(1,128)S(1)}, s32[1,3]{1,0:T(1,128)}, u32[]{:S(2)}) copy-start(s32[1,3]{1,0:T(1,128)} %cell.3) | copy-start | bytes 40
  27.1 1.1 %copy-start.7 = (f32[1,2]{1,0:T(1,128)S(1)}, f32[1,2]{1,0:T(1,128)}, u32[]{:S(2)}) copy-start(f32[1,2]{1,0:T(1,128)} %amp.3) | copy-start | bytes 28
  28.1 13.7 %copy-start.8 = (s32[1,256,3]{1,0,2:T(1,128)S(1)}, s32[1,256,3]{1,0,2:T(1,128)}, u32[]{:S(2)}) copy-start(s32[1,256,3]{1,0,2:T(1,128)} %param.18) | copy-start | bytes 9220
  28.1 13.7 %copy-start.5 = (f32[1,256,2]{1,2,0:T(2,128)S(1)}, f32[1,256,2]{1,2,0:T(2,128)}, u32[]{:S(2)}) copy-start(f32[1,256,2]{1,2,0:T(2,128)} %param.19) | copy-start | bytes 6148
  29.2 13.4 %copy-start.3 = (f32[1,32,16,256]{3,2,1,0:T(8,128)S(1)}, f32[1,32,16,256]{3,2,1,0:T(8,128)}, u32[]{:S(2)}) copy-start(f32[1,32,16,256]{3,2,1,0:T(8,128)} %param.15) | copy-start | bytes 1572868
  29.2 15.1 %collective-permute-start.4 = (f32[32,8,256]{2,1,0:T(8,128)S(1)}, f32[32,8,256]{2,1,0:T(8,128)S(1)}, u32[]{:S(2)}, u32[]{:S(2)}) collective-permute-start(f32[32,8,256]{2,1,0:T(8,128)S(1)} %get-tuple-element.42), channel_id=1, source_target_pairs={{1,2},{2,1},{3,4},{4,3},{5,6},{6,5},{7,8},{8,7},{9,10},{10,9},{11,... | collective-permute-start | bytes 786440 | tf_op jit(solution)/shard_map/ppermute | solution.py:21
  36.0 8.5 %collective-permute-start.5 = (f32[32,8,256]{2,1,0:T(8,128)S(1)}, f32[32,8,256]{2,1,0:T(8,128)S(1)}, u32[]{:S(2)}, u32[]{:S(2)}) collective-permute-start(f32[32,8,256]{2,1,0:T(8,128)S(1)} %get-tuple-element.43), channel_id=1, source_target_pairs={{0,1},{1,0},{2,3},{3,2},{4,5},{5,4},{6,7},{7,6},{8,9},{9,8},{10,11... | collective-permute-start | bytes 786440 | tf_op jit(solution)/shard_map/ppermute | solution.py:21
  38.0 6.3 %collective-permute-start.6 = (f32[8,16,256]{2,1,0:T(8,128)S(1)}, f32[8,16,256]{2,1,0:T(8,128)S(1)}, u32[]{:S(2)}, u32[]{:S(2)}) collective-permute-start(f32[8,16,256]{2,1,0:T(8,128)S(1)} %get-tuple-element.44), channel_id=1, source_target_pairs={{32,64},{64,32},{33,65},{65,33},{34,66},{66,34},{35,67},{67,35},{3... | collective-permute-start | bytes 393224 | tf_op jit(solution)/shard_map/ppermute | solution.py:21
  39.9 4.4 %collective-permute-start.7 = (f32[8,16,256]{2,1,0:T(8,128)S(1)}, f32[8,16,256]{2,1,0:T(8,128)S(1)}, u32[]{:S(2)}, u32[]{:S(2)}) collective-permute-start(f32[8,16,256]{2,1,0:T(8,128)S(1)} %get-tuple-element.45), channel_id=1, source_target_pairs={{0,32},{32,0},{64,96},{96,64},{1,33},{33,1},{65,97},{97,65},{2,34}... | collective-permute-start | bytes 393224 | tf_op jit(solution)/shard_map/ppermute | solution.py:21
  45.6 14.1 %collective-permute-start.8 = (f32[32,8,256]{2,1,0:T(8,128)S(1)}, f32[32,8,256]{2,1,0:T(8,128)S(1)}, u32[]{:S(2)}, u32[]{:S(2)}) collective-permute-start(f32[32,8,256]{2,1,0:T(8,128)S(1)} %get-tuple-element.54), channel_id=1, source_target_pairs={{1,2},{2,1},{3,4},{4,3},{5,6},{6,5},{7,8},{8,7},{9,10},{10,9},{11,... | collective-permute-start | bytes 786440 | tf_op jit(solution)/shard_map/ppermute | solution.py:21
  49.8 10.3 %collective-permute-start.9 = (f32[32,8,256]{2,1,0:T(8,128)S(1)}, f32[32,8,256]{2,1,0:T(8,128)S(1)}, u32[]{:S(2)}, u32[]{:S(2)}) collective-permute-start(f32[32,8,256]{2,1,0:T(8,128)S(1)} %get-tuple-element.55), channel_id=1, source_target_pairs={{0,1},{1,0},{2,3},{3,2},{4,5},{5,4},{6,7},{7,6},{8,9},{9,8},{10,11... | collective-permute-start | bytes 786440 | tf_op jit(solution)/shard_map/ppermute | solution.py:21
  51.8 6.3 %collective-permute-start.10 = (f32[8,16,256]{2,1,0:T(8,128)S(1)}, f32[8,16,256]{2,1,0:T(8,128)S(1)}, u32[]{:S(2)}, u32[]{:S(2)}) collective-permute-start(f32[8,16,256]{2,1,0:T(8,128)S(1)} %get-tuple-element.56), channel_id=1, source_target_pairs={{32,64},{64,32},{33,65},{65,33},{34,66},{66,34},{35,67},{67,35},{3... | collective-permute-start | bytes 393224 | tf_op jit(solution)/shard_map/ppermute | solution.py:21
  54.6 3.5 %collective-permute-start.11 = (f32[8,16,256]{2,1,0:T(8,128)S(1)}, f32[8,16,256]{2,1,0:T(8,128)S(1)}, u32[]{:S(2)}, u32[]{:S(2)}) collective-permute-start(f32[8,16,256]{2,1,0:T(8,128)S(1)} %get-tuple-element.57), channel_id=1, source_target_pairs={{0,32},{32,0},{64,96},{96,64},{1,33},{33,1},{65,97},{97,65},{2,34}... | collective-permute-start | bytes 393224 | tf_op jit(solution)/shard_map/ppermute | solution.py:21
  60.9 11.4 %collective-permute-start.12 = (f32[32,16,128]{2,1,0:T(8,128)S(1)}, f32[32,16,128]{2,1,0:T(8,128)S(1)}, u32[]{:S(2)}, u32[]{:S(2)}) collective-permute-start(f32[32,16,128]{2,1,0:T(8,128)S(1)} %get-tuple-element.65), channel_id=1, source_target_pairs={{0,256},{128,384},{256,0},{384,128},{1,257},{129,385},{257,1},{385... | collective-permute-start | bytes 786440 | tf_op jit(solution)/shard_map/ppermute | solution.py:34
  66.3 11.4 %collective-permute-start.13 = (f32[32,16,128]{2,1,0:T(8,128)S(1)}, f32[32,16,128]{2,1,0:T(8,128)S(1)}, u32[]{:S(2)}, u32[]{:S(2)}) collective-permute-start(f32[32,16,128]{2,1,0:T(8,128)S(1)} %get-tuple-element.66), channel_id=1, source_target_pairs={{128,256},{256,128},{384,0},{0,384},{129,257},{257,129},{385,1},{1... | collective-permute-start | bytes 786440 | tf_op jit(solution)/shard_map/ppermute | solution.py:29
  69.4 8.9 %collective-permute-start.14 = (f32[32,16,128]{2,1,0:T(8,128)S(1)}, f32[32,16,128]{2,1,0:T(8,128)S(1)}, u32[]{:S(2)}, u32[]{:S(2)}) collective-permute-start(f32[32,16,128]{2,1,0:T(8,128)S(1)} %get-tuple-element.67), channel_id=1, source_target_pairs={{0,128},{128,0},{256,384},{384,256},{1,129},{129,1},{257,385},{385... | collective-permute-start | bytes 786440 | tf_op jit(solution)/shard_map/ppermute | solution.py:29

commit v8 on v7

--- a/solution.py
+++ b/solution.py
@@ -147,8 +147,16 @@
 
 
 def within(field):
-    size_x = field.shape[0]
-    return lambda x, z: field[x, :, z] if 0 <= x < size_x else None
+    size_x, held = field.shape[0], {}
+
+    def plane(x, z):
+        if not 0 <= x < size_x:
+            return None
+        if (x, z.start) not in held:
+            held[x, z.start] = field[x, :, z]
+        return held[x, z.start]
+
+    return plane
 
 
 def halves():
@@ -205,11 +213,10 @@
     return lax.broadcasted_iota(jnp.int32, shape, dim)
 
 
-def matrices_kernel(size_x, size_y, along_y, along_z):
-    depth = along_z.shape[0]
-    rows = size_x // 2 * size_y
-    along_z[...] = weight(index((depth, depth), 0) - index((depth, depth), 1)).astype(jnp.bfloat16)
-    here, there = index((rows, rows), 0), index((rows, rows), 1)
+def difference_matrices(size_y, along_y, along_z):
+    shape = along_z.shape
+    along_z[...] = weight(index(shape, 0) - index(shape, 1)).astype(jnp.bfloat16)
+    here, there = index(along_y.shape, 0), index(along_y.shape, 1)
     near = jnp.where(here // size_y == there // size_y, weight(here - there), 0.0)
     along_y[...] = near.astype(jnp.bfloat16)
 
@@ -227,7 +234,8 @@
         outer[field] = both.astype(jnp.bfloat16)
 
 
-def inject_kernel(size_x, size_y, cells, res, other, inject0, inject1, outer):
+def tables_kernel(size_x, size_y, cells, res, other, inject0, inject1, along_y, along_z, outer):
+    difference_matrices(size_y, along_y, along_z)
     outer_matrices(size_x, size_y, outer)
     depth = inject0.shape[2]
     half = size_x // 2
@@ -249,16 +257,18 @@
             out[part * half : (part + 1) * half] = done.reshape(half, size_y, depth)
 
 
-def first_inner_kernel(wave1, yb, ya, along_y, along_z, lap1, flat, outer, row):
+def first_inner_kernel(wave1, yb, ya, next0, next1, cell, amp, lap1, flat, along_y, along_z, outer, row):
     size_x, size_y = wave1.shape[0], wave1.shape[1]
+    difference_matrices(size_y, along_y, along_z)
     outer_matrices(size_x, size_y, outer)
     flat_part(wave1, along_y, along_z, flat)
     half = size_x // 2
     for part in range(2):
         row[part * half : (part + 1) * half] = outer_part(ya, yb, 0, outer, part)
-    for x in range(size_x):
-        for z in halves():
-            lap = across(within(wave1), x, z) + flat[x, :, z] * (1.0 / SCALE)
+    planes = within(wave1)
+    for z in halves():
+        for x in range(size_x):
+            lap = across(planes, x, z) + flat[x, :, z] * (1.0 / SCALE)
             lap1[x, :, z] = lap + spread(row[x, :, z], size_y)
 
 
@@ -304,13 +314,14 @@
     flat_part(wave2, along_y, along_z, flat)
     flat_part(image, along_y, along_z, flat2)
     plane, amounts = source_of(cell, amp, 1, wave1.shape[0], wave1.shape[1])
-    for x in range(wave1.shape[0]):
-        for h, z in enumerate(halves()):
-            lap = across(within(wave2), x, z) + flat[x, :, z] * (1.0 / SCALE)
+    waves, images = within(wave2), within(image)
+    for h, z in enumerate(halves()):
+        for x in range(wave1.shape[0]):
+            lap = across(waves, x, z) + flat[x, :, z] * (1.0 / SCALE)
             lap2[x, :, z] = lap
-            wave = 2.0 * wave2[x, :, z] - wave1[x, :, z] + vel[x, :, z] * lap
+            wave = 2.0 * waves(x, z) - wave1[x, :, z] + vel[x, :, z] * lap
             wave3[x, :, z] = wave + jnp.where(plane == x, amounts[h], 0.0)
-            adj = across(within(image), x, z) + flat2[x, :, z] * (1.0 / SCALE)
+            adj = across(images, x, z) + flat2[x, :, z] * (1.0 / SCALE)
             adj3[x, :, z] = 2.0 * adj4[x, :, z] - adj5[x, :, z] + adj + inject[x, :, z]
 
 
@@ -338,10 +349,11 @@
 ):
     flat_part(wave3, along_y, along_z, flat)
     flat_part(image3, along_y, along_z, flat2)
-    for x in range(wave3.shape[0]):
-        for z in halves():
-            lap3 = across(within(wave3), x, z) + flat[x, :, z] * (1.0 / SCALE)
-            adj = across(within(image3), x, z) + flat2[x, :, z] * (1.0 / SCALE)
+    waves, images = within(wave3), within(image3)
+    for z in halves():
+        for x in range(wave3.shape[0]):
+            lap3 = across(waves, x, z) + flat[x, :, z] * (1.0 / SCALE)
+            adj = across(images, x, z) + flat2[x, :, z] * (1.0 / SCALE)
             old, mid = adj4[x, :, z], adj3[x, :, z]
             adj = 2.0 * mid - old + adj + inject[x, :, z]
             adj2[x, :, z] = adj
@@ -396,7 +408,6 @@
     whole = pltpu.VMEM((size_x, size_y, depth), F32)
     side = pltpu.VMEM((8, size_y, depth), F32)
     rows, bf16 = size_x // 2 * size_y, jnp.bfloat16
-    outer_dims = (2, size_x // 2 * 8, size_x // 2 * 16)
     rows8 = pltpu.VMEM((size_x, 8, depth), F32)
 
     copies = pl.pallas_call(
@@ -412,24 +423,22 @@
         edges_kernel, (shaped(size_x // 2, 8, depth),) * 2 + (shaped(4, size_y, depth),) * 2, n_in=1, room=1
     )(wave1)
     halos = exchange(edges)
-    along_y, along_z = call(
-        functools.partial(matrices_kernel, size_x, size_y),
-        (jax.ShapeDtypeStruct((rows, rows), bf16), jax.ShapeDtypeStruct((depth, depth), bf16)), room=1,
-    )()
     yb, ya, xb, xa = halos
-    lap1 = call(first_inner_kernel, block, (whole, pltpu.VMEM(outer_dims, bf16), rows8), n_in=5, room=2)(
-        wave1, yb, ya, along_y, along_z
+    matrices = ((rows, rows), (depth, depth), (2, size_x // 2 * 8, size_x // 2 * 16))
+    own = tuple(pltpu.VMEM(dims, bf16) for dims in matrices)
+    lap1 = call(first_inner_kernel, block, (whole, *own, rows8), n_in=7, room=2)(
+        wave1, yb, ya, wave0, adj4, src_cell, src_amp
     )
     lap1 = call(first_kernel, block, (side,), n_in=3, room=1, aliases={0: 0})(lap1, xb, xa)
     vel, wave2, image, *edges = call(
         second_kernel, (block,) * 3 + (edge_y,) * 2 + (edge_x,) * 2,
         smem=1, n_in=7, room=4,
     )(offsets, column, lap1, wave0, wave1, adj4, src_cell, src_amp)
-    inject0, inject1, outer = pl.pallas_call(
-        functools.partial(inject_kernel, size_x, size_y),
-        out_shape=(block, block, jax.ShapeDtypeStruct(outer_dims, bf16)),
+    inject0, inject1, along_y, along_z, outer = pl.pallas_call(
+        functools.partial(tables_kernel, size_x, size_y),
+        out_shape=(block, block, *(jax.ShapeDtypeStruct(dims, bf16) for dims in matrices)),
         in_specs=[pl.BlockSpec(memory_space=pltpu.VMEM)] * 2 + [pl.BlockSpec(memory_space=pl.ANY)],
-        out_specs=(pl.BlockSpec(memory_space=pltpu.VMEM),) * 3,
+        out_specs=(pl.BlockSpec(memory_space=pltpu.VMEM),) * 5,
         compiler_params=pltpu.CompilerParams(vmem_limit_bytes=4 << 20),
     )(jnp.transpose(rec_cell[0]), jnp.transpose(rec_res[0]), vel)
     halos = exchange(edges)

time: 79.7 us -> 79.5 us (level)
    pallas_call x3 -> x2, Pallas kernels: 1.66 us -> 1.67 us  [the longest x1 0.85 us: local(): call(first_inner_kernel, block, (whole, *own, rows8), n_in=7, room=2)]
where the time goes in v8:
time: 79.5 us; the launch traced here: 78.8 us
  starting transfers between devices  56.1 us (71%)
  Pallas kernels  10.4 us (13%)
  waiting for transfers between devices  9.09 us (11%)
  local copies, waits for them, and re-layouts  1.64 us (2%)
  between operations  1.61 us (2%)
    ppermute x12, starting transfers between devices, swap(): return lax.ppermute(value, axis, pairs)  41.2 us
    ppermute x2, waiting for transfers between devices, swap_shot(): return lax.ppermute(value, 'shot', pairs)  5.99 us
    ppermute x1, starting transfers between devices, swap_across(): lax.ppermute(value, 'shot', [(i, (i + size // 2) % size) for i in range(s...  5.43 us
    ppermute x2, starting transfers between devices, swap_shot(): return lax.ppermute(value, 'shot', pairs)  5 us
    all_to_all x1, starting transfers between devices, local(): column = lax.all_to_all(copies, 'shot', 0, 0)  4.44 us
    ppermute x12, waiting for transfers between devices, swap(): return lax.ppermute(value, axis, pairs)  2.93 us
    unnamed x19, local copies, waits for them, and re-layouts  1.64 us
    pallas_call x1, Pallas kernels, local(): call(third_inner_kernel, (block,) * 3, (whole,) * 2, n_in=11, room=10)  1.64 us
  transfers between devices with their start and end apart: 16, of which 8 were waited for; matrix products, arithmetic and copies ran while one was open for 0% of the time, Pallas kernels for 7%

profile of v8, /device:TPU:24, one launch (start us, length us, event | category | flops | bytes accessed | tf_op | source)
XLA Modules:
  0.0 78.8 jit_solution(9263883611807210557)
XLA Ops:
  0.6 0.9 %copy-done.4 = f32[32,16,128]{2,1,0:T(8,128)S(1)} copy-done((f32[32,16,128]{2,1,0:T(8,128)S(1)}, f32[32,16,128]{2,1,0:T(8,128)}, u32[]{:S(2)}) %copy-start.4) | copy-done | bytes 262168
  1.6 1.0 %shard_map.113 = f32[4,32,16,128]{3,2,1,0:T(8,128)} custom-call(f32[32,16,128]{2,1,0:T(8,128)S(1)} %copy-done.4), custom_call_target="tpu_custom_call" | custom-call | tf_op jit(solution)/shard_map/pallas_call | solution.py:413
  2.6 4.4 %all-to-all-start = ((f32[4,32,16,128]{3,2,1,0:T(8,128)}), f32[4,32,16,128]{3,2,1,0:T(8,128)S(1)}, u32[]{:S(2)}, u32[]{:S(2)}) async-start(f32[4,32,16,128]{3,2,1,0:T(8,128)} %shard_map.113), calls=%async_computation | async-start | bytes 2097152 | tf_op jit(solution)/shard_map/all_to_all | solution.py:421
  7.1 12.2 %collective-permute-start = (f32[16,8,256]{2,1,0:T(8,128)S(1)}, f32[16,8,256]{2,1,0:T(8,128)S(1)}, u32[]{:S(2)}, u32[]{:S(2)}) collective-permute-start(f32[16,8,256]{2,1,0:T(8,128)S(1)} %get-tuple-element.36), channel_id=1, source_target_pairs={{1,2},{2,1},{3,4},{4,3},{5,6},{6,5},{7,8},{8,7},{9,10},{10,9},{11,... | collective-permute-start | bytes 393224 | tf_op jit(solution)/shard_map/ppermute | solution.py:21
  19.4 1.9 %collective-permute-start.1 = (f32[16,8,256]{2,1,0:T(8,128)S(1)}, f32[16,8,256]{2,1,0:T(8,128)S(1)}, u32[]{:S(2)}, u32[]{:S(2)}) collective-permute-start(f32[16,8,256]{2,1,0:T(8,128)S(1)} %get-tuple-element.37), channel_id=1, source_target_pairs={{0,1},{1,0},{2,3},{3,2},{4,5},{5,4},{6,7},{7,6},{8,9},{9,8},{10,11... | collective-permute-start | bytes 393224 | tf_op jit(solution)/shard_map/ppermute | solution.py:21
  21.3 1.9 %collective-permute-start.2 = (f32[4,16,256]{2,1,0:T(8,128)S(1)}, f32[4,16,256]{2,1,0:T(8,128)S(1)}, u32[]{:S(2)}, u32[]{:S(2)}) collective-permute-start(f32[4,16,256]{2,1,0:T(8,128)S(1)} %get-tuple-element.38), channel_id=1, source_target_pairs={{32,64},{64,32},{33,65},{65,33},{34,66},{66,34},{35,67},{67,35},{3... | collective-permute-start | bytes 196616 | tf_op jit(solution)/shard_map/ppermute | solution.py:21
  23.2 1.9 %collective-permute-start.3 = (f32[4,16,256]{2,1,0:T(8,128)S(1)}, f32[4,16,256]{2,1,0:T(8,128)S(1)}, u32[]{:S(2)}, u32[]{:S(2)}) collective-permute-start(f32[4,16,256]{2,1,0:T(8,128)S(1)} %get-tuple-element.39), channel_id=1, source_target_pairs={{0,32},{32,0},{64,96},{96,64},{1,33},{33,1},{65,97},{97,65},{2,34}... | collective-permute-start | bytes 196616 | tf_op jit(solution)/shard_map/ppermute | solution.py:21
  26.2 0.6 copy-done.5
  26.9 0.8 %shard_map.115.inner = f32[32,16,256]{2,1,0:T(8,128)S(1)} custom-call(f32[32,16,256]{2,1,0:T(8,128)S(1)} %bitcast.19, f32[16,8,256]{2,1,0:T(8,128)S(1)} %collective-permute-done.yb, f32[16,8,256]{2,1,0:T(8,128)S(1)} %collective-permute-done.1.ya, f32[32,16,256]{2,1,0:T(8,128)S(1)} %bitcast.22, f32[32,16,256]{2,1,0:T(8,128)S(1)} %bitcast.13, ...), custom_call_target="tpu_custom_call" | custom-call | tf_op jit(solution)/shard_map/pallas_call | solution.py:429
  27.9 1.0 %shard_map.117 = (f32[32,16,256]{2,1,0:T(8,128)S(1)}, f32[32,16,256]{2,1,0:T(8,128)S(1)}, f32[32,16,256]{2,1,0:T(8,128)S(1)}, f32[32,8,256]{2,1,0:T(8,128)S(1)},...) custom-call(s32[1]{0:T(128)S(6)} %copy.23.offsets, ...), custom_call_target="tpu_custom_call" | custom-call | tf_op jit(solution)/shard_map/pallas_call | solution.py:433
  28.9 6.5 %collective-permute-start.4 = (f32[32,8,256]{2,1,0:T(8,128)S(1)}, f32[32,8,256]{2,1,0:T(8,128)S(1)}, u32[]{:S(2)}, u32[]{:S(2)}) collective-permute-start(f32[32,8,256]{2,1,0:T(8,128)S(1)} %get-tuple-element.40), channel_id=1, source_target_pairs={{1,2},{2,1},{3,4},{4,3},{5,6},{6,5},{7,8},{8,7},{9,10},{10,9},{11,... | collective-permute-start | bytes 786440 | tf_op jit(solution)/shard_map/ppermute | solution.py:21
  35.4 1.9 %collective-permute-start.5 = (f32[32,8,256]{2,1,0:T(8,128)S(1)}, f32[32,8,256]{2,1,0:T(8,128)S(1)}, u32[]{:S(2)}, u32[]{:S(2)}) collective-permute-start(f32[32,8,256]{2,1,0:T(8,128)S(1)} %get-tuple-element.41), channel_id=1, source_target_pairs={{0,1},{1,0},{2,3},{3,2},{4,5},{5,4},{6,7},{7,6},{8,9},{9,8},{10,11... | collective-permute-start | bytes 786440 | tf_op jit(solution)/shard_map/ppermute | solution.py:21
  37.3 1.9 %collective-permute-start.6 = (f32[8,16,256]{2,1,0:T(8,128)S(1)}, f32[8,16,256]{2,1,0:T(8,128)S(1)}, u32[]{:S(2)}, u32[]{:S(2)}) collective-permute-start(f32[8,16,256]{2,1,0:T(8,128)S(1)} %get-tuple-element.42), channel_id=1, source_target_pairs={{32,64},{64,32},{33,65},{65,33},{34,66},{66,34},{35,67},{67,35},{3... | collective-permute-start | bytes 393224 | tf_op jit(solution)/shard_map/ppermute | solution.py:21
  39.2 1.9 %collective-permute-start.7 = (f32[8,16,256]{2,1,0:T(8,128)S(1)}, f32[8,16,256]{2,1,0:T(8,128)S(1)}, u32[]{:S(2)}, u32[]{:S(2)}) collective-permute-start(f32[8,16,256]{2,1,0:T(8,128)S(1)} %get-tuple-element.43), channel_id=1, source_target_pairs={{0,32},{32,0},{64,96},{96,64},{1,33},{33,1},{65,97},{97,65},{2,34}... | collective-permute-start | bytes 393224 | tf_op jit(solution)/shard_map/ppermute | solution.py:21
  41.2 0.8 %shard_map.118 = (f32[32,16,256]{2,1,0:T(8,128)S(1)}, f32[32,16,256]{2,1,0:T(8,128)S(1)}, bf16[256,256]{1,0:T(8,128)(2,1)S(1)}, bf16[256,256]{1,0:T(8,128)(2,1)S(1)}, bf16[2,128,256]{2,1,0:T(8,128)(2,1)S(1)}) custom-call(s32[3,256]{1,0:T(4,128)S(1)} %bitcast.25, f32[2,256]{1,0:T(2,128)S(1)} %bitcast.26, f32[32,16,256]{2,1,0:T(8,128)S(1)} %get-tuple-element.45.other.vel), custom_call_target="tpu_custom_call" | custom-call | tf_op jit(solution)/shard_map/pallas_call | solution.py:437
  42.0 1.6 %shard_map.119 = (f32[32,16,256]{2,1,0:T(8,128)S(1)}, f32[32,16,256]{2,1,0:T(8,128)S(1)}, f32[32,16,256]{2,1,0:T(8,128)S(1)}) custom-call(f32[32,16,256]{2,1,0:T(8,128)S(1)} %bitcast.21, f32[32,16,256]{2,1,0:T(8,128)S(1)} %get-tuple-element.44.wave2, f32[32,16,256]{2,1,0:T(8,128)S(1)} %bitcast.15, f32[32,16,256]{2,1,0:T(8,128)S(1)} %bitcast.24, ...), custom_call_target="tpu_custom_call" | custom-call | tf_op jit(solution)/shard_map/pallas_call | solution.py:445
  43.9 1.1 %shard_map.120 = (f32[32,16,256]{2,1,0:T(8,128)S(1)}, f32[32,16,256]{2,1,0:T(8,128)S(1)}, f32[32,16,256]{2,1,0:T(8,128)S(1)}, f32[32,16,256]{2,1,0:T(8,128)S(1)}...) custom-call(f32[32,8,256]{2,1,0:T(8,128)S(1)} %collective-permute-do, ...), custom_call_target="tpu_custom_call", output_to_operand_aliasing={{0}: (4, {}), {1}: (5, {}), {2}: (6, {})} | custom-call | tf_op jit(solution)/shard_map/pallas_call | solution.py:448
  44.9 4.6 %collective-permute-start.8 = (f32[32,8,256]{2,1,0:T(8,128)S(1)}, f32[32,8,256]{2,1,0:T(8,128)S(1)}, u32[]{:S(2)}, u32[]{:S(2)}) collective-permute-start(f32[32,8,256]{2,1,0:T(8,128)S(1)} %get-tuple-element.54), channel_id=1, source_target_pairs={{1,2},{2,1},{3,4},{4,3},{5,6},{6,5},{7,8},{8,7},{9,10},{10,9},{11,... | collective-permute-start | bytes 786440 | tf_op jit(solution)/shard_map/ppermute | solution.py:21
  49.6 1.9 %collective-permute-start.9 = (f32[32,8,256]{2,1,0:T(8,128)S(1)}, f32[32,8,256]{2,1,0:T(8,128)S(1)}, u32[]{:S(2)}, u32[]{:S(2)}) collective-permute-start(f32[32,8,256]{2,1,0:T(8,128)S(1)} %get-tuple-element.55), channel_id=1, source_target_pairs={{0,1},{1,0},{2,3},{3,2},{4,5},{5,4},{6,7},{7,6},{8,9},{9,8},{10,11... | collective-permute-start | bytes 786440 | tf_op jit(solution)/shard_map/ppermute | solution.py:21
  51.5 2.5 %collective-permute-start.10 = (f32[8,16,256]{2,1,0:T(8,128)S(1)}, f32[8,16,256]{2,1,0:T(8,128)S(1)}, u32[]{:S(2)}, u32[]{:S(2)}) collective-permute-start(f32[8,16,256]{2,1,0:T(8,128)S(1)} %get-tuple-element.56), channel_id=1, source_target_pairs={{32,64},{64,32},{33,65},{65,33},{34,66},{66,34},{35,67},{67,35},{3... | collective-permute-start | bytes 393224 | tf_op jit(solution)/shard_map/ppermute | solution.py:21
  54.0 1.9 %collective-permute-start.11 = (f32[8,16,256]{2,1,0:T(8,128)S(1)}, f32[8,16,256]{2,1,0:T(8,128)S(1)}, u32[]{:S(2)}, u32[]{:S(2)}) collective-permute-start(f32[8,16,256]{2,1,0:T(8,128)S(1)} %get-tuple-element.57), channel_id=1, source_target_pairs={{0,32},{32,0},{64,96},{96,64},{1,33},{33,1},{65,97},{97,65},{2,34}... | collective-permute-start | bytes 393224 | tf_op jit(solution)/shard_map/ppermute | solution.py:21
  56.0 1.6 %shard_map.121 = (f32[32,16,256]{2,1,0:T(8,128)S(1)}, f32[32,16,256]{2,1,0:T(8,128)S(1)}) custom-call(f32[32,16,256]{2,1,0:T(8,128)S(1)} %get-tuple-element.58.wave3, f32[32,16,256]{2,1,0:T(8,128)S(1)} %get-tuple-element.59.image3, f32[32,16,256]{2,1,0:T(8,128)S(1)} %get-tuple-element.60.adj3, f32[32,16,256]{2,1,0:T(8,128)S(1)} %bitcast.16, ...), custom_call_target="tpu_custom_call" | custom-call | tf_op jit(solution)/shard_map/pallas_call | solution.py:453
  57.8 1.3 %collective-permute-done.8.yb = f32[32,8,256]{2,1,0:T(8,128)S(1)} collective-permute-done((f32[32,8,256]{2,1,0:T(8,128)S(1)}, f32[32,8,256]{2,1,0:T(8,128)S(1)}, u32[]{:S(2)}, u32[]{:S(2)}) %collective-permute-start.8) | collective-permute-done | bytes 262176 | tf_op jit(solution)/shard_map/ppermute | solution.py:21
  59.1 0.8 collective-permute-done.9.ya
  59.9 0.7 shard_map.122
  60.6 5.4 %collective-permute-start.12 = (f32[32,16,128]{2,1,0:T(8,128)S(1)}, f32[32,16,128]{2,1,0:T(8,128)S(1)}, u32[]{:S(2)}, u32[]{:S(2)}) collective-permute-start(f32[32,16,128]{2,1,0:T(8,128)S(1)} %get-tuple-element.65), channel_id=1, source_target_pairs={{0,256},{128,384},{256,0},{384,128},{1,257},{129,385},{257,1},{385... | collective-permute-start | bytes 786440 | tf_op jit(solution)/shard_map/ppermute | solution.py:34
  66.1 3.1 %collective-permute-start.13 = (f32[32,16,128]{2,1,0:T(8,128)S(1)}, f32[32,16,128]{2,1,0:T(8,128)S(1)}, u32[]{:S(2)}, u32[]{:S(2)}) collective-permute-start(f32[32,16,128]{2,1,0:T(8,128)S(1)} %get-tuple-element.66), channel_id=1, source_target_pairs={{128,256},{256,128},{384,0},{0,384},{129,257},{257,129},{385,1},{1... | collective-permute-start | bytes 786440 | tf_op jit(solution)/shard_map/ppermute | solution.py:29
  69.2 1.9 %collective-permute-start.14 = (f32[32,16,128]{2,1,0:T(8,128)S(1)}, f32[32,16,128]{2,1,0:T(8,128)S(1)}, u32[]{:S(2)}, u32[]{:S(2)}) collective-permute-start(f32[32,16,128]{2,1,0:T(8,128)S(1)} %get-tuple-element.67), channel_id=1, source_target_pairs={{0,128},{128,0},{256,384},{384,256},{1,129},{129,1},{257,385},{385... | collective-permute-start | bytes 786440 | tf_op jit(solution)/shard_map/ppermute | solution.py:29
  71.1 0.8 %shard_map.124 = f32[32,16,256]{2,1,0:T(8,128)} custom-call(f32[32,16,256]{2,1,0:T(8,128)S(1)} %get-tuple-element.68.adj2_in, f32[32,16,256]{2,1,0:T(8,128)S(1)} %get-tuple-element.69.extra), custom_call_target="tpu_custom_call" | custom-call | tf_op jit(solution)/shard_map/pallas_call | solution.py:460
  72.1 5.4 %collective-permute-done.13.b = f32[32,16,128]{2,1,0:T(8,128)S(1)} collective-permute-done((f32[32,16,128]{2,1,0:T(8,128)S(1)}, f32[32,16,128]{2,1,0:T(8,128)S(1)}, u32[]{:S(2)}, u32[]{:S(2)}) %collective-permute-start.13) | collective-permute-done | bytes 262176 | tf_op jit(solution)/shard_map/ppermute | solution.py:29
  77.5 0.5 collective-permute-done.14.a
  78.1 0.8 shard_map.123
  (31 shorter events, 1.2 us)
Async XLA Ops:
  0.6 1.0 %copy-start.4 = (f32[32,16,128]{2,1,0:T(8,128)S(1)}, f32[32,16,128]{2,1,0:T(8,128)}, u32[]{:S(2)}) copy-start(f32[32,16,128]{2,1,0:T(8,128)} %tile.1) | copy-start | bytes 786436
  2.6 4.5 %copy-start.1 = (f32[1,32,16,256]{3,2,1,0:T(8,128)S(1)}, f32[1,32,16,256]{3,2,1,0:T(8,128)}, u32[]{:S(2)}) copy-start(f32[1,32,16,256]{3,2,1,0:T(8,128)} %param.13) | copy-start | bytes 1572868
  2.6 23.6 %copy-start.2 = (f32[1,32,16,256]{3,2,1,0:T(8,128)S(1)}, f32[1,32,16,256]{3,2,1,0:T(8,128)}, u32[]{:S(2)}) copy-start(f32[1,32,16,256]{3,2,1,0:T(8,128)} %param.12) | copy-start | bytes 1572868
  2.6 25.2 %all-to-all-start = ((f32[4,32,16,128]{3,2,1,0:T(8,128)}), f32[4,32,16,128]{3,2,1,0:T(8,128)S(1)}, u32[]{:S(2)}, u32[]{:S(2)}) async-start(f32[4,32,16,128]{3,2,1,0:T(8,128)} %shard_map.113), calls=%async_computation | async-start | bytes 2097152 | tf_op jit(solution)/shard_map/all_to_all | solution.py:421
  7.1 19.2 %copy-start = (f32[1,32,16,256]{3,2,1,0:T(8,128)S(1)}, f32[1,32,16,256]{3,2,1,0:T(8,128)}, u32[]{:S(2)}) copy-start(f32[1,32,16,256]{3,2,1,0:T(8,128)} %param.14) | copy-start | bytes 1572868
  7.1 18.6 %collective-permute-start = (f32[16,8,256]{2,1,0:T(8,128)S(1)}, f32[16,8,256]{2,1,0:T(8,128)S(1)}, u32[]{:S(2)}, u32[]{:S(2)}) collective-permute-start(f32[16,8,256]{2,1,0:T(8,128)S(1)} %get-tuple-element.36), channel_id=1, source_target_pairs={{1,2},{2,1},{3,4},{4,3},{5,6},{6,5},{7,8},{8,7},{9,10},{10,9},{11,... | collective-permute-start | bytes 393224 | tf_op jit(solution)/shard_map/ppermute | solution.py:21
  19.4 6.9 %collective-permute-start.1 = (f32[16,8,256]{2,1,0:T(8,128)S(1)}, f32[16,8,256]{2,1,0:T(8,128)S(1)}, u32[]{:S(2)}, u32[]{:S(2)}) collective-permute-start(f32[16,8,256]{2,1,0:T(8,128)S(1)} %get-tuple-element.37), channel_id=1, source_target_pairs={{0,1},{1,0},{2,3},{3,2},{4,5},{5,4},{6,7},{7,6},{8,9},{9,8},{10,11... | collective-permute-start | bytes 393224 | tf_op jit(solution)/shard_map/ppermute | solution.py:21
  21.3 6.5 %collective-permute-start.2 = (f32[4,16,256]{2,1,0:T(8,128)S(1)}, f32[4,16,256]{2,1,0:T(8,128)S(1)}, u32[]{:S(2)}, u32[]{:S(2)}) collective-permute-start(f32[4,16,256]{2,1,0:T(8,128)S(1)} %get-tuple-element.38), channel_id=1, source_target_pairs={{32,64},{64,32},{33,65},{65,33},{34,66},{66,34},{35,67},{67,35},{3... | collective-permute-start | bytes 196616 | tf_op jit(solution)/shard_map/ppermute | solution.py:21
  23.2 4.5 %collective-permute-start.3 = (f32[4,16,256]{2,1,0:T(8,128)S(1)}, f32[4,16,256]{2,1,0:T(8,128)S(1)}, u32[]{:S(2)}, u32[]{:S(2)}) collective-permute-start(f32[4,16,256]{2,1,0:T(8,128)S(1)} %get-tuple-element.39), channel_id=1, source_target_pairs={{0,32},{32,0},{64,96},{96,64},{1,33},{33,1},{65,97},{97,65},{2,34}... | collective-permute-start | bytes 196616 | tf_op jit(solution)/shard_map/ppermute | solution.py:21
  26.2 0.7 copy-start.5
  26.2 0.7 copy-start.6
  27.9 13.3 %copy-start.8 = (s32[1,256,3]{1,0,2:T(1,128)S(1)}, s32[1,256,3]{1,0,2:T(1,128)}, u32[]{:S(2)}) copy-start(s32[1,256,3]{1,0,2:T(1,128)} %param.18) | copy-start | bytes 9220
  27.9 13.3 %copy-start.7 = (f32[1,256,2]{1,2,0:T(2,128)S(1)}, f32[1,256,2]{1,2,0:T(2,128)}, u32[]{:S(2)}) copy-start(f32[1,256,2]{1,2,0:T(2,128)} %param.19) | copy-start | bytes 6148
  28.9 13.1 %copy-start.3 = (f32[1,32,16,256]{3,2,1,0:T(8,128)S(1)}, f32[1,32,16,256]{3,2,1,0:T(8,128)}, u32[]{:S(2)}) copy-start(f32[1,32,16,256]{3,2,1,0:T(8,128)} %param.15) | copy-start | bytes 1572868
  28.9 14.8 %collective-permute-start.4 = (f32[32,8,256]{2,1,0:T(8,128)S(1)}, f32[32,8,256]{2,1,0:T(8,128)S(1)}, u32[]{:S(2)}, u32[]{:S(2)}) collective-permute-start(f32[32,8,256]{2,1,0:T(8,128)S(1)} %get-tuple-element.40), channel_id=1, source_target_pairs={{1,2},{2,1},{3,4},{4,3},{5,6},{6,5},{7,8},{8,7},{9,10},{10,9},{11,... | collective-permute-start | bytes 786440 | tf_op jit(solution)/shard_map/ppermute | solution.py:21
  35.4 8.5 %collective-permute-start.5 = (f32[32,8,256]{2,1,0:T(8,128)S(1)}, f32[32,8,256]{2,1,0:T(8,128)S(1)}, u32[]{:S(2)}, u32[]{:S(2)}) collective-permute-start(f32[32,8,256]{2,1,0:T(8,128)S(1)} %get-tuple-element.41), channel_id=1, source_target_pairs={{0,1},{1,0},{2,3},{3,2},{4,5},{5,4},{6,7},{7,6},{8,9},{9,8},{10,11... | collective-permute-start | bytes 786440 | tf_op jit(solution)/shard_map/ppermute | solution.py:21
  37.3 6.4 %collective-permute-start.6 = (f32[8,16,256]{2,1,0:T(8,128)S(1)}, f32[8,16,256]{2,1,0:T(8,128)S(1)}, u32[]{:S(2)}, u32[]{:S(2)}) collective-permute-start(f32[8,16,256]{2,1,0:T(8,128)S(1)} %get-tuple-element.42), channel_id=1, source_target_pairs={{32,64},{64,32},{33,65},{65,33},{34,66},{66,34},{35,67},{67,35},{3... | collective-permute-start | bytes 393224 | tf_op jit(solution)/shard_map/ppermute | solution.py:21
  39.2 4.5 %collective-permute-start.7 = (f32[8,16,256]{2,1,0:T(8,128)S(1)}, f32[8,16,256]{2,1,0:T(8,128)S(1)}, u32[]{:S(2)}, u32[]{:S(2)}) collective-permute-start(f32[8,16,256]{2,1,0:T(8,128)S(1)} %get-tuple-element.43), channel_id=1, source_target_pairs={{0,32},{32,0},{64,96},{96,64},{1,33},{33,1},{65,97},{97,65},{2,34}... | collective-permute-start | bytes 393224 | tf_op jit(solution)/shard_map/ppermute | solution.py:21
  44.9 14.2 %collective-permute-start.8 = (f32[32,8,256]{2,1,0:T(8,128)S(1)}, f32[32,8,256]{2,1,0:T(8,128)S(1)}, u32[]{:S(2)}, u32[]{:S(2)}) collective-permute-start(f32[32,8,256]{2,1,0:T(8,128)S(1)} %get-tuple-element.54), channel_id=1, source_target_pairs={{1,2},{2,1},{3,4},{4,3},{5,6},{6,5},{7,8},{8,7},{9,10},{10,9},{11,... | collective-permute-start | bytes 786440 | tf_op jit(solution)/shard_map/ppermute | solution.py:21
  49.6 10.3 %collective-permute-start.9 = (f32[32,8,256]{2,1,0:T(8,128)S(1)}, f32[32,8,256]{2,1,0:T(8,128)S(1)}, u32[]{:S(2)}, u32[]{:S(2)}) collective-permute-start(f32[32,8,256]{2,1,0:T(8,128)S(1)} %get-tuple-element.55), channel_id=1, source_target_pairs={{0,1},{1,0},{2,3},{3,2},{4,5},{5,4},{6,7},{7,6},{8,9},{9,8},{10,11... | collective-permute-start | bytes 786440 | tf_op jit(solution)/shard_map/ppermute | solution.py:21
  51.5 6.3 %collective-permute-start.10 = (f32[8,16,256]{2,1,0:T(8,128)S(1)}, f32[8,16,256]{2,1,0:T(8,128)S(1)}, u32[]{:S(2)}, u32[]{:S(2)}) collective-permute-start(f32[8,16,256]{2,1,0:T(8,128)S(1)} %get-tuple-element.56), channel_id=1, source_target_pairs={{32,64},{64,32},{33,65},{65,33},{34,66},{66,34},{35,67},{67,35},{3... | collective-permute-start | bytes 393224 | tf_op jit(solution)/shard_map/ppermute | solution.py:21
  54.0 3.7 %collective-permute-start.11 = (f32[8,16,256]{2,1,0:T(8,128)S(1)}, f32[8,16,256]{2,1,0:T(8,128)S(1)}, u32[]{:S(2)}, u32[]{:S(2)}) collective-permute-start(f32[8,16,256]{2,1,0:T(8,128)S(1)} %get-tuple-element.57), channel_id=1, source_target_pairs={{0,32},{32,0},{64,96},{96,64},{1,33},{33,1},{65,97},{97,65},{2,34}... | collective-permute-start | bytes 393224 | tf_op jit(solution)/shard_map/ppermute | solution.py:21
  60.6 11.5 %collective-permute-start.12 = (f32[32,16,128]{2,1,0:T(8,128)S(1)}, f32[32,16,128]{2,1,0:T(8,128)S(1)}, u32[]{:S(2)}, u32[]{:S(2)}) collective-permute-start(f32[32,16,128]{2,1,0:T(8,128)S(1)} %get-tuple-element.65), channel_id=1, source_target_pairs={{0,256},{128,384},{256,0},{384,128},{1,257},{129,385},{257,1},{385... | collective-permute-start | bytes 786440 | tf_op jit(solution)/shard_map/ppermute | solution.py:34
  66.1 11.5 %collective-permute-start.13 = (f32[32,16,128]{2,1,0:T(8,128)S(1)}, f32[32,16,128]{2,1,0:T(8,128)S(1)}, u32[]{:S(2)}, u32[]{:S(2)}) collective-permute-start(f32[32,16,128]{2,1,0:T(8,128)S(1)} %get-tuple-element.66), channel_id=1, source_target_pairs={{128,256},{256,128},{384,0},{0,384},{129,257},{257,129},{385,1},{1... | collective-permute-start | bytes 786440 | tf_op jit(solution)/shard_map/ppermute | solution.py:29
  69.2 8.9 %collective-permute-start.14 = (f32[32,16,128]{2,1,0:T(8,128)S(1)}, f32[32,16,128]{2,1,0:T(8,128)S(1)}, u32[]{:S(2)}, u32[]{:S(2)}) collective-permute-start(f32[32,16,128]{2,1,0:T(8,128)S(1)} %get-tuple-element.67), channel_id=1, source_target_pairs={{0,128},{128,0},{256,384},{384,256},{1,129},{129,1},{257,385},{385... | collective-permute-start | bytes 786440 | tf_op jit(solution)/shard_map/ppermute | solution.py:29

commit v9 on v8

--- a/solution.py
+++ b/solution.py
@@ -90,14 +90,16 @@
         out[at : at + chunk] = total.reshape(chunk, size_y, depth)
 
 
-def outer_part(ya, yb, at, outer, field):
+def outer_part(ya, yb, at, outer):
     depth = ya.shape[2]
-    chunk = outer.shape[1] // 8
+    fields, rows = outer.shape[0], outer.shape[1]
+    chunk = rows // 8
     a, b = (m[at : at + chunk].reshape(chunk * 8, depth) for m in (ya, yb))
     even_y = even("gy")
     below, above = three(jnp.where(even_y, b, a)), three(jnp.where(even_y, a, b))
-    total = sum(product(outer[field], jnp.concatenate(pair, axis=0)) for pair in zip(below, above))
-    return total.reshape(chunk, 8, depth) * (1.0 / SCALE)
+    matrix = outer[...].reshape(fields * rows, outer.shape[2])
+    total = sum(product(matrix, jnp.concatenate(pair, axis=0)) for pair in zip(below, above))
+    return total.reshape(fields, chunk, 8, depth) * (1.0 / SCALE)
 
 
 def spread(rows, size_y):
@@ -121,10 +123,12 @@
 
 def outer_parts(ya, yb, xa, xb, outer, sides, rows):
     chunk = outer.shape[1] // 8
-    for field, (side, row) in enumerate(zip(sides, rows)):
+    for at in range(0, rows[0].shape[0], chunk):
+        both = outer_part(ya, yb, at, outer)
+        for field, row in enumerate(rows):
+            row[at : at + chunk] = both[field]
+    for field, side in enumerate(sides):
         outside_x(xa, xb, 4 * field, side)
-        for at in range(0, row.shape[0], chunk):
-            row[at : at + chunk] = outer_part(ya, yb, at, outer, field)
 
 
 def outer_of(side, row, x, z):
@@ -262,9 +266,8 @@
     difference_matrices(size_y, along_y, along_z)
     outer_matrices(size_x, size_y, outer)
     flat_part(wave1, along_y, along_z, flat)
-    half = size_x // 2
-    for part in range(2):
-        row[part * half : (part + 1) * half] = outer_part(ya, yb, 0, outer, part)
+    both = outer_part(ya, yb, 0, outer)
+    row[...] = both.reshape(size_x, 8, both.shape[3])
     planes = within(wave1)
     for z in halves():
         for x in range(size_x):

time: 79.5 us -> 79.4 us (level)
  no operation moved by 1% of the time
where the time goes in v9:
time: 79.4 us; the launch traced here: 78.8 us
  starting transfers between devices  56.1 us (71%)
  Pallas kernels  10.4 us (13%)
  waiting for transfers between devices  9.05 us (11%)
  local copies, waits for them, and re-layouts  1.64 us (2%)
  between operations  1.61 us (2%)
    ppermute x12, starting transfers between devices, swap(): return lax.ppermute(value, axis, pairs)  41.3 us
    ppermute x2, waiting for transfers between devices, swap_shot(): return lax.ppermute(value, 'shot', pairs)  6.03 us
    ppermute x1, starting transfers between devices, swap_across(): lax.ppermute(value, 'shot', [(i, (i + size // 2) % size) for i in range(s...  5.44 us
    ppermute x2, starting transfers between devices, swap_shot(): return lax.ppermute(value, 'shot', pairs)  4.99 us
    all_to_all x1, starting transfers between devices, local(): column = lax.all_to_all(copies, 'shot', 0, 0)  4.44 us
    ppermute x12, waiting for transfers between devices, swap(): return lax.ppermute(value, axis, pairs)  2.87 us
    unnamed x19, local copies, waits for them, and re-layouts  1.64 us
    pallas_call x1, Pallas kernels, local(): call(third_inner_kernel, (block,) * 3, (whole,) * 2, n_in=11, room=10)  1.64 us
  transfers between devices with their start and end apart: 16, of which 8 were waited for; matrix products, arithmetic and copies ran while one was open for 0% of the time, Pallas kernels for 7%

profile of v9, /device:TPU:24, one launch (start us, length us, event | category | flops | bytes accessed | tf_op | source)
XLA Modules:
  0.0 78.8 jit_solution(12680737918888795882)
XLA Ops:
  0.6 0.9 %copy-done.4 = f32[32,16,128]{2,1,0:T(8,128)S(1)} copy-done((f32[32,16,128]{2,1,0:T(8,128)S(1)}, f32[32,16,128]{2,1,0:T(8,128)}, u32[]{:S(2)}) %copy-start.4) | copy-done | bytes 262168
  1.6 1.0 %shard_map.113 = f32[4,32,16,128]{3,2,1,0:T(8,128)} custom-call(f32[32,16,128]{2,1,0:T(8,128)S(1)} %copy-done.4), custom_call_target="tpu_custom_call" | custom-call | tf_op jit(solution)/shard_map/pallas_call | solution.py:416
  2.6 4.4 %all-to-all-start = ((f32[4,32,16,128]{3,2,1,0:T(8,128)}), f32[4,32,16,128]{3,2,1,0:T(8,128)S(1)}, u32[]{:S(2)}, u32[]{:S(2)}) async-start(f32[4,32,16,128]{3,2,1,0:T(8,128)} %shard_map.113), calls=%async_computation | async-start | bytes 2097152 | tf_op jit(solution)/shard_map/all_to_all | solution.py:424
  7.1 12.2 %collective-permute-start = (f32[16,8,256]{2,1,0:T(8,128)S(1)}, f32[16,8,256]{2,1,0:T(8,128)S(1)}, u32[]{:S(2)}, u32[]{:S(2)}) collective-permute-start(f32[16,8,256]{2,1,0:T(8,128)S(1)} %get-tuple-element.36), channel_id=1, source_target_pairs={{1,2},{2,1},{3,4},{4,3},{5,6},{6,5},{7,8},{8,7},{9,10},{10,9},{11,... | collective-permute-start | bytes 393224 | tf_op jit(solution)/shard_map/ppermute | solution.py:21
  19.4 1.9 %collective-permute-start.1 = (f32[16,8,256]{2,1,0:T(8,128)S(1)}, f32[16,8,256]{2,1,0:T(8,128)S(1)}, u32[]{:S(2)}, u32[]{:S(2)}) collective-permute-start(f32[16,8,256]{2,1,0:T(8,128)S(1)} %get-tuple-element.37), channel_id=1, source_target_pairs={{0,1},{1,0},{2,3},{3,2},{4,5},{5,4},{6,7},{7,6},{8,9},{9,8},{10,11... | collective-permute-start | bytes 393224 | tf_op jit(solution)/shard_map/ppermute | solution.py:21
  21.3 1.9 %collective-permute-start.2 = (f32[4,16,256]{2,1,0:T(8,128)S(1)}, f32[4,16,256]{2,1,0:T(8,128)S(1)}, u32[]{:S(2)}, u32[]{:S(2)}) collective-permute-start(f32[4,16,256]{2,1,0:T(8,128)S(1)} %get-tuple-element.38), channel_id=1, source_target_pairs={{32,64},{64,32},{33,65},{65,33},{34,66},{66,34},{35,67},{67,35},{3... | collective-permute-start | bytes 196616 | tf_op jit(solution)/shard_map/ppermute | solution.py:21
  23.2 1.9 %collective-permute-start.3 = (f32[4,16,256]{2,1,0:T(8,128)S(1)}, f32[4,16,256]{2,1,0:T(8,128)S(1)}, u32[]{:S(2)}, u32[]{:S(2)}) collective-permute-start(f32[4,16,256]{2,1,0:T(8,128)S(1)} %get-tuple-element.39), channel_id=1, source_target_pairs={{0,32},{32,0},{64,96},{96,64},{1,33},{33,1},{65,97},{97,65},{2,34}... | collective-permute-start | bytes 196616 | tf_op jit(solution)/shard_map/ppermute | solution.py:21
  26.2 0.6 copy-done.5
  26.9 0.8 %shard_map.115.inner = f32[32,16,256]{2,1,0:T(8,128)S(1)} custom-call(f32[32,16,256]{2,1,0:T(8,128)S(1)} %bitcast.19, f32[16,8,256]{2,1,0:T(8,128)S(1)} %collective-permute-done.yb, f32[16,8,256]{2,1,0:T(8,128)S(1)} %collective-permute-done.1.ya, f32[32,16,256]{2,1,0:T(8,128)S(1)} %bitcast.22, f32[32,16,256]{2,1,0:T(8,128)S(1)} %bitcast.13, ...), custom_call_target="tpu_custom_call" | custom-call | tf_op jit(solution)/shard_map/pallas_call | solution.py:432
  27.8 1.0 %shard_map.117 = (f32[32,16,256]{2,1,0:T(8,128)S(1)}, f32[32,16,256]{2,1,0:T(8,128)S(1)}, f32[32,16,256]{2,1,0:T(8,128)S(1)}, f32[32,8,256]{2,1,0:T(8,128)S(1)},...) custom-call(s32[1]{0:T(128)S(6)} %copy.23.offsets, ...), custom_call_target="tpu_custom_call" | custom-call | tf_op jit(solution)/shard_map/pallas_call | solution.py:436
  28.8 6.5 %collective-permute-start.4 = (f32[32,8,256]{2,1,0:T(8,128)S(1)}, f32[32,8,256]{2,1,0:T(8,128)S(1)}, u32[]{:S(2)}, u32[]{:S(2)}) collective-permute-start(f32[32,8,256]{2,1,0:T(8,128)S(1)} %get-tuple-element.40), channel_id=1, source_target_pairs={{1,2},{2,1},{3,4},{4,3},{5,6},{6,5},{7,8},{8,7},{9,10},{10,9},{11,... | collective-permute-start | bytes 786440 | tf_op jit(solution)/shard_map/ppermute | solution.py:21
  35.4 1.9 %collective-permute-start.5 = (f32[32,8,256]{2,1,0:T(8,128)S(1)}, f32[32,8,256]{2,1,0:T(8,128)S(1)}, u32[]{:S(2)}, u32[]{:S(2)}) collective-permute-start(f32[32,8,256]{2,1,0:T(8,128)S(1)} %get-tuple-element.41), channel_id=1, source_target_pairs={{0,1},{1,0},{2,3},{3,2},{4,5},{5,4},{6,7},{7,6},{8,9},{9,8},{10,11... | collective-permute-start | bytes 786440 | tf_op jit(solution)/shard_map/ppermute | solution.py:21
  37.3 1.9 %collective-permute-start.6 = (f32[8,16,256]{2,1,0:T(8,128)S(1)}, f32[8,16,256]{2,1,0:T(8,128)S(1)}, u32[]{:S(2)}, u32[]{:S(2)}) collective-permute-start(f32[8,16,256]{2,1,0:T(8,128)S(1)} %get-tuple-element.42), channel_id=1, source_target_pairs={{32,64},{64,32},{33,65},{65,33},{34,66},{66,34},{35,67},{67,35},{3... | collective-permute-start | bytes 393224 | tf_op jit(solution)/shard_map/ppermute | solution.py:21
  39.2 1.9 %collective-permute-start.7 = (f32[8,16,256]{2,1,0:T(8,128)S(1)}, f32[8,16,256]{2,1,0:T(8,128)S(1)}, u32[]{:S(2)}, u32[]{:S(2)}) collective-permute-start(f32[8,16,256]{2,1,0:T(8,128)S(1)} %get-tuple-element.43), channel_id=1, source_target_pairs={{0,32},{32,0},{64,96},{96,64},{1,33},{33,1},{65,97},{97,65},{2,34}... | collective-permute-start | bytes 393224 | tf_op jit(solution)/shard_map/ppermute | solution.py:21
  41.2 0.8 %shard_map.118 = (f32[32,16,256]{2,1,0:T(8,128)S(1)}, f32[32,16,256]{2,1,0:T(8,128)S(1)}, bf16[256,256]{1,0:T(8,128)(2,1)S(1)}, bf16[256,256]{1,0:T(8,128)(2,1)S(1)}, bf16[2,128,256]{2,1,0:T(8,128)(2,1)S(1)}) custom-call(s32[3,256]{1,0:T(4,128)S(1)} %bitcast.25, f32[2,256]{1,0:T(2,128)S(1)} %bitcast.26, f32[32,16,256]{2,1,0:T(8,128)S(1)} %get-tuple-element.45.other.vel), custom_call_target="tpu_custom_call" | custom-call | tf_op jit(solution)/shard_map/pallas_call | solution.py:440
  42.0 1.6 %shard_map.119 = (f32[32,16,256]{2,1,0:T(8,128)S(1)}, f32[32,16,256]{2,1,0:T(8,128)S(1)}, f32[32,16,256]{2,1,0:T(8,128)S(1)}) custom-call(f32[32,16,256]{2,1,0:T(8,128)S(1)} %bitcast.21, f32[32,16,256]{2,1,0:T(8,128)S(1)} %get-tuple-element.44.wave2, f32[32,16,256]{2,1,0:T(8,128)S(1)} %bitcast.15, f32[32,16,256]{2,1,0:T(8,128)S(1)} %bitcast.24, ...), custom_call_target="tpu_custom_call" | custom-call | tf_op jit(solution)/shard_map/pallas_call | solution.py:448
  43.9 1.1 %shard_map.120 = (f32[32,16,256]{2,1,0:T(8,128)S(1)}, f32[32,16,256]{2,1,0:T(8,128)S(1)}, f32[32,16,256]{2,1,0:T(8,128)S(1)}, f32[32,16,256]{2,1,0:T(8,128)S(1)}...) custom-call(f32[32,8,256]{2,1,0:T(8,128)S(1)} %collective-permute-do, ...), custom_call_target="tpu_custom_call", output_to_operand_aliasing={{0}: (4, {}), {1}: (5, {}), {2}: (6, {})} | custom-call | tf_op jit(solution)/shard_map/pallas_call | solution.py:451
  44.9 4.6 %collective-permute-start.8 = (f32[32,8,256]{2,1,0:T(8,128)S(1)}, f32[32,8,256]{2,1,0:T(8,128)S(1)}, u32[]{:S(2)}, u32[]{:S(2)}) collective-permute-start(f32[32,8,256]{2,1,0:T(8,128)S(1)} %get-tuple-element.54), channel_id=1, source_target_pairs={{1,2},{2,1},{3,4},{4,3},{5,6},{6,5},{7,8},{8,7},{9,10},{10,9},{11,... | collective-permute-start | bytes 786440 | tf_op jit(solution)/shard_map/ppermute | solution.py:21
  49.5 1.9 %collective-permute-start.9 = (f32[32,8,256]{2,1,0:T(8,128)S(1)}, f32[32,8,256]{2,1,0:T(8,128)S(1)}, u32[]{:S(2)}, u32[]{:S(2)}) collective-permute-start(f32[32,8,256]{2,1,0:T(8,128)S(1)} %get-tuple-element.55), channel_id=1, source_target_pairs={{0,1},{1,0},{2,3},{3,2},{4,5},{5,4},{6,7},{7,6},{8,9},{9,8},{10,11... | collective-permute-start | bytes 786440 | tf_op jit(solution)/shard_map/ppermute | solution.py:21
  51.5 2.6 %collective-permute-start.10 = (f32[8,16,256]{2,1,0:T(8,128)S(1)}, f32[8,16,256]{2,1,0:T(8,128)S(1)}, u32[]{:S(2)}, u32[]{:S(2)}) collective-permute-start(f32[8,16,256]{2,1,0:T(8,128)S(1)} %get-tuple-element.56), channel_id=1, source_target_pairs={{32,64},{64,32},{33,65},{65,33},{34,66},{66,34},{35,67},{67,35},{3... | collective-permute-start | bytes 393224 | tf_op jit(solution)/shard_map/ppermute | solution.py:21
  54.1 1.9 %collective-permute-start.11 = (f32[8,16,256]{2,1,0:T(8,128)S(1)}, f32[8,16,256]{2,1,0:T(8,128)S(1)}, u32[]{:S(2)}, u32[]{:S(2)}) collective-permute-start(f32[8,16,256]{2,1,0:T(8,128)S(1)} %get-tuple-element.57), channel_id=1, source_target_pairs={{0,32},{32,0},{64,96},{96,64},{1,33},{33,1},{65,97},{97,65},{2,34}... | collective-permute-start | bytes 393224 | tf_op jit(solution)/shard_map/ppermute | solution.py:21
  56.0 1.6 %shard_map.121 = (f32[32,16,256]{2,1,0:T(8,128)S(1)}, f32[32,16,256]{2,1,0:T(8,128)S(1)}) custom-call(f32[32,16,256]{2,1,0:T(8,128)S(1)} %get-tuple-element.58.wave3, f32[32,16,256]{2,1,0:T(8,128)S(1)} %get-tuple-element.59.image3, f32[32,16,256]{2,1,0:T(8,128)S(1)} %get-tuple-element.60.adj3, f32[32,16,256]{2,1,0:T(8,128)S(1)} %bitcast.16, ...), custom_call_target="tpu_custom_call" | custom-call | tf_op jit(solution)/shard_map/pallas_call | solution.py:456
  57.8 1.4 %collective-permute-done.8.yb = f32[32,8,256]{2,1,0:T(8,128)S(1)} collective-permute-done((f32[32,8,256]{2,1,0:T(8,128)S(1)}, f32[32,8,256]{2,1,0:T(8,128)S(1)}, u32[]{:S(2)}, u32[]{:S(2)}) %collective-permute-start.8) | collective-permute-done | bytes 262176 | tf_op jit(solution)/shard_map/ppermute | solution.py:21
  59.2 0.7 collective-permute-done.9.ya
  59.9 0.7 shard_map.122
  60.6 5.4 %collective-permute-start.12 = (f32[32,16,128]{2,1,0:T(8,128)S(1)}, f32[32,16,128]{2,1,0:T(8,128)S(1)}, u32[]{:S(2)}, u32[]{:S(2)}) collective-permute-start(f32[32,16,128]{2,1,0:T(8,128)S(1)} %get-tuple-element.65), channel_id=1, source_target_pairs={{0,256},{128,384},{256,0},{384,128},{1,257},{129,385},{257,1},{385... | collective-permute-start | bytes 786440 | tf_op jit(solution)/shard_map/ppermute | solution.py:34
  66.0 3.1 %collective-permute-start.13 = (f32[32,16,128]{2,1,0:T(8,128)S(1)}, f32[32,16,128]{2,1,0:T(8,128)S(1)}, u32[]{:S(2)}, u32[]{:S(2)}) collective-permute-start(f32[32,16,128]{2,1,0:T(8,128)S(1)} %get-tuple-element.66), channel_id=1, source_target_pairs={{128,256},{256,128},{384,0},{0,384},{129,257},{257,129},{385,1},{1... | collective-permute-start | bytes 786440 | tf_op jit(solution)/shard_map/ppermute | solution.py:29
  69.1 1.9 %collective-permute-start.14 = (f32[32,16,128]{2,1,0:T(8,128)S(1)}, f32[32,16,128]{2,1,0:T(8,128)S(1)}, u32[]{:S(2)}, u32[]{:S(2)}) collective-permute-start(f32[32,16,128]{2,1,0:T(8,128)S(1)} %get-tuple-element.67), channel_id=1, source_target_pairs={{0,128},{128,0},{256,384},{384,256},{1,129},{129,1},{257,385},{385... | collective-permute-start | bytes 786440 | tf_op jit(solution)/shard_map/ppermute | solution.py:29
  71.0 0.8 %shard_map.124 = f32[32,16,256]{2,1,0:T(8,128)} custom-call(f32[32,16,256]{2,1,0:T(8,128)S(1)} %get-tuple-element.68.adj2_in, f32[32,16,256]{2,1,0:T(8,128)S(1)} %get-tuple-element.69.extra), custom_call_target="tpu_custom_call" | custom-call | tf_op jit(solution)/shard_map/pallas_call | solution.py:463
  72.0 5.5 %collective-permute-done.13.b = f32[32,16,128]{2,1,0:T(8,128)S(1)} collective-permute-done((f32[32,16,128]{2,1,0:T(8,128)S(1)}, f32[32,16,128]{2,1,0:T(8,128)S(1)}, u32[]{:S(2)}, u32[]{:S(2)}) %collective-permute-start.13) | collective-permute-done | bytes 262176 | tf_op jit(solution)/shard_map/ppermute | solution.py:29
  77.5 0.6 collective-permute-done.14.a
  78.1 0.8 shard_map.123
  (31 shorter events, 1.1 us)
Async XLA Ops:
  0.6 1.0 %copy-start.4 = (f32[32,16,128]{2,1,0:T(8,128)S(1)}, f32[32,16,128]{2,1,0:T(8,128)}, u32[]{:S(2)}) copy-start(f32[32,16,128]{2,1,0:T(8,128)} %tile.1) | copy-start | bytes 786436
  2.6 4.5 %copy-start.1 = (f32[1,32,16,256]{3,2,1,0:T(8,128)S(1)}, f32[1,32,16,256]{3,2,1,0:T(8,128)}, u32[]{:S(2)}) copy-start(f32[1,32,16,256]{3,2,1,0:T(8,128)} %param.13) | copy-start | bytes 1572868
  2.6 23.6 %copy-start.2 = (f32[1,32,16,256]{3,2,1,0:T(8,128)S(1)}, f32[1,32,16,256]{3,2,1,0:T(8,128)}, u32[]{:S(2)}) copy-start(f32[1,32,16,256]{3,2,1,0:T(8,128)} %param.12) | copy-start | bytes 1572868
  2.6 25.2 %all-to-all-start = ((f32[4,32,16,128]{3,2,1,0:T(8,128)}), f32[4,32,16,128]{3,2,1,0:T(8,128)S(1)}, u32[]{:S(2)}, u32[]{:S(2)}) async-start(f32[4,32,16,128]{3,2,1,0:T(8,128)} %shard_map.113), calls=%async_computation | async-start | bytes 2097152 | tf_op jit(solution)/shard_map/all_to_all | solution.py:424
  7.1 19.2 %copy-start = (f32[1,32,16,256]{3,2,1,0:T(8,128)S(1)}, f32[1,32,16,256]{3,2,1,0:T(8,128)}, u32[]{:S(2)}) copy-start(f32[1,32,16,256]{3,2,1,0:T(8,128)} %param.14) | copy-start | bytes 1572868
  7.1 18.6 %collective-permute-start = (f32[16,8,256]{2,1,0:T(8,128)S(1)}, f32[16,8,256]{2,1,0:T(8,128)S(1)}, u32[]{:S(2)}, u32[]{:S(2)}) collective-permute-start(f32[16,8,256]{2,1,0:T(8,128)S(1)} %get-tuple-element.36), channel_id=1, source_target_pairs={{1,2},{2,1},{3,4},{4,3},{5,6},{6,5},{7,8},{8,7},{9,10},{10,9},{11,... | collective-permute-start | bytes 393224 | tf_op jit(solution)/shard_map/ppermute | solution.py:21
  19.4 6.9 %collective-permute-start.1 = (f32[16,8,256]{2,1,0:T(8,128)S(1)}, f32[16,8,256]{2,1,0:T(8,128)S(1)}, u32[]{:S(2)}, u32[]{:S(2)}) collective-permute-start(f32[16,8,256]{2,1,0:T(8,128)S(1)} %get-tuple-element.37), channel_id=1, source_target_pairs={{0,1},{1,0},{2,3},{3,2},{4,5},{5,4},{6,7},{7,6},{8,9},{9,8},{10,11... | collective-permute-start | bytes 393224 | tf_op jit(solution)/shard_map/ppermute | solution.py:21
  21.3 6.4 %collective-permute-start.2 = (f32[4,16,256]{2,1,0:T(8,128)S(1)}, f32[4,16,256]{2,1,0:T(8,128)S(1)}, u32[]{:S(2)}, u32[]{:S(2)}) collective-permute-start(f32[4,16,256]{2,1,0:T(8,128)S(1)} %get-tuple-element.38), channel_id=1, source_target_pairs={{32,64},{64,32},{33,65},{65,33},{34,66},{66,34},{35,67},{67,35},{3... | collective-permute-start | bytes 196616 | tf_op jit(solution)/shard_map/ppermute | solution.py:21
  23.2 4.5 %collective-permute-start.3 = (f32[4,16,256]{2,1,0:T(8,128)S(1)}, f32[4,16,256]{2,1,0:T(8,128)S(1)}, u32[]{:S(2)}, u32[]{:S(2)}) collective-permute-start(f32[4,16,256]{2,1,0:T(8,128)S(1)} %get-tuple-element.39), channel_id=1, source_target_pairs={{0,32},{32,0},{64,96},{96,64},{1,33},{33,1},{65,97},{97,65},{2,34}... | collective-permute-start | bytes 196616 | tf_op jit(solution)/shard_map/ppermute | solution.py:21
  26.2 0.7 copy-start.5
  26.2 0.7 copy-start.6
  27.8 13.4 %copy-start.8 = (s32[1,256,3]{1,0,2:T(1,128)S(1)}, s32[1,256,3]{1,0,2:T(1,128)}, u32[]{:S(2)}) copy-start(s32[1,256,3]{1,0,2:T(1,128)} %param.18) | copy-start | bytes 9220
  27.8 13.4 %copy-start.7 = (f32[1,256,2]{1,2,0:T(2,128)S(1)}, f32[1,256,2]{1,2,0:T(2,128)}, u32[]{:S(2)}) copy-start(f32[1,256,2]{1,2,0:T(2,128)} %param.19) | copy-start | bytes 6148
  28.8 13.2 %copy-start.3 = (f32[1,32,16,256]{3,2,1,0:T(8,128)S(1)}, f32[1,32,16,256]{3,2,1,0:T(8,128)}, u32[]{:S(2)}) copy-start(f32[1,32,16,256]{3,2,1,0:T(8,128)} %param.15) | copy-start | bytes 1572868
  28.8 14.9 %collective-permute-start.4 = (f32[32,8,256]{2,1,0:T(8,128)S(1)}, f32[32,8,256]{2,1,0:T(8,128)S(1)}, u32[]{:S(2)}, u32[]{:S(2)}) collective-permute-start(f32[32,8,256]{2,1,0:T(8,128)S(1)} %get-tuple-element.40), channel_id=1, source_target_pairs={{1,2},{2,1},{3,4},{4,3},{5,6},{6,5},{7,8},{8,7},{9,10},{10,9},{11,... | collective-permute-start | bytes 786440 | tf_op jit(solution)/shard_map/ppermute | solution.py:21
  35.4 8.5 %collective-permute-start.5 = (f32[32,8,256]{2,1,0:T(8,128)S(1)}, f32[32,8,256]{2,1,0:T(8,128)S(1)}, u32[]{:S(2)}, u32[]{:S(2)}) collective-permute-start(f32[32,8,256]{2,1,0:T(8,128)S(1)} %get-tuple-element.41), channel_id=1, source_target_pairs={{0,1},{1,0},{2,3},{3,2},{4,5},{5,4},{6,7},{7,6},{8,9},{9,8},{10,11... | collective-permute-start | bytes 786440 | tf_op jit(solution)/shard_map/ppermute | solution.py:21
  37.3 6.4 %collective-permute-start.6 = (f32[8,16,256]{2,1,0:T(8,128)S(1)}, f32[8,16,256]{2,1,0:T(8,128)S(1)}, u32[]{:S(2)}, u32[]{:S(2)}) collective-permute-start(f32[8,16,256]{2,1,0:T(8,128)S(1)} %get-tuple-element.42), channel_id=1, source_target_pairs={{32,64},{64,32},{33,65},{65,33},{34,66},{66,34},{35,67},{67,35},{3... | collective-permute-start | bytes 393224 | tf_op jit(solution)/shard_map/ppermute | solution.py:21
  39.2 4.5 %collective-permute-start.7 = (f32[8,16,256]{2,1,0:T(8,128)S(1)}, f32[8,16,256]{2,1,0:T(8,128)S(1)}, u32[]{:S(2)}, u32[]{:S(2)}) collective-permute-start(f32[8,16,256]{2,1,0:T(8,128)S(1)} %get-tuple-element.43), channel_id=1, source_target_pairs={{0,32},{32,0},{64,96},{96,64},{1,33},{33,1},{65,97},{97,65},{2,34}... | collective-permute-start | bytes 393224 | tf_op jit(solution)/shard_map/ppermute | solution.py:21
  44.9 14.2 %collective-permute-start.8 = (f32[32,8,256]{2,1,0:T(8,128)S(1)}, f32[32,8,256]{2,1,0:T(8,128)S(1)}, u32[]{:S(2)}, u32[]{:S(2)}) collective-permute-start(f32[32,8,256]{2,1,0:T(8,128)S(1)} %get-tuple-element.54), channel_id=1, source_target_pairs={{1,2},{2,1},{3,4},{4,3},{5,6},{6,5},{7,8},{8,7},{9,10},{10,9},{11,... | collective-permute-start | bytes 786440 | tf_op jit(solution)/shard_map/ppermute | solution.py:21
  49.5 10.3 %collective-permute-start.9 = (f32[32,8,256]{2,1,0:T(8,128)S(1)}, f32[32,8,256]{2,1,0:T(8,128)S(1)}, u32[]{:S(2)}, u32[]{:S(2)}) collective-permute-start(f32[32,8,256]{2,1,0:T(8,128)S(1)} %get-tuple-element.55), channel_id=1, source_target_pairs={{0,1},{1,0},{2,3},{3,2},{4,5},{5,4},{6,7},{7,6},{8,9},{9,8},{10,11... | collective-permute-start | bytes 786440 | tf_op jit(solution)/shard_map/ppermute | solution.py:21
  51.5 6.3 %collective-permute-start.10 = (f32[8,16,256]{2,1,0:T(8,128)S(1)}, f32[8,16,256]{2,1,0:T(8,128)S(1)}, u32[]{:S(2)}, u32[]{:S(2)}) collective-permute-start(f32[8,16,256]{2,1,0:T(8,128)S(1)} %get-tuple-element.56), channel_id=1, source_target_pairs={{32,64},{64,32},{33,65},{65,33},{34,66},{66,34},{35,67},{67,35},{3... | collective-permute-start | bytes 393224 | tf_op jit(solution)/shard_map/ppermute | solution.py:21
  54.1 3.7 %collective-permute-start.11 = (f32[8,16,256]{2,1,0:T(8,128)S(1)}, f32[8,16,256]{2,1,0:T(8,128)S(1)}, u32[]{:S(2)}, u32[]{:S(2)}) collective-permute-start(f32[8,16,256]{2,1,0:T(8,128)S(1)} %get-tuple-element.57), channel_id=1, source_target_pairs={{0,32},{32,0},{64,96},{96,64},{1,33},{33,1},{65,97},{97,65},{2,34}... | collective-permute-start | bytes 393224 | tf_op jit(solution)/shard_map/ppermute | solution.py:21
  60.6 11.4 %collective-permute-start.12 = (f32[32,16,128]{2,1,0:T(8,128)S(1)}, f32[32,16,128]{2,1,0:T(8,128)S(1)}, u32[]{:S(2)}, u32[]{:S(2)}) collective-permute-start(f32[32,16,128]{2,1,0:T(8,128)S(1)} %get-tuple-element.65), channel_id=1, source_target_pairs={{0,256},{128,384},{256,0},{384,128},{1,257},{129,385},{257,1},{385... | collective-permute-start | bytes 786440 | tf_op jit(solution)/shard_map/ppermute | solution.py:34
  66.0 11.5 %collective-permute-start.13 = (f32[32,16,128]{2,1,0:T(8,128)S(1)}, f32[32,16,128]{2,1,0:T(8,128)S(1)}, u32[]{:S(2)}, u32[]{:S(2)}) collective-permute-start(f32[32,16,128]{2,1,0:T(8,128)S(1)} %get-tuple-element.66), channel_id=1, source_target_pairs={{128,256},{256,128},{384,0},{0,384},{129,257},{257,129},{385,1},{1... | collective-permute-start | bytes 786440 | tf_op jit(solution)/shard_map/ppermute | solution.py:29
  69.1 8.9 %collective-permute-start.14 = (f32[32,16,128]{2,1,0:T(8,128)S(1)}, f32[32,16,128]{2,1,0:T(8,128)S(1)}, u32[]{:S(2)}, u32[]{:S(2)}) collective-permute-start(f32[32,16,128]{2,1,0:T(8,128)S(1)} %get-tuple-element.67), channel_id=1, source_target_pairs={{0,128},{128,0},{256,384},{384,256},{1,129},{129,1},{257,385},{385... | collective-permute-start | bytes 786440 | tf_op jit(solution)/shard_map/ppermute | solution.py:29

commit v10 on v9

--- a/solution.py
+++ b/solution.py
@@ -167,13 +167,19 @@
     return [slice(h * HALF, (h + 1) * HALF) for h in range(2)]
 
 
-def put_edges(field, row, ya, yb, xa, xb, plane):
-    even_y, even_x = even("gy"), even("gx")
-    size_x, size_y = field.shape[0], field.shape[1]
-    first, last = field[:, 0:4, :], field[:, size_y - 4 : size_y, :]
-    ya[:, row : row + 4, :] = jnp.where(even_y, last, first)
-    yb[:, row : row + 4, :] = jnp.where(even_y, first, last)
-    top = size_x - 4
+def put_rows(one, two, ya, yb, x, z):
+    size_y = one.shape[0]
+    upper = lax.broadcasted_iota(jnp.int32, (8, HALF), 0) < 4
+    first = jnp.where(upper, one[0:8], pltpu.roll(two[0:8], 4, 0))
+    last = jnp.where(upper, pltpu.roll(one[size_y - 8 :], 4, 0), two[size_y - 8 :])
+    even_y = even("gy")
+    ya[x, :, z] = jnp.where(even_y, last, first)
+    yb[x, :, z] = jnp.where(even_y, first, last)
+
+
+def put_planes(field, xa, xb, plane):
+    even_x = even("gx")
+    top = field.shape[0] - 4
     xa[plane : plane + 4] = field[pl.ds(jnp.where(even_x, top, 0), 4)]
     xb[plane : plane + 4] = field[pl.ds(jnp.where(even_x, 0, top), 4)]
 
@@ -300,14 +306,17 @@
         for h, z in enumerate(halves()):
             v = jnp.where(lane < HALF - shift_by, rolled[h], rolled[h + 1])
             vel[x, :, z] = v
-            image[x, :, z] = v * adj4[x, :, z]
             wave = 2.0 * wave1[x, :, z] - wave0[x, :, z] + v * lap1[x, :, z]
-            wave2[x, :, z] = wave + jnp.where(plane == x, amounts[h], 0.0)
+            wave = wave + jnp.where(plane == x, amounts[h], 0.0)
+            product4 = v * adj4[x, :, z]
+            wave2[x, :, z] = wave
+            image[x, :, z] = product4
+            put_rows(wave, product4, ya, yb, x, z)
         return 0
 
     lax.fori_loop(0, size_x, body, 0, unroll=4)
-    put_edges(wave2, 0, ya, yb, xa, xb, 0)
-    put_edges(image, 4, ya, yb, xa, xb, 4)
+    put_planes(wave2, xa, xb, 0)
+    put_planes(image, xa, xb, 4)
 
 
 def third_inner_kernel(
@@ -338,12 +347,14 @@
             v = vel[x, :, z]
             extra = outer_of(side, row, x, z)
             lap2[x, :, z] = lap2_in[x, :, z] + extra
-            wave3[x, :, z] = wave3_in[x, :, z] + v * extra
+            wave = wave3_in[x, :, z] + v * extra
+            wave3[x, :, z] = wave
             adj = adj3_in[x, :, z] + outer_of(side2, row2, x, z)
             adj3[x, :, z] = adj
             image3[x, :, z] = v * adj
-    put_edges(wave3, 0, pya, pyb, pxa, pxb, 0)
-    put_edges(image3, 4, pya, pyb, pxa, pxb, 4)
+            put_rows(wave, v * adj, pya, pyb, x, z)
+    put_planes(wave3, pxa, pxb, 0)
+    put_planes(image3, pxa, pxb, 4)
 
 
 def fourth_inner_kernel(

time: 79.4 us -> 79.1 us (level)
  no operation moved by 1% of the time
where the time goes in v10:
time: 79.1 us; the launch traced here: 78.5 us
  starting transfers between devices  56.1 us (71%)
  Pallas kernels  10.1 us (13%)
  waiting for transfers between devices  9.04 us (11%)
  local copies, waits for them, and re-layouts  1.64 us (2%)
  between operations  1.6 us (2%)
    ppermute x12, starting transfers between devices, swap(): return lax.ppermute(value, axis, pairs)  41.3 us
    ppermute x2, waiting for transfers between devices, swap_shot(): return lax.ppermute(value, 'shot', pairs)  6 us
    ppermute x1, starting transfers between devices, swap_across(): lax.ppermute(value, 'shot', [(i, (i + size // 2) % size) for i in range(s...  5.44 us
    ppermute x2, starting transfers between devices, swap_shot(): return lax.ppermute(value, 'shot', pairs)  4.99 us
    all_to_all x1, starting transfers between devices, local(): column = lax.all_to_all(copies, 'shot', 0, 0)  4.44 us
    ppermute x12, waiting for transfers between devices, swap(): return lax.ppermute(value, axis, pairs)  2.88 us
    unnamed x19, local copies, waits for them, and re-layouts  1.64 us
    pallas_call x1, Pallas kernels, local(): call(third_inner_kernel, (block,) * 3, (whole,) * 2, n_in=11, room=10)  1.63 us
  transfers between devices with their start and end apart: 16, of which 8 were waited for; matrix products, arithmetic and copies ran while one was open for 0% of the time, Pallas kernels for 7%

profile of v10, /device:TPU:24, one launch (start us, length us, event | category | flops | bytes accessed | tf_op | source)
XLA Modules:
  0.0 78.5 jit_solution(13860651519351076084)
XLA Ops:
  0.6 0.9 %copy-done.4 = f32[32,16,128]{2,1,0:T(8,128)S(1)} copy-done((f32[32,16,128]{2,1,0:T(8,128)S(1)}, f32[32,16,128]{2,1,0:T(8,128)}, u32[]{:S(2)}) %copy-start.4) | copy-done | bytes 262168
  1.6 1.0 %shard_map.113 = f32[4,32,16,128]{3,2,1,0:T(8,128)} custom-call(f32[32,16,128]{2,1,0:T(8,128)S(1)} %copy-done.4), custom_call_target="tpu_custom_call" | custom-call | tf_op jit(solution)/shard_map/pallas_call | solution.py:427
  2.6 4.4 %all-to-all-start = ((f32[4,32,16,128]{3,2,1,0:T(8,128)}), f32[4,32,16,128]{3,2,1,0:T(8,128)S(1)}, u32[]{:S(2)}, u32[]{:S(2)}) async-start(f32[4,32,16,128]{3,2,1,0:T(8,128)} %shard_map.113), calls=%async_computation | async-start | bytes 2097152 | tf_op jit(solution)/shard_map/all_to_all | solution.py:435
  7.1 12.2 %collective-permute-start = (f32[16,8,256]{2,1,0:T(8,128)S(1)}, f32[16,8,256]{2,1,0:T(8,128)S(1)}, u32[]{:S(2)}, u32[]{:S(2)}) collective-permute-start(f32[16,8,256]{2,1,0:T(8,128)S(1)} %get-tuple-element.36), channel_id=1, source_target_pairs={{1,2},{2,1},{3,4},{4,3},{5,6},{6,5},{7,8},{8,7},{9,10},{10,9},{11,... | collective-permute-start | bytes 393224 | tf_op jit(solution)/shard_map/ppermute | solution.py:21
  19.4 1.9 %collective-permute-start.1 = (f32[16,8,256]{2,1,0:T(8,128)S(1)}, f32[16,8,256]{2,1,0:T(8,128)S(1)}, u32[]{:S(2)}, u32[]{:S(2)}) collective-permute-start(f32[16,8,256]{2,1,0:T(8,128)S(1)} %get-tuple-element.37), channel_id=1, source_target_pairs={{0,1},{1,0},{2,3},{3,2},{4,5},{5,4},{6,7},{7,6},{8,9},{9,8},{10,11... | collective-permute-start | bytes 393224 | tf_op jit(solution)/shard_map/ppermute | solution.py:21
  21.3 1.9 %collective-permute-start.2 = (f32[4,16,256]{2,1,0:T(8,128)S(1)}, f32[4,16,256]{2,1,0:T(8,128)S(1)}, u32[]{:S(2)}, u32[]{:S(2)}) collective-permute-start(f32[4,16,256]{2,1,0:T(8,128)S(1)} %get-tuple-element.38), channel_id=1, source_target_pairs={{32,64},{64,32},{33,65},{65,33},{34,66},{66,34},{35,67},{67,35},{3... | collective-permute-start | bytes 196616 | tf_op jit(solution)/shard_map/ppermute | solution.py:21
  23.2 1.9 %collective-permute-start.3 = (f32[4,16,256]{2,1,0:T(8,128)S(1)}, f32[4,16,256]{2,1,0:T(8,128)S(1)}, u32[]{:S(2)}, u32[]{:S(2)}) collective-permute-start(f32[4,16,256]{2,1,0:T(8,128)S(1)} %get-tuple-element.39), channel_id=1, source_target_pairs={{0,32},{32,0},{64,96},{96,64},{1,33},{33,1},{65,97},{97,65},{2,34}... | collective-permute-start | bytes 196616 | tf_op jit(solution)/shard_map/ppermute | solution.py:21
  26.2 0.6 copy-done.5
  26.9 0.8 %shard_map.115.inner = f32[32,16,256]{2,1,0:T(8,128)S(1)} custom-call(f32[32,16,256]{2,1,0:T(8,128)S(1)} %bitcast.19, f32[16,8,256]{2,1,0:T(8,128)S(1)} %collective-permute-done.yb, f32[16,8,256]{2,1,0:T(8,128)S(1)} %collective-permute-done.1.ya, f32[32,16,256]{2,1,0:T(8,128)S(1)} %bitcast.22, f32[32,16,256]{2,1,0:T(8,128)S(1)} %bitcast.13, ...), custom_call_target="tpu_custom_call" | custom-call | tf_op jit(solution)/shard_map/pallas_call | solution.py:443
  27.8 0.9 %shard_map.117 = (f32[32,16,256]{2,1,0:T(8,128)S(1)}, f32[32,16,256]{2,1,0:T(8,128)S(1)}, f32[32,16,256]{2,1,0:T(8,128)S(1)}, f32[32,8,256]{2,1,0:T(8,128)S(1)},...) custom-call(s32[1]{0:T(128)S(6)} %copy.23.offsets, ...), custom_call_target="tpu_custom_call" | custom-call | tf_op jit(solution)/shard_map/pallas_call | solution.py:447
  28.7 6.5 %collective-permute-start.4 = (f32[32,8,256]{2,1,0:T(8,128)S(1)}, f32[32,8,256]{2,1,0:T(8,128)S(1)}, u32[]{:S(2)}, u32[]{:S(2)}) collective-permute-start(f32[32,8,256]{2,1,0:T(8,128)S(1)} %get-tuple-element.40), channel_id=1, source_target_pairs={{1,2},{2,1},{3,4},{4,3},{5,6},{6,5},{7,8},{8,7},{9,10},{10,9},{11,... | collective-permute-start | bytes 786440 | tf_op jit(solution)/shard_map/ppermute | solution.py:21
  35.3 1.9 %collective-permute-start.5 = (f32[32,8,256]{2,1,0:T(8,128)S(1)}, f32[32,8,256]{2,1,0:T(8,128)S(1)}, u32[]{:S(2)}, u32[]{:S(2)}) collective-permute-start(f32[32,8,256]{2,1,0:T(8,128)S(1)} %get-tuple-element.41), channel_id=1, source_target_pairs={{0,1},{1,0},{2,3},{3,2},{4,5},{5,4},{6,7},{7,6},{8,9},{9,8},{10,11... | collective-permute-start | bytes 786440 | tf_op jit(solution)/shard_map/ppermute | solution.py:21
  37.2 1.9 %collective-permute-start.6 = (f32[8,16,256]{2,1,0:T(8,128)S(1)}, f32[8,16,256]{2,1,0:T(8,128)S(1)}, u32[]{:S(2)}, u32[]{:S(2)}) collective-permute-start(f32[8,16,256]{2,1,0:T(8,128)S(1)} %get-tuple-element.42), channel_id=1, source_target_pairs={{32,64},{64,32},{33,65},{65,33},{34,66},{66,34},{35,67},{67,35},{3... | collective-permute-start | bytes 393224 | tf_op jit(solution)/shard_map/ppermute | solution.py:21
  39.1 1.9 %collective-permute-start.7 = (f32[8,16,256]{2,1,0:T(8,128)S(1)}, f32[8,16,256]{2,1,0:T(8,128)S(1)}, u32[]{:S(2)}, u32[]{:S(2)}) collective-permute-start(f32[8,16,256]{2,1,0:T(8,128)S(1)} %get-tuple-element.43), channel_id=1, source_target_pairs={{0,32},{32,0},{64,96},{96,64},{1,33},{33,1},{65,97},{97,65},{2,34}... | collective-permute-start | bytes 393224 | tf_op jit(solution)/shard_map/ppermute | solution.py:21
  41.1 0.8 %shard_map.118 = (f32[32,16,256]{2,1,0:T(8,128)S(1)}, f32[32,16,256]{2,1,0:T(8,128)S(1)}, bf16[256,256]{1,0:T(8,128)(2,1)S(1)}, bf16[256,256]{1,0:T(8,128)(2,1)S(1)}, bf16[2,128,256]{2,1,0:T(8,128)(2,1)S(1)}) custom-call(s32[3,256]{1,0:T(4,128)S(1)} %bitcast.25, f32[2,256]{1,0:T(2,128)S(1)} %bitcast.26, f32[32,16,256]{2,1,0:T(8,128)S(1)} %get-tuple-element.45.other.vel), custom_call_target="tpu_custom_call" | custom-call | tf_op jit(solution)/shard_map/pallas_call | solution.py:451
  41.9 1.6 %shard_map.119 = (f32[32,16,256]{2,1,0:T(8,128)S(1)}, f32[32,16,256]{2,1,0:T(8,128)S(1)}, f32[32,16,256]{2,1,0:T(8,128)S(1)}) custom-call(f32[32,16,256]{2,1,0:T(8,128)S(1)} %bitcast.21, f32[32,16,256]{2,1,0:T(8,128)S(1)} %get-tuple-element.44.wave2, f32[32,16,256]{2,1,0:T(8,128)S(1)} %bitcast.15, f32[32,16,256]{2,1,0:T(8,128)S(1)} %bitcast.24, ...), custom_call_target="tpu_custom_call" | custom-call | tf_op jit(solution)/shard_map/pallas_call | solution.py:459
  43.8 0.9 %shard_map.120 = (f32[32,16,256]{2,1,0:T(8,128)S(1)}, f32[32,16,256]{2,1,0:T(8,128)S(1)}, f32[32,16,256]{2,1,0:T(8,128)S(1)}, f32[32,16,256]{2,1,0:T(8,128)S(1)}...) custom-call(f32[32,8,256]{2,1,0:T(8,128)S(1)} %collective-permute-do, ...), custom_call_target="tpu_custom_call", output_to_operand_aliasing={{0}: (4, {}), {1}: (5, {}), {2}: (6, {})} | custom-call | tf_op jit(solution)/shard_map/pallas_call | solution.py:462
  44.6 4.6 %collective-permute-start.8 = (f32[32,8,256]{2,1,0:T(8,128)S(1)}, f32[32,8,256]{2,1,0:T(8,128)S(1)}, u32[]{:S(2)}, u32[]{:S(2)}) collective-permute-start(f32[32,8,256]{2,1,0:T(8,128)S(1)} %get-tuple-element.54), channel_id=1, source_target_pairs={{1,2},{2,1},{3,4},{4,3},{5,6},{6,5},{7,8},{8,7},{9,10},{10,9},{11,... | collective-permute-start | bytes 786440 | tf_op jit(solution)/shard_map/ppermute | solution.py:21
  49.2 1.9 %collective-permute-start.9 = (f32[32,8,256]{2,1,0:T(8,128)S(1)}, f32[32,8,256]{2,1,0:T(8,128)S(1)}, u32[]{:S(2)}, u32[]{:S(2)}) collective-permute-start(f32[32,8,256]{2,1,0:T(8,128)S(1)} %get-tuple-element.55), channel_id=1, source_target_pairs={{0,1},{1,0},{2,3},{3,2},{4,5},{5,4},{6,7},{7,6},{8,9},{9,8},{10,11... | collective-permute-start | bytes 786440 | tf_op jit(solution)/shard_map/ppermute | solution.py:21
  51.1 2.6 %collective-permute-start.10 = (f32[8,16,256]{2,1,0:T(8,128)S(1)}, f32[8,16,256]{2,1,0:T(8,128)S(1)}, u32[]{:S(2)}, u32[]{:S(2)}) collective-permute-start(f32[8,16,256]{2,1,0:T(8,128)S(1)} %get-tuple-element.56), channel_id=1, source_target_pairs={{32,64},{64,32},{33,65},{65,33},{34,66},{66,34},{35,67},{67,35},{3... | collective-permute-start | bytes 393224 | tf_op jit(solution)/shard_map/ppermute | solution.py:21
  53.7 1.9 %collective-permute-start.11 = (f32[8,16,256]{2,1,0:T(8,128)S(1)}, f32[8,16,256]{2,1,0:T(8,128)S(1)}, u32[]{:S(2)}, u32[]{:S(2)}) collective-permute-start(f32[8,16,256]{2,1,0:T(8,128)S(1)} %get-tuple-element.57), channel_id=1, source_target_pairs={{0,32},{32,0},{64,96},{96,64},{1,33},{33,1},{65,97},{97,65},{2,34}... | collective-permute-start | bytes 393224 | tf_op jit(solution)/shard_map/ppermute | solution.py:21
  55.7 1.6 %shard_map.121 = (f32[32,16,256]{2,1,0:T(8,128)S(1)}, f32[32,16,256]{2,1,0:T(8,128)S(1)}) custom-call(f32[32,16,256]{2,1,0:T(8,128)S(1)} %get-tuple-element.58.wave3, f32[32,16,256]{2,1,0:T(8,128)S(1)} %get-tuple-element.59.image3, f32[32,16,256]{2,1,0:T(8,128)S(1)} %get-tuple-element.60.adj3, f32[32,16,256]{2,1,0:T(8,128)S(1)} %bitcast.16, ...), custom_call_target="tpu_custom_call" | custom-call | tf_op jit(solution)/shard_map/pallas_call | solution.py:467
  57.4 1.4 %collective-permute-done.8.yb = f32[32,8,256]{2,1,0:T(8,128)S(1)} collective-permute-done((f32[32,8,256]{2,1,0:T(8,128)S(1)}, f32[32,8,256]{2,1,0:T(8,128)S(1)}, u32[]{:S(2)}, u32[]{:S(2)}) %collective-permute-start.8) | collective-permute-done | bytes 262176 | tf_op jit(solution)/shard_map/ppermute | solution.py:21
  58.8 0.7 collective-permute-done.9.ya
  59.5 0.7 shard_map.122
  60.3 5.4 %collective-permute-start.12 = (f32[32,16,128]{2,1,0:T(8,128)S(1)}, f32[32,16,128]{2,1,0:T(8,128)S(1)}, u32[]{:S(2)}, u32[]{:S(2)}) collective-permute-start(f32[32,16,128]{2,1,0:T(8,128)S(1)} %get-tuple-element.65), channel_id=1, source_target_pairs={{0,256},{128,384},{256,0},{384,128},{1,257},{129,385},{257,1},{385... | collective-permute-start | bytes 786440 | tf_op jit(solution)/shard_map/ppermute | solution.py:34
  65.7 3.1 %collective-permute-start.13 = (f32[32,16,128]{2,1,0:T(8,128)S(1)}, f32[32,16,128]{2,1,0:T(8,128)S(1)}, u32[]{:S(2)}, u32[]{:S(2)}) collective-permute-start(f32[32,16,128]{2,1,0:T(8,128)S(1)} %get-tuple-element.66), channel_id=1, source_target_pairs={{128,256},{256,128},{384,0},{0,384},{129,257},{257,129},{385,1},{1... | collective-permute-start | bytes 786440 | tf_op jit(solution)/shard_map/ppermute | solution.py:29
  68.8 1.9 %collective-permute-start.14 = (f32[32,16,128]{2,1,0:T(8,128)S(1)}, f32[32,16,128]{2,1,0:T(8,128)S(1)}, u32[]{:S(2)}, u32[]{:S(2)}) collective-permute-start(f32[32,16,128]{2,1,0:T(8,128)S(1)} %get-tuple-element.67), channel_id=1, source_target_pairs={{0,128},{128,0},{256,384},{384,256},{1,129},{129,1},{257,385},{385... | collective-permute-start | bytes 786440 | tf_op jit(solution)/shard_map/ppermute | solution.py:29
  70.7 0.8 %shard_map.124 = f32[32,16,256]{2,1,0:T(8,128)} custom-call(f32[32,16,256]{2,1,0:T(8,128)S(1)} %get-tuple-element.68.adj2_in, f32[32,16,256]{2,1,0:T(8,128)S(1)} %get-tuple-element.69.extra), custom_call_target="tpu_custom_call" | custom-call | tf_op jit(solution)/shard_map/pallas_call | solution.py:474
  71.7 5.5 %collective-permute-done.13.b = f32[32,16,128]{2,1,0:T(8,128)S(1)} collective-permute-done((f32[32,16,128]{2,1,0:T(8,128)S(1)}, f32[32,16,128]{2,1,0:T(8,128)S(1)}, u32[]{:S(2)}, u32[]{:S(2)}) %collective-permute-start.13) | collective-permute-done | bytes 262176 | tf_op jit(solution)/shard_map/ppermute | solution.py:29
  77.2 0.5 collective-permute-done.14.a
  77.7 0.8 shard_map.123
  (31 shorter events, 1.1 us)
Async XLA Ops:
  0.6 1.0 %copy-start.4 = (f32[32,16,128]{2,1,0:T(8,128)S(1)}, f32[32,16,128]{2,1,0:T(8,128)}, u32[]{:S(2)}) copy-start(f32[32,16,128]{2,1,0:T(8,128)} %tile.1) | copy-start | bytes 786436
  2.6 4.5 %copy-start.1 = (f32[1,32,16,256]{3,2,1,0:T(8,128)S(1)}, f32[1,32,16,256]{3,2,1,0:T(8,128)}, u32[]{:S(2)}) copy-start(f32[1,32,16,256]{3,2,1,0:T(8,128)} %param.13) | copy-start | bytes 1572868
  2.6 23.6 %copy-start.2 = (f32[1,32,16,256]{3,2,1,0:T(8,128)S(1)}, f32[1,32,16,256]{3,2,1,0:T(8,128)}, u32[]{:S(2)}) copy-start(f32[1,32,16,256]{3,2,1,0:T(8,128)} %param.12) | copy-start | bytes 1572868
  2.6 25.2 %all-to-all-start = ((f32[4,32,16,128]{3,2,1,0:T(8,128)}), f32[4,32,16,128]{3,2,1,0:T(8,128)S(1)}, u32[]{:S(2)}, u32[]{:S(2)}) async-start(f32[4,32,16,128]{3,2,1,0:T(8,128)} %shard_map.113), calls=%async_computation | async-start | bytes 2097152 | tf_op jit(solution)/shard_map/all_to_all | solution.py:435
  7.1 19.2 %copy-start = (f32[1,32,16,256]{3,2,1,0:T(8,128)S(1)}, f32[1,32,16,256]{3,2,1,0:T(8,128)}, u32[]{:S(2)}) copy-start(f32[1,32,16,256]{3,2,1,0:T(8,128)} %param.14) | copy-start | bytes 1572868
  7.1 18.6 %collective-permute-start = (f32[16,8,256]{2,1,0:T(8,128)S(1)}, f32[16,8,256]{2,1,0:T(8,128)S(1)}, u32[]{:S(2)}, u32[]{:S(2)}) collective-permute-start(f32[16,8,256]{2,1,0:T(8,128)S(1)} %get-tuple-element.36), channel_id=1, source_target_pairs={{1,2},{2,1},{3,4},{4,3},{5,6},{6,5},{7,8},{8,7},{9,10},{10,9},{11,... | collective-permute-start | bytes 393224 | tf_op jit(solution)/shard_map/ppermute | solution.py:21
  19.4 6.9 %collective-permute-start.1 = (f32[16,8,256]{2,1,0:T(8,128)S(1)}, f32[16,8,256]{2,1,0:T(8,128)S(1)}, u32[]{:S(2)}, u32[]{:S(2)}) collective-permute-start(f32[16,8,256]{2,1,0:T(8,128)S(1)} %get-tuple-element.37), channel_id=1, source_target_pairs={{0,1},{1,0},{2,3},{3,2},{4,5},{5,4},{6,7},{7,6},{8,9},{9,8},{10,11... | collective-permute-start | bytes 393224 | tf_op jit(solution)/shard_map/ppermute | solution.py:21
  21.3 6.4 %collective-permute-start.2 = (f32[4,16,256]{2,1,0:T(8,128)S(1)}, f32[4,16,256]{2,1,0:T(8,128)S(1)}, u32[]{:S(2)}, u32[]{:S(2)}) collective-permute-start(f32[4,16,256]{2,1,0:T(8,128)S(1)} %get-tuple-element.38), channel_id=1, source_target_pairs={{32,64},{64,32},{33,65},{65,33},{34,66},{66,34},{35,67},{67,35},{3... | collective-permute-start | bytes 196616 | tf_op jit(solution)/shard_map/ppermute | solution.py:21
  23.2 4.5 %collective-permute-start.3 = (f32[4,16,256]{2,1,0:T(8,128)S(1)}, f32[4,16,256]{2,1,0:T(8,128)S(1)}, u32[]{:S(2)}, u32[]{:S(2)}) collective-permute-start(f32[4,16,256]{2,1,0:T(8,128)S(1)} %get-tuple-element.39), channel_id=1, source_target_pairs={{0,32},{32,0},{64,96},{96,64},{1,33},{33,1},{65,97},{97,65},{2,34}... | collective-permute-start | bytes 196616 | tf_op jit(solution)/shard_map/ppermute | solution.py:21
  26.2 0.7 copy-start.5
  26.2 0.7 copy-start.6
  27.8 13.3 %copy-start.8 = (s32[1,256,3]{1,0,2:T(1,128)S(1)}, s32[1,256,3]{1,0,2:T(1,128)}, u32[]{:S(2)}) copy-start(s32[1,256,3]{1,0,2:T(1,128)} %param.18) | copy-start | bytes 9220
  27.8 13.3 %copy-start.7 = (f32[1,256,2]{1,2,0:T(2,128)S(1)}, f32[1,256,2]{1,2,0:T(2,128)}, u32[]{:S(2)}) copy-start(f32[1,256,2]{1,2,0:T(2,128)} %param.19) | copy-start | bytes 6148
  28.7 13.2 %copy-start.3 = (f32[1,32,16,256]{3,2,1,0:T(8,128)S(1)}, f32[1,32,16,256]{3,2,1,0:T(8,128)}, u32[]{:S(2)}) copy-start(f32[1,32,16,256]{3,2,1,0:T(8,128)} %param.15) | copy-start | bytes 1572868
  28.7 14.9 %collective-permute-start.4 = (f32[32,8,256]{2,1,0:T(8,128)S(1)}, f32[32,8,256]{2,1,0:T(8,128)S(1)}, u32[]{:S(2)}, u32[]{:S(2)}) collective-permute-start(f32[32,8,256]{2,1,0:T(8,128)S(1)} %get-tuple-element.40), channel_id=1, source_target_pairs={{1,2},{2,1},{3,4},{4,3},{5,6},{6,5},{7,8},{8,7},{9,10},{10,9},{11,... | collective-permute-start | bytes 786440 | tf_op jit(solution)/shard_map/ppermute | solution.py:21
  35.3 8.5 %collective-permute-start.5 = (f32[32,8,256]{2,1,0:T(8,128)S(1)}, f32[32,8,256]{2,1,0:T(8,128)S(1)}, u32[]{:S(2)}, u32[]{:S(2)}) collective-permute-start(f32[32,8,256]{2,1,0:T(8,128)S(1)} %get-tuple-element.41), channel_id=1, source_target_pairs={{0,1},{1,0},{2,3},{3,2},{4,5},{5,4},{6,7},{7,6},{8,9},{9,8},{10,11... | collective-permute-start | bytes 786440 | tf_op jit(solution)/shard_map/ppermute | solution.py:21
  37.2 6.4 %collective-permute-start.6 = (f32[8,16,256]{2,1,0:T(8,128)S(1)}, f32[8,16,256]{2,1,0:T(8,128)S(1)}, u32[]{:S(2)}, u32[]{:S(2)}) collective-permute-start(f32[8,16,256]{2,1,0:T(8,128)S(1)} %get-tuple-element.42), channel_id=1, source_target_pairs={{32,64},{64,32},{33,65},{65,33},{34,66},{66,34},{35,67},{67,35},{3... | collective-permute-start | bytes 393224 | tf_op jit(solution)/shard_map/ppermute | solution.py:21
  39.1 4.5 %collective-permute-start.7 = (f32[8,16,256]{2,1,0:T(8,128)S(1)}, f32[8,16,256]{2,1,0:T(8,128)S(1)}, u32[]{:S(2)}, u32[]{:S(2)}) collective-permute-start(f32[8,16,256]{2,1,0:T(8,128)S(1)} %get-tuple-element.43), channel_id=1, source_target_pairs={{0,32},{32,0},{64,96},{96,64},{1,33},{33,1},{65,97},{97,65},{2,34}... | collective-permute-start | bytes 393224 | tf_op jit(solution)/shard_map/ppermute | solution.py:21
  44.6 14.2 %collective-permute-start.8 = (f32[32,8,256]{2,1,0:T(8,128)S(1)}, f32[32,8,256]{2,1,0:T(8,128)S(1)}, u32[]{:S(2)}, u32[]{:S(2)}) collective-permute-start(f32[32,8,256]{2,1,0:T(8,128)S(1)} %get-tuple-element.54), channel_id=1, source_target_pairs={{1,2},{2,1},{3,4},{4,3},{5,6},{6,5},{7,8},{8,7},{9,10},{10,9},{11,... | collective-permute-start | bytes 786440 | tf_op jit(solution)/shard_map/ppermute | solution.py:21
  49.2 10.3 %collective-permute-start.9 = (f32[32,8,256]{2,1,0:T(8,128)S(1)}, f32[32,8,256]{2,1,0:T(8,128)S(1)}, u32[]{:S(2)}, u32[]{:S(2)}) collective-permute-start(f32[32,8,256]{2,1,0:T(8,128)S(1)} %get-tuple-element.55), channel_id=1, source_target_pairs={{0,1},{1,0},{2,3},{3,2},{4,5},{5,4},{6,7},{7,6},{8,9},{9,8},{10,11... | collective-permute-start | bytes 786440 | tf_op jit(solution)/shard_map/ppermute | solution.py:21
  51.1 6.3 %collective-permute-start.10 = (f32[8,16,256]{2,1,0:T(8,128)S(1)}, f32[8,16,256]{2,1,0:T(8,128)S(1)}, u32[]{:S(2)}, u32[]{:S(2)}) collective-permute-start(f32[8,16,256]{2,1,0:T(8,128)S(1)} %get-tuple-element.56), channel_id=1, source_target_pairs={{32,64},{64,32},{33,65},{65,33},{34,66},{66,34},{35,67},{67,35},{3... | collective-permute-start | bytes 393224 | tf_op jit(solution)/shard_map/ppermute | solution.py:21
  53.7 3.7 %collective-permute-start.11 = (f32[8,16,256]{2,1,0:T(8,128)S(1)}, f32[8,16,256]{2,1,0:T(8,128)S(1)}, u32[]{:S(2)}, u32[]{:S(2)}) collective-permute-start(f32[8,16,256]{2,1,0:T(8,128)S(1)} %get-tuple-element.57), channel_id=1, source_target_pairs={{0,32},{32,0},{64,96},{96,64},{1,33},{33,1},{65,97},{97,65},{2,34}... | collective-permute-start | bytes 393224 | tf_op jit(solution)/shard_map/ppermute | solution.py:21
  60.3 11.5 %collective-permute-start.12 = (f32[32,16,128]{2,1,0:T(8,128)S(1)}, f32[32,16,128]{2,1,0:T(8,128)S(1)}, u32[]{:S(2)}, u32[]{:S(2)}) collective-permute-start(f32[32,16,128]{2,1,0:T(8,128)S(1)} %get-tuple-element.65), channel_id=1, source_target_pairs={{0,256},{128,384},{256,0},{384,128},{1,257},{129,385},{257,1},{385... | collective-permute-start | bytes 786440 | tf_op jit(solution)/shard_map/ppermute | solution.py:34
  65.7 11.5 %collective-permute-start.13 = (f32[32,16,128]{2,1,0:T(8,128)S(1)}, f32[32,16,128]{2,1,0:T(8,128)S(1)}, u32[]{:S(2)}, u32[]{:S(2)}) collective-permute-start(f32[32,16,128]{2,1,0:T(8,128)S(1)} %get-tuple-element.66), channel_id=1, source_target_pairs={{128,256},{256,128},{384,0},{0,384},{129,257},{257,129},{385,1},{1... | collective-permute-start | bytes 786440 | tf_op jit(solution)/shard_map/ppermute | solution.py:29
  68.8 8.9 %collective-permute-start.14 = (f32[32,16,128]{2,1,0:T(8,128)S(1)}, f32[32,16,128]{2,1,0:T(8,128)S(1)}, u32[]{:S(2)}, u32[]{:S(2)}) collective-permute-start(f32[32,16,128]{2,1,0:T(8,128)S(1)} %get-tuple-element.67), channel_id=1, source_target_pairs={{0,128},{128,0},{256,384},{384,256},{1,129},{129,1},{257,385},{385... | collective-permute-start | bytes 786440 | tf_op jit(solution)/shard_map/ppermute | solution.py:29

commit v11 on v10

--- a/solution.py
+++ b/solution.py
@@ -244,10 +244,14 @@
         outer[field] = both.astype(jnp.bfloat16)
 
 
-def tables_kernel(size_x, size_y, cells, res, other, inject0, inject1, along_y, along_z, outer):
+def tables_kernel(size_x, size_y, cells, res, other, inject, along_y, along_z, outer):
     difference_matrices(size_y, along_y, along_z)
     outer_matrices(size_x, size_y, outer)
-    depth = inject0.shape[2]
+    inject_kernel(size_x, size_y, 0, cells, res, other, inject)
+
+
+def inject_kernel(size_x, size_y, step, cells, res, other, inject):
+    depth = inject.shape[2]
     half = size_x // 2
     rows = half * size_y
     count = cells.shape[1]
@@ -256,15 +260,12 @@
     inside = (x >= 0) & (x < size_x) & (y >= 0) & (y < size_y)
     place = jnp.where(inside, x * size_y + y, -1)
     deep = index((depth, count), 0) == cells[2:3, :]
-    parts = [three(jnp.where(deep, res[n : n + 1, :], 0.0)) for n in range(2)]
+    parts = three(jnp.where(deep, res[step : step + 1, :], 0.0))
     for part in range(2):
         at = index((rows, count), 0) + part * rows
         flat = jnp.where(at == place, 1.0, 0.0).astype(jnp.bfloat16)
-        for n, out in enumerate((inject0, inject1)):
-            done = sum(
-                lax.dot_general(flat, p, (((1,), (1,)), ((), ())), preferred_element_type=F32) for p in parts[n]
-            )
-            out[part * half : (part + 1) * half] = done.reshape(half, size_y, depth)
+        done = sum(lax.dot_general(flat, p, (((1,), (1,)), ((), ())), preferred_element_type=F32) for p in parts)
+        inject[part * half : (part + 1) * half] = done.reshape(half, size_y, depth)
 
 
 def first_inner_kernel(wave1, yb, ya, next0, next1, cell, amp, lap1, flat, along_y, along_z, outer, row):
@@ -448,13 +449,14 @@
         second_kernel, (block,) * 3 + (edge_y,) * 2 + (edge_x,) * 2,
         smem=1, n_in=7, room=4,
     )(offsets, column, lap1, wave0, wave1, adj4, src_cell, src_amp)
-    inject0, inject1, along_y, along_z, outer = pl.pallas_call(
+    cells, res = jnp.transpose(rec_cell[0]), jnp.transpose(rec_res[0])
+    inject0, along_y, along_z, outer = pl.pallas_call(
         functools.partial(tables_kernel, size_x, size_y),
-        out_shape=(block, block, *(jax.ShapeDtypeStruct(dims, bf16) for dims in matrices)),
+        out_shape=(block, *(jax.ShapeDtypeStruct(dims, bf16) for dims in matrices)),
         in_specs=[pl.BlockSpec(memory_space=pltpu.VMEM)] * 2 + [pl.BlockSpec(memory_space=pl.ANY)],
-        out_specs=(pl.BlockSpec(memory_space=pltpu.VMEM),) * 5,
+        out_specs=(pl.BlockSpec(memory_space=pltpu.VMEM),) * 4,
         compiler_params=pltpu.CompilerParams(vmem_limit_bytes=4 << 20),
-    )(jnp.transpose(rec_cell[0]), jnp.transpose(rec_res[0]), vel)
+    )(cells, res, vel)
     halos = exchange(edges)
     inner = call(third_inner_kernel, (block,) * 3, (whole,) * 2, n_in=11, room=10)(
         wave1, wave2, adj4, adj5, vel, image, src_cell, src_amp, inject0, along_y, along_z
@@ -464,6 +466,13 @@
         room=10, aliases={4: 0, 5: 1, 6: 2},
     )(*halos, *inner, vel, outer)
     halos = exchange(edges)
+    inject1 = pl.pallas_call(
+        functools.partial(inject_kernel, size_x, size_y, 1),
+        out_shape=block,
+        in_specs=[pl.BlockSpec(memory_space=pltpu.VMEM)] * 2 + [pl.BlockSpec(memory_space=pl.ANY)],
+        out_specs=pl.BlockSpec(memory_space=pltpu.VMEM),
+        compiler_params=pltpu.CompilerParams(vmem_limit_bytes=4 << 20),
+    )(cells, res, adj3)
     inner_adj2, inner_grad = call(fourth_inner_kernel, (block,) * 2, (whole,) * 2, n_in=9, room=10)(
         wave3, image3, adj3, adj4, lap1, lap2, inject1, along_y, along_z
     )

time: 79.1 us -> 78.7 us (level)
  transfers between devices with their start and end apart: 16 -> 16, of which waited for: 8 -> 7; matrix products, arithmetic and copies ran while one was open for 0% -> 0% of each run, Pallas kernels for 7% -> 8%
where the time goes in v11:
time: 78.7 us; the launch traced here: 78.1 us
  starting transfers between devices  55.9 us (71%)
  Pallas kernels  10.3 us (13%)
  waiting for transfers between devices  8.67 us (11%)
  local copies, waits for them, and re-layouts  1.64 us (2%)
  between operations  1.61 us (2%)
    ppermute x12, starting transfers between devices, swap(): return lax.ppermute(value, axis, pairs)  41 us
    ppermute x2, waiting for transfers between devices, swap_shot(): return lax.ppermute(value, 'shot', pairs)  5.97 us
    ppermute x1, starting transfers between devices, swap_across(): lax.ppermute(value, 'shot', [(i, (i + size // 2) % size) for i in range(s...  5.44 us
    ppermute x2, starting transfers between devices, swap_shot(): return lax.ppermute(value, 'shot', pairs)  4.99 us
    all_to_all x1, starting transfers between devices, local(): column = lax.all_to_all(copies, 'shot', 0, 0)  4.44 us
    ppermute x12, waiting for transfers between devices, swap(): return lax.ppermute(value, axis, pairs)  2.69 us
    unnamed x19, local copies, waits for them, and re-layouts  1.64 us
    pallas_call x1, Pallas kernels, local(): call(third_inner_kernel, (block,) * 3, (whole,) * 2, n_in=11, room=10)  1.64 us
  transfers between devices with their start and end apart: 16, of which 7 were waited for; matrix products, arithmetic and copies ran while one was open for 0% of the time, Pallas kernels for 8%

profile of v11, /device:TPU:24, one launch (start us, length us, event | category | flops | bytes accessed | tf_op | source)
XLA Modules:
  0.0 78.1 jit_solution(8502624342367684837)
XLA Ops:
  0.6 0.9 %copy-done.4 = f32[32,16,128]{2,1,0:T(8,128)S(1)} copy-done((f32[32,16,128]{2,1,0:T(8,128)S(1)}, f32[32,16,128]{2,1,0:T(8,128)}, u32[]{:S(2)}) %copy-start.4) | copy-done | bytes 262168
  1.6 1.0 %shard_map.113 = f32[4,32,16,128]{3,2,1,0:T(8,128)} custom-call(f32[32,16,128]{2,1,0:T(8,128)S(1)} %copy-done.4), custom_call_target="tpu_custom_call" | custom-call | tf_op jit(solution)/shard_map/pallas_call | solution.py:428
  2.6 4.4 %all-to-all-start = ((f32[4,32,16,128]{3,2,1,0:T(8,128)}), f32[4,32,16,128]{3,2,1,0:T(8,128)S(1)}, u32[]{:S(2)}, u32[]{:S(2)}) async-start(f32[4,32,16,128]{3,2,1,0:T(8,128)} %shard_map.113), calls=%async_computation | async-start | bytes 2097152 | tf_op jit(solution)/shard_map/all_to_all | solution.py:436
  7.1 12.2 %collective-permute-start = (f32[16,8,256]{2,1,0:T(8,128)S(1)}, f32[16,8,256]{2,1,0:T(8,128)S(1)}, u32[]{:S(2)}, u32[]{:S(2)}) collective-permute-start(f32[16,8,256]{2,1,0:T(8,128)S(1)} %get-tuple-element.35), channel_id=1, source_target_pairs={{1,2},{2,1},{3,4},{4,3},{5,6},{6,5},{7,8},{8,7},{9,10},{10,9},{11,... | collective-permute-start | bytes 393224 | tf_op jit(solution)/shard_map/ppermute | solution.py:21
  19.4 1.9 %collective-permute-start.1 = (f32[16,8,256]{2,1,0:T(8,128)S(1)}, f32[16,8,256]{2,1,0:T(8,128)S(1)}, u32[]{:S(2)}, u32[]{:S(2)}) collective-permute-start(f32[16,8,256]{2,1,0:T(8,128)S(1)} %get-tuple-element.36), channel_id=1, source_target_pairs={{0,1},{1,0},{2,3},{3,2},{4,5},{5,4},{6,7},{7,6},{8,9},{9,8},{10,11... | collective-permute-start | bytes 393224 | tf_op jit(solution)/shard_map/ppermute | solution.py:21
  21.3 1.9 %collective-permute-start.2 = (f32[4,16,256]{2,1,0:T(8,128)S(1)}, f32[4,16,256]{2,1,0:T(8,128)S(1)}, u32[]{:S(2)}, u32[]{:S(2)}) collective-permute-start(f32[4,16,256]{2,1,0:T(8,128)S(1)} %get-tuple-element.37), channel_id=1, source_target_pairs={{32,64},{64,32},{33,65},{65,33},{34,66},{66,34},{35,67},{67,35},{3... | collective-permute-start | bytes 196616 | tf_op jit(solution)/shard_map/ppermute | solution.py:21
  23.2 1.9 %collective-permute-start.3 = (f32[4,16,256]{2,1,0:T(8,128)S(1)}, f32[4,16,256]{2,1,0:T(8,128)S(1)}, u32[]{:S(2)}, u32[]{:S(2)}) collective-permute-start(f32[4,16,256]{2,1,0:T(8,128)S(1)} %get-tuple-element.38), channel_id=1, source_target_pairs={{0,32},{32,0},{64,96},{96,64},{1,33},{33,1},{65,97},{97,65},{2,34}... | collective-permute-start | bytes 196616 | tf_op jit(solution)/shard_map/ppermute | solution.py:21
  26.2 0.6 copy-done.6
  26.9 0.8 %shard_map.115.inner = f32[32,16,256]{2,1,0:T(8,128)S(1)} custom-call(f32[32,16,256]{2,1,0:T(8,128)S(1)} %bitcast.19, f32[16,8,256]{2,1,0:T(8,128)S(1)} %collective-permute-done.yb, f32[16,8,256]{2,1,0:T(8,128)S(1)} %collective-permute-done.1.ya, f32[32,16,256]{2,1,0:T(8,128)S(1)} %bitcast.22, f32[32,16,256]{2,1,0:T(8,128)S(1)} %bitcast.13, ...), custom_call_target="tpu_custom_call" | custom-call | tf_op jit(solution)/shard_map/pallas_call | solution.py:444
  27.8 0.9 %shard_map.117 = (f32[32,16,256]{2,1,0:T(8,128)S(1)}, f32[32,16,256]{2,1,0:T(8,128)S(1)}, f32[32,16,256]{2,1,0:T(8,128)S(1)}, f32[32,8,256]{2,1,0:T(8,128)S(1)},...) custom-call(s32[1]{0:T(128)S(6)} %copy.23.offsets, ...), custom_call_target="tpu_custom_call" | custom-call | tf_op jit(solution)/shard_map/pallas_call | solution.py:448
  28.7 6.5 %collective-permute-start.4 = (f32[32,8,256]{2,1,0:T(8,128)S(1)}, f32[32,8,256]{2,1,0:T(8,128)S(1)}, u32[]{:S(2)}, u32[]{:S(2)}) collective-permute-start(f32[32,8,256]{2,1,0:T(8,128)S(1)} %get-tuple-element.39), channel_id=1, source_target_pairs={{1,2},{2,1},{3,4},{4,3},{5,6},{6,5},{7,8},{8,7},{9,10},{10,9},{11,... | collective-permute-start | bytes 786440 | tf_op jit(solution)/shard_map/ppermute | solution.py:21
  35.3 1.9 %collective-permute-start.5 = (f32[32,8,256]{2,1,0:T(8,128)S(1)}, f32[32,8,256]{2,1,0:T(8,128)S(1)}, u32[]{:S(2)}, u32[]{:S(2)}) collective-permute-start(f32[32,8,256]{2,1,0:T(8,128)S(1)} %get-tuple-element.40), channel_id=1, source_target_pairs={{0,1},{1,0},{2,3},{3,2},{4,5},{5,4},{6,7},{7,6},{8,9},{9,8},{10,11... | collective-permute-start | bytes 786440 | tf_op jit(solution)/shard_map/ppermute | solution.py:21
  37.2 1.9 %collective-permute-start.6 = (f32[8,16,256]{2,1,0:T(8,128)S(1)}, f32[8,16,256]{2,1,0:T(8,128)S(1)}, u32[]{:S(2)}, u32[]{:S(2)}) collective-permute-start(f32[8,16,256]{2,1,0:T(8,128)S(1)} %get-tuple-element.41), channel_id=1, source_target_pairs={{32,64},{64,32},{33,65},{65,33},{34,66},{66,34},{35,67},{67,35},{3... | collective-permute-start | bytes 393224 | tf_op jit(solution)/shard_map/ppermute | solution.py:21
  39.1 1.9 %collective-permute-start.7 = (f32[8,16,256]{2,1,0:T(8,128)S(1)}, f32[8,16,256]{2,1,0:T(8,128)S(1)}, u32[]{:S(2)}, u32[]{:S(2)}) collective-permute-start(f32[8,16,256]{2,1,0:T(8,128)S(1)} %get-tuple-element.42), channel_id=1, source_target_pairs={{0,32},{32,0},{64,96},{96,64},{1,33},{33,1},{65,97},{97,65},{2,34}... | collective-permute-start | bytes 393224 | tf_op jit(solution)/shard_map/ppermute | solution.py:21
  41.1 0.6 shard_map.118
  41.7 1.6 %shard_map.119 = (f32[32,16,256]{2,1,0:T(8,128)S(1)}, f32[32,16,256]{2,1,0:T(8,128)S(1)}, f32[32,16,256]{2,1,0:T(8,128)S(1)}) custom-call(f32[32,16,256]{2,1,0:T(8,128)S(1)} %bitcast.21, f32[32,16,256]{2,1,0:T(8,128)S(1)} %get-tuple-element.43.wave2, f32[32,16,256]{2,1,0:T(8,128)S(1)} %bitcast.15, f32[32,16,256]{2,1,0:T(8,128)S(1)} %bitcast.24, ...), custom_call_target="tpu_custom_call" | custom-call | tf_op jit(solution)/shard_map/pallas_call | solution.py:461
  43.8 0.9 %shard_map.120 = (f32[32,16,256]{2,1,0:T(8,128)S(1)}, f32[32,16,256]{2,1,0:T(8,128)S(1)}, f32[32,16,256]{2,1,0:T(8,128)S(1)}, f32[32,16,256]{2,1,0:T(8,128)S(1)}...) custom-call(f32[32,8,256]{2,1,0:T(8,128)S(1)} %collective-permute-do, ...), custom_call_target="tpu_custom_call", output_to_operand_aliasing={{0}: (4, {}), {1}: (5, {}), {2}: (6, {})} | custom-call | tf_op jit(solution)/shard_map/pallas_call | solution.py:464
  44.6 4.5 %collective-permute-start.8 = (f32[32,8,256]{2,1,0:T(8,128)S(1)}, f32[32,8,256]{2,1,0:T(8,128)S(1)}, u32[]{:S(2)}, u32[]{:S(2)}) collective-permute-start(f32[32,8,256]{2,1,0:T(8,128)S(1)} %get-tuple-element.53), channel_id=1, source_target_pairs={{1,2},{2,1},{3,4},{4,3},{5,6},{6,5},{7,8},{8,7},{9,10},{10,9},{11,... | collective-permute-start | bytes 786440 | tf_op jit(solution)/shard_map/ppermute | solution.py:21
  49.1 1.9 %collective-permute-start.9 = (f32[32,8,256]{2,1,0:T(8,128)S(1)}, f32[32,8,256]{2,1,0:T(8,128)S(1)}, u32[]{:S(2)}, u32[]{:S(2)}) collective-permute-start(f32[32,8,256]{2,1,0:T(8,128)S(1)} %get-tuple-element.54), channel_id=1, source_target_pairs={{0,1},{1,0},{2,3},{3,2},{4,5},{5,4},{6,7},{7,6},{8,9},{9,8},{10,11... | collective-permute-start | bytes 786440 | tf_op jit(solution)/shard_map/ppermute | solution.py:21
  51.1 2.4 %collective-permute-start.10 = (f32[8,16,256]{2,1,0:T(8,128)S(1)}, f32[8,16,256]{2,1,0:T(8,128)S(1)}, u32[]{:S(2)}, u32[]{:S(2)}) collective-permute-start(f32[8,16,256]{2,1,0:T(8,128)S(1)} %get-tuple-element.55), channel_id=1, source_target_pairs={{32,64},{64,32},{33,65},{65,33},{34,66},{66,34},{35,67},{67,35},{3... | collective-permute-start | bytes 393224 | tf_op jit(solution)/shard_map/ppermute | solution.py:21
  53.5 1.9 %collective-permute-start.11 = (f32[8,16,256]{2,1,0:T(8,128)S(1)}, f32[8,16,256]{2,1,0:T(8,128)S(1)}, u32[]{:S(2)}, u32[]{:S(2)}) collective-permute-start(f32[8,16,256]{2,1,0:T(8,128)S(1)} %get-tuple-element.56), channel_id=1, source_target_pairs={{0,32},{32,0},{64,96},{96,64},{1,33},{33,1},{65,97},{97,65},{2,34}... | collective-permute-start | bytes 393224 | tf_op jit(solution)/shard_map/ppermute | solution.py:21
  55.8 1.6 %shard_map.122 = (f32[32,16,256]{2,1,0:T(8,128)S(1)}, f32[32,16,256]{2,1,0:T(8,128)S(1)}) custom-call(f32[32,16,256]{2,1,0:T(8,128)S(1)} %get-tuple-element.57.wave3, f32[32,16,256]{2,1,0:T(8,128)S(1)} %get-tuple-element.58.image3, f32[32,16,256]{2,1,0:T(8,128)S(1)} %get-tuple-element.59.other.adj3, f32[32,16,256]{2,1,0:T(8,128)S(1)} %bitcast.16, ...), custom_call_target="tpu_custom_call" | custom-call | tf_op jit(solution)/shard_map/pallas_call | solution.py:476
  57.4 1.2 %collective-permute-done.8.yb = f32[32,8,256]{2,1,0:T(8,128)S(1)} collective-permute-done((f32[32,8,256]{2,1,0:T(8,128)S(1)}, f32[32,8,256]{2,1,0:T(8,128)S(1)}, u32[]{:S(2)}, u32[]{:S(2)}) %collective-permute-start.8) | collective-permute-done | bytes 262176 | tf_op jit(solution)/shard_map/ppermute | solution.py:21
  58.6 0.7 collective-permute-done.9.ya
  59.3 0.7 shard_map.123
  60.0 5.4 %collective-permute-start.12 = (f32[32,16,128]{2,1,0:T(8,128)S(1)}, f32[32,16,128]{2,1,0:T(8,128)S(1)}, u32[]{:S(2)}, u32[]{:S(2)}) collective-permute-start(f32[32,16,128]{2,1,0:T(8,128)S(1)} %get-tuple-element.63), channel_id=1, source_target_pairs={{0,256},{128,384},{256,0},{384,128},{1,257},{129,385},{257,1},{385... | collective-permute-start | bytes 786440 | tf_op jit(solution)/shard_map/ppermute | solution.py:34
  65.5 3.1 %collective-permute-start.13 = (f32[32,16,128]{2,1,0:T(8,128)S(1)}, f32[32,16,128]{2,1,0:T(8,128)S(1)}, u32[]{:S(2)}, u32[]{:S(2)}) collective-permute-start(f32[32,16,128]{2,1,0:T(8,128)S(1)} %get-tuple-element.64), channel_id=1, source_target_pairs={{128,256},{256,128},{384,0},{0,384},{129,257},{257,129},{385,1},{1... | collective-permute-start | bytes 786440 | tf_op jit(solution)/shard_map/ppermute | solution.py:29
  68.5 1.9 %collective-permute-start.14 = (f32[32,16,128]{2,1,0:T(8,128)S(1)}, f32[32,16,128]{2,1,0:T(8,128)S(1)}, u32[]{:S(2)}, u32[]{:S(2)}) collective-permute-start(f32[32,16,128]{2,1,0:T(8,128)S(1)} %get-tuple-element.65), channel_id=1, source_target_pairs={{0,128},{128,0},{256,384},{384,256},{1,129},{129,1},{257,385},{385... | collective-permute-start | bytes 786440 | tf_op jit(solution)/shard_map/ppermute | solution.py:29
  70.5 0.9 %shard_map.125 = f32[32,16,256]{2,1,0:T(8,128)} custom-call(f32[32,16,256]{2,1,0:T(8,128)S(1)} %get-tuple-element.66.adj2_in, f32[32,16,256]{2,1,0:T(8,128)S(1)} %get-tuple-element.67.extra), custom_call_target="tpu_custom_call" | custom-call | tf_op jit(solution)/shard_map/pallas_call | solution.py:483
  71.3 5.4 %collective-permute-done.13.b = f32[32,16,128]{2,1,0:T(8,128)S(1)} collective-permute-done((f32[32,16,128]{2,1,0:T(8,128)S(1)}, f32[32,16,128]{2,1,0:T(8,128)S(1)}, u32[]{:S(2)}, u32[]{:S(2)}) %collective-permute-start.13) | collective-permute-done | bytes 262176 | tf_op jit(solution)/shard_map/ppermute | solution.py:29
  76.8 0.5 collective-permute-done.14.a
  77.3 0.8 shard_map.124
  (32 shorter events, 1.5 us)
Async XLA Ops:
  0.6 1.0 %copy-start.4 = (f32[32,16,128]{2,1,0:T(8,128)S(1)}, f32[32,16,128]{2,1,0:T(8,128)}, u32[]{:S(2)}) copy-start(f32[32,16,128]{2,1,0:T(8,128)} %tile.1) | copy-start | bytes 786436
  2.6 4.5 %copy-start.1 = (f32[1,32,16,256]{3,2,1,0:T(8,128)S(1)}, f32[1,32,16,256]{3,2,1,0:T(8,128)}, u32[]{:S(2)}) copy-start(f32[1,32,16,256]{3,2,1,0:T(8,128)} %param.13) | copy-start | bytes 1572868
  2.6 23.6 %copy-start.2 = (f32[1,32,16,256]{3,2,1,0:T(8,128)S(1)}, f32[1,32,16,256]{3,2,1,0:T(8,128)}, u32[]{:S(2)}) copy-start(f32[1,32,16,256]{3,2,1,0:T(8,128)} %param.12) | copy-start | bytes 1572868
  2.6 25.2 %all-to-all-start = ((f32[4,32,16,128]{3,2,1,0:T(8,128)}), f32[4,32,16,128]{3,2,1,0:T(8,128)S(1)}, u32[]{:S(2)}, u32[]{:S(2)}) async-start(f32[4,32,16,128]{3,2,1,0:T(8,128)} %shard_map.113), calls=%async_computation | async-start | bytes 2097152 | tf_op jit(solution)/shard_map/all_to_all | solution.py:436
  7.1 19.2 %copy-start = (f32[1,32,16,256]{3,2,1,0:T(8,128)S(1)}, f32[1,32,16,256]{3,2,1,0:T(8,128)}, u32[]{:S(2)}) copy-start(f32[1,32,16,256]{3,2,1,0:T(8,128)} %param.14) | copy-start | bytes 1572868
  7.1 18.6 %collective-permute-start = (f32[16,8,256]{2,1,0:T(8,128)S(1)}, f32[16,8,256]{2,1,0:T(8,128)S(1)}, u32[]{:S(2)}, u32[]{:S(2)}) collective-permute-start(f32[16,8,256]{2,1,0:T(8,128)S(1)} %get-tuple-element.35), channel_id=1, source_target_pairs={{1,2},{2,1},{3,4},{4,3},{5,6},{6,5},{7,8},{8,7},{9,10},{10,9},{11,... | collective-permute-start | bytes 393224 | tf_op jit(solution)/shard_map/ppermute | solution.py:21
  19.4 6.9 %collective-permute-start.1 = (f32[16,8,256]{2,1,0:T(8,128)S(1)}, f32[16,8,256]{2,1,0:T(8,128)S(1)}, u32[]{:S(2)}, u32[]{:S(2)}) collective-permute-start(f32[16,8,256]{2,1,0:T(8,128)S(1)} %get-tuple-element.36), channel_id=1, source_target_pairs={{0,1},{1,0},{2,3},{3,2},{4,5},{5,4},{6,7},{7,6},{8,9},{9,8},{10,11... | collective-permute-start | bytes 393224 | tf_op jit(solution)/shard_map/ppermute | solution.py:21
  21.3 6.4 %collective-permute-start.2 = (f32[4,16,256]{2,1,0:T(8,128)S(1)}, f32[4,16,256]{2,1,0:T(8,128)S(1)}, u32[]{:S(2)}, u32[]{:S(2)}) collective-permute-start(f32[4,16,256]{2,1,0:T(8,128)S(1)} %get-tuple-element.37), channel_id=1, source_target_pairs={{32,64},{64,32},{33,65},{65,33},{34,66},{66,34},{35,67},{67,35},{3... | collective-permute-start | bytes 196616 | tf_op jit(solution)/shard_map/ppermute | solution.py:21
  23.2 4.5 %collective-permute-start.3 = (f32[4,16,256]{2,1,0:T(8,128)S(1)}, f32[4,16,256]{2,1,0:T(8,128)S(1)}, u32[]{:S(2)}, u32[]{:S(2)}) collective-permute-start(f32[4,16,256]{2,1,0:T(8,128)S(1)} %get-tuple-element.38), channel_id=1, source_target_pairs={{0,32},{32,0},{64,96},{96,64},{1,33},{33,1},{65,97},{97,65},{2,34}... | collective-permute-start | bytes 196616 | tf_op jit(solution)/shard_map/ppermute | solution.py:21
  26.2 0.7 copy-start.6
  26.2 0.7 copy-start.7
  27.8 13.3 %copy-start.8 = (s32[1,256,3]{1,0,2:T(1,128)S(1)}, s32[1,256,3]{1,0,2:T(1,128)}, u32[]{:S(2)}) copy-start(s32[1,256,3]{1,0,2:T(1,128)} %param.18) | copy-start | bytes 9220
  27.8 13.3 %copy-start.5 = (f32[1,256,2]{1,2,0:T(2,128)S(1)}, f32[1,256,2]{1,2,0:T(2,128)}, u32[]{:S(2)}) copy-start(f32[1,256,2]{1,2,0:T(2,128)} %param.19) | copy-start | bytes 6148
  28.7 13.0 %copy-start.3 = (f32[1,32,16,256]{3,2,1,0:T(8,128)S(1)}, f32[1,32,16,256]{3,2,1,0:T(8,128)}, u32[]{:S(2)}) copy-start(f32[1,32,16,256]{3,2,1,0:T(8,128)} %param.15) | copy-start | bytes 1572868
  28.7 14.8 %collective-permute-start.4 = (f32[32,8,256]{2,1,0:T(8,128)S(1)}, f32[32,8,256]{2,1,0:T(8,128)S(1)}, u32[]{:S(2)}, u32[]{:S(2)}) collective-permute-start(f32[32,8,256]{2,1,0:T(8,128)S(1)} %get-tuple-element.39), channel_id=1, source_target_pairs={{1,2},{2,1},{3,4},{4,3},{5,6},{6,5},{7,8},{8,7},{9,10},{10,9},{11,... | collective-permute-start | bytes 786440 | tf_op jit(solution)/shard_map/ppermute | solution.py:21
  35.3 8.5 %collective-permute-start.5 = (f32[32,8,256]{2,1,0:T(8,128)S(1)}, f32[32,8,256]{2,1,0:T(8,128)S(1)}, u32[]{:S(2)}, u32[]{:S(2)}) collective-permute-start(f32[32,8,256]{2,1,0:T(8,128)S(1)} %get-tuple-element.40), channel_id=1, source_target_pairs={{0,1},{1,0},{2,3},{3,2},{4,5},{5,4},{6,7},{7,6},{8,9},{9,8},{10,11... | collective-permute-start | bytes 786440 | tf_op jit(solution)/shard_map/ppermute | solution.py:21
  37.2 6.3 %collective-permute-start.6 = (f32[8,16,256]{2,1,0:T(8,128)S(1)}, f32[8,16,256]{2,1,0:T(8,128)S(1)}, u32[]{:S(2)}, u32[]{:S(2)}) collective-permute-start(f32[8,16,256]{2,1,0:T(8,128)S(1)} %get-tuple-element.41), channel_id=1, source_target_pairs={{32,64},{64,32},{33,65},{65,33},{34,66},{66,34},{35,67},{67,35},{3... | collective-permute-start | bytes 393224 | tf_op jit(solution)/shard_map/ppermute | solution.py:21
  39.1 4.4 %collective-permute-start.7 = (f32[8,16,256]{2,1,0:T(8,128)S(1)}, f32[8,16,256]{2,1,0:T(8,128)S(1)}, u32[]{:S(2)}, u32[]{:S(2)}) collective-permute-start(f32[8,16,256]{2,1,0:T(8,128)S(1)} %get-tuple-element.42), channel_id=1, source_target_pairs={{0,32},{32,0},{64,96},{96,64},{1,33},{33,1},{65,97},{97,65},{2,34}... | collective-permute-start | bytes 393224 | tf_op jit(solution)/shard_map/ppermute | solution.py:21
  44.6 14.0 %collective-permute-start.8 = (f32[32,8,256]{2,1,0:T(8,128)S(1)}, f32[32,8,256]{2,1,0:T(8,128)S(1)}, u32[]{:S(2)}, u32[]{:S(2)}) collective-permute-start(f32[32,8,256]{2,1,0:T(8,128)S(1)} %get-tuple-element.53), channel_id=1, source_target_pairs={{1,2},{2,1},{3,4},{4,3},{5,6},{6,5},{7,8},{8,7},{9,10},{10,9},{11,... | collective-permute-start | bytes 786440 | tf_op jit(solution)/shard_map/ppermute | solution.py:21
  49.1 10.2 %collective-permute-start.9 = (f32[32,8,256]{2,1,0:T(8,128)S(1)}, f32[32,8,256]{2,1,0:T(8,128)S(1)}, u32[]{:S(2)}, u32[]{:S(2)}) collective-permute-start(f32[32,8,256]{2,1,0:T(8,128)S(1)} %get-tuple-element.54), channel_id=1, source_target_pairs={{0,1},{1,0},{2,3},{3,2},{4,5},{5,4},{6,7},{7,6},{8,9},{9,8},{10,11... | collective-permute-start | bytes 786440 | tf_op jit(solution)/shard_map/ppermute | solution.py:21
  51.1 6.4 %collective-permute-start.10 = (f32[8,16,256]{2,1,0:T(8,128)S(1)}, f32[8,16,256]{2,1,0:T(8,128)S(1)}, u32[]{:S(2)}, u32[]{:S(2)}) collective-permute-start(f32[8,16,256]{2,1,0:T(8,128)S(1)} %get-tuple-element.55), channel_id=1, source_target_pairs={{32,64},{64,32},{33,65},{65,33},{34,66},{66,34},{35,67},{67,35},{3... | collective-permute-start | bytes 393224 | tf_op jit(solution)/shard_map/ppermute | solution.py:21
  53.5 3.9 %collective-permute-start.11 = (f32[8,16,256]{2,1,0:T(8,128)S(1)}, f32[8,16,256]{2,1,0:T(8,128)S(1)}, u32[]{:S(2)}, u32[]{:S(2)}) collective-permute-start(f32[8,16,256]{2,1,0:T(8,128)S(1)} %get-tuple-element.56), channel_id=1, source_target_pairs={{0,32},{32,0},{64,96},{96,64},{1,33},{33,1},{65,97},{97,65},{2,34}... | collective-permute-start | bytes 393224 | tf_op jit(solution)/shard_map/ppermute | solution.py:21
  60.0 11.3 %collective-permute-start.12 = (f32[32,16,128]{2,1,0:T(8,128)S(1)}, f32[32,16,128]{2,1,0:T(8,128)S(1)}, u32[]{:S(2)}, u32[]{:S(2)}) collective-permute-start(f32[32,16,128]{2,1,0:T(8,128)S(1)} %get-tuple-element.63), channel_id=1, source_target_pairs={{0,256},{128,384},{256,0},{384,128},{1,257},{129,385},{257,1},{385... | collective-permute-start | bytes 786440 | tf_op jit(solution)/shard_map/ppermute | solution.py:34
  65.5 11.3 %collective-permute-start.13 = (f32[32,16,128]{2,1,0:T(8,128)S(1)}, f32[32,16,128]{2,1,0:T(8,128)S(1)}, u32[]{:S(2)}, u32[]{:S(2)}) collective-permute-start(f32[32,16,128]{2,1,0:T(8,128)S(1)} %get-tuple-element.64), channel_id=1, source_target_pairs={{128,256},{256,128},{384,0},{0,384},{129,257},{257,129},{385,1},{1... | collective-permute-start | bytes 786440 | tf_op jit(solution)/shard_map/ppermute | solution.py:29
  68.5 8.8 %collective-permute-start.14 = (f32[32,16,128]{2,1,0:T(8,128)S(1)}, f32[32,16,128]{2,1,0:T(8,128)S(1)}, u32[]{:S(2)}, u32[]{:S(2)}) collective-permute-start(f32[32,16,128]{2,1,0:T(8,128)S(1)} %get-tuple-element.65), channel_id=1, source_target_pairs={{0,128},{128,0},{256,384},{384,256},{1,129},{129,1},{257,385},{385... | collective-permute-start | bytes 786440 | tf_op jit(solution)/shard_map/ppermute | solution.py:29
